TPU v7x, 32 devices: a whole 2x2x4 slice. The times are simulated.
32 devices in a mesh: dp: 4 (over y, x), ctx: 8 (over z, core).
Axes of the slice: x: 2, y: 2, z: 4, core: 2. Of those that a mesh axis runs over, the one named last changes fastest.
Arguments:
- tokens: bfloat16 [8, 1536, 2304], P('dp', 'ctx'), may hold values from -7 to 7
- span_start: int32 [8, 2], P('dp'), may hold values from 0 to 1408, as said below
- span_len: int32 [8, 2], P('dp'), may hold values from 128 to 256, as said below
- query_weight: bfloat16 [2048, 2304], P('ctx'), may hold values from -1 to 1
- key_weight: bfloat16 [1024, 2304], P('ctx'), may hold values from -1 to 1
- value_weight: bfloat16 [1024, 2304], P('ctx'), may hold values from -0.125 to 0.125
- output_weight: bfloat16 [2048, 2304], P('ctx'), may hold values from -0.125 to 0.125
- gate_weight: bfloat16 [9216, 2304], P('ctx'), may hold values from -0.125 to 0.125
- up_weight: bfloat16 [9216, 2304], P('ctx'), may hold values from -0.125 to 0.125
- down_weight: bfloat16 [9216, 2304], P('ctx'), may hold values from -0.0625 to 0.0625
- inbound_gain: bfloat16 [2304], P('ctx'), may hold values from 0.099609375 to 1.8984375
- attended_gain: bfloat16 [2304], P('ctx'), may hold values from 0.099609375 to 1.8984375
- prefeed_gain: bfloat16 [2304], P('ctx'), may hold values from 0.099609375 to 1.8984375
- postfeed_gain: bfloat16 [2304], P('ctx'), may hold values from 0.099609375 to 1.8984375
- cotangent: bfloat16 [8, 1536, 2304], P('dp', 'ctx'), may hold values from -6 to 6
Outputs:
- layer_output: bfloat16 [8, 1536, 2304], P('dp', 'ctx')
- tokens_grad: bfloat16 [8, 1536, 2304], P('dp', 'ctx')
- query_grad: float32 [2048, 2304], P('ctx')
- key_grad: float32 [1024, 2304], P('ctx')
- value_grad: float32 [1024, 2304], P('ctx')
- output_grad: float32 [2048, 2304], P('ctx')
- gate_grad: float32 [9216, 2304], P('ctx')
- up_grad: float32 [9216, 2304], P('ctx')
- down_grad: float32 [9216, 2304], P('ctx')
- inbound_grad: float32 [2304], P('ctx')
- attended_grad: float32 [2304], P('ctx')
- prefeed_grad: float32 [2304], P('ctx')
- postfeed_grad: float32 [2304], P('ctx')
Inputs may be any that keep to these rules, and one draw needn't show every extreme that they name: `span_start`: in each sequence the 2 spans lie in order without intersection; span s lies within positions s * 768 to (s + 1) * 768 - 1. `span_len`: one span of each sequence has exactly 256 tokens.
All inputs are finite; a program needn't handle non-finite values.
Results may differ from a plain program's by a relative error of at most 0.025.
Values may be sent and summed in bfloat16 or wider, within the bound.
No kernel may reach another device: no remote copies, remote signals or barrier semaphores. Data moves between devices by JAX's collectives and lax.ppermute only.
A program may use at most 576 MiB of HBM per device.

v0:
```python
import jax
import jax.numpy as jnp
from jax import lax
from jax.sharding import PartitionSpec as P

HEADS = 8
KV_HEADS = 4
HEAD_DIM = 256


epsilon = 1e-06
soft_cap = 50.0
masked_score = -1e30
rope_base = 10000.0


def root_norm(values, gain_vector):
    return (
        values
        * lax.rsqrt(jnp.mean(values * values, axis=-1, keepdims=True) + epsilon)
        * gain_vector
    )


def contract_last(left_side, right_side):
    return lax.dot_general(
        left_side, right_side, (((1,), (1,)), ((), ())), preferred_element_type=jnp.float32
    )


def contract_first(left_side, right_side):
    return lax.dot_general(
        left_side, right_side, (((0,), (0,)), ((), ())), preferred_element_type=jnp.float32
    )


def matmul(left_side, right_side):
    return jnp.dot(left_side, right_side, preferred_element_type=jnp.float32)


def rope_tables(places):
    half_width = HEAD_DIM // 2
    inverse = rope_base ** (-(jnp.arange(half_width, dtype=jnp.float32) * 2.0 / HEAD_DIM))
    angles = places.astype(jnp.float32)[:, None] * inverse[None, :]
    return (jnp.cos(angles)[None, :, None, :], jnp.sin(angles)[None, :, None, :])


def rotate(head_vectors, cosine, sine_table):
    half_width = HEAD_DIM // 2
    first_half = head_vectors[..., :half_width]
    second_half = head_vectors[..., half_width:]
    return jnp.concatenate(
        [
            first_half * cosine - second_half * sine_table,
            second_half * cosine + first_half * sine_table,
        ],
        axis=-1,
    )


def span_labels(places, starts, lengths):
    inside = (places[:, None] >= starts[None, :]) & (places[:, None] < (starts + lengths)[None, :])
    labels = jnp.arange(1, starts.shape[0] + 1, dtype=jnp.int32)
    return jnp.sum(jnp.where(inside, labels[None, :], 0), axis=1) - 1


def visible(query_place, key_place, starts, lengths):
    query_span = span_labels(query_place, starts, lengths)
    key_span = span_labels(key_place, starts, lengths)
    causal = key_place[None, :] <= query_place[:, None]
    shared = (query_span[:, None] == key_span[None, :]) & (query_span[:, None] >= 0)
    return causal | shared


def gelu_product(gate_value, up_value):
    return jax.nn.gelu(gate_value, approximate=True) * up_value


def gelu_backward(gate_value, up_value, product_grad):
    unused, backward = jax.vjp(gelu_product, gate_value, up_value)
    gate_back, up_back = backward(product_grad)
    return (gate_back.astype(jnp.bfloat16), up_back.astype(jnp.bfloat16))


def capped_scores(query_heads, key_heads):
    raw_scores = jnp.einsum(
        "ikgd,jkd->kgij", query_heads, key_heads, preferred_element_type=jnp.float32
    )
    return soft_cap * jnp.tanh(raw_scores / soft_cap)


def attend_forward(query_heads, key_heads, value_heads, allowed):
    capped = capped_scores(query_heads, key_heads)
    masked = jnp.where(allowed, capped, masked_score)
    row_peak = jnp.max(masked, axis=-1, keepdims=True)
    unscaled = jnp.where(allowed, jnp.exp(masked - row_peak), 0.0)
    row_totals = jnp.sum(unscaled, axis=-1, keepdims=True)
    softmax_low = (unscaled / row_totals).astype(jnp.bfloat16)
    attended = jnp.einsum(
        "kgij,jkd->ikgd", softmax_low, value_heads, preferred_element_type=jnp.float32
    )
    return (attended, row_peak + jnp.log(row_totals))


def attend_backward(query_heads, key_heads, value_heads, allowed, log_total, mixed_grad):
    capped = capped_scores(query_heads, key_heads)
    softmax_rows = jnp.exp(jnp.where(allowed, capped - log_total, masked_score))
    row_grad = jnp.einsum(
        "ikgd,jkd->kgij", mixed_grad, value_heads, preferred_element_type=jnp.float32
    )
    row_inner = jnp.sum(softmax_rows * row_grad, axis=-1, keepdims=True)
    squashed = capped / soft_cap
    score_grad = (softmax_rows * (row_grad - row_inner) * (1.0 - squashed * squashed)).astype(
        jnp.bfloat16
    )
    query_rot = jnp.einsum(
        "kgij,jkd->ikgd", score_grad, key_heads, preferred_element_type=jnp.float32
    )
    key_rot = jnp.einsum(
        "kgij,ikgd->jkd", score_grad, query_heads, preferred_element_type=jnp.float32
    )
    value_sum = jnp.einsum(
        "kgij,ikgd->jkd",
        softmax_rows.astype(jnp.bfloat16),
        mixed_grad,
        preferred_element_type=jnp.float32,
    )
    return (query_rot, key_rot, value_sum)


def scatter_rows(left_side, right_side):
    return lax.psum_scatter(
        contract_first(left_side, right_side).astype(jnp.bfloat16),
        "ctx",
        scatter_dimension=0,
        tiled=True,
    ).astype(jnp.float32)


def on_device(
    tokens,
    span_start,
    span_len,
    query_weight,
    key_weight,
    value_weight,
    output_weight,
    gate_weight,
    up_weight,
    down_weight,
    inbound_gain,
    attended_gain,
    prefeed_gain,
    postfeed_gain,
    cotangent,
):
    seq_count, local_len, model_width = tokens.shape
    row_count = seq_count * local_len
    full_len = local_len * lax.axis_size("ctx")
    group_size = HEADS // KV_HEADS
    query_width = HEADS * HEAD_DIM
    key_width = KV_HEADS * HEAD_DIM
    query_scale = HEAD_DIM ** (-0.5)
    (
        query_full,
        key_full,
        value_full,
        output_full,
        inbound_full,
        attended_full,
        prefeed_full,
        postfeed_full,
    ) = (
        lax.all_gather(query_weight, "ctx", axis=0, tiled=True),
        lax.all_gather(key_weight, "ctx", axis=0, tiled=True),
        lax.all_gather(value_weight, "ctx", axis=0, tiled=True),
        lax.all_gather(output_weight, "ctx", axis=0, tiled=True),
        lax.all_gather(inbound_gain, "ctx", axis=0, tiled=True),
        lax.all_gather(attended_gain, "ctx", axis=0, tiled=True),
        lax.all_gather(prefeed_gain, "ctx", axis=0, tiled=True),
        lax.all_gather(postfeed_gain, "ctx", axis=0, tiled=True),
    )
    query_place = lax.axis_index("ctx") * local_len + jnp.arange(local_len, dtype=jnp.int32)
    key_place = jnp.arange(full_len, dtype=jnp.int32)
    cosine, sine_table = rope_tables(query_place)
    residual = tokens.reshape(row_count, model_width).astype(jnp.float32)
    normed_in, inbound_back = jax.vjp(root_norm, residual, inbound_full.astype(jnp.float32))
    hidden_in = normed_in.astype(jnp.bfloat16)
    queries_raw = contract_last(hidden_in, query_full)
    keys_raw = contract_last(hidden_in, key_full)
    values_raw = contract_last(hidden_in, value_full)
    query_low = (
        rotate(queries_raw.reshape(seq_count, local_len, HEADS, HEAD_DIM), cosine, sine_table)
        * query_scale
    ).astype(jnp.bfloat16)
    key_low = (
        rotate(keys_raw.reshape(seq_count, local_len, KV_HEADS, HEAD_DIM), cosine, sine_table)
        .astype(jnp.bfloat16)
        .reshape(seq_count, local_len, key_width)
    )
    value_low = values_raw.astype(jnp.bfloat16).reshape(seq_count, local_len, key_width)
    key_all, value_all = (
        lax.all_gather(key_low, "ctx", axis=1, tiled=True),
        lax.all_gather(value_low, "ctx", axis=1, tiled=True),
    )

    def forward_one(seq_items):
        seq_query, seq_key, seq_value, starts, lengths = seq_items
        allowed = visible(query_place, key_place, starts, lengths)
        return attend_forward(
            seq_query.reshape(local_len, KV_HEADS, group_size, HEAD_DIM),
            seq_key.reshape(full_len, KV_HEADS, HEAD_DIM),
            seq_value.reshape(full_len, KV_HEADS, HEAD_DIM),
            allowed,
        )

    mixed_all, log_total = lax.map(
        forward_one, (query_low, key_all, value_all, span_start, span_len)
    )
    attended = mixed_all.reshape(row_count, query_width).astype(jnp.bfloat16)
    branch = matmul(attended, output_full)
    branch_norm, attended_back = jax.vjp(root_norm, branch, attended_full.astype(jnp.float32))
    middle = residual + branch_norm
    normed_ff, prefeed_back = jax.vjp(root_norm, middle, prefeed_full.astype(jnp.float32))
    hidden_ff = normed_ff.astype(jnp.bfloat16)
    gate_rows = lax.all_gather(gate_weight, "ctx", axis=0, tiled=True)
    up_rows = lax.all_gather(up_weight, "ctx", axis=0, tiled=True)
    down_rows = lax.all_gather(down_weight, "ctx", axis=0, tiled=True)
    gate_part = contract_last(hidden_ff, gate_rows)
    up_part = contract_last(hidden_ff, up_rows)
    product_part = gelu_product(gate_part, up_part).astype(jnp.bfloat16)
    feed_sum = matmul(product_part, down_rows)
    feed_norm, postfeed_back = jax.vjp(root_norm, feed_sum, postfeed_full.astype(jnp.float32))
    layer_output = (
        (middle + feed_norm).astype(jnp.bfloat16).reshape(seq_count, local_len, model_width)
    )
    upstream = cotangent.reshape(row_count, model_width).astype(jnp.float32)
    feed_grad, postfeed_term = postfeed_back(upstream)
    feed_low = feed_grad.astype(jnp.bfloat16)
    gate_rows = lax.all_gather(gate_weight, "ctx", axis=0, tiled=True)
    up_rows = lax.all_gather(up_weight, "ctx", axis=0, tiled=True)
    down_rows = lax.all_gather(down_weight, "ctx", axis=0, tiled=True)
    product_grad = contract_last(feed_low, down_rows)
    gate_back, up_back = gelu_backward(gate_part, up_part, product_grad)
    hidden_grad = matmul(gate_back, gate_rows) + matmul(up_back, up_rows)
    gate_shard = scatter_rows(gate_back, hidden_ff)
    up_shard = scatter_rows(up_back, hidden_ff)
    down_shard = scatter_rows(product_part, feed_low)
    middle_term, prefeed_term = prefeed_back(hidden_grad)
    middle_grad = upstream + middle_term
    branch_grad, attended_term = attended_back(middle_grad)
    branch_low = branch_grad.astype(jnp.bfloat16)
    mixed_grad = contract_last(branch_low, output_full).astype(jnp.bfloat16)
    output_term = contract_first(attended, branch_low)

    def backward_one(seq_items):
        seq_query, seq_key, seq_value, starts, lengths, seq_total, seq_grad = seq_items
        allowed = visible(query_place, key_place, starts, lengths)
        return attend_backward(
            seq_query.reshape(local_len, KV_HEADS, group_size, HEAD_DIM),
            seq_key.reshape(full_len, KV_HEADS, HEAD_DIM),
            seq_value.reshape(full_len, KV_HEADS, HEAD_DIM),
            allowed,
            seq_total,
            seq_grad,
        )

    query_rot, key_parts, value_parts = lax.map(
        backward_one,
        (
            query_low,
            key_all,
            value_all,
            span_start,
            span_len,
            log_total,
            mixed_grad.reshape(seq_count, local_len, KV_HEADS, group_size, HEAD_DIM),
        ),
    )
    key_sums, value_sums = (
        lax.psum_scatter(
            key_parts.reshape(seq_count, full_len, key_width).astype(jnp.bfloat16),
            "ctx",
            scatter_dimension=1,
            tiled=True,
        ).astype(jnp.float32),
        lax.psum_scatter(
            value_parts.reshape(seq_count, full_len, key_width).astype(jnp.bfloat16),
            "ctx",
            scatter_dimension=1,
            tiled=True,
        ).astype(jnp.float32),
    )
    query_back = (
        (
            rotate(query_rot.reshape(seq_count, local_len, HEADS, HEAD_DIM), cosine, -sine_table)
            * query_scale
        )
        .astype(jnp.bfloat16)
        .reshape(row_count, query_width)
    )
    key_back = (
        rotate(key_sums.reshape(seq_count, local_len, KV_HEADS, HEAD_DIM), cosine, -sine_table)
        .astype(jnp.bfloat16)
        .reshape(row_count, key_width)
    )
    value_back = value_sums.astype(jnp.bfloat16).reshape(row_count, key_width)
    hidden_in_grad = (
        matmul(query_back, query_full) + matmul(key_back, key_full) + matmul(value_back, value_full)
    )
    token_term, inbound_term = inbound_back(hidden_in_grad)
    tokens_grad = (
        (middle_grad + token_term).astype(jnp.bfloat16).reshape(seq_count, local_len, model_width)
    )
    query_term = contract_first(query_back, hidden_in)
    key_term = contract_first(key_back, hidden_in)
    value_term = contract_first(value_back, hidden_in)
    (
        query_part,
        key_part,
        value_part,
        output_part,
        inbound_part,
        attended_part,
        prefeed_part,
        postfeed_part,
    ) = (
        lax.psum_scatter(
            query_term.astype(jnp.bfloat16), "ctx", scatter_dimension=0, tiled=True
        ).astype(jnp.float32),
        lax.psum_scatter(
            key_term.astype(jnp.bfloat16), "ctx", scatter_dimension=0, tiled=True
        ).astype(jnp.float32),
        lax.psum_scatter(
            value_term.astype(jnp.bfloat16), "ctx", scatter_dimension=0, tiled=True
        ).astype(jnp.float32),
        lax.psum_scatter(
            output_term.astype(jnp.bfloat16), "ctx", scatter_dimension=0, tiled=True
        ).astype(jnp.float32),
        lax.psum_scatter(
            inbound_term.astype(jnp.bfloat16), "ctx", scatter_dimension=0, tiled=True
        ).astype(jnp.float32),
        lax.psum_scatter(
            attended_term.astype(jnp.bfloat16), "ctx", scatter_dimension=0, tiled=True
        ).astype(jnp.float32),
        lax.psum_scatter(
            prefeed_term.astype(jnp.bfloat16), "ctx", scatter_dimension=0, tiled=True
        ).astype(jnp.float32),
        lax.psum_scatter(
            postfeed_term.astype(jnp.bfloat16), "ctx", scatter_dimension=0, tiled=True
        ).astype(jnp.float32),
    )
    summed = (
        lax.psum(query_part.astype(jnp.bfloat16), "dp").astype(jnp.float32),
        lax.psum(key_part.astype(jnp.bfloat16), "dp").astype(jnp.float32),
        lax.psum(value_part.astype(jnp.bfloat16), "dp").astype(jnp.float32),
        lax.psum(output_part.astype(jnp.bfloat16), "dp").astype(jnp.float32),
        lax.psum(gate_shard.astype(jnp.bfloat16), "dp").astype(jnp.float32),
        lax.psum(up_shard.astype(jnp.bfloat16), "dp").astype(jnp.float32),
        lax.psum(down_shard.astype(jnp.bfloat16), "dp").astype(jnp.float32),
        lax.psum(inbound_part.astype(jnp.bfloat16), "dp").astype(jnp.float32),
        lax.psum(attended_part.astype(jnp.bfloat16), "dp").astype(jnp.float32),
        lax.psum(prefeed_part.astype(jnp.bfloat16), "dp").astype(jnp.float32),
        lax.psum(postfeed_part.astype(jnp.bfloat16), "dp").astype(jnp.float32),
    )
    return (
        layer_output,
        tokens_grad,
        summed[0],
        summed[1],
        summed[2],
        summed[3],
        summed[4],
        summed[5],
        summed[6],
        summed[7],
        summed[8],
        summed[9],
        summed[10],
    )


def solution(mesh):
    return jax.shard_map(
        on_device,
        mesh=mesh,
        in_specs=(
            P("dp", "ctx", None),
            P("dp", None),
            P("dp", None),
            P("ctx", None),
            P("ctx", None),
            P("ctx", None),
            P("ctx", None),
            P("ctx", None),
            P("ctx", None),
            P("ctx", None),
            P("ctx"),
            P("ctx"),
            P("ctx"),
            P("ctx"),
            P("dp", "ctx", None),
        ),
        out_specs=(
            P("dp", "ctx", None),
            P("dp", "ctx", None),
            P("ctx", None),
            P("ctx", None),
            P("ctx", None),
            P("ctx", None),
            P("ctx", None),
            P("ctx", None),
            P("ctx", None),
            P("ctx"),
            P("ctx"),
            P("ctx"),
            P("ctx"),
        ),
        check_vma=False,
    )
```

profile of v0, /device:TPU:0, one launch (start us, length us, event | category | flops | bytes accessed | tf_op | source)
XLA Modules:
  0.0 3861.1 jit_solution(18176509292947363322)
XLA Ops:
  15.0 32.2 all-reduce.9
  49.3 15.1 all-gather.10.cloned.1.call-done
  73.4 43.3 %all-gather.14.cloned.1.call-done = bf16[1024,2304]{1,0:T(8,128)(2,1)} async-done(((bf16[128,2304]{1,0:T(8,128)(2,1)}), bf16[1024,2304]{1,0:T(8,128)(2,1)}) %all-gather.14.cloned.1.call-update) | async-done | bytes 4718608 | tf_op jit(solution)/shard_map/all_gather | solution.py:175
  128.3 79.6 %all-gather.18.cloned.1.call-done = bf16[2048,2304]{1,0:T(8,128)(2,1)} async-done(((bf16[256,2304]{1,0:T(8,128)(2,1)}), bf16[2048,2304]{1,0:T(8,128)(2,1)}) %all-gather.18.cloned.1.call-update) | async-done | bytes 9437200 | tf_op jit(solution)/shard_map/all_gather | solution.py:174
  207.9 7.0 fusion.102
  215.8 57.5 %all-gather.12.cloned.1.call-done = bf16[2,1536,1024]{2,0,1:T(2,128)(2,1)} async-done(((bf16[2,192,1024]{2,0,1:T(2,128)(2,1)}), bf16[2,1536,1024]{2,0,1:T(2,128)(2,1)}) %all-gather.12.cloned.1.call-update) | async-done | bytes 6291472 | tf_op jit(solution)/shard_map/all_gather | solution.py:204
  273.2 16.3 copy.73
  289.5 49.1 %all-gather.16.cloned.1.call-done = bf16[2,1536,1024]{2,1,0:T(8,128)(2,1)} async-done(((bf16[2,192,1024]{2,1,0:T(8,128)(2,1)}), bf16[2,1536,1024]{2,1,0:T(8,128)(2,1)}) %all-gather.16.cloned.1.call-update) | async-done | bytes 6291472 | tf_op jit(solution)/shard_map/all_gather | solution.py:203
  338.7 8.7 copy.74
  347.4 24.5 while.38
  377.6 52.0 %all-gather.20.cloned.1.call-done = bf16[2048,2304]{1,0:T(8,128)(2,1)} async-done(((bf16[256,2304]{1,0:T(8,128)(2,1)}), bf16[2048,2304]{1,0:T(8,128)(2,1)}) %all-gather.20.cloned.1.call-update) | async-done | bytes 9437200 | tf_op jit(solution)/shard_map/all_gather | solution.py:177
  429.6 7.2 multiply_reduce_fusion.6
  441.5 351.4 %all-gather.22.cloned.1.call-done = bf16[9216,2304]{1,0:T(8,128)(2,1)} async-done(((bf16[1152,2304]{1,0:T(8,128)(2,1)}), bf16[9216,2304]{1,0:T(8,128)(2,1)}) %all-gather.22.cloned.1.call-update) | async-done | bytes 42467344 | tf_op jit(solution)/shard_map/all_gather | solution.py:226
  792.9 30.1 fusion.115
  823.0 333.3 %all-gather.24.cloned.1.call-done = bf16[9216,2304]{1,0:T(8,128)(2,1)} async-done(((bf16[1152,2304]{1,0:T(8,128)(2,1)}), bf16[9216,2304]{1,0:T(8,128)(2,1)}) %all-gather.24.cloned.1.call-update) | async-done | bytes 42467344 | tf_op jit(solution)/shard_map/all_gather | solution.py:227
  1156.3 33.2 multiply_convert_fusion.1
  1189.5 330.2 %all-gather.26.cloned.1.call-done = bf16[9216,2304]{1,0:T(8,128)(2,1)} async-done(((bf16[1152,2304]{1,0:T(8,128)(2,1)}), bf16[9216,2304]{1,0:T(8,128)(2,1)}) %all-gather.26.cloned.1.call-update) | async-done | bytes 42467344 | tf_op jit(solution)/shard_map/all_gather | solution.py:228
  1519.7 24.5 multiply_reduce_fusion.4
  1549.2 35.4 multiply_convert_fusion
  1584.6 25.6 fusion.116
  1610.3 26.6 multiply_reduce_fusion
  1652.3 128.7 %while.39 = (s32[]{:T(128)}, f32[2,192,4,2,256]{4,1,3,2,0:T(8,128)}, bf16[2,1536,4,256]{1,3,2,0:T(8,128)(2,1)}, bf16[2,1536,4,256]{1,3,2,0:T(8,128)(2,1)}, bf16[...) while((s32[]{:T(128)}, ...), condition=%wide.region_17.18_spmd.clone.clone.clone, body=%wide.region_13.17_spmd.clone.clone.sunk.clone | while | flops 6123576832 | bytes 170148624 | solution.py:268
  1667.5 16.5 bitcast_dynamic-update-slice_fusion.17
  1683.9 23.6 bitcast_dynamic-update-slice_fusion.18
  1707.6 9.0 bitcast_dynamic-update-slice_fusion.19
  1731.6 16.5 bitcast_dynamic-update-slice_fusion.17
  1748.1 23.6 bitcast_dynamic-update-slice_fusion.18
  1771.6 9.2 bitcast_dynamic-update-slice_fusion.19
  1781.0 8.6 copy.80
  1789.7 8.7 copy.84
  1803.8 7.5 convolution_convert_fusion.4
  1812.8 9.3 convolution_convert_fusion.3
  1822.2 36.0 reduce-scatter.10.cloned.1.call-done
  1866.7 62.0 %reduce-scatter.12.cloned.1.call-done = bf16[2,192,1024]{2,1,0:T(8,128)(2,1)} async-done(((bf16[2,1536,1024]{2,1,0:T(8,128)(2,1)}), bf16[2,192,1024]{2,1,0:T(8,128)(2,1)}) %reduce-scatter.12.cloned.1.call-update) | async-done | bytes 786448 | tf_op jit(solution)/shard_map/reduce_scatter | solution.py:287
  1936.7 33.3 convolution_convert_fusion.2
  1970.0 33.8 convolution_convert_fusion.1
  2005.3 33.5 convolution_convert_fusion
  2038.9 91.2 %reduce-scatter.20.cloned.1.call-done = bf16[256,2304]{1,0:T(8,128)(2,1)} async-done(((bf16[2048,2304]{1,0:T(8,128)(2,1)}), bf16[256,2304]{1,0:T(8,128)(2,1)}) %reduce-scatter.20.cloned.1.call-update) | async-done | bytes 1179664 | tf_op jit(solution)/shard_map/reduce_scatter | solution.py:337
  2130.1 55.5 %reduce-scatter.16.cloned.1.call-done = bf16[128,2304]{1,0:T(8,128)(2,1)} async-done(((bf16[1024,2304]{1,0:T(8,128)(2,1)}), bf16[128,2304]{1,0:T(8,128)(2,1)}) %reduce-scatter.16.cloned.1.call-update) | async-done | bytes 589840 | tf_op jit(solution)/shard_map/reduce_scatter | solution.py:331
  2185.6 55.5 %reduce-scatter.18.cloned.1.call-done = bf16[128,2304]{1,0:T(8,128)(2,1)} async-done(((bf16[1024,2304]{1,0:T(8,128)(2,1)}), bf16[128,2304]{1,0:T(8,128)(2,1)}) %reduce-scatter.18.cloned.1.call-update) | async-done | bytes 589840 | tf_op jit(solution)/shard_map/reduce_scatter | solution.py:334
  2241.1 409.9 %reduce-scatter.22.cloned.1.call-done = bf16[1152,2304]{1,0:T(8,128)(2,1)} async-done(((bf16[9216,2304]{1,0:T(8,128)(2,1)}), bf16[1152,2304]{1,0:T(8,128)(2,1)}) %reduce-scatter.22.cloned.1.call-update) | async-done | bytes 5308432 | tf_op jit(solution)/shard_map/reduce_scatter | solution.py:132
  2651.0 410.0 %reduce-scatter.24.cloned.1.call-done = bf16[1152,2304]{1,0:T(8,128)(2,1)} async-done(((bf16[9216,2304]{1,0:T(8,128)(2,1)}), bf16[1152,2304]{1,0:T(8,128)(2,1)}) %reduce-scatter.24.cloned.1.call-update) | async-done | bytes 5308432 | tf_op jit(solution)/shard_map/reduce_scatter | solution.py:132
  3061.0 409.9 %reduce-scatter.26.cloned.1.call-done = bf16[1152,2304]{1,0:T(8,128)(2,1)} async-done(((bf16[9216,2304]{1,0:T(8,128)(2,1)}), bf16[1152,2304]{1,0:T(8,128)(2,1)}) %reduce-scatter.26.cloned.1.call-update) | async-done | bytes 5308432 | tf_op jit(solution)/shard_map/reduce_scatter | solution.py:132
  3472.3 6.9 fusion.117
  3485.0 6.4 fusion.95
  3491.4 26.0 all-reduce.8
  3517.7 10.1 all-reduce.10
  3535.9 295.7 %all-reduce.14.cloned.1.call-done = (bf16[256,2304]{1,0:T(8,128)(2,1)}, bf16[128,2304]{1,0:T(8,128)(2,1)}, bf16[128,2304]{1,0:T(8,128)(2,1)}, bf16[256,2304]{1,0...) async-done(((bf16[256,2304]{1,0:T(8,128)(2,1)}, bf16[128,2304]{1,0:T(8,128)(2,1)}, bf16[128,2304]{1,0:T(8,128)(2,1)}, ...) | async-done | bytes 19464208 | tf_op jit(solution)/shard_map/psum | solution.py:354
  (331 shorter events, 177.3 us)
Async XLA Ops:
  7.2 40.0 %copy-start.5 = (bf16[2,192,2304]{2,1,0:T(8,128)(2,1)S(1)}, bf16[2,192,2304]{2,1,0:T(8,128)(2,1)}, u32[]{:S(2)}) copy-start(bf16[2,192,2304]{2,1,0:T(8,128)(2,1)} %param.19) | copy-start | bytes 5308420
  7.2 57.3 %all-gather.10.cloned.1.call-start = ((), (), s32[]{:S(2)}) async-start(), calls=%async_computation.9 | async-start | bytes 5308416 | tf_op jit(solution)/shard_map/all_gather | solution.py:176
  7.9 108.8 %all-gather.14.cloned.1.call-start = ((), (), s32[]{:S(2)}) async-start(), calls=%async_computation.11 | async-start | bytes 5308416 | tf_op jit(solution)/shard_map/all_gather | solution.py:175
  8.7 199.2 %all-gather.18.cloned.1.call-start = ((), (), s32[]{:S(2)}) async-start(), calls=%async_computation.13 | async-start | bytes 10616832 | tf_op jit(solution)/shard_map/all_gather | solution.py:174
  9.4 263.8 %all-gather.12.cloned.1.call-start = ((), (), s32[]{:S(2)}) async-start(), calls=%async_computation.10 | async-start | bytes 7077888 | tf_op jit(solution)/shard_map/all_gather | solution.py:204
  47.2 24.5 copy-start.32
  70.5 268.1 %all-gather.16.cloned.1.call-start = ((), (), s32[]{:S(2)}) async-start(), calls=%async_computation.12 | async-start | bytes 7077888 | tf_op jit(solution)/shard_map/all_gather | solution.py:203
  71.7 143.2 %copy-start.15 = (f32[192,128]{1,0:T(8,128)}, f32[192,128]{1,0:T(8,128)S(1)}, u32[]{:S(2)}) copy-start(f32[192,128]{1,0:T(8,128)S(1)} %get-tuple-element.661) | copy-start | bytes 294916
  122.9 306.7 %all-gather.20.cloned.1.call-start = ((), (), s32[]{:S(2)}) async-start(), calls=%async_computation.14 | async-start | bytes 10616832 | tf_op jit(solution)/shard_map/all_gather | solution.py:177
  123.5 669.4 %all-gather.22.cloned.1.call-start = ((), (), s32[]{:S(2)}) async-start(), calls=%async_computation.15 | async-start | bytes 47775744 | tf_op jit(solution)/shard_map/all_gather | solution.py:226
  124.2 1032.1 %all-gather.24.cloned.1.call-start = ((), (), s32[]{:S(2)}) async-start(), calls=%async_computation.16 | async-start | bytes 47775744 | tf_op jit(solution)/shard_map/all_gather | solution.py:227
  125.0 1394.7 %all-gather.26.cloned.1.call-start = ((), (), s32[]{:S(2)}) async-start(), calls=%async_computation.17 | async-start | bytes 47775744 | tf_op jit(solution)/shard_map/all_gather | solution.py:228
  125.8 1732.4 %reduce-scatter.10.cloned.1.call-start = ((), (), s32[]{:S(2)}) async-start(), calls=%async_computation.18 | async-start | bytes 7077888 | tf_op jit(solution)/shard_map/reduce_scatter | solution.py:281
  289.5 57.9 %copy-start.41 = (s32[2,2]{1,0:T(2,128)S(1)}, s32[2,2]{1,0:T(2,128)}, u32[]{:S(2)}) copy-start(s32[2,2]{1,0:T(2,128)} %param.20) | copy-start | bytes 52
  289.5 57.9 %copy-start.43 = (s32[2,2]{1,0:T(2,128)S(1)}, s32[2,2]{1,0:T(2,128)}, u32[]{:S(2)}) copy-start(s32[2,2]{1,0:T(2,128)} %param.21) | copy-start | bytes 52
  372.0 64.8 %copy-start.3 = (bf16[2,192,8,256]{3,1,2,0:T(8,128)(2,1)}, bf16[2,192,8,256]{3,1,2,0:T(8,128)(2,1)S(1)}, u32[]{:S(2)}) copy-start(bf16[2,192,8,256]{3,1,2,0:T(8,128)(2,1)S(1)} %get-tuple-element.973) | copy-start | bytes 4718596
  372.0 64.8 %copy-start.37 = (f32[2,4,2,192,1]{3,2,1,4,0:T(2,128)}, f32[2,4,2,192,1]{3,2,1,4,0:T(2,128)S(1)}, u32[]{:S(2)}) copy-start(f32[2,4,2,192,1]{3,2,1,4,0:T(2,128)S(1)} %get-tuple-element.911) | copy-start | bytes 36868
  377.6 59.2 %copy-start.23 = (bf16[384,2048]{1,0:T(8,128)(2,1)}, bf16[384,2048]{1,0:T(8,128)(2,1)S(1)}, u32[]{:S(2)}) copy-start(bf16[384,2048]{1,0:T(8,128)(2,1)S(1)} %convert_element_type.258) | copy-start | bytes 4718596
  377.6 59.8 %copy-start.30 = (f32[2304]{0:T(1024)S(1)}, f32[2304]{0:T(1024)}, u32[]{:S(2)}) copy-start(f32[2304]{0:T(1024)} %convert_element_type.259) | copy-start | bytes 27652
  429.6 7.8 copy-start.6
  1519.7 24.5 copy-start.12
  1519.7 24.5 copy-start.36
  1584.6 25.6 copy-start.35
  1584.6 25.6 copy-start.48
  1610.2 26.6 copy-start.50
  1610.3 26.6 copy-start.9
  1610.3 26.6 copy-start.31
  1610.3 26.6 copy-start.40
  1636.9 9.1 slice-start.4
  1636.9 9.1 slice-start.5
  1646.0 6.3 copy-start.38
  1683.9 23.6 copy-start.1
  1748.1 23.6 copy-start.1
  1789.7 139.0 %reduce-scatter.12.cloned.1.call-start = ((), (), s32[]{:S(2)}) async-start(), calls=%async_computation.19 | async-start | bytes 7077888 | tf_op jit(solution)/shard_map/reduce_scatter | solution.py:287
  1798.5 240.4 %reduce-scatter.14.cloned.1.call-start = ((), (), s32[]{:S(2)}) async-start(), calls=%async_computation.20 | async-start | bytes 10616832 | tf_op jit(solution)/shard_map/reduce_scatter | solution.py:328
  1811.3 318.8 %reduce-scatter.20.cloned.1.call-start = ((), (), s32[]{:S(2)}) async-start(), calls=%async_computation.23 | async-start | bytes 10616832 | tf_op jit(solution)/shard_map/reduce_scatter | solution.py:337
  1822.1 363.5 %reduce-scatter.16.cloned.1.call-start = ((), (), s32[]{:S(2)}) async-start(), calls=%async_computation.21 | async-start | bytes 5308416 | tf_op jit(solution)/shard_map/reduce_scatter | solution.py:331
  1866.6 374.5 %reduce-scatter.18.cloned.1.call-start = ((), (), s32[]{:S(2)}) async-start(), calls=%async_computation.22 | async-start | bytes 5308416 | tf_op jit(solution)/shard_map/reduce_scatter | solution.py:334
  1934.8 716.2 %reduce-scatter.22.cloned.1.call-start = ((), (), s32[]{:S(2)}) async-start(), calls=%async_computation.24 | async-start | bytes 47775744 | tf_op jit(solution)/shard_map/reduce_scatter | solution.py:132
  1970.0 1091.0 %reduce-scatter.24.cloned.1.call-start = ((), (), s32[]{:S(2)}) async-start(), calls=%async_computation.25 | async-start | bytes 47775744 | tf_op jit(solution)/shard_map/reduce_scatter | solution.py:132
  2003.8 1467.0 %reduce-scatter.26.cloned.1.call-start = ((), (), s32[]{:S(2)}) async-start(), calls=%async_computation.26 | async-start | bytes 47775744 | tf_op jit(solution)/shard_map/reduce_scatter | solution.py:132
  2038.8 1792.8 %all-reduce.14.cloned.1.call-start = ((), (), s32[]{:S(2)}) async-start(), calls=%async_computation.27 | async-start | bytes 38928384 | tf_op jit(solution)/shard_map/psum | solution.py:354
  3485.0 6.4 copy-start.45
  3485.0 6.4 copy-start.46
  3485.0 6.4 copy-start.57
  3485.0 45.2 %copy-start.52 = (f32[384]{0:T(512)S(1)}, f32[384]{0:T(512)}, u32[]{:S(2)}) copy-start(f32[384]{0:T(512)} %copy-done.51) | copy-start | bytes 4612
  3836.8 7.6 slice-start.2
  3838.4 11.0 slice-start
  (45 other events, 142.2 us)
Sparse Core Ops, SparseCore 0:
  9.7 54.7 all-gather.9
  66.1 50.5 all-gather.13
  118.3 89.5 all-gather.17
  210.0 63.2 all-gather.11
  275.3 63.3 all-gather.15
  340.2 89.4 all-gather.19
  431.3 361.6 all-gather.21
  794.6 361.6 all-gather.23
  1158.0 361.7 all-gather.25
  1789.8 68.3 reduce-scatter.9
  1860.5 68.1 reduce-scatter.11
  1931.4 97.8 reduce-scatter.13
  2032.2 97.8 reduce-scatter.19
  2132.2 53.3 reduce-scatter.15
  2187.8 53.3 reduce-scatter.17
  2243.3 407.5 reduce-scatter.21
  2653.3 407.6 reduce-scatter.23
  3063.2 407.6 reduce-scatter.25
  3476.4 355.1 all-reduce.13
where the time goes:
time: 3870 us; the launch traced here: 3860 us
  waiting for transfers between devices  3140 us (81%)
  matrix products  480 us (12%)
  local copies, waits for them, and re-layouts  93.9 us (2%)
  blocking collectives  68.3 us (2%)
  other arithmetic  58.8 us (2%)
    reduce_scatter x3, waiting for transfers between devices, scatter_rows(): lax.psum_scatter(contract_first(left_side, right_side).astype(jnp.bfloat1...  1230 us
    all_gather x1, waiting for transfers between devices, on_device(): gate_rows = lax.all_gather(gate_weight, 'ctx', axis=0, tiled=True)  351 us
    all_gather x1, waiting for transfers between devices, on_device(): up_rows = lax.all_gather(up_weight, 'ctx', axis=0, tiled=True)  333 us
    all_gather x1, waiting for transfers between devices, on_device(): down_rows = lax.all_gather(down_weight, 'ctx', axis=0, tiled=True)  330 us
    psum x1, waiting for transfers between devices, on_device(): lax.psum(query_part.astype(jnp.bfloat16), 'dp').astype(jnp.float32)  296 us
    dot_general x7, matrix products, contract_first(): lax.dot_general(left_side, right_side, (((0,), (0,)), ((), ())), preferre...  128 us
    dot_general x7, matrix products, contract_last(): lax.dot_general(left_side, right_side, (((1,), (1,)), ((), ())), preferre...  119 us
    dot_general x7, matrix products, matmul(): return jnp.dot(left_side, right_side, preferred_element_type=jnp.float32)  103 us
  transfers between devices with their start and end apart: 19, of which 18 were waited for; matrix products, arithmetic and copies ran while one was open for 8% of the time, Pallas kernels for 0%

commit v1 on v0

v1 whole, which is shorter than its diff:
```python
import functools

import jax
import jax.numpy as jnp
from jax import lax
from jax.experimental import pallas as pl
from jax.experimental.pallas import tpu as pltpu
from jax.sharding import PartitionSpec as P

HEADS = 8
KV_HEADS = 4
HEAD_DIM = 256
HALF = HEAD_DIM // 2

epsilon = 1e-06
soft_cap = 50.0
rope_base = 10000.0
gelu_a = 0.7978845608028654
gelu_b = 0.044715

bf16 = jnp.bfloat16
f32 = jnp.float32


def nt(left_side, right_side):
    return lax.dot_general(
        left_side, right_side, (((1,), (1,)), ((), ())), preferred_element_type=f32
    )


def nn(left_side, right_side):
    return lax.dot_general(
        left_side, right_side, (((1,), (0,)), ((), ())), preferred_element_type=f32
    )


def tn(left_side, right_side):
    return lax.dot_general(
        left_side, right_side, (((0,), (0,)), ((), ())), preferred_element_type=f32
    )


class Line:
    def __init__(self, size, index):
        self.chips = size // 2
        self.z = index // 2
        self.c = index % 2
        self.core_pairs = [(i, i ^ 1) for i in range(size)]

    def pairs(self, step, low, high):
        return [
            (2 * z + c, 2 * (z + step) + c)
            for z in range(low, high)
            for c in range(2)
            if 0 <= z + step < self.chips
        ]

    def right(self, block, low, high):
        return lax.ppermute(block, "ctx", self.pairs(1, low, high))

    def left(self, block, low, high):
        n = self.chips
        return lax.ppermute(block, "ctx", self.pairs(-1, n - high, n - low))

    def swap(self, block):
        return lax.ppermute(block, "ctx", self.core_pairs)

    def exchange(self, own=None, parts=None):
        n, z = self.chips, self.z
        mirror = n - 1 - z
        gathers, sums = own is not None, parts is not None
        from_left, from_right = [own], [own]
        sum_left = sum_right = None
        lag = 1 if gathers else 0
        last = n if gathers and sums else n - 1
        for s in range(1, last + 1):
            to_right = to_left = None
            low, high = 0, n
            if gathers and s <= n - 1:
                to_right, to_left = from_left[s - 1], from_right[s - 1]
                low = s - 1
            j = s - lag
            if sums and j >= 1:
                sum_r, sum_l = parts[n - j], parts[j]
                if sum_left is not None:
                    sum_r = (sum_r.astype(f32) + sum_left.astype(f32)).astype(bf16)
                    sum_l = (sum_l.astype(f32) + sum_right.astype(f32)).astype(bf16)
                if to_right is None:
                    to_right, to_left, high = sum_r, sum_l, j
                else:
                    to_right = jnp.where(z >= s - 1, to_right, sum_r)
                    to_left = jnp.where(mirror >= s - 1, to_left, sum_l)
                    low = 0
            got_left = self.right(to_right, low, high)
            got_right = self.left(to_left, low, high)
            if gathers and s <= n - 1:
                from_left.append(got_left)
                from_right.append(got_right)
            if sums and j >= 1:
                sum_left, sum_right = got_left, got_right
        blocks = None
        if gathers:
            blocks = [own]
            for k in range(1, n):
                blocks.append(jnp.where(z + k < n, from_right[k], from_left[n - k]))
        terms = None
        if sums:
            terms = (parts[0], sum_left, sum_right)
        return blocks, terms


def total(terms):
    return sum(t.astype(f32) for t in terms[1:]) + terms[0].astype(f32)


def spans_of(place, info, spans, none):
    label = jnp.full(place.shape, none, jnp.int32)
    for s in range(spans):
        start, stop = info[2 + s], info[2 + spans + s]
        label = jnp.where((place >= start) & (place < stop), s, label)
    return label


def seen_block(query_block, key_block, width, info, spans):
    seen = key_block <= query_block
    for s in range(spans):
        start, stop = info[2 + s], info[2 + spans + s]
        seen = seen | ((start < (query_block + 1) * width) & (stop > key_block * width))
    return seen


def block_mask(query_block, key_block, rows, info, spans):
    c = info[1]
    width = 2 * rows
    query_place = (
        query_block * width + c * rows + lax.broadcasted_iota(jnp.int32, (rows, 1), 0)
    )
    j = lax.broadcasted_iota(jnp.int32, (1, width), 1)
    key_place = key_block * width + j + jnp.where(j < rows, c * rows, -c * rows)
    query_span = spans_of(query_place, info, spans, -2)
    key_span = spans_of(key_place, info, spans, -1)
    return (key_place <= query_place) | (key_span == query_span)


def forward_kernel(spans, heads, info, q_ref, k_ref, v_ref, o_ref, acc_ref, sum_ref):
    chips, width, _ = k_ref.shape
    rows = width // 2
    query_block = lax.rem(info[0] + pl.program_id(0), chips)
    acc_ref[...] = jnp.zeros_like(acc_ref)
    sum_ref[...] = jnp.zeros_like(sum_ref)
    for kk in range(chips):
        key_block = lax.rem(info[0] + kk, chips)

        @pl.when(seen_block(query_block, key_block, width, info, spans))
        def _():
            allowed = block_mask(query_block, key_block, rows, info, spans)
            keys, values = k_ref[kk], v_ref[kk]
            for h in range(heads):
                scores = nt(q_ref[0, :, h * HEAD_DIM : (h + 1) * HEAD_DIM], keys)
                weights = jnp.where(
                    allowed, jnp.exp(soft_cap * jnp.tanh(scores * (1.0 / soft_cap))), 0.0
                )
                sum_ref[h] += jnp.sum(weights, axis=1, keepdims=True)
                acc_ref[h] += nn(weights.astype(bf16), values)

    for h in range(heads):
        o_ref[0, :, h * HEAD_DIM : (h + 1) * HEAD_DIM] = (acc_ref[h] / sum_ref[h]).astype(bf16)


def backward_kernel(
    spans,
    heads,
    info,
    q_ref,
    k_ref,
    v_ref,
    g_ref,
    dq_ref,
    dk_ref,
    dv_ref,
    p_ref,
    r_ref,
    t_ref,
    sum_ref,
    inner_ref,
    acc_ref,
):
    chips, width, _ = k_ref.shape
    rows = width // 2
    query_block = lax.rem(info[0] + pl.program_id(0), chips)

    @pl.when(pl.program_id(0) == 0)
    def _():
        dk_ref[...] = jnp.zeros_like(dk_ref)
        dv_ref[...] = jnp.zeros_like(dv_ref)

    acc_ref[...] = jnp.zeros_like(acc_ref)
    sum_ref[...] = jnp.zeros_like(sum_ref)
    inner_ref[...] = jnp.zeros_like(inner_ref)
    for kk in range(chips):
        key_block = lax.rem(info[0] + kk, chips)

        @pl.when(seen_block(query_block, key_block, width, info, spans))
        def _():
            allowed = block_mask(query_block, key_block, rows, info, spans)
            keys, values = k_ref[kk], v_ref[kk]
            for h in range(heads):
                head = slice(h * HEAD_DIM, (h + 1) * HEAD_DIM)
                squashed = jnp.tanh(nt(q_ref[0, :, head], keys) * (1.0 / soft_cap))
                weights = jnp.where(allowed, jnp.exp(soft_cap * squashed), 0.0)
                row_grad = nt(g_ref[0, :, head], values)
                sum_ref[h] += jnp.sum(weights, axis=1, keepdims=True)
                inner_ref[h] += jnp.sum(weights * row_grad, axis=1, keepdims=True)
                p_ref[kk, h] = weights
                r_ref[kk, h] = row_grad
                t_ref[kk, h] = 1.0 - squashed * squashed

    for kk in range(chips):
        key_block = lax.rem(info[0] + kk, chips)

        @pl.when(seen_block(query_block, key_block, width, info, spans))
        def _():
            keys = k_ref[kk]
            for h in range(heads):
                head = slice(h * HEAD_DIM, (h + 1) * HEAD_DIM)
                inverse = 1.0 / sum_ref[h]
                weights = p_ref[kk, h] * inverse
                inner = inner_ref[h] * inverse
                score_grad = (weights * (r_ref[kk, h] - inner) * t_ref[kk, h]).astype(bf16)
                acc_ref[h] += nn(score_grad, keys)
                dk_ref[kk] += tn(score_grad, q_ref[0, :, head])
                dv_ref[kk] += tn(weights.astype(bf16), g_ref[0, :, head])

    for h in range(heads):
        dq_ref[0, :, h * HEAD_DIM : (h + 1) * HEAD_DIM] = acc_ref[h]


def block_spec(shape):
    return pl.BlockSpec((1,) + tuple(shape[1:]), lambda i, info: (i, 0, 0))


def whole_spec(shape):
    return pl.BlockSpec(tuple(shape), lambda i, info: (0,) * len(shape))


def attend_forward(info, queries, keys, values, spans):
    chips, rows, features = queries.shape
    heads = features // HEAD_DIM
    flops = 4 * chips * rows * heads * chips * 2 * rows * HEAD_DIM
    return pl.pallas_call(
        functools.partial(forward_kernel, spans, heads),
        out_shape=jax.ShapeDtypeStruct(queries.shape, bf16),
        grid_spec=pltpu.PrefetchScalarGridSpec(
            num_scalar_prefetch=1,
            grid=(chips,),
            in_specs=[block_spec(queries.shape), whole_spec(keys.shape), whole_spec(values.shape)],
            out_specs=block_spec(queries.shape),
            scratch_shapes=[
                pltpu.VMEM((heads, rows, HEAD_DIM), f32),
                pltpu.VMEM((heads, rows, 1), f32),
            ],
        ),
        compiler_params=pltpu.CompilerParams(vmem_limit_bytes=32 * 1024 * 1024),
        cost_estimate=pl.CostEstimate(
            flops=flops, bytes_accessed=6 * 1024 * 1024, transcendentals=flops // 512
        ),
    )(info, queries, keys, values)


def attend_backward(info, queries, keys, values, grads, spans):
    chips, rows, features = queries.shape
    heads = features // HEAD_DIM
    flops = 10 * chips * rows * heads * chips * 2 * rows * HEAD_DIM
    square = pltpu.VMEM((chips, heads, rows, 2 * rows), f32)
    return pl.pallas_call(
        functools.partial(backward_kernel, spans, heads),
        out_shape=(
            jax.ShapeDtypeStruct(queries.shape, f32),
            jax.ShapeDtypeStruct(keys.shape, f32),
            jax.ShapeDtypeStruct(values.shape, f32),
        ),
        grid_spec=pltpu.PrefetchScalarGridSpec(
            num_scalar_prefetch=1,
            grid=(chips,),
            in_specs=[
                block_spec(queries.shape),
                whole_spec(keys.shape),
                whole_spec(values.shape),
                block_spec(queries.shape),
            ],
            out_specs=(
                block_spec(queries.shape),
                whole_spec(keys.shape),
                whole_spec(values.shape),
            ),
            scratch_shapes=[
                square,
                square,
                square,
                pltpu.VMEM((heads, rows, 1), f32),
                pltpu.VMEM((heads, rows, 1), f32),
                pltpu.VMEM((heads, rows, HEAD_DIM), f32),
            ],
        ),
        compiler_params=pltpu.CompilerParams(vmem_limit_bytes=40 * 1024 * 1024),
        cost_estimate=pl.CostEstimate(
            flops=flops, bytes_accessed=12 * 1024 * 1024, transcendentals=flops // 1280
        ),
    )(info, queries, keys, values, grads)


def rotate(vectors, cosine, sine):
    first, second = vectors[..., :HALF], vectors[..., HALF:]
    return jnp.concatenate(
        [first * cosine - second * sine, second * cosine + first * sine], axis=-1
    )


def inverse_root(values):
    return lax.rsqrt(jnp.mean(values * values, axis=-1, keepdims=True) + epsilon)


def norm_backward(normed, root, gain, grad):
    scaled = grad * gain
    return root * (scaled - normed * jnp.mean(scaled * normed, axis=-1, keepdims=True))


def on_device(
    tokens,
    span_start,
    span_len,
    query_weight,
    key_weight,
    value_weight,
    output_weight,
    gate_weight,
    up_weight,
    down_weight,
    inbound_gain,
    attended_gain,
    prefeed_gain,
    postfeed_gain,
    cotangent,
):
    seq_count, rows, width = tokens.shape
    size = lax.axis_size("ctx")
    index = lax.axis_index("ctx")
    line = Line(size, index)
    chips, z, c = line.chips, line.z, line.c
    spans = span_start.shape[1]
    group = size // KV_HEADS
    member = index % group
    every = chips * rows

    def pair_rows(block):
        other = line.swap(block)
        return jnp.concatenate([jnp.where(c == 0, block, other), jnp.where(c == 0, other, block)])

    def shifted(block, k):
        pairs = [(i, i - i % group + (i % group + k) % group) for i in range(size)]
        return lax.ppermute(block, "ctx", pairs)

    def group_rows(block):
        if group == 2:
            return pair_rows(block)
        count = block.shape[0]
        out = jnp.zeros((group * count, width), block.dtype)
        out = lax.dynamic_update_slice(out, block, (member * count, 0))
        for k in range(1, group):
            place = lax.rem(member + group - k, group) * count
            out = lax.dynamic_update_slice(out, shifted(block, k), (place, 0))
        return out

    def group_sum(grad):
        count = grad.shape[0] // group
        own = lax.dynamic_slice(grad, (member * count, 0), (count, width))
        for k in range(1, group):
            place = lax.rem(member + k, group) * count
            sent = lax.dynamic_slice(grad, (place, 0), (count, width))
            own = own + shifted(sent.astype(bf16), k).astype(f32)
        return own

    def pair_sum(grad):
        count = grad.shape[0] // 2
        own = lax.dynamic_slice(grad, (c * count, 0), (count, width))
        sent = lax.dynamic_slice(grad, ((1 - c) * count, 0), (count, width))
        return own + line.swap(sent.astype(bf16)).astype(f32)

    gains_own = jnp.stack([inbound_gain, attended_gain, prefeed_gain, postfeed_gain])
    gains = lax.all_gather(gains_own, "ctx", axis=1, tiled=True).astype(f32)
    inbound, attended_g, prefeed, postfeed = (gains[i][None, :] for i in range(4))

    qkv_weight = jnp.concatenate(
        [pair_rows(query_weight), group_rows(key_weight), group_rows(value_weight)]
    )
    out_weight = pair_rows(output_weight)
    gate_rows = (gate_weight, line.swap(gate_weight))
    up_rows = (up_weight, line.swap(up_weight))
    down_rows = (down_weight, line.swap(down_weight))

    query_width = out_weight.shape[0]
    heads = query_width // HEAD_DIM

    block_of = lax.rem(z + jnp.arange(chips, dtype=jnp.int32), chips)
    places = (
        block_of[:, None] * (2 * rows) + c * rows + jnp.arange(rows, dtype=jnp.int32)[None, :]
    ).reshape(every)
    inverse = rope_base ** (-(jnp.arange(HALF, dtype=f32) * 2.0 / HEAD_DIM))
    angles = places.astype(f32)[:, None] * inverse[None, :]
    cosine, sine = jnp.cos(angles)[:, None, :], jnp.sin(angles)[:, None, :]
    query_scale = HEAD_DIM ** (-0.5)

    def split(block_rows):
        return [block_rows[k * rows : (k + 1) * rows] for k in range(chips)]

    def join(blocks):
        return jnp.concatenate(blocks)

    infos = [
        jnp.concatenate(
            [jnp.stack([z, c]), span_start[s], span_start[s] + span_len[s]]
        ).astype(jnp.int32)
        for s in range(seq_count)
    ]

    class Sequence:
        def __init__(self, s):
            self.s = s
            self.own = tokens[s]

        def attention(self, blocks):
            self.tokens = join(blocks)
            values = self.tokens.astype(f32)
            self.root_in = inverse_root(values)
            self.hidden = (values * self.root_in * inbound).astype(bf16)
            raw = nt(self.hidden, qkv_weight)
            queries = raw[:, :query_width].reshape(every, heads, HEAD_DIM)
            queries = (rotate(queries, cosine, sine) * query_scale).astype(bf16)
            keys = raw[:, query_width : query_width + HEAD_DIM].reshape(every, 1, HEAD_DIM)
            keys = rotate(keys, cosine, sine).astype(bf16).reshape(every, HEAD_DIM)
            values = raw[:, query_width + HEAD_DIM :].astype(bf16)
            mine = jnp.concatenate([keys, values], axis=1).reshape(chips, rows, 2 * HEAD_DIM)
            both = jnp.concatenate([mine, line.swap(mine)], axis=1)
            self.queries = queries.reshape(chips, rows, query_width)
            self.keys, self.values = both[:, :, :HEAD_DIM], both[:, :, HEAD_DIM:]
            self.attended = attend_forward(
                infos[self.s], self.queries, self.keys, self.values, spans
            ).reshape(every, query_width)
            return split(nn(self.attended, out_weight).astype(bf16))

        def after_branch(self, terms):
            branch = total(terms)
            self.root_branch = inverse_root(branch)
            self.normed_branch = branch * self.root_branch
            self.middle = self.own.astype(f32) + self.normed_branch * attended_g
            self.root_middle = inverse_root(self.middle)
            return (self.middle * self.root_middle * prefeed).astype(bf16)

        def feed(self, blocks):
            self.hidden_ff = join(blocks)
            self.product, self.slope, self.gelu = [], [], []
            out = None
            for gate_w, up_w, down_w in zip(gate_rows, up_rows, down_rows):
                gate = nt(self.hidden_ff, gate_w)
                up = nt(self.hidden_ff, up_w)
                tanh = jnp.tanh(gelu_a * (gate + gelu_b * gate * gate * gate))
                half = 0.5 * (1.0 + tanh)
                gelu = gate * half
                slope = half + 0.5 * gate * (1.0 - tanh * tanh) * (
                    gelu_a * (1.0 + 3.0 * gelu_b * gate * gate)
                )
                self.product.append((gelu * up).astype(bf16))
                self.gelu.append(gelu.astype(bf16))
                self.slope.append((up * slope).astype(bf16))
            out = sum(nn(p, w) for p, w in zip(self.product, down_rows))
            return split(out.astype(bf16))

        def after_feed(self, terms):
            feed = total(terms)
            root = inverse_root(feed)
            normed = feed * root
            self.upstream = cotangent[self.s].astype(f32)
            self.output = (self.middle + normed * postfeed).astype(bf16)
            self.postfeed_term = jnp.sum(self.upstream * normed, axis=0)
            return norm_backward(normed, root, postfeed, self.upstream).astype(bf16)

        def feed_back(self, blocks):
            self.feed_low = join(blocks)
            self.gate_back, self.up_back = [], []
            for down_w, gelu, slope in zip(down_rows, self.gelu, self.slope):
                grad = nt(self.feed_low, down_w)
                self.gate_back.append((grad * slope.astype(f32)).astype(bf16))
                self.up_back.append((grad * gelu.astype(f32)).astype(bf16))
            out = sum(
                nn(g, w)
                for g, w in zip(self.gate_back + self.up_back, list(gate_rows) + list(up_rows))
            )
            return split(out.astype(bf16))

        def after_feed_back(self, terms):
            grad = total(terms)
            normed = self.middle * self.root_middle
            self.prefeed_term = jnp.sum(grad * normed, axis=0)
            self.middle_grad = self.upstream + norm_backward(
                normed, self.root_middle, prefeed, grad
            )
            self.attended_term = jnp.sum(self.middle_grad * self.normed_branch, axis=0)
            return norm_backward(
                self.normed_branch, self.root_branch, attended_g, self.middle_grad
            ).astype(bf16)

        def attention_back(self, blocks):
            self.branch_low = join(blocks)
            mixed = nt(self.branch_low, out_weight).astype(bf16)
            query_rot, key_rot, value_sum = attend_backward(
                infos[self.s],
                self.queries,
                self.keys,
                self.values,
                mixed.reshape(chips, rows, query_width),
                spans,
            )
            sums = jnp.concatenate([key_rot, value_sum], axis=2)
            sums = sums[:, :rows] + line.swap(sums[:, rows:].astype(bf16)).astype(f32)
            sums = sums.reshape(every, 2 * HEAD_DIM)
            query_rot = query_rot.reshape(every, heads, HEAD_DIM)
            query_back = (rotate(query_rot, cosine, -sine) * query_scale).astype(bf16)
            key_back = rotate(sums[:, :HEAD_DIM].reshape(every, 1, HEAD_DIM), cosine, -sine)
            self.back = jnp.concatenate(
                [
                    query_back.reshape(every, query_width),
                    key_back.reshape(every, HEAD_DIM).astype(bf16),
                    sums[:, HEAD_DIM:].astype(bf16),
                ],
                axis=1,
            )
            grad = nn(self.back, qkv_weight)
            self.inbound_term = jnp.sum(grad * (self.tokens.astype(f32) * self.root_in), axis=0)
            return split(grad.astype(bf16))

        def after_attention_back(self, terms):
            grad = total(terms)
            values = self.own.astype(f32)
            root = inverse_root(values)
            return (self.middle_grad + norm_backward(values * root, root, inbound, grad)).astype(
                bf16
            )

    a, b = (Sequence(s) for s in range(seq_count))

    blocks, _ = line.exchange(own=a.own)
    parts_a = a.attention(blocks)
    blocks, terms = line.exchange(own=b.own, parts=parts_a)
    hidden_a = a.after_branch(terms)
    parts_b = b.attention(blocks)
    blocks, terms = line.exchange(own=hidden_a, parts=parts_b)
    hidden_b = b.after_branch(terms)
    parts_a = a.feed(blocks)
    blocks, terms = line.exchange(own=hidden_b, parts=parts_a)
    low_a = a.after_feed(terms)
    parts_b = b.feed(blocks)
    blocks, terms = line.exchange(own=low_a, parts=parts_b)
    low_b = b.after_feed(terms)
    parts_a = a.feed_back(blocks)
    blocks, terms = line.exchange(own=low_b, parts=parts_a)
    branch_a = a.after_feed_back(terms)
    parts_b = b.feed_back(blocks)
    blocks, terms = line.exchange(own=branch_a, parts=parts_b)
    branch_b = b.after_feed_back(terms)
    parts_a = a.attention_back(blocks)
    blocks, terms = line.exchange(own=branch_b, parts=parts_a)
    tokens_grad_a = a.after_attention_back(terms)
    parts_b = b.attention_back(blocks)
    _, terms = line.exchange(parts=parts_b)
    tokens_grad_b = b.after_attention_back(terms)

    def feed_grad(left_name, right_name):
        halves = []
        right = join([getattr(s, right_name) for s in (a, b)])
        for i in range(2):
            left = join([getattr(s, left_name)[i] for s in (a, b)])
            halves.append(tn(left, right))
        return halves[0] + line.swap(halves[1].astype(bf16)).astype(f32)

    down_grad = feed_grad("product", "feed_low")
    gate_grad = feed_grad("gate_back", "hidden_ff")
    up_grad = feed_grad("up_back", "hidden_ff")
    feed_sums = lax.psum((down_grad.astype(bf16), gate_grad.astype(bf16), up_grad.astype(bf16)), "dp")
    output_grad = pair_sum(
        tn(join([a.attended, b.attended]), join([a.branch_low, b.branch_low]))
    ).astype(bf16)
    qkv_grad = tn(join([a.back, b.back]), join([a.hidden, b.hidden]))
    query_grad = pair_sum(qkv_grad[:query_width]).astype(bf16)
    key_grad = group_sum(qkv_grad[query_width : query_width + HEAD_DIM]).astype(bf16)
    value_grad = group_sum(qkv_grad[query_width + HEAD_DIM :]).astype(bf16)
    feed_sums, late = lax.optimization_barrier(
        (feed_sums, (query_grad, key_grad, value_grad, output_grad))
    )
    late_sums = lax.psum(late, "dp")

    gain_terms = jnp.stack(
        [
            a.inbound_term + b.inbound_term,
            a.attended_term + b.attended_term,
            a.prefeed_term + b.prefeed_term,
            a.postfeed_term + b.postfeed_term,
        ]
    )
    gain_sums = lax.psum(gain_terms, ("dp", "ctx"))
    count = inbound_gain.shape[0]
    gain_sums = lax.dynamic_slice(gain_sums, (0, index * count), (4, count))

    return (
        jnp.stack([a.output, b.output]),
        jnp.stack([tokens_grad_a, tokens_grad_b]),
        late_sums[0].astype(f32),
        late_sums[1].astype(f32),
        late_sums[2].astype(f32),
        late_sums[3].astype(f32),
        feed_sums[1].astype(f32),
        feed_sums[2].astype(f32),
        feed_sums[0].astype(f32),
        gain_sums[0],
        gain_sums[1],
        gain_sums[2],
        gain_sums[3],
    )


def solution(mesh):
    rows = P("ctx", None)
    gain = P("ctx")
    tokens = P("dp", "ctx", None)
    spans = P("dp", None)
    return jax.shard_map(
        on_device,
        mesh=mesh,
        in_specs=(tokens, spans, spans) + (rows,) * 7 + (gain,) * 4 + (tokens,),
        out_specs=(tokens, tokens) + (rows,) * 7 + (gain,) * 4,
        check_vma=False,
    )
```

time: 3870 us -> 1490 us (0.39)
  waiting for transfers between devices: 3140 us -> 555 us
  starting transfers between devices: 1.23 us -> 200 us
  other arithmetic: 58.8 us -> 169 us
  matrix products: 480 us -> 376 us
  local copies, waits for them, and re-layouts: 93.9 us -> 34.9 us
  Pallas kernels: 0 us -> 46.1 us
    reduce_scatter x9 -> x0, waiting for transfers between devices: 1530 us -> none  [the longest x3 1230 us: scatter_rows(): lax.psum_scatter(contract_first(left_side, right_side).astype(jnp.bfloat1...]
    all_gather x9 -> x0, waiting for transfers between devices: 1310 us -> none  [the longest x1 351 us: on_device(): gate_rows = lax.all_gather(gate_weight, 'ctx', axis=0, tiled=True)]
    ppermute x0 -> x86, waiting for transfers between devices: none -> 349 us  [the longest x34 227 us: left(): return lax.ppermute(block, 'ctx', self.pairs(-1, n - high, n - low))]
    ppermute x0 -> x86, starting transfers between devices: none -> 200 us  [the longest x34 152 us: right(): return lax.ppermute(block, 'ctx', self.pairs(1, low, high))]
    dot_general x35 -> x40, matrix products: 480 us -> 376 us  [the longest x16 145 us: nt(): lax.dot_general(left_side, right_side, (((1,), (1,)), ((), ())), preferre...]
    psum x1 -> x2, waiting for transfers between devices: 296 us -> 206 us  [the longest x1 188 us: on_device(): lax.psum((down_grad.astype(bf16), gate_grad.astype(bf16), up_grad.astype(...]
    unnamed x2 -> x0, blocking collectives: 58.2 us -> none
    pallas_call x0 -> x4, Pallas kernels: none -> 46.1 us  [the longest x2 30.6 us: attend_backward(): pl.pallas_call(functools.partial(backward_kernel, spans, heads), out_shap...]
  transfers between devices with their start and end apart: 19 -> 88, of which waited for: 18 -> 45; matrix products, arithmetic and copies ran while one was open for 8% -> 35% of each run, Pallas kernels for 0% -> 3%
where the time goes in v1:
time: 1490 us; the launch traced here: 1480 us
  waiting for transfers between devices  555 us (37%)
  matrix products  376 us (25%)
  starting transfers between devices  200 us (13%)
  other arithmetic  169 us (11%)
  blocking collectives  85.1 us (6%)
  Pallas kernels  46.1 us (3%)
  local copies, waits for them, and re-layouts  34.9 us (2%)
  between operations  18.1 us (1%)
    ppermute x34, waiting for transfers between devices, left(): return lax.ppermute(block, 'ctx', self.pairs(-1, n - high, n - low))  227 us
    psum x1, waiting for transfers between devices, on_device(): lax.psum((down_grad.astype(bf16), gate_grad.astype(bf16), up_grad.astype(...  188 us
    ppermute x34, starting transfers between devices, right(): return lax.ppermute(block, 'ctx', self.pairs(1, low, high))  152 us
    dot_general x16, matrix products, nt(): lax.dot_general(left_side, right_side, (((1,), (1,)), ((), ())), preferre...  145 us
    dot_general x16, matrix products, nn(): lax.dot_general(left_side, right_side, (((1,), (0,)), ((), ())), preferre...  140 us
    ppermute x34, waiting for transfers between devices, right(): return lax.ppermute(block, 'ctx', self.pairs(1, low, high))  121 us
    dot_general x8, matrix products, tn(): lax.dot_general(left_side, right_side, (((0,), (0,)), ((), ())), preferre...  90.2 us
    ppermute x34, starting transfers between devices, left(): return lax.ppermute(block, 'ctx', self.pairs(-1, n - high, n - low))  45 us
  transfers between devices with their start and end apart: 88, of which 45 were waited for; matrix products, arithmetic and copies ran while one was open for 35% of the time, Pallas kernels for 3%

profile of v1, /device:TPU:0, one launch (start us, length us, event | category | flops | bytes accessed | tf_op | source)
XLA Modules:
  0.0 1483.1 jit_solution(1972723054767746961)
XLA Ops:
  24.8 42.0 %all-gather = bf16[8,288,4]{1,2,0:T(4,128)(2,1)S(1)} all-gather(bf16[1,288,4]{1,2,0:T(4,128)(2,1)S(1)} %maximum_bitcast_fusion.2), channel_id=1, replica_groups=mesh['dp'=4,'ctx'=8] {'ctx'}, dimensions={0}, use_global_device_ids=true | all-gather | bytes 20736 | tf_op jit(solution)/shard_map/all_gather | solution.py:390
  78.2 21.7 %collective-permute-done.4 = bf16[192,2304]{1,0:T(8,128)(2,1)S(1)} collective-permute-done((bf16[192,2304]{1,0:T(8,128)(2,1)}, bf16[192,2304]{1,0:T(8,128)(2,1)S(1)}, u32[]{:S(2)}, u32[]{:S(2)}) %collective-permute-start.4) | collective-permute-done | bytes 884768 | tf_op jit(solution)/shard_map/ppermute | solution.py:63
  103.4 19.4 %collective-permute-done.5 = bf16[192,2304]{1,0:T(8,128)(2,1)S(1)} collective-permute-done((bf16[192,2304]{1,0:T(8,128)(2,1)S(1)}, bf16[192,2304]{1,0:T(8,128)(2,1)S(1)}, u32[]{:S(2)}, u32[]{:S(2)}) %collective-permute-start.5) | collective-permute-done | bytes 884768 | tf_op jit(solution)/shard_map/ppermute | solution.py:63
  160.1 18.9 %collective-permute-done.12 = bf16[192,2304]{1,0:T(8,128)(2,1)} collective-permute-done((bf16[192,2304]{1,0:T(8,128)(2,1)}, bf16[192,2304]{1,0:T(8,128)(2,1)}, u32[]{:S(2)}, u32[]{:S(2)}) %collective-permute-start.12) | collective-permute-done | bytes 884768 | tf_op jit(solution)/shard_map/ppermute | solution.py:59
  188.8 17.8 %collective-permute-done.16 = bf16[192,2304]{1,0:T(8,128)(2,1)} collective-permute-done((bf16[192,2304]{1,0:T(8,128)(2,1)}, bf16[192,2304]{1,0:T(8,128)(2,1)}, u32[]{:S(2)}, u32[]{:S(2)}) %collective-permute-start.16) | collective-permute-done | bytes 884768 | tf_op jit(solution)/shard_map/ppermute | solution.py:63
  211.3 19.8 %collective-permute-done.17 = bf16[192,2304]{1,0:T(8,128)(2,1)S(1)} collective-permute-done((bf16[192,2304]{1,0:T(8,128)(2,1)S(1)}, bf16[192,2304]{1,0:T(8,128)(2,1)S(1)}, u32[]{:S(2)}, u32[]{:S(2)}) %collective-permute-start.17) | collective-permute-done | bytes 884768 | tf_op jit(solution)/shard_map/ppermute | solution.py:63
  307.4 16.2 %collective-permute-done.22 = bf16[192,2304]{1,0:T(8,128)(2,1)S(1)} collective-permute-done((bf16[192,2304]{1,0:T(8,128)(2,1)S(1)}, bf16[192,2304]{1,0:T(8,128)(2,1)S(1)}, u32[]{:S(2)}, u32[]{:S(2)}) %collective-permute-start.22) | collective-permute-done | bytes 884768 | tf_op jit(solution)/shard_map/ppermute | solution.py:59
  333.2 14.2 collective-permute-done.23
  368.4 11.2 multiply_convert_fusion.11
  379.6 9.7 fusion.249
  389.3 11.6 multiply_convert_fusion.10
  440.0 13.0 collective-permute-done.36
  461.1 12.1 collective-permute-done.37
  494.7 11.4 multiply_convert_fusion.9
  506.0 9.7 fusion.245
  515.8 11.4 multiply_convert_fusion.8
  527.2 9.7 fusion.261
  568.9 12.7 collective-permute-done.40
  597.7 12.7 collective-permute-done.44
  612.2 22.9 %collective-permute-done.45 = bf16[192,2304]{1,0:T(8,128)(2,1)S(1)} collective-permute-done((bf16[192,2304]{1,0:T(8,128)(2,1)S(1)}, bf16[192,2304]{1,0:T(8,128)(2,1)S(1)}, u32[]{:S(2)}, u32[]{:S(2)}) %collective-permute-start.45) | collective-permute-done | bytes 884768 | tf_op jit(solution)/shard_map/ppermute | solution.py:63
  644.5 12.7 multiply_convert_fusion.7
  657.2 10.0 fusion.262
  667.1 9.2 fusion.264
  676.4 12.6 multiply_convert_fusion.4
  689.0 10.0 fusion.263
  710.2 11.9 add_convert_fusion.1
  776.3 12.1 multiply_convert_fusion.3
  788.4 10.6 fusion.267
  799.0 9.4 fusion.265
  808.3 12.7 multiply_convert_fusion
  821.0 13.3 convolution_convert_fusion.1
  834.4 9.5 fusion.266
  858.5 14.1 add_convert_fusion
  881.9 10.6 convolution_convert_fusion
  901.5 13.2 convolution_convert_fusion.2
  918.8 20.6 %collective-permute-done.60 = bf16[192,2304]{1,0:T(8,128)(2,1)S(1)} collective-permute-done((bf16[192,2304]{1,0:T(8,128)(2,1)S(1)}, bf16[192,2304]{1,0:T(8,128)(2,1)S(1)}, u32[]{:S(2)}, u32[]{:S(2)}) %collective-permute-start.60) | collective-permute-done | bytes 884768 | tf_op jit(solution)/shard_map/ppermute | solution.py:63
  942.6 14.7 shard_map.248
  974.6 9.3 fusion.10
  1006.8 12.0 fusion.2
  1031.5 13.9 fusion
  1057.6 11.9 fusion.1
  1090.7 15.9 %shard_map.249 = (f32[4,192,512]{2,1,0:T(8,128)S(1)}, f32[4,384,256]{2,1,0:T(8,128)S(1)}, f32[4,384,256]{2,1,0:T(8,128)S(1)}) custom-call(s32[6]{0:T(128)S(1)} %copy-done.13, bf16[4,192,512]{2,1,0:T(8,128)(2,1)S(1)} %copy-done.1, bf16[4,384,256]{2,1,0:T(8,128)(2,1)S(1)} %copy-done.7, bf16[4,384,256]{2,1,0:T(8,128)(2,1)S(1)} %copy-done.5, ...), custom_call_target="tpu_custom_call" | custom-call | flops 6039797760 | bytes 12582912 | tf_op jit(solution)/shard_map/pallas_call | solution.py:275
  1124.6 11.1 fusion.13
  1137.4 9.4 fusion.8
  1156.2 13.5 collective-permute-done.73
  1180.4 187.5 %all-reduce.7.cloned.1.call-done = (bf16[1152,2304]{1,0:T(8,128)(2,1)}, bf16[1152,2304]{1,0:T(8,128)(2,1)}, bf16[1152,2304]{1,0:T(8,128)(2,1)}) async-done(((bf16[1152,2304]{1,0:T(8,128)(2,1)}, bf16[1152,2304]{1,0:T(8,128)(2,1)}, bf16[1152,2304]{1,0:T(8,128)(2,1)}), (bf16[1152,2304]{1,0:T(8,128)(2,1)}, bf16[1152,2304]{1,0:T(8,128)(2,1)}, bf16[1152,2304]{1,0:T(8,128)(2,1)})) %all-reduce.7.cloned.1.call-update) | async-done | bytes 15925264 | tf_op jit(solution)/shard_map/psum | solution.py:588
  1380.2 43.0 %psum.63 = f32[4,2304]{1,0:T(4,128)} all-reduce(f32[4,2304]{1,0:T(4,128)} %pad_maximum_fusion.17), channel_id=1, replica_groups=mesh['dp'=4,'ctx'=8] {'dp','ctx'}, use_global_device_ids=true, to_apply=%region_33.34 | all-reduce | flops 9216 | bytes 73728 | tf_op jit(solution)/shard_map/psum | solution.py:609
  1450.6 18.7 %all-reduce.5.cloned.1.call-done = (bf16[256,2304]{1,0:T(8,128)(2,1)}, bf16[128,2304]{1,0:T(8,128)(2,1)}, bf16[128,2304]{1,0:T(8,128)(2,1)}, bf16[256,2304]{1,0:T(8,128)(2,1)}) async-done(((bf16[256,2304]{1,0:T(8,128)(2,1)}, bf16[128,2304]{1,0:T(8,128)(2,1)}, bf16[128,2304]{1,0:T(8,128)(2,1)}, bf16[256,2304]{1,0:T(8,128)(2,1)}), (bf16[256,2304]{1,0:T(8,128)(2,1)}, bf16[128,2304]{1,0:T(8,128)(2,1)}, ...) | async-done | bytes 3538960 | tf_op jit(solution)/shard_map/psum | solution.py:599
  (779 shorter events, 593.3 us)
Async XLA Ops:
  7.3 1360.6 %all-reduce.7.cloned.1.call-start = ((), (), s32[]{:S(2)}) async-start(), calls=%async_computation.1 | async-start | bytes 31850496 | tf_op jit(solution)/shard_map/psum | solution.py:588
  9.9 63.9 %collective-permute-start.1 = (bf16[192,2304]{1,0:T(8,128)(2,1)S(1)}, bf16[192,2304]{1,0:T(8,128)(2,1)}, u32[]{:S(2)}, u32[]{:S(2)}) collective-permute-start(bf16[192,2304]{1,0:T(8,128)(2,1)S(1)} %get-tuple-element.198), channel_id=1, source_target_pairs={{0,2},{1,3},{2,4},{3,5},{4,6},{5,7},{8,10},{9,11},{10,12},{11,13},... | collective-permute-start | bytes 2654216 | tf_op jit(solution)/shard_map/ppermute | solution.py:59
  15.8 60.1 %collective-permute-start = (bf16[192,2304]{1,0:T(8,128)(2,1)S(1)}, bf16[192,2304]{1,0:T(8,128)(2,1)}, u32[]{:S(2)}, u32[]{:S(2)}) collective-permute-start(bf16[192,2304]{1,0:T(8,128)(2,1)S(1)} %get-tuple-element.198), channel_id=1, source_target_pairs={{2,0},{3,1},{4,2},{5,3},{6,4},{7,5},{10,8},{11,9},{12,10},{13,11},... | collective-permute-start | bytes 2654216 | tf_op jit(solution)/shard_map/ppermute | solution.py:63
  17.1 143.0 %collective-permute-start.15 = (bf16[192,2304]{1,0:T(8,128)(2,1)}, bf16[192,2304]{1,0:T(8,128)(2,1)}, u32[]{:S(2)}, u32[]{:S(2)}) collective-permute-start(bf16[192,2304]{1,0:T(8,128)(2,1)} %get-tuple-element.199), channel_id=1, source_target_pairs={{2,0},{3,1},{4,2},{5,3},{6,4},{7,5},{10,8},{11,9},{12,10},{13,11},... | collective-permute-start | bytes 2654216 | tf_op jit(solution)/shard_map/ppermute | solution.py:63
  18.4 135.3 %collective-permute-start.11 = (bf16[192,2304]{1,0:T(8,128)(2,1)}, bf16[192,2304]{1,0:T(8,128)(2,1)}, u32[]{:S(2)}, u32[]{:S(2)}) collective-permute-start(bf16[192,2304]{1,0:T(8,128)(2,1)} %get-tuple-element.199), channel_id=1, source_target_pairs={{0,2},{1,3},{2,4},{3,5},{4,6},{5,7},{8,10},{9,11},{10,12},{11,13},... | collective-permute-start | bytes 2654216 | tf_op jit(solution)/shard_map/ppermute | solution.py:59
  24.5 46.7 %collective-permute-start.6 = (bf16[256,2304]{1,0:T(8,128)(2,1)S(1)}, bf16[256,2304]{1,0:T(8,128)(2,1)}, u32[]{:S(2)}, u32[]{:S(2)}) collective-permute-start(bf16[256,2304]{1,0:T(8,128)(2,1)S(1)} %copy-done.67), channel_id=1, source_target_pairs={{0,1},{1,0},{2,3},{3,2},{4,5},{5,4},{6,7},{7,6},{8,9},{9,8},{10,11... | collective-permute-start | bytes 3538952 | tf_op jit(solution)/shard_map/ppermute | solution.py:66
  75.7 60.6 %collective-permute-start.10 = (bf16[256,2304]{1,0:T(8,128)(2,1)S(1)}, bf16[256,2304]{1,0:T(8,128)(2,1)S(1)}, u32[]{:S(2)}, u32[]{:S(2)}) collective-permute-start(bf16[256,2304]{1,0:T(8,128)(2,1)S(1)} %copy-done.93), channel_id=1, source_target_pairs={{0,1},{1,0},{2,3},{3,2},{4,5},{5,4},{6,7},{7,6},{8,9},{9,8},{10,11... | collective-permute-start | bytes 3538952 | tf_op jit(solution)/shard_map/ppermute | solution.py:66
  75.9 24.0 %collective-permute-start.4 = (bf16[192,2304]{1,0:T(8,128)(2,1)}, bf16[192,2304]{1,0:T(8,128)(2,1)S(1)}, u32[]{:S(2)}, u32[]{:S(2)}) collective-permute-start(bf16[192,2304]{1,0:T(8,128)(2,1)} %collective-permute-done), channel_id=1, source_target_pairs={{2,0},{3,1},{4,2},{5,3},{10,8},{11,9},{12,10},{13,11},{18,16},{19,... | collective-permute-start | bytes 2654216 | tf_op jit(solution)/shard_map/ppermute | solution.py:63
  77.3 24.5 %collective-permute-start.3 = (bf16[192,2304]{1,0:T(8,128)(2,1)S(1)}, bf16[192,2304]{1,0:T(8,128)(2,1)S(1)}, u32[]{:S(2)}, u32[]{:S(2)}) collective-permute-start(bf16[192,2304]{1,0:T(8,128)(2,1)S(1)} %collective-permute-done.2), channel_id=1, source_target_pairs={{4,6},{5,7},{12,14},{13,15},{20,22},{21,23},{28,30},{29,31}} | collective-permute-start | bytes 2654216 | tf_op jit(solution)/shard_map/ppermute | solution.py:59
  99.9 23.0 %collective-permute-start.5 = (bf16[192,2304]{1,0:T(8,128)(2,1)S(1)}, bf16[192,2304]{1,0:T(8,128)(2,1)S(1)}, u32[]{:S(2)}, u32[]{:S(2)}) collective-permute-start(bf16[192,2304]{1,0:T(8,128)(2,1)S(1)} %collective-permute-done.4), channel_id=1, source_target_pairs={{2,0},{3,1},{10,8},{11,9},{18,16},{19,17},{26,24},{27,25}} | collective-permute-start | bytes 2654216 | tf_op jit(solution)/shard_map/ppermute | solution.py:63
  154.8 24.2 %collective-permute-start.12 = (bf16[192,2304]{1,0:T(8,128)(2,1)}, bf16[192,2304]{1,0:T(8,128)(2,1)}, u32[]{:S(2)}, u32[]{:S(2)}) collective-permute-start(bf16[192,2304]{1,0:T(8,128)(2,1)} %broadcast_select_fusion.15), channel_id=1, source_target_pairs={{0,2},{1,3},{2,4},{3,5},{4,6},{5,7},{8,10},{9,11},{10,12},{11,13},... | collective-permute-start | bytes 2654216 | tf_op jit(solution)/shard_map/ppermute | solution.py:59
  182.4 24.2 %collective-permute-start.16 = (bf16[192,2304]{1,0:T(8,128)(2,1)}, bf16[192,2304]{1,0:T(8,128)(2,1)}, u32[]{:S(2)}, u32[]{:S(2)}) collective-permute-start(bf16[192,2304]{1,0:T(8,128)(2,1)} %get-tuple-element.183), channel_id=1, source_target_pairs={{2,0},{3,1},{4,2},{5,3},{6,4},{7,5},{10,8},{11,9},{12,10},{13,11},... | collective-permute-start | bytes 2654216 | tf_op jit(solution)/shard_map/ppermute | solution.py:63
  183.7 26.1 %collective-permute-start.13 = (bf16[192,2304]{1,0:T(8,128)(2,1)}, bf16[192,2304]{1,0:T(8,128)(2,1)S(1)}, u32[]{:S(2)}, u32[]{:S(2)}) collective-permute-start(bf16[192,2304]{1,0:T(8,128)(2,1)} %get-tuple-element.182), channel_id=1, source_target_pairs={{0,2},{1,3},{2,4},{3,5},{4,6},{5,7},{8,10},{9,11},{10,12},{11,13},... | collective-permute-start | bytes 2654216 | tf_op jit(solution)/shard_map/ppermute | solution.py:59
  208.6 22.6 %collective-permute-start.17 = (bf16[192,2304]{1,0:T(8,128)(2,1)S(1)}, bf16[192,2304]{1,0:T(8,128)(2,1)S(1)}, u32[]{:S(2)}, u32[]{:S(2)}) collective-permute-start(bf16[192,2304]{1,0:T(8,128)(2,1)S(1)} %get-tuple-element.206), channel_id=1, source_target_pairs={{2,0},{3,1},{4,2},{5,3},{6,4},{7,5},{10,8},{11,9},{12,10},{13,11},... | collective-permute-start | bytes 2654216 | tf_op jit(solution)/shard_map/ppermute | solution.py:63
  244.7 24.5 %collective-permute-start.14 = (bf16[192,2304]{1,0:T(8,128)(2,1)}, bf16[192,2304]{1,0:T(8,128)(2,1)S(1)}, u32[]{:S(2)}, u32[]{:S(2)}) collective-permute-start(bf16[192,2304]{1,0:T(8,128)(2,1)} %get-tuple-element.180), channel_id=1, source_target_pairs={{0,2},{1,3},{2,4},{3,5},{4,6},{5,7},{8,10},{9,11},{10,12},{11,13},... | collective-permute-start | bytes 2654216 | tf_op jit(solution)/shard_map/ppermute | solution.py:59
  249.4 24.0 %collective-permute-start.18 = (bf16[192,2304]{1,0:T(8,128)(2,1)}, bf16[192,2304]{1,0:T(8,128)(2,1)}, u32[]{:S(2)}, u32[]{:S(2)}) collective-permute-start(bf16[192,2304]{1,0:T(8,128)(2,1)} %get-tuple-element.181), channel_id=1, source_target_pairs={{2,0},{3,1},{4,2},{5,3},{6,4},{7,5},{10,8},{11,9},{12,10},{13,11},... | collective-permute-start | bytes 2654216 | tf_op jit(solution)/shard_map/ppermute | solution.py:63
  280.8 22.6 %collective-permute-start.19 = (bf16[192,2304]{1,0:T(8,128)(2,1)S(1)}, bf16[192,2304]{1,0:T(8,128)(2,1)S(1)}, u32[]{:S(2)}, u32[]{:S(2)}) collective-permute-start(bf16[192,2304]{1,0:T(8,128)(2,1)S(1)} %get-tuple-element.101), channel_id=1, source_target_pairs={{2,0},{3,1},{4,2},{5,3},{6,4},{7,5},{10,8},{11,9},{12,10},{13,11},... | collective-permute-start | bytes 2654216 | tf_op jit(solution)/shard_map/ppermute | solution.py:63
  332.5 47.1 %collective-permute-start.26 = (bf16[1152,2304]{1,0:T(8,128)(2,1)}, bf16[1152,2304]{1,0:T(8,128)(2,1)}, u32[]{:S(2)}, u32[]{:S(2)}) collective-permute-start(bf16[1152,2304]{1,0:T(8,128)(2,1)} %param.22), channel_id=1, source_target_pairs={{0,1},{1,0},{2,3},{3,2},{4,5},{5,4},{6,7},{7,6},{8,9},{9,8},{10,11... | collective-permute-start | bytes 15925256 | tf_op jit(solution)/shard_map/ppermute | solution.py:66
  332.6 56.7 %collective-permute-start.27 = (bf16[1152,2304]{1,0:T(8,128)(2,1)}, bf16[1152,2304]{1,0:T(8,128)(2,1)}, u32[]{:S(2)}, u32[]{:S(2)}) collective-permute-start(bf16[1152,2304]{1,0:T(8,128)(2,1)} %param.23), channel_id=1, source_target_pairs={{0,1},{1,0},{2,3},{3,2},{4,5},{5,4},{6,7},{7,6},{8,9},{9,8},{10,11... | collective-permute-start | bytes 15925256 | tf_op jit(solution)/shard_map/ppermute | solution.py:66
  333.1 85.2 %collective-permute-start.28 = (bf16[1152,2304]{1,0:T(8,128)(2,1)}, bf16[1152,2304]{1,0:T(8,128)(2,1)}, u32[]{:S(2)}, u32[]{:S(2)}) collective-permute-start(bf16[1152,2304]{1,0:T(8,128)(2,1)} %param.24), channel_id=1, source_target_pairs={{0,1},{1,0},{2,3},{3,2},{4,5},{5,4},{6,7},{7,6},{8,9},{9,8},{10,11... | collective-permute-start | bytes 15925256 | tf_op jit(solution)/shard_map/ppermute | solution.py:66
  352.0 56.2 %collective-permute-start.29 = (bf16[192,2304]{1,0:T(8,128)(2,1)S(1)}, bf16[192,2304]{1,0:T(8,128)(2,1)S(1)}, u32[]{:S(2)}, u32[]{:S(2)}) collective-permute-start(bf16[192,2304]{1,0:T(8,128)(2,1)S(1)} %get-tuple-element.174), channel_id=1, source_target_pairs={{0,2},{1,3},{2,4},{3,5},{4,6},{5,7},{8,10},{9,11},{10,12},{11,13},... | collective-permute-start | bytes 2654216 | tf_op jit(solution)/shard_map/ppermute | solution.py:59
  354.5 53.7 %collective-permute-start.30 = (bf16[192,2304]{1,0:T(8,128)(2,1)S(1)}, bf16[192,2304]{1,0:T(8,128)(2,1)S(1)}, u32[]{:S(2)}, u32[]{:S(2)}) collective-permute-start(bf16[192,2304]{1,0:T(8,128)(2,1)S(1)} %get-tuple-element.175), channel_id=1, source_target_pairs={{2,0},{3,1},{4,2},{5,3},{6,4},{7,5},{10,8},{11,9},{12,10},{13,11},... | collective-permute-start | bytes 2654216 | tf_op jit(solution)/shard_map/ppermute | solution.py:63
  476.4 60.5 %collective-permute-start.34 = (bf16[192,2304]{1,0:T(8,128)(2,1)S(1)}, bf16[192,2304]{1,0:T(8,128)(2,1)S(1)}, u32[]{:S(2)}, u32[]{:S(2)}) collective-permute-start(bf16[192,2304]{1,0:T(8,128)(2,1)S(1)} %get-tuple-element.168), channel_id=1, source_target_pairs={{0,2},{1,3},{2,4},{3,5},{4,6},{5,7},{8,10},{9,11},{10,12},{11,13},... | collective-permute-start | bytes 2654216 | tf_op jit(solution)/shard_map/ppermute | solution.py:59
  480.9 56.1 %collective-permute-start.38 = (bf16[192,2304]{1,0:T(8,128)(2,1)S(1)}, bf16[192,2304]{1,0:T(8,128)(2,1)S(1)}, u32[]{:S(2)}, u32[]{:S(2)}) collective-permute-start(bf16[192,2304]{1,0:T(8,128)(2,1)S(1)} %get-tuple-element.169), channel_id=1, source_target_pairs={{2,0},{3,1},{4,2},{5,3},{6,4},{7,5},{10,8},{11,9},{12,10},{13,11},... | collective-permute-start | bytes 2654216 | tf_op jit(solution)/shard_map/ppermute | solution.py:63
  587.0 23.4 %collective-permute-start.44 = (bf16[192,2304]{1,0:T(8,128)(2,1)S(1)}, bf16[192,2304]{1,0:T(8,128)(2,1)S(1)}, u32[]{:S(2)}, u32[]{:S(2)}) collective-permute-start(bf16[192,2304]{1,0:T(8,128)(2,1)S(1)} %get-tuple-element.167), channel_id=1, source_target_pairs={{2,0},{3,1},{4,2},{5,3},{6,4},{7,5},{10,8},{11,9},{12,10},{13,11},... | collective-permute-start | bytes 2654216 | tf_op jit(solution)/shard_map/ppermute | solution.py:63
  610.9 24.2 %collective-permute-start.45 = (bf16[192,2304]{1,0:T(8,128)(2,1)S(1)}, bf16[192,2304]{1,0:T(8,128)(2,1)S(1)}, u32[]{:S(2)}, u32[]{:S(2)}) collective-permute-start(bf16[192,2304]{1,0:T(8,128)(2,1)S(1)} %get-tuple-element.204), channel_id=1, source_target_pairs={{2,0},{3,1},{4,2},{5,3},{6,4},{7,5},{10,8},{11,9},{12,10},{13,11},... | collective-permute-start | bytes 2654216 | tf_op jit(solution)/shard_map/ppermute | solution.py:63
  635.6 63.4 %collective-permute-start.42 = (bf16[192,2304]{1,0:T(8,128)(2,1)S(1)}, bf16[192,2304]{1,0:T(8,128)(2,1)S(1)}, u32[]{:S(2)}, u32[]{:S(2)}) collective-permute-start(bf16[192,2304]{1,0:T(8,128)(2,1)S(1)} %get-tuple-element.164), channel_id=1, source_target_pairs={{0,2},{1,3},{2,4},{3,5},{4,6},{5,7},{8,10},{9,11},{10,12},{11,13},... | collective-permute-start | bytes 2654216 | tf_op jit(solution)/shard_map/ppermute | solution.py:59
  640.0 58.9 %collective-permute-start.46 = (bf16[192,2304]{1,0:T(8,128)(2,1)S(1)}, bf16[192,2304]{1,0:T(8,128)(2,1)S(1)}, u32[]{:S(2)}, u32[]{:S(2)}) collective-permute-start(bf16[192,2304]{1,0:T(8,128)(2,1)S(1)} %get-tuple-element.165), channel_id=1, source_target_pairs={{2,0},{3,1},{4,2},{5,3},{6,4},{7,5},{10,8},{11,9},{12,10},{13,11},... | collective-permute-start | bytes 2654216 | tf_op jit(solution)/shard_map/ppermute | solution.py:63
  764.6 79.3 %collective-permute-start.50 = (bf16[192,2304]{1,0:T(8,128)(2,1)S(1)}, bf16[192,2304]{1,0:T(8,128)(2,1)S(1)}, u32[]{:S(2)}, u32[]{:S(2)}) collective-permute-start(bf16[192,2304]{1,0:T(8,128)(2,1)S(1)} %get-tuple-element.158), channel_id=1, source_target_pairs={{0,2},{1,3},{2,4},{3,5},{4,6},{5,7},{8,10},{9,11},{10,12},{11,13},... | collective-permute-start | bytes 2654216 | tf_op jit(solution)/shard_map/ppermute | solution.py:59
  770.4 73.5 %collective-permute-start.54 = (bf16[192,2304]{1,0:T(8,128)(2,1)S(1)}, bf16[192,2304]{1,0:T(8,128)(2,1)S(1)}, u32[]{:S(2)}, u32[]{:S(2)}) collective-permute-start(bf16[192,2304]{1,0:T(8,128)(2,1)S(1)} %get-tuple-element.159), channel_id=1, source_target_pairs={{2,0},{3,1},{4,2},{5,3},{6,4},{7,5},{10,8},{11,9},{12,10},{13,11},... | collective-permute-start | bytes 2654216 | tf_op jit(solution)/shard_map/ppermute | solution.py:63
  914.7 92.1 %collective-permute-start.81 = (bf16[1152,2304]{1,0:T(8,128)(2,1)}, bf16[1152,2304]{1,0:T(8,128)(2,1)}, u32[]{:S(2)}, u32[]{:S(2)}) collective-permute-start(bf16[1152,2304]{1,0:T(8,128)(2,1)} %convolution_convert_fusion), channel_id=1, source_target_pairs={{0,1},{1,0},{2,3},{3,2},{4,5},{5,4},{6,7},{7,6},{8,9},{9,8},{10,11... | collective-permute-start | bytes 15925256 | tf_op jit(solution)/shard_map/ppermute | solution.py:66
  914.7 116.7 %collective-permute-start.79 = (bf16[1152,2304]{1,0:T(8,128)(2,1)}, bf16[1152,2304]{1,0:T(8,128)(2,1)}, u32[]{:S(2)}, u32[]{:S(2)}) collective-permute-start(bf16[1152,2304]{1,0:T(8,128)(2,1)} %convolution_convert_fusion.2), channel_id=1, source_target_pairs={{0,1},{1,0},{2,3},{3,2},{4,5},{5,4},{6,7},{7,6},{8,9},{9,8},{10,11... | collective-permute-start | bytes 15925256 | tf_op jit(solution)/shard_map/ppermute | solution.py:66
  915.2 142.3 %collective-permute-start.80 = (bf16[1152,2304]{1,0:T(8,128)(2,1)}, bf16[1152,2304]{1,0:T(8,128)(2,1)}, u32[]{:S(2)}, u32[]{:S(2)}) collective-permute-start(bf16[1152,2304]{1,0:T(8,128)(2,1)} %convolution_convert_fusion.1), channel_id=1, source_target_pairs={{0,1},{1,0},{2,3},{3,2},{4,5},{5,4},{6,7},{7,6},{8,9},{9,8},{10,11... | collective-permute-start | bytes 15925256 | tf_op jit(solution)/shard_map/ppermute | solution.py:66
  915.2 24.2 %collective-permute-start.60 = (bf16[192,2304]{1,0:T(8,128)(2,1)S(1)}, bf16[192,2304]{1,0:T(8,128)(2,1)S(1)}, u32[]{:S(2)}, u32[]{:S(2)}) collective-permute-start(bf16[192,2304]{1,0:T(8,128)(2,1)S(1)} %get-tuple-element.155), channel_id=1, source_target_pairs={{2,0},{3,1},{4,2},{5,3},{6,4},{7,5},{10,8},{11,9},{12,10},{13,11},... | collective-permute-start | bytes 2654216 | tf_op jit(solution)/shard_map/ppermute | solution.py:63
  960.6 23.5 %collective-permute-start.62 = (bf16[192,2304]{1,0:T(8,128)(2,1)}, bf16[192,2304]{1,0:T(8,128)(2,1)}, u32[]{:S(2)}, u32[]{:S(2)}) collective-permute-start(bf16[192,2304]{1,0:T(8,128)(2,1)} %get-tuple-element.152), channel_id=1, source_target_pairs={{0,2},{1,3},{2,4},{3,5},{4,6},{5,7},{8,10},{9,11},{10,12},{11,13},... | collective-permute-start | bytes 2654216 | tf_op jit(solution)/shard_map/ppermute | solution.py:59
  969.3 23.9 %collective-permute-start.63 = (bf16[192,2304]{1,0:T(8,128)(2,1)S(1)}, bf16[192,2304]{1,0:T(8,128)(2,1)S(1)}, u32[]{:S(2)}, u32[]{:S(2)}) collective-permute-start(bf16[192,2304]{1,0:T(8,128)(2,1)S(1)} %copy-done.107), channel_id=1, source_target_pairs={{2,0},{3,1},{4,2},{5,3},{6,4},{7,5},{10,8},{11,9},{12,10},{13,11},... | collective-permute-start | bytes 2654216 | tf_op jit(solution)/shard_map/ppermute | solution.py:63
  1000.9 22.8 %collective-permute-start.68 = (bf16[192,2304]{1,0:T(8,128)(2,1)S(1)}, bf16[192,2304]{1,0:T(8,128)(2,1)S(1)}, u32[]{:S(2)}, u32[]{:S(2)}) collective-permute-start(bf16[192,2304]{1,0:T(8,128)(2,1)S(1)} %get-tuple-element.77), channel_id=1, source_target_pairs={{2,0},{3,1},{4,2},{5,3},{6,4},{7,5},{10,8},{11,9},{12,10},{13,11},... | collective-permute-start | bytes 2654216 | tf_op jit(solution)/shard_map/ppermute | solution.py:63
  1002.2 22.7 %collective-permute-start.64 = (bf16[192,2304]{1,0:T(8,128)(2,1)S(1)}, bf16[192,2304]{1,0:T(8,128)(2,1)S(1)}, u32[]{:S(2)}, u32[]{:S(2)}) collective-permute-start(bf16[192,2304]{1,0:T(8,128)(2,1)S(1)} %get-tuple-element.77), channel_id=1, source_target_pairs={{0,2},{1,3},{2,4},{3,5},{4,6},{5,7},{8,10},{9,11},{10,12},{11,13},... | collective-permute-start | bytes 2654216 | tf_op jit(solution)/shard_map/ppermute | solution.py:59
  1025.1 22.4 %collective-permute-start.69 = (bf16[192,2304]{1,0:T(8,128)(2,1)S(1)}, bf16[192,2304]{1,0:T(8,128)(2,1)S(1)}, u32[]{:S(2)}, u32[]{:S(2)}) collective-permute-start(bf16[192,2304]{1,0:T(8,128)(2,1)S(1)} %get-tuple-element.150), channel_id=1, source_target_pairs={{2,0},{3,1},{4,2},{5,3},{6,4},{7,5},{10,8},{11,9},{12,10},{13,11},... | collective-permute-start | bytes 2654216 | tf_op jit(solution)/shard_map/ppermute | solution.py:63
  1069.5 399.8 %all-reduce.5.cloned.1.call-start = ((), (), s32[]{:S(2)}) async-start(), calls=%async_computation | async-start | bytes 7077888 | tf_op jit(solution)/shard_map/psum | solution.py:599
  1076.9 347.9 %collective-permute-start.67 = (bf16[192,2304]{1,0:T(8,128)(2,1)}, bf16[192,2304]{1,0:T(8,128)(2,1)}, u32[]{:S(2)}, u32[]{:S(2)}) collective-permute-start(bf16[192,2304]{1,0:T(8,128)(2,1)} %get-tuple-element.140), channel_id=1, source_target_pairs={{0,2},{1,3},{2,4},{3,5},{4,6},{5,7},{8,10},{9,11},{10,12},{11,13},... | collective-permute-start | bytes 2654216 | tf_op jit(solution)/shard_map/ppermute | solution.py:59
  1082.2 342.6 %collective-permute-start.71 = (bf16[192,2304]{1,0:T(8,128)(2,1)}, bf16[192,2304]{1,0:T(8,128)(2,1)}, u32[]{:S(2)}, u32[]{:S(2)}) collective-permute-start(bf16[192,2304]{1,0:T(8,128)(2,1)} %get-tuple-element.141), channel_id=1, source_target_pairs={{2,0},{3,1},{4,2},{5,3},{6,4},{7,5},{10,8},{11,9},{12,10},{13,11},... | collective-permute-start | bytes 2654216 | tf_op jit(solution)/shard_map/ppermute | solution.py:63
  1115.0 37.2 %collective-permute-start.85 = (bf16[256,2304]{1,0:T(8,128)(2,1)}, bf16[256,2304]{1,0:T(8,128)(2,1)}, u32[]{:S(2)}, u32[]{:S(2)}) collective-permute-start(bf16[256,2304]{1,0:T(8,128)(2,1)} %dynamic-slice_convert_fusion), channel_id=1, source_target_pairs={{0,1},{1,0},{2,3},{3,2},{4,5},{5,4},{6,7},{7,6},{8,9},{9,8},{10,11... | collective-permute-start | bytes 3538952 | tf_op jit(solution)/shard_map/ppermute | solution.py:66
  1147.3 22.3 %collective-permute-start.73 = (bf16[192,2304]{1,0:T(8,128)(2,1)S(1)}, bf16[192,2304]{1,0:T(8,128)(2,1)S(1)}, u32[]{:S(2)}, u32[]{:S(2)}) collective-permute-start(bf16[192,2304]{1,0:T(8,128)(2,1)S(1)} %get-tuple-element.146), channel_id=1, source_target_pairs={{0,2},{1,3},{8,10},{9,11},{16,18},{17,19},{24,26},{25,27}} | collective-permute-start | bytes 2654216 | tf_op jit(solution)/shard_map/ppermute | solution.py:59
  1171.3 196.8 %collective-permute-start.74 = (bf16[192,2304]{1,0:T(8,128)(2,1)}, bf16[192,2304]{1,0:T(8,128)(2,1)}, u32[]{:S(2)}, u32[]{:S(2)}) collective-permute-start(bf16[192,2304]{1,0:T(8,128)(2,1)} %get-tuple-element.144), channel_id=1, source_target_pairs={{0,2},{1,3},{2,4},{3,5},{8,10},{9,11},{10,12},{11,13},{16,18},{17,... | collective-permute-start | bytes 2654216 | tf_op jit(solution)/shard_map/ppermute | solution.py:59
  1176.7 191.4 %collective-permute-start.77 = (bf16[192,2304]{1,0:T(8,128)(2,1)}, bf16[192,2304]{1,0:T(8,128)(2,1)}, u32[]{:S(2)}, u32[]{:S(2)}) collective-permute-start(bf16[192,2304]{1,0:T(8,128)(2,1)} %get-tuple-element.145), channel_id=1, source_target_pairs={{4,2},{5,3},{6,4},{7,5},{12,10},{13,11},{14,12},{15,13},{20,18},{2... | collective-permute-start | bytes 2654216 | tf_op jit(solution)/shard_map/ppermute | solution.py:63
  1371.8 53.0 %collective-permute-start.75 = (bf16[192,2304]{1,0:T(8,128)(2,1)}, bf16[192,2304]{1,0:T(8,128)(2,1)}, u32[]{:S(2)}, u32[]{:S(2)}) collective-permute-start(bf16[192,2304]{1,0:T(8,128)(2,1)} %get-tuple-element.142), channel_id=1, source_target_pairs={{0,2},{1,3},{2,4},{3,5},{4,6},{5,7},{8,10},{9,11},{10,12},{11,13},... | collective-permute-start | bytes 2654216 | tf_op jit(solution)/shard_map/ppermute | solution.py:59
  1376.1 48.7 %collective-permute-start.78 = (bf16[192,2304]{1,0:T(8,128)(2,1)}, bf16[192,2304]{1,0:T(8,128)(2,1)}, u32[]{:S(2)}, u32[]{:S(2)}) collective-permute-start(bf16[192,2304]{1,0:T(8,128)(2,1)} %get-tuple-element.143), channel_id=1, source_target_pairs={{2,0},{3,1},{4,2},{5,3},{6,4},{7,5},{10,8},{11,9},{12,10},{13,11},... | collective-permute-start | bytes 2654216 | tf_op jit(solution)/shard_map/ppermute | solution.py:63
  (243 other events, 4425.8 us)
Sparse Core Ops, SparseCore 0:
  1069.6 298.2 all-reduce.6
  1372.3 96.9 all-reduce.4

commit v2 on v1

--- a/solution.py
+++ b/solution.py
@@ -65,52 +65,68 @@
     def swap(self, block):
         return lax.ppermute(block, "ctx", self.core_pairs)
 
-    def exchange(self, own=None, parts=None):
-        n, z = self.chips, self.z
-        mirror = n - 1 - z
-        gathers, sums = own is not None, parts is not None
-        from_left, from_right = [own], [own]
-        sum_left = sum_right = None
-        lag = 1 if gathers else 0
-        last = n if gathers and sums else n - 1
-        for s in range(1, last + 1):
-            to_right = to_left = None
-            low, high = 0, n
-            if gathers and s <= n - 1:
-                to_right, to_left = from_left[s - 1], from_right[s - 1]
-                low = s - 1
-            j = s - lag
-            if sums and j >= 1:
-                sum_r, sum_l = parts[n - j], parts[j]
-                if sum_left is not None:
-                    sum_r = (sum_r.astype(f32) + sum_left.astype(f32)).astype(bf16)
-                    sum_l = (sum_l.astype(f32) + sum_right.astype(f32)).astype(bf16)
-                if to_right is None:
-                    to_right, to_left, high = sum_r, sum_l, j
-                else:
-                    to_right = jnp.where(z >= s - 1, to_right, sum_r)
-                    to_left = jnp.where(mirror >= s - 1, to_left, sum_l)
-                    low = 0
-            got_left = self.right(to_right, low, high)
-            got_right = self.left(to_left, low, high)
-            if gathers and s <= n - 1:
-                from_left.append(got_left)
-                from_right.append(got_right)
-            if sums and j >= 1:
-                sum_left, sum_right = got_left, got_right
-        blocks = None
-        if gathers:
-            blocks = [own]
-            for k in range(1, n):
-                blocks.append(jnp.where(z + k < n, from_right[k], from_left[n - k]))
-        terms = None
-        if sums:
-            terms = (parts[0], sum_left, sum_right)
-        return blocks, terms
+    def shift(self, block, k):
+        return jnp.roll(block, k, axis=0)
+
+
+def tied(*values):
+    return lax.optimization_barrier(values)
+
+
+class Exchange:
+    def __init__(self, line, own=None, sums=True):
+        self.line, self.own, self.sums = line, own, sums
+        self.parts = None
+        self.s = 0
+        self.from_left, self.from_right = [own], [own]
+        self.sum_left = self.sum_right = None
+
+    def step(self, work=None, inputs=()):
+        line, n, z = self.line, self.line.chips, self.line.z
+        gathers = self.own is not None
+        self.s += 1
+        s = self.s
+        to_right = to_left = None
+        low, high = 0, n
+        if gathers and s <= n - 1:
+            to_right, to_left = self.from_left[s - 1], self.from_right[s - 1]
+            low = s - 1
+        j = s - 1 if gathers else s
+        if self.sums and j >= 1:
+            sum_r, sum_l = self.parts[n - j], self.parts[j]
+            if self.sum_left is not None:
+                sum_r = (sum_r.astype(f32) + self.sum_left.astype(f32)).astype(bf16)
+                sum_l = (sum_l.astype(f32) + self.sum_right.astype(f32)).astype(bf16)
+            if to_right is None:
+                to_right, to_left, high = sum_r, sum_l, j
+            else:
+                to_right = jnp.where(z >= s - 1, to_right, sum_r)
+                to_left = jnp.where(n - 1 - z >= s - 1, to_left, sum_l)
+                low = 0
+        to_right, to_left, inputs = tied(to_right, to_left, inputs)
+        got_left = line.right(to_right, low, high)
+        got_right = line.left(to_left, low, high)
+        outs = work(*inputs) if work is not None else ()
+        got_left, got_right, outs = tied(got_left, got_right, outs)
+        if gathers and s <= n - 1:
+            self.from_left.append(got_left)
+            self.from_right.append(got_right)
+        if self.sums and j >= 1:
+            self.sum_left, self.sum_right = got_left, got_right
+        return outs
+
+    def blocks(self):
+        n, z = self.line.chips, self.line.z
+        return [self.own] + [
+            jnp.where(z + k < n, self.from_right[k], self.from_left[n - k]) for k in range(1, n)
+        ]
+
+    def terms(self):
+        return (self.parts[0], self.sum_left, self.sum_right)
 
 
 def total(terms):
-    return sum(t.astype(f32) for t in terms[1:]) + terms[0].astype(f32)
+    return sum(t.astype(f32) for t in terms)
 
 
 def spans_of(place, info, spans, none):
@@ -309,6 +325,40 @@
     )(info, queries, keys, values, grads)
 
 
+def gate_up_kernel(h_ref, gate_ref, up_ref, product_ref, gelu_ref, slope_ref):
+    gate = nt(h_ref[...], gate_ref[...])
+    up = nt(h_ref[...], up_ref[...])
+    square = gate * gate
+    tanh = jnp.tanh(gate * (gelu_a + (gelu_a * gelu_b) * square))
+    half = 0.5 + 0.5 * tanh
+    gelu = gate * half
+    slope = half + gate * (0.5 - 0.5 * tanh * tanh) * (gelu_a + (3.0 * gelu_a * gelu_b) * square)
+    product_ref[...] = (gelu * up).astype(bf16)
+    gelu_ref[...] = gelu.astype(bf16)
+    slope_ref[...] = (up * slope).astype(bf16)
+
+
+def gate_up(hidden, gate_w, up_w):
+    m, width = hidden.shape
+    n = gate_w.shape[0]
+    tile = next(t for t in (768, 384, 256, 128) if n % t == 0)
+    weight_spec = pl.BlockSpec((tile, width), lambda i: (i, 0))
+    out_spec = pl.BlockSpec((m, tile), lambda i: (0, i))
+    return pl.pallas_call(
+        gate_up_kernel,
+        out_shape=(jax.ShapeDtypeStruct((m, n), bf16),) * 3,
+        grid=(n // tile,),
+        in_specs=[pl.BlockSpec((m, width), lambda i: (0, 0)), weight_spec, weight_spec],
+        out_specs=(out_spec,) * 3,
+        compiler_params=pltpu.CompilerParams(vmem_limit_bytes=56 * 1024 * 1024),
+        cost_estimate=pl.CostEstimate(
+            flops=4 * m * n * width,
+            bytes_accessed=4 * n * width + 2 * m * width + 6 * m * n,
+            transcendentals=m * n,
+        ),
+    )(hidden, gate_w, up_w)
+
+
 def rotate(vectors, cosine, sine):
     first, second = vectors[..., :HALF], vectors[..., HALF:]
     return jnp.concatenate(
@@ -373,7 +423,7 @@
 
     def group_sum(grad):
         count = grad.shape[0] // group
-        own = lax.dynamic_slice(grad, (member * count, 0), (count, width))
+        own = lax.dynamic_slice(grad, (member * count, 0), (count, width)).astype(f32)
         for k in range(1, group):
             place = lax.rem(member + k, group) * count
             sent = lax.dynamic_slice(grad, (place, 0), (count, width))
@@ -382,21 +432,29 @@
 
     def pair_sum(grad):
         count = grad.shape[0] // 2
-        own = lax.dynamic_slice(grad, (c * count, 0), (count, width))
+        own = lax.dynamic_slice(grad, (c * count, 0), (count, width)).astype(f32)
         sent = lax.dynamic_slice(grad, ((1 - c) * count, 0), (count, width))
         return own + line.swap(sent.astype(bf16)).astype(f32)
 
-    gains_own = jnp.stack([inbound_gain, attended_gain, prefeed_gain, postfeed_gain])
-    gains = lax.all_gather(gains_own, "ctx", axis=1, tiled=True).astype(f32)
-    inbound, attended_g, prefeed, postfeed = (gains[i][None, :] for i in range(4))
+    def both_rows(block):
+        return jnp.concatenate([block, line.swap(block)])
 
     qkv_weight = jnp.concatenate(
         [pair_rows(query_weight), group_rows(key_weight), group_rows(value_weight)]
     )
     out_weight = pair_rows(output_weight)
-    gate_rows = (gate_weight, line.swap(gate_weight))
-    up_rows = (up_weight, line.swap(up_weight))
-    down_rows = (down_weight, line.swap(down_weight))
+    gate_rows, up_rows, down_rows = map(both_rows, (gate_weight, up_weight, down_weight))
+
+    count = inbound_gain.shape[0]
+    pad = 16
+    gains_own = jnp.stack([inbound_gain, attended_gain, prefeed_gain, postfeed_gain])
+    gains_other = line.swap(gains_own)
+    gains_row = jnp.where(
+        c == 0,
+        jnp.concatenate([gains_own, gains_other]),
+        jnp.concatenate([gains_other, gains_own]),
+    ).reshape(1, 8 * count)
+    gains_rows = jnp.pad(gains_row, ((0, pad - 1), (0, width - 8 * count)))
 
     query_width = out_weight.shape[0]
     heads = query_width // HEAD_DIM
@@ -428,12 +486,12 @@
             self.s = s
             self.own = tokens[s]
 
-        def attention(self, blocks):
-            self.tokens = join(blocks)
-            values = self.tokens.astype(f32)
-            self.root_in = inverse_root(values)
-            self.hidden = (values * self.root_in * inbound).astype(bf16)
-            raw = nt(self.hidden, qkv_weight)
+        def project(self, *blocks):
+            merged = join(blocks)
+            values = merged.astype(f32)
+            root_in = inverse_root(values)
+            hidden = (values * root_in * gain[0]).astype(bf16)
+            raw = nt(hidden, qkv_weight)
             queries = raw[:, :query_width].reshape(every, heads, HEAD_DIM)
             queries = (rotate(queries, cosine, sine) * query_scale).astype(bf16)
             keys = raw[:, query_width : query_width + HEAD_DIM].reshape(every, 1, HEAD_DIM)
@@ -441,82 +499,64 @@
             values = raw[:, query_width + HEAD_DIM :].astype(bf16)
             mine = jnp.concatenate([keys, values], axis=1).reshape(chips, rows, 2 * HEAD_DIM)
             both = jnp.concatenate([mine, line.swap(mine)], axis=1)
-            self.queries = queries.reshape(chips, rows, query_width)
-            self.keys, self.values = both[:, :, :HEAD_DIM], both[:, :, HEAD_DIM:]
-            self.attended = attend_forward(
-                infos[self.s], self.queries, self.keys, self.values, spans
-            ).reshape(every, query_width)
-            return split(nn(self.attended, out_weight).astype(bf16))
+            queries = queries.reshape(chips, rows, query_width)
+            return merged, root_in, hidden, queries, both[:, :, :HEAD_DIM], both[:, :, HEAD_DIM:]
+
+        def attend(self, queries, keys, values):
+            attended = attend_forward(infos[self.s], queries, keys, values, spans)
+            attended = attended.reshape(every, query_width)
+            return attended, nn(attended, out_weight).astype(bf16)
 
         def after_branch(self, terms):
             branch = total(terms)
             self.root_branch = inverse_root(branch)
             self.normed_branch = branch * self.root_branch
-            self.middle = self.own.astype(f32) + self.normed_branch * attended_g
+            self.middle = self.own.astype(f32) + self.normed_branch * gain[1]
             self.root_middle = inverse_root(self.middle)
-            return (self.middle * self.root_middle * prefeed).astype(bf16)
-
-        def feed(self, blocks):
-            self.hidden_ff = join(blocks)
-            self.product, self.slope, self.gelu = [], [], []
-            out = None
-            for gate_w, up_w, down_w in zip(gate_rows, up_rows, down_rows):
-                gate = nt(self.hidden_ff, gate_w)
-                up = nt(self.hidden_ff, up_w)
-                tanh = jnp.tanh(gelu_a * (gate + gelu_b * gate * gate * gate))
-                half = 0.5 * (1.0 + tanh)
-                gelu = gate * half
-                slope = half + 0.5 * gate * (1.0 - tanh * tanh) * (
-                    gelu_a * (1.0 + 3.0 * gelu_b * gate * gate)
-                )
-                self.product.append((gelu * up).astype(bf16))
-                self.gelu.append(gelu.astype(bf16))
-                self.slope.append((up * slope).astype(bf16))
-            out = sum(nn(p, w) for p, w in zip(self.product, down_rows))
-            return split(out.astype(bf16))
+            return (self.middle * self.root_middle * gain[2]).astype(bf16)
+
+        def feed(self, *blocks):
+            hidden_ff = join(blocks)
+            return (hidden_ff,) + tuple(gate_up(hidden_ff, gate_rows, up_rows))
+
+        def feed_down(self, product):
+            return nn(product, down_rows).astype(bf16)
 
         def after_feed(self, terms):
             feed = total(terms)
             root = inverse_root(feed)
             normed = feed * root
             self.upstream = cotangent[self.s].astype(f32)
-            self.output = (self.middle + normed * postfeed).astype(bf16)
+            self.output = (self.middle + normed * gain[3]).astype(bf16)
             self.postfeed_term = jnp.sum(self.upstream * normed, axis=0)
-            return norm_backward(normed, root, postfeed, self.upstream).astype(bf16)
-
-        def feed_back(self, blocks):
-            self.feed_low = join(blocks)
-            self.gate_back, self.up_back = [], []
-            for down_w, gelu, slope in zip(down_rows, self.gelu, self.slope):
-                grad = nt(self.feed_low, down_w)
-                self.gate_back.append((grad * slope.astype(f32)).astype(bf16))
-                self.up_back.append((grad * gelu.astype(f32)).astype(bf16))
-            out = sum(
-                nn(g, w)
-                for g, w in zip(self.gate_back + self.up_back, list(gate_rows) + list(up_rows))
-            )
-            return split(out.astype(bf16))
+            return norm_backward(normed, root, gain[3], self.upstream).astype(bf16)
+
+        def feed_back(self, feed_low, gelu, slope):
+            grad = nt(feed_low, down_rows)
+            return (grad * slope.astype(f32)).astype(bf16), (grad * gelu.astype(f32)).astype(bf16)
+
+        def feed_in(self, gate_back, up_back):
+            return (nn(gate_back, gate_rows) + nn(up_back, up_rows)).astype(bf16)
 
         def after_feed_back(self, terms):
             grad = total(terms)
             normed = self.middle * self.root_middle
             self.prefeed_term = jnp.sum(grad * normed, axis=0)
             self.middle_grad = self.upstream + norm_backward(
-                normed, self.root_middle, prefeed, grad
+                normed, self.root_middle, gain[2], grad
             )
             self.attended_term = jnp.sum(self.middle_grad * self.normed_branch, axis=0)
             return norm_backward(
-                self.normed_branch, self.root_branch, attended_g, self.middle_grad
+                self.normed_branch, self.root_branch, gain[1], self.middle_grad
             ).astype(bf16)
 
-        def attention_back(self, blocks):
-            self.branch_low = join(blocks)
-            mixed = nt(self.branch_low, out_weight).astype(bf16)
+        def attend_back(self, branch_low, queries, keys, values):
+            mixed = nt(branch_low, out_weight).astype(bf16)
             query_rot, key_rot, value_sum = attend_backward(
                 infos[self.s],
-                self.queries,
-                self.keys,
-                self.values,
+                queries,
+                keys,
+                values,
                 mixed.reshape(chips, rows, query_width),
                 spans,
             )
@@ -526,7 +566,7 @@
             query_rot = query_rot.reshape(every, heads, HEAD_DIM)
             query_back = (rotate(query_rot, cosine, -sine) * query_scale).astype(bf16)
             key_back = rotate(sums[:, :HEAD_DIM].reshape(every, 1, HEAD_DIM), cosine, -sine)
-            self.back = jnp.concatenate(
+            return jnp.concatenate(
                 [
                     query_back.reshape(every, query_width),
                     key_back.reshape(every, HEAD_DIM).astype(bf16),
@@ -534,70 +574,159 @@
                 ],
                 axis=1,
             )
-            grad = nn(self.back, qkv_weight)
-            self.inbound_term = jnp.sum(grad * (self.tokens.astype(f32) * self.root_in), axis=0)
-            return split(grad.astype(bf16))
-
-        def after_attention_back(self, terms):
+
+        def project_back(self, back, merged, root_in):
+            grad = nn(back, qkv_weight)
+            inbound_term = jnp.sum(grad * (merged.astype(f32) * root_in), axis=0)
+            return grad.astype(bf16), inbound_term
+
+        def after_project_back(self, terms):
             grad = total(terms)
             values = self.own.astype(f32)
             root = inverse_root(values)
-            return (self.middle_grad + norm_backward(values * root, root, inbound, grad)).astype(
+            return (self.middle_grad + norm_backward(values * root, root, gain[0], grad)).astype(
                 bf16
             )
 
+    def weight_grad(left_a, left_b, right_a, right_b):
+        return tn(join([left_a, left_b]), join([right_a, right_b])).astype(bf16)
+
+    def group_of(own, first, first_inputs, middle, last):
+        ex = Exchange(line, own)
+        firsts = ex.step(first, first_inputs)
+        ex.parts = split(firsts[0])
+        middles = []
+        for i in range(chips - 2):
+            middles.append(ex.step(*(middle[i] if i < len(middle) else ())))
+        lasts = ex.step(*last(ex.blocks()))
+        return firsts, middles, lasts, ex.terms()
+
+    data = lax.axis_size("dp")
+
+    def data_sum(values, order):
+        groups = [[(i + order) % data for i in range(data)]]
+        return lax.psum(values, "dp", axis_index_groups=groups)
+
+    def core_sum(grad):
+        count = grad.shape[0] // 2
+        return (grad[:count].astype(f32) + line.swap(grad[count:]).astype(f32)).astype(bf16)
+
     a, b = (Sequence(s) for s in range(seq_count))
 
-    blocks, _ = line.exchange(own=a.own)
-    parts_a = a.attention(blocks)
-    blocks, terms = line.exchange(own=b.own, parts=parts_a)
+    ex = Exchange(line, jnp.concatenate([a.own, gains_rows]), sums=False)
+    for _ in range(chips - 1):
+        ex.step()
+    blocks = ex.blocks()
+    gain = jnp.stack([block[rows, : 8 * count] for block in blocks])
+    gain = line.shift(gain, z).reshape(chips, 2, 4, count)
+    gain = gain.transpose(2, 0, 1, 3).reshape(4, 1, width).astype(f32)
+
+    def a_attention(*blocks):
+        projected = a.project(*blocks)
+        attended, out = a.attend(*projected[3:])
+        return (out, attended) + projected
+
+    firsts, _, lasts, terms = group_of(
+        b.own,
+        a_attention,
+        [block[:rows] for block in blocks],
+        [],
+        lambda blocks: (b.project, blocks),
+    )
+    _, a.attended, a.tokens, a.root_in, a.hidden, a.queries, a.keys, a.values = firsts
+    b.tokens, b.root_in, b.hidden, b.queries, b.keys, b.values = lasts
     hidden_a = a.after_branch(terms)
-    parts_b = b.attention(blocks)
-    blocks, terms = line.exchange(own=hidden_a, parts=parts_b)
+
+    def b_attention(*projected):
+        attended, out = b.attend(*projected)
+        return out, attended
+
+    firsts, _, lasts, terms = group_of(
+        hidden_a,
+        b_attention,
+        (b.queries, b.keys, b.values),
+        [],
+        lambda blocks: (a.feed, blocks),
+    )
+    b.attended = firsts[1]
+    a.hidden_ff, a.product, a.gelu, a.slope = lasts
     hidden_b = b.after_branch(terms)
-    parts_a = a.feed(blocks)
-    blocks, terms = line.exchange(own=hidden_b, parts=parts_a)
+
+    firsts, _, lasts, terms = group_of(
+        hidden_b,
+        lambda product: (a.feed_down(product),),
+        (a.product,),
+        [],
+        lambda blocks: (b.feed, blocks),
+    )
+    b.hidden_ff, b.product, b.gelu, b.slope = lasts
     low_a = a.after_feed(terms)
-    parts_b = b.feed(blocks)
-    blocks, terms = line.exchange(own=low_a, parts=parts_b)
+
+    def a_feed_back(*blocks):
+        feed_low = join(blocks)
+        return (feed_low,) + a.feed_back(feed_low, a.gelu, a.slope)
+
+    firsts, _, lasts, terms = group_of(
+        low_a,
+        lambda product: (b.feed_down(product),),
+        (b.product,),
+        [],
+        lambda blocks: (a_feed_back, blocks),
+    )
+    a.feed_low, a.gate_back, a.up_back = lasts
     low_b = b.after_feed(terms)
-    parts_a = a.feed_back(blocks)
-    blocks, terms = line.exchange(own=low_b, parts=parts_a)
+
+    def b_feed_back(*blocks):
+        feed_low = join(blocks)
+        down_grad = weight_grad(a.product, b.product, a.feed_low, feed_low)
+        return (feed_low, down_grad) + b.feed_back(feed_low, b.gelu, b.slope)
+
+    firsts, _, lasts, terms = group_of(
+        low_b,
+        lambda gate_back, up_back: (a.feed_in(gate_back, up_back),),
+        (a.gate_back, a.up_back),
+        [],
+        lambda blocks: (b_feed_back, blocks),
+    )
+    b.feed_low, down_grad, b.gate_back, b.up_back = lasts
+    down_sum = data_sum(core_sum(down_grad), 0)
     branch_a = a.after_feed_back(terms)
-    parts_b = b.feed_back(blocks)
-    blocks, terms = line.exchange(own=branch_a, parts=parts_b)
+
+    def a_attention_back(*blocks):
+        branch_low = join(blocks)
+        return branch_low, a.attend_back(branch_low, a.queries, a.keys, a.values)
+
+    def left_grad(left_a, left_b):
+        return (weight_grad(left_a, left_b, a.hidden_ff, b.hidden_ff),)
+
+    firsts, middles, lasts, terms = group_of(
+        branch_a,
+        lambda gate_back, up_back: (b.feed_in(gate_back, up_back),),
+        (b.gate_back, b.up_back),
+        [(left_grad, (a.gate_back, b.gate_back)), (left_grad, (a.up_back, b.up_back))],
+        lambda blocks: (a_attention_back, blocks),
+    )
+    gate_grad, up_grad = middles[0][0], middles[1][0]
+    gate_sum, up_sum = data_sum((core_sum(gate_grad), core_sum(up_grad)), 1)
+    a.branch_low, a.back = lasts
     branch_b = b.after_feed_back(terms)
-    parts_a = a.attention_back(blocks)
-    blocks, terms = line.exchange(own=branch_b, parts=parts_a)
-    tokens_grad_a = a.after_attention_back(terms)
-    parts_b = b.attention_back(blocks)
-    _, terms = line.exchange(parts=parts_b)
-    tokens_grad_b = b.after_attention_back(terms)
-
-    def feed_grad(left_name, right_name):
-        halves = []
-        right = join([getattr(s, right_name) for s in (a, b)])
-        for i in range(2):
-            left = join([getattr(s, left_name)[i] for s in (a, b)])
-            halves.append(tn(left, right))
-        return halves[0] + line.swap(halves[1].astype(bf16)).astype(f32)
-
-    down_grad = feed_grad("product", "feed_low")
-    gate_grad = feed_grad("gate_back", "hidden_ff")
-    up_grad = feed_grad("up_back", "hidden_ff")
-    feed_sums = lax.psum((down_grad.astype(bf16), gate_grad.astype(bf16), up_grad.astype(bf16)), "dp")
-    output_grad = pair_sum(
-        tn(join([a.attended, b.attended]), join([a.branch_low, b.branch_low]))
-    ).astype(bf16)
-    qkv_grad = tn(join([a.back, b.back]), join([a.hidden, b.hidden]))
-    query_grad = pair_sum(qkv_grad[:query_width]).astype(bf16)
-    key_grad = group_sum(qkv_grad[query_width : query_width + HEAD_DIM]).astype(bf16)
-    value_grad = group_sum(qkv_grad[query_width + HEAD_DIM :]).astype(bf16)
-    feed_sums, late = lax.optimization_barrier(
-        (feed_sums, (query_grad, key_grad, value_grad, output_grad))
-    )
-    late_sums = lax.psum(late, "dp")
-
+
+    def b_attention_back(*blocks):
+        branch_low = join(blocks)
+        return branch_low, b.attend_back(branch_low, b.queries, b.keys, b.values)
+
+    firsts, _, lasts, terms = group_of(
+        branch_b,
+        a.project_back,
+        (a.back, a.tokens, a.root_in),
+        [],
+        lambda blocks: (b_attention_back, blocks),
+    )
+    a.inbound_term = firsts[1]
+    b.branch_low, b.back = lasts
+    tokens_grad_a = a.after_project_back(terms)
+
+    grad, b.inbound_term = b.project_back(b.back, b.tokens, b.root_in)
     gain_terms = jnp.stack(
         [
             a.inbound_term + b.inbound_term,
@@ -605,10 +734,40 @@
             a.prefeed_term + b.prefeed_term,
             a.postfeed_term + b.postfeed_term,
         ]
-    )
-    gain_sums = lax.psum(gain_terms, ("dp", "ctx"))
-    count = inbound_gain.shape[0]
-    gain_sums = lax.dynamic_slice(gain_sums, (0, index * count), (4, count))
+    ).astype(bf16)
+    gain_terms = gain_terms.reshape(4, chips, 2, count).transpose(1, 2, 0, 3)
+    gain_terms = line.shift(gain_terms.reshape(chips, 1, 8 * count), -z)
+    gain_terms = jnp.pad(gain_terms, ((0, 0), (0, pad - 1), (0, width - 8 * count)))
+    ex = Exchange(line)
+    ex.parts = [jnp.concatenate([part, gain_terms[k]]) for k, part in enumerate(split(grad))]
+
+    def attention_grads(back_a, back_b):
+        qkv_grad = weight_grad(back_a, back_b, a.hidden, b.hidden)
+        output_grad = weight_grad(a.attended, b.attended, a.branch_low, b.branch_low)
+        return qkv_grad, output_grad
+
+    qkv_grad, output_grad = ex.step(attention_grads, (a.back, b.back))
+    for _ in range(chips - 2):
+        ex.step()
+    grad = total(ex.terms())
+    tokens_grad_b = b.after_project_back([grad[:rows]])
+
+    late_sums = data_sum(
+        tuple(
+            value.astype(bf16)
+            for value in (
+                pair_sum(qkv_grad[:query_width]),
+                group_sum(qkv_grad[query_width : query_width + HEAD_DIM]),
+                group_sum(qkv_grad[query_width + HEAD_DIM :]),
+                pair_sum(output_grad),
+            )
+        ),
+        2,
+    )
+    row = grad[rows, : 8 * count].reshape(2, 4, count)
+    mine = jnp.where(c == 0, row[0], row[1])
+    other = jnp.where(c == 0, row[1], row[0])
+    gain_sums = lax.psum(mine + line.swap(other.astype(bf16)).astype(f32), "dp")
 
     return (
         jnp.stack([a.output, b.output]),
@@ -617,9 +776,9 @@
         late_sums[1].astype(f32),
         late_sums[2].astype(f32),
         late_sums[3].astype(f32),
-        feed_sums[1].astype(f32),
-        feed_sums[2].astype(f32),
-        feed_sums[0].astype(f32),
+        gate_sum.astype(f32),
+        up_sum.astype(f32),
+        down_sum.astype(f32),
         gain_sums[0],
         gain_sums[1],
         gain_sums[2],

time: 1490 us -> 1440 us (0.966)
  matrix products: 376 us -> 219 us
  local copies, waits for them, and re-layouts: 34.9 us -> 126 us
  blocking collectives: 85.1 us -> 8.15 us
  waiting for transfers between devices: 555 us -> 613 us
  Pallas kernels: 46.1 us -> 90.9 us
  starting transfers between devices: 200 us -> 169 us
  other arithmetic: 169 us -> 186 us
    ppermute x34, waiting for transfers between devices: 121 us -> 220 us  [right(): return lax.ppermute(block, 'ctx', self.pairs(1, low, high))]
    dot_general x16 -> x6, matrix products: 145 us -> 46 us  [nt(): lax.dot_general(left_side, right_side, (((1,), (1,)), ((), ())), preferre...]
    ppermute x34, waiting for transfers between devices: 227 us -> 140 us  [left(): return lax.ppermute(block, 'ctx', self.pairs(-1, n - high, n - low))]
    dot_general x16 -> x10, matrix products: 140 us -> 93.7 us  [nn(): lax.dot_general(left_side, right_side, (((1,), (0,)), ((), ())), preferre...]
    pallas_call x0 -> x2, Pallas kernels: none -> 45.5 us  [gate_up(): pl.pallas_call(gate_up_kernel, out_shape=(jax.ShapeDtypeStruct((m, n), bf...]
    psum x2 -> x3, waiting for transfers between devices: 206 us -> 250 us  [data_sum(): return lax.psum(values, 'dp', axis_index_groups=groups)]
    all_gather x1 -> x0, blocking collectives: 42 us -> none  [on_device(): gains = lax.all_gather(gains_own, 'ctx', axis=1, tiled=True).astype(f32)]
    unnamed x410 -> x381, local copies, waits for them, and re-layouts: 11.9 us -> 53.6 us
  transfers between devices with their start and end apart: 88 -> 91, of which waited for: 45 -> 49; matrix products, arithmetic and copies ran while one was open for 35% -> 29% of each run, Pallas kernels for 3% -> 5%
where the time goes in v2:
time: 1440 us; the launch traced here: 1430 us
  waiting for transfers between devices  613 us (43%)
  matrix products  219 us (15%)
  other arithmetic  186 us (13%)
  starting transfers between devices  169 us (12%)
  local copies, waits for them, and re-layouts  126 us (9%)
  Pallas kernels  90.9 us (6%)
  between operations  17.3 us (1%)
    psum x3, waiting for transfers between devices, data_sum(): return lax.psum(values, 'dp', axis_index_groups=groups)  250 us
    ppermute x34, waiting for transfers between devices, right(): return lax.ppermute(block, 'ctx', self.pairs(1, low, high))  220 us
    ppermute x34, waiting for transfers between devices, left(): return lax.ppermute(block, 'ctx', self.pairs(-1, n - high, n - low))  140 us
    ppermute x34, starting transfers between devices, right(): return lax.ppermute(block, 'ctx', self.pairs(1, low, high))  112 us
    dot_general x10, matrix products, nn(): lax.dot_general(left_side, right_side, (((1,), (0,)), ((), ())), preferre...  93.7 us
    dot_general x5, matrix products, tn(): lax.dot_general(left_side, right_side, (((0,), (0,)), ((), ())), preferre...  79.7 us
    unnamed x381, local copies, waits for them, and re-layouts  53.6 us
    ppermute x34, starting transfers between devices, left(): return lax.ppermute(block, 'ctx', self.pairs(-1, n - high, n - low))  53.2 us
  transfers between devices with their start and end apart: 91, of which 49 were waited for; matrix products, arithmetic and copies ran while one was open for 29% of the time, Pallas kernels for 5%

profile of v2, /device:TPU:0, one launch (start us, length us, event | category | flops | bytes accessed | tf_op | source)
XLA Modules:
  0.0 1428.2 jit_solution(4326421046879215907)
XLA Ops:
  24.7 16.0 %collective-permute-done.1 = bf16[208,2304]{1,0:T(8,128)(2,1)} collective-permute-done((bf16[208,2304]{1,0:T(8,128)(2,1)}, bf16[208,2304]{1,0:T(8,128)(2,1)}, u32[]{:S(2)}, u32[]{:S(2)}) %collective-permute-start.1) | collective-permute-done | bytes 958496 | tf_op jit(solution)/shard_map/ppermute | solution.py:59
  52.0 23.7 %collective-permute-done.4 = bf16[208,2304]{1,0:T(8,128)(2,1)S(1)} collective-permute-done((bf16[208,2304]{1,0:T(8,128)(2,1)}, bf16[208,2304]{1,0:T(8,128)(2,1)S(1)}, u32[]{:S(2)}, u32[]{:S(2)}) %collective-permute-start.4) | collective-permute-done | bytes 958496 | tf_op jit(solution)/shard_map/ppermute | solution.py:63
  81.1 20.1 %collective-permute-done.6 = bf16[208,2304]{1,0:T(8,128)(2,1)S(1)} collective-permute-done((bf16[208,2304]{1,0:T(8,128)(2,1)S(1)}, bf16[208,2304]{1,0:T(8,128)(2,1)S(1)}, u32[]{:S(2)}, u32[]{:S(2)}) %collective-permute-start.6) | collective-permute-done | bytes 958496 | tf_op jit(solution)/shard_map/ppermute | solution.py:63
  132.1 7.4 shard_map.246
  153.9 14.6 %collective-permute-done.14 = bf16[192,2304]{1,0:T(8,128)(2,1)S(1)} collective-permute-done((bf16[192,2304]{1,0:T(8,128)(2,1)S(1)}, bf16[192,2304]{1,0:T(8,128)(2,1)S(1)}, u32[]{:S(2)}, u32[]{:S(2)}) %collective-permute-start.14) | collective-permute-done | bytes 884768 | tf_op jit(solution)/shard_map/ppermute | solution.py:59
  181.9 11.2 collective-permute-done.16
  220.4 10.0 collective-permute-start.19
  257.6 7.9 shard_map.247
  283.5 12.0 collective-permute-done.23
  306.7 13.4 collective-permute-done.25
  332.6 22.8 %shard_map.248 = (bf16[768,2304]{1,0:T(8,128)(2,1)}, bf16[768,2304]{1,0:T(8,128)(2,1)}, bf16[768,2304]{1,0:T(8,128)(2,1)}) custom-call(bf16[768,2304]{1,0:T(8,128)(2,1)} %constant_dynamic-update-slice_fusion.8.h_ref, bf16[2304,2304]{1,0:T(8,128)(2,1)} %constant_dynamic-update-slice_fusion.12.gate_ref, ...), custom_call_target="tpu_custom_call" | custom-call | flops 16307453952 | bytes 35389440 | tf_op jit(solution)/shard_map/pallas_call | solution.py:347
  366.9 12.1 convolution_convert_fusion.4
  390.8 13.5 collective-permute-done.34
  415.8 11.7 collective-permute-done.36
  445.4 22.7 %shard_map.249 = (bf16[768,2304]{1,0:T(8,128)(2,1)}, bf16[768,2304]{1,0:T(8,128)(2,1)}, bf16[768,2304]{1,0:T(8,128)(2,1)}) custom-call(bf16[768,2304]{1,0:T(8,128)(2,1)} %constant_dynamic-update-slice_fusion.18.h_ref, bf16[2304,2304]{1,0:T(8,128)(2,1)} %constant_dynamic-update-slice_fusion.12.gate_ref, ...), custom_call_target="tpu_custom_call" | custom-call | flops 16307453952 | bytes 35389440 | tf_op jit(solution)/shard_map/pallas_call | solution.py:347
  481.5 12.1 convolution_convert_fusion.3
  501.2 10.7 collective-permute-done.42
  521.9 9.2 collective-permute-done.44
  546.4 17.1 %multiply_convert_fusion.2 = (bf16[768,2304]{1,0:T(8,128)(2,1)}, bf16[768,2304]{1,0:T(8,128)(2,1)}) fusion(bf16[768,2304]{1,0:T(8,128)(2,1)} %get-tuple-element.370, bf16[768,2304]{1,0:T(8,128)(2,1)} %get-tuple-element.369, bf16[768,2304]{1,0:T(8,128)(2,1)} %constant_dynamic-update-slice_fusion.22, bf16[2304,2304]{1,0:T(8,128)(2,1)} %constant_dynamic-update-slice_fusion.16), kind=kOutput, calls=%fused_computation.39 | convolution fusion | flops 8164343808 | bytes 28311552 | tf_op jit(solution)/shard_map/dot_general | solution.py:26
  579.0 13.8 fusion.160
  592.8 11.1 add_convert_fusion.4
  614.1 8.8 collective-permute-done.50
  658.0 20.6 %convolution_convert_fusion.2 = bf16[2304,2304]{1,0:T(8,128)(2,1)} fusion(bf16[1536,2304]{1,0:T(8,128)(2,1)S(1)} %get-tuple-element.621, bf16[768,2304]{1,0:T(8,128)(2,1)} %get-tuple-element.351, bf16[768,2304]{1,0:T(8,128)(2,1)S(1)} %copy-done.152), kind=kOutput, calls=%fused_computation.2 | convolution fusion | flops 16326918144 | bytes 24772608 | tf_op jit(solution)/shard_map/dot_general | solution.py:38
  678.7 17.2 %multiply_convert_fusion = (bf16[768,2304]{1,0:T(8,128)(2,1)}, bf16[768,2304]{1,0:T(8,128)(2,1)}) fusion(bf16[768,2304]{1,0:T(8,128)(2,1)} %get-tuple-element.398, bf16[768,2304]{1,0:T(8,128)(2,1)} %get-tuple-element.397, bf16[768,2304]{1,0:T(8,128)(2,1)} %copy-done.117, bf16[2304,2304]{1,0:T(8,128)(2,1)} %constant_dynamic-update-slice_fusion.16), kind=kOutput, calls=%fused_computation.36 | convolution fusion | flops 8164343808 | bytes 28311552 | tf_op jit(solution)/shard_map/dot_general | solution.py:26
  704.6 15.1 %fusion.161 = f32[768,2304]{1,0:T(8,128)} fusion(bf16[768,2304]{1,0:T(8,128)(2,1)S(1)} %copy-done.148, bf16[2304,2304]{1,0:T(8,128)(2,1)} %constant_dynamic-update-slice_fusion.14.up_ref), kind=kOutput, calls=%fused_computation.456 | convolution fusion | flops 8153726976 | bytes 21233664 | tf_op jit(solution)/shard_map/dot_general | solution.py:32
  725.7 10.5 add_convert_fusion.3
  736.2 7.7 collective-permute-done.56
  751.9 21.4 %convolution_convert_fusion.1 = bf16[2304,2304]{1,0:T(8,128)(2,1)} fusion(bf16[1536,2304]{1,0:T(8,128)(2,1)} %constant_dynamic-update-slice_fusion.35, bf16[768,2304]{1,0:T(8,128)(2,1)S(1)} %copy-done.150, bf16[768,2304]{1,0:T(8,128)(2,1)S(1)} %copy-done.147), kind=kOutput, calls=%fused_computation.1 | convolution fusion | flops 16326918144 | bytes 24772608 | tf_op jit(solution)/shard_map/dot_general | solution.py:38
  780.0 21.3 %convolution_convert_fusion = bf16[2304,2304]{1,0:T(8,128)(2,1)} fusion(bf16[1536,2304]{1,0:T(8,128)(2,1)} %constant_dynamic-update-slice_fusion.35, bf16[768,2304]{1,0:T(8,128)(2,1)S(1)} %copy-done.149, bf16[768,2304]{1,0:T(8,128)(2,1)S(1)} %copy-done.146), kind=kOutput, calls=%fused_computation | convolution fusion | flops 16326918144 | bytes 24772608 | tf_op jit(solution)/shard_map/dot_general | solution.py:38
  807.7 14.6 %shard_map.250 = (f32[4,192,512]{2,1,0:T(8,128)S(1)}, f32[4,384,256]{2,1,0:T(8,128)S(1)}, f32[4,384,256]{2,1,0:T(8,128)S(1)}) custom-call(s32[6]{0:T(128)S(1)} %copy-done.15, bf16[4,192,512]{2,1,0:T(8,128)(2,1)S(1)} %copy-done.3, bf16[4,384,256]{2,1,0:T(8,128)(2,1)S(1)} %copy-done.11, bf16[4,384,256]{2,1,0:T(8,128)(2,1)S(1)} %copy-done.9, ...), custom_call_target="tpu_custom_call" | custom-call | flops 6039797760 | bytes 12582912 | tf_op jit(solution)/shard_map/pallas_call | solution.py:291
  866.7 7.3 multiply_reduce_fusion.1
  874.0 9.4 collective-permute-done.65
  892.9 16.2 %collective-permute-done.67 = bf16[192,2304]{1,0:T(8,128)(2,1)S(1)} collective-permute-done((bf16[192,2304]{1,0:T(8,128)(2,1)S(1)}, bf16[192,2304]{1,0:T(8,128)(2,1)S(1)}, u32[]{:S(2)}, u32[]{:S(2)}) %collective-permute-start.67) | collective-permute-done | bytes 884768 | tf_op jit(solution)/shard_map/ppermute | solution.py:59
  950.0 15.5 %shard_map.251 = (f32[4,192,512]{2,1,0:T(8,128)S(1)}, f32[4,384,256]{2,1,0:T(8,128)S(1)}, f32[4,384,256]{2,1,0:T(8,128)S(1)}) custom-call(s32[6]{0:T(128)S(1)} %copy-done.13, bf16[4,192,512]{2,1,0:T(8,128)(2,1)S(1)} %copy-done.1, bf16[4,384,256]{2,1,0:T(8,128)(2,1)S(1)} %copy-done.7, bf16[4,384,256]{2,1,0:T(8,128)(2,1)S(1)} %copy-done.5, ...), custom_call_target="tpu_custom_call" | custom-call | flops 6039797760 | bytes 12582912 | tf_op jit(solution)/shard_map/pallas_call | solution.py:291
  968.9 6.1 add_convert_fusion
  991.2 8.7 collective-permute-done.71
  1004.9 7.8 fusion.153
  1022.6 10.4 fusion.23
  1050.1 7.8 add_convert_fusion.2
  1057.8 7.7 add_convert_fusion.1
  1073.2 20.2 %collective-permute-done.76 = bf16[208,2304]{1,0:T(8,128)(2,1)S(1)} collective-permute-done((bf16[208,2304]{1,0:T(8,128)(2,1)S(1)}, bf16[208,2304]{1,0:T(8,128)(2,1)S(1)}, u32[]{:S(2)}, u32[]{:S(2)}) %collective-permute-start.76) | collective-permute-done | bytes 958496 | tf_op jit(solution)/shard_map/ppermute | solution.py:59
  1093.9 7.1 collective-permute-start.78
  1103.7 17.3 %collective-permute-done.78 = bf16[208,2304]{1,0:T(8,128)(2,1)S(1)} collective-permute-done((bf16[208,2304]{1,0:T(8,128)(2,1)S(1)}, bf16[208,2304]{1,0:T(8,128)(2,1)S(1)}, u32[]{:S(2)}, u32[]{:S(2)}) %collective-permute-start.78) | collective-permute-done | bytes 958496 | tf_op jit(solution)/shard_map/ppermute | solution.py:59
  1135.8 8.1 psum.63
  1144.6 7.4 convert_element_type.867
  1152.0 44.2 %all-reduce.12.cloned.1.call-done = (bf16[256,2304]{1,0:T(8,128)(2,1)}, bf16[128,2304]{1,0:T(8,128)(2,1)}, bf16[128,2304]{1,0:T(8,128)(2,1)}, bf16[256,2304]{1,0:T(8,128)(2,1)}) async-done(((bf16[256,2304]{1,0:T(8,128)(2,1)}, bf16[128,2304]{1,0:T(8,128)(2,1)}, bf16[128,2304]{1,0:T(8,128)(2,1)}, bf16[256,2304]{1,0:T(8,128)(2,1)}), (bf16[256,2304]{1,0:T(8,128)(2,1)}, bf16[128,2304]{1,0:T(8,128)(2,1)}, ...) | async-done | bytes 3538960 | tf_op jit(solution)/shard_map/psum | solution.py:608
  1202.9 206.1 %all-reduce.10.cloned.1.call-done = (bf16[1152,2304]{1,0:T(8,128)(2,1)}, bf16[1152,2304]{1,0:T(8,128)(2,1)}) async-done(((bf16[1152,2304]{1,0:T(8,128)(2,1)}, bf16[1152,2304]{1,0:T(8,128)(2,1)}), (bf16[1152,2304]{1,0:T(8,128)(2,1)}, bf16[1152,2304]{1,0:T(8,128)(2,1)})) %all-reduce.10.cloned.1.call-update) | async-done | bytes 10616848 | tf_op jit(solution)/shard_map/psum | solution.py:608
  1409.0 7.6 convert_element_type.859
  (785 shorter events, 566.0 us)
Async XLA Ops:
  7.2 1137.4 %all-reduce.8.cloned.1.call-start = ((), (), s32[]{:S(2)}) async-start(), calls=%async_computation | async-start | bytes 10616832 | tf_op jit(solution)/shard_map/psum | solution.py:608
  10.5 38.0 %collective-permute-start.10 = (bf16[128,2304]{1,0:T(8,128)(2,1)}, bf16[128,2304]{1,0:T(8,128)(2,1)}, u32[]{:S(2)}, u32[]{:S(2)}) collective-permute-start(bf16[128,2304]{1,0:T(8,128)(2,1)} %param.19), channel_id=1, source_target_pairs={{0,1},{1,0},{2,3},{3,2},{4,5},{5,4},{6,7},{7,6},{8,9},{9,8},{10,11... | collective-permute-start | bytes 1769480 | tf_op jit(solution)/shard_map/ppermute | solution.py:66
  10.6 40.8 %collective-permute-start.11 = (bf16[128,2304]{1,0:T(8,128)(2,1)}, bf16[128,2304]{1,0:T(8,128)(2,1)}, u32[]{:S(2)}, u32[]{:S(2)}) collective-permute-start(bf16[128,2304]{1,0:T(8,128)(2,1)} %param.20), channel_id=1, source_target_pairs={{0,1},{1,0},{2,3},{3,2},{4,5},{5,4},{6,7},{7,6},{8,9},{9,8},{10,11... | collective-permute-start | bytes 1769480 | tf_op jit(solution)/shard_map/ppermute | solution.py:66
  11.0 34.8 %collective-permute-start.9 = (bf16[256,2304]{1,0:T(8,128)(2,1)}, bf16[256,2304]{1,0:T(8,128)(2,1)}, u32[]{:S(2)}, u32[]{:S(2)}) collective-permute-start(bf16[256,2304]{1,0:T(8,128)(2,1)} %param.18), channel_id=1, source_target_pairs={{0,1},{1,0},{2,3},{3,2},{4,5},{5,4},{6,7},{7,6},{8,9},{9,8},{10,11... | collective-permute-start | bytes 3538952 | tf_op jit(solution)/shard_map/ppermute | solution.py:66
  14.8 25.9 %collective-permute-start.1 = (bf16[208,2304]{1,0:T(8,128)(2,1)}, bf16[208,2304]{1,0:T(8,128)(2,1)}, u32[]{:S(2)}, u32[]{:S(2)}) collective-permute-start(bf16[208,2304]{1,0:T(8,128)(2,1)} %fusion.98), channel_id=1, source_target_pairs={{0,2},{1,3},{2,4},{3,5},{4,6},{5,7},{8,10},{9,11},{10,12},{11,13},... | collective-permute-start | bytes 2875400 | tf_op jit(solution)/shard_map/ppermute | solution.py:59
  20.6 25.1 %collective-permute-start.2 = (bf16[208,2304]{1,0:T(8,128)(2,1)}, bf16[208,2304]{1,0:T(8,128)(2,1)}, u32[]{:S(2)}, u32[]{:S(2)}) collective-permute-start(bf16[208,2304]{1,0:T(8,128)(2,1)} %fusion.98), channel_id=1, source_target_pairs={{2,0},{3,1},{4,2},{5,3},{6,4},{7,5},{10,8},{11,9},{12,10},{13,11},... | collective-permute-start | bytes 2875400 | tf_op jit(solution)/shard_map/ppermute | solution.py:63
  40.7 75.5 %collective-permute-start.13 = (bf16[256,2304]{1,0:T(8,128)(2,1)}, bf16[256,2304]{1,0:T(8,128)(2,1)}, u32[]{:S(2)}, u32[]{:S(2)}) collective-permute-start(bf16[256,2304]{1,0:T(8,128)(2,1)} %param.21), channel_id=1, source_target_pairs={{0,1},{1,0},{2,3},{3,2},{4,5},{5,4},{6,7},{7,6},{8,9},{9,8},{10,11... | collective-permute-start | bytes 3538952 | tf_op jit(solution)/shard_map/ppermute | solution.py:66
  45.8 206.5 %collective-permute-start.29 = (bf16[1152,2304]{1,0:T(8,128)(2,1)}, bf16[1152,2304]{1,0:T(8,128)(2,1)}, u32[]{:S(2)}, u32[]{:S(2)}) collective-permute-start(bf16[1152,2304]{1,0:T(8,128)(2,1)} %param.22), channel_id=1, source_target_pairs={{0,1},{1,0},{2,3},{3,2},{4,5},{5,4},{6,7},{7,6},{8,9},{9,8},{10,11... | collective-permute-start | bytes 15925256 | tf_op jit(solution)/shard_map/ppermute | solution.py:66
  48.5 27.3 %collective-permute-start.4 = (bf16[208,2304]{1,0:T(8,128)(2,1)}, bf16[208,2304]{1,0:T(8,128)(2,1)S(1)}, u32[]{:S(2)}, u32[]{:S(2)}) collective-permute-start(bf16[208,2304]{1,0:T(8,128)(2,1)} %collective-permute-done.2), channel_id=1, source_target_pairs={{2,0},{3,1},{4,2},{5,3},{10,8},{11,9},{12,10},{13,11},{18,16},{19,... | collective-permute-start | bytes 2875400 | tf_op jit(solution)/shard_map/ppermute | solution.py:63
  51.4 226.8 %collective-permute-start.30 = (bf16[1152,2304]{1,0:T(8,128)(2,1)}, bf16[1152,2304]{1,0:T(8,128)(2,1)}, u32[]{:S(2)}, u32[]{:S(2)}) collective-permute-start(bf16[1152,2304]{1,0:T(8,128)(2,1)} %param.23), channel_id=1, source_target_pairs={{0,1},{1,0},{2,3},{3,2},{4,5},{5,4},{6,7},{7,6},{8,9},{9,8},{10,11... | collective-permute-start | bytes 15925256 | tf_op jit(solution)/shard_map/ppermute | solution.py:66
  76.5 24.7 %collective-permute-start.6 = (bf16[208,2304]{1,0:T(8,128)(2,1)S(1)}, bf16[208,2304]{1,0:T(8,128)(2,1)S(1)}, u32[]{:S(2)}, u32[]{:S(2)}) collective-permute-start(bf16[208,2304]{1,0:T(8,128)(2,1)S(1)} %collective-permute-done.4), channel_id=1, source_target_pairs={{2,0},{3,1},{10,8},{11,9},{18,16},{19,17},{26,24},{27,25}} | collective-permute-start | bytes 2875400 | tf_op jit(solution)/shard_map/ppermute | solution.py:63
  122.9 23.8 %collective-permute-start.8 = (bf16[192,2304]{1,0:T(8,128)(2,1)S(1)}, bf16[192,2304]{1,0:T(8,128)(2,1)}, u32[]{:S(2)}, u32[]{:S(2)}) collective-permute-start(bf16[192,2304]{1,0:T(8,128)(2,1)S(1)} %copy-done.67), channel_id=1, source_target_pairs={{2,0},{3,1},{4,2},{5,3},{6,4},{7,5},{10,8},{11,9},{12,10},{13,11},... | collective-permute-start | bytes 2654216 | tf_op jit(solution)/shard_map/ppermute | solution.py:63
  149.8 22.8 %collective-permute-start.15 = (bf16[192,2304]{1,0:T(8,128)(2,1)S(1)}, bf16[192,2304]{1,0:T(8,128)(2,1)S(1)}, u32[]{:S(2)}, u32[]{:S(2)}) collective-permute-start(bf16[192,2304]{1,0:T(8,128)(2,1)S(1)} %get-tuple-element.277), channel_id=1, source_target_pairs={{2,0},{3,1},{4,2},{5,3},{6,4},{7,5},{10,8},{11,9},{12,10},{13,11},... | collective-permute-start | bytes 2654216 | tf_op jit(solution)/shard_map/ppermute | solution.py:63
  210.8 29.1 %collective-permute-start.20 = (bf16[4,192,512]{2,1,0:T(8,128)(2,1)}, bf16[4,192,512]{2,1,0:T(8,128)(2,1)}, u32[]{:S(2)}, u32[]{:S(2)}) collective-permute-start(bf16[4,192,512]{2,1,0:T(8,128)(2,1)} %pad_maximum_fusion.11), channel_id=1, source_target_pairs={{0,1},{1,0},{2,3},{3,2},{4,5},{5,4},{6,7},{7,6},{8,9},{9,8},{10,11... | collective-permute-start | bytes 2359304 | tf_op jit(solution)/shard_map/ppermute | solution.py:66
  217.0 24.8 %collective-permute-start.18 = (bf16[192,2304]{1,0:T(8,128)(2,1)}, bf16[192,2304]{1,0:T(8,128)(2,1)S(1)}, u32[]{:S(2)}, u32[]{:S(2)}) collective-permute-start(bf16[192,2304]{1,0:T(8,128)(2,1)} %get-tuple-element.284), channel_id=1, source_target_pairs={{0,2},{1,3},{2,4},{3,5},{4,6},{5,7},{8,10},{9,11},{10,12},{11,13},... | collective-permute-start | bytes 2654216 | tf_op jit(solution)/shard_map/ppermute | solution.py:59
  220.4 23.9 %collective-permute-start.19 = (bf16[192,2304]{1,0:T(8,128)(2,1)}, bf16[192,2304]{1,0:T(8,128)(2,1)S(1)}, u32[]{:S(2)}, u32[]{:S(2)}) collective-permute-start(bf16[192,2304]{1,0:T(8,128)(2,1)} %get-tuple-element.285), channel_id=1, source_target_pairs={{2,0},{3,1},{4,2},{5,3},{6,4},{7,5},{10,8},{11,9},{12,10},{13,11},... | collective-permute-start | bytes 2654216 | tf_op jit(solution)/shard_map/ppermute | solution.py:63
  239.9 64.0 %collective-permute-start.33 = (bf16[1152,2304]{1,0:T(8,128)(2,1)}, bf16[1152,2304]{1,0:T(8,128)(2,1)S(1)}, u32[]{:S(2)}, u32[]{:S(2)}) collective-permute-start(bf16[1152,2304]{1,0:T(8,128)(2,1)} %param.24), channel_id=1, source_target_pairs={{0,1},{1,0},{2,3},{3,2},{4,5},{5,4},{6,7},{7,6},{8,9},{9,8},{10,11... | collective-permute-start | bytes 15925256 | tf_op jit(solution)/shard_map/ppermute | solution.py:66
  247.4 22.9 %collective-permute-start.21 = (bf16[192,2304]{1,0:T(8,128)(2,1)S(1)}, bf16[192,2304]{1,0:T(8,128)(2,1)S(1)}, u32[]{:S(2)}, u32[]{:S(2)}) collective-permute-start(bf16[192,2304]{1,0:T(8,128)(2,1)S(1)} %multiply_convert_fusion.7), channel_id=1, source_target_pairs={{0,2},{1,3},{2,4},{3,5},{4,6},{5,7},{8,10},{9,11},{10,12},{11,13},... | collective-permute-start | bytes 2654216 | tf_op jit(solution)/shard_map/ppermute | solution.py:59
  251.0 23.5 %collective-permute-start.22 = (bf16[192,2304]{1,0:T(8,128)(2,1)S(1)}, bf16[192,2304]{1,0:T(8,128)(2,1)S(1)}, u32[]{:S(2)}, u32[]{:S(2)}) collective-permute-start(bf16[192,2304]{1,0:T(8,128)(2,1)S(1)} %multiply_convert_fusion.7), channel_id=1, source_target_pairs={{2,0},{3,1},{4,2},{5,3},{6,4},{7,5},{10,8},{11,9},{12,10},{13,11},... | collective-permute-start | bytes 2654216 | tf_op jit(solution)/shard_map/ppermute | solution.py:63
  325.2 30.3 %collective-permute-start.27 = (bf16[192,2304]{1,0:T(8,128)(2,1)S(1)}, bf16[192,2304]{1,0:T(8,128)(2,1)S(1)}, u32[]{:S(2)}, u32[]{:S(2)}) collective-permute-start(bf16[192,2304]{1,0:T(8,128)(2,1)S(1)} %get-tuple-element.311), channel_id=1, source_target_pairs={{0,2},{1,3},{2,4},{3,5},{4,6},{5,7},{8,10},{9,11},{10,12},{11,13},... | collective-permute-start | bytes 2654216 | tf_op jit(solution)/shard_map/ppermute | solution.py:59
  327.4 28.1 %collective-permute-start.28 = (bf16[192,2304]{1,0:T(8,128)(2,1)S(1)}, bf16[192,2304]{1,0:T(8,128)(2,1)S(1)}, u32[]{:S(2)}, u32[]{:S(2)}) collective-permute-start(bf16[192,2304]{1,0:T(8,128)(2,1)S(1)} %get-tuple-element.312), channel_id=1, source_target_pairs={{2,0},{3,1},{4,2},{5,3},{6,4},{7,5},{10,8},{11,9},{12,10},{13,11},... | collective-permute-start | bytes 2654216 | tf_op jit(solution)/shard_map/ppermute | solution.py:63
  438.2 29.8 %collective-permute-start.38 = (bf16[192,2304]{1,0:T(8,128)(2,1)}, bf16[192,2304]{1,0:T(8,128)(2,1)S(1)}, u32[]{:S(2)}, u32[]{:S(2)}) collective-permute-start(bf16[192,2304]{1,0:T(8,128)(2,1)} %get-tuple-element.337), channel_id=1, source_target_pairs={{0,2},{1,3},{2,4},{3,5},{4,6},{5,7},{8,10},{9,11},{10,12},{11,13},... | collective-permute-start | bytes 2654216 | tf_op jit(solution)/shard_map/ppermute | solution.py:59
  440.0 28.1 %collective-permute-start.39 = (bf16[192,2304]{1,0:T(8,128)(2,1)}, bf16[192,2304]{1,0:T(8,128)(2,1)}, u32[]{:S(2)}, u32[]{:S(2)}) collective-permute-start(bf16[192,2304]{1,0:T(8,128)(2,1)} %get-tuple-element.338), channel_id=1, source_target_pairs={{2,0},{3,1},{4,2},{5,3},{6,4},{7,5},{10,8},{11,9},{12,10},{13,11},... | collective-permute-start | bytes 2654216 | tf_op jit(solution)/shard_map/ppermute | solution.py:63
  537.4 26.2 %collective-permute-start.46 = (bf16[192,2304]{1,0:T(8,128)(2,1)}, bf16[192,2304]{1,0:T(8,128)(2,1)}, u32[]{:S(2)}, u32[]{:S(2)}) collective-permute-start(bf16[192,2304]{1,0:T(8,128)(2,1)} %get-tuple-element.363), channel_id=1, source_target_pairs={{0,2},{1,3},{2,4},{3,5},{4,6},{5,7},{8,10},{9,11},{10,12},{11,13},... | collective-permute-start | bytes 2654216 | tf_op jit(solution)/shard_map/ppermute | solution.py:59
  572.7 31.3 %collective-permute-start.48 = (bf16[192,2304]{1,0:T(8,128)(2,1)S(1)}, bf16[192,2304]{1,0:T(8,128)(2,1)S(1)}, u32[]{:S(2)}, u32[]{:S(2)}) collective-permute-start(bf16[192,2304]{1,0:T(8,128)(2,1)S(1)} %get-tuple-element.392), channel_id=1, source_target_pairs={{0,2},{1,3},{2,4},{3,5},{4,6},{5,7},{8,10},{9,11},{10,12},{11,13},... | collective-permute-start | bytes 2654216 | tf_op jit(solution)/shard_map/ppermute | solution.py:59
  577.5 26.5 %collective-permute-start.49 = (bf16[192,2304]{1,0:T(8,128)(2,1)S(1)}, bf16[192,2304]{1,0:T(8,128)(2,1)S(1)}, u32[]{:S(2)}, u32[]{:S(2)}) collective-permute-start(bf16[192,2304]{1,0:T(8,128)(2,1)S(1)} %get-tuple-element.392), channel_id=1, source_target_pairs={{2,0},{3,1},{4,2},{5,3},{6,4},{7,5},{10,8},{11,9},{12,10},{13,11},... | collective-permute-start | bytes 2654216 | tf_op jit(solution)/shard_map/ppermute | solution.py:63
  649.2 46.8 %collective-permute-start.54 = (bf16[192,2304]{1,0:T(8,128)(2,1)}, bf16[192,2304]{1,0:T(8,128)(2,1)}, u32[]{:S(2)}, u32[]{:S(2)}) collective-permute-start(bf16[192,2304]{1,0:T(8,128)(2,1)} %get-tuple-element.390), channel_id=1, source_target_pairs={{0,2},{1,3},{2,4},{3,5},{4,6},{5,7},{8,10},{9,11},{10,12},{11,13},... | collective-permute-start | bytes 2654216 | tf_op jit(solution)/shard_map/ppermute | solution.py:59
  653.2 42.7 %collective-permute-start.55 = (bf16[192,2304]{1,0:T(8,128)(2,1)}, bf16[192,2304]{1,0:T(8,128)(2,1)}, u32[]{:S(2)}, u32[]{:S(2)}) collective-permute-start(bf16[192,2304]{1,0:T(8,128)(2,1)} %get-tuple-element.391), channel_id=1, source_target_pairs={{2,0},{3,1},{4,2},{5,3},{6,4},{7,5},{10,8},{11,9},{12,10},{13,11},... | collective-permute-start | bytes 2654216 | tf_op jit(solution)/shard_map/ppermute | solution.py:63
  719.7 24.2 %collective-permute-start.56 = (bf16[192,2304]{1,0:T(8,128)(2,1)S(1)}, bf16[192,2304]{1,0:T(8,128)(2,1)S(1)}, u32[]{:S(2)}, u32[]{:S(2)}) collective-permute-start(bf16[192,2304]{1,0:T(8,128)(2,1)S(1)} %multiply_convert_fusion.5), channel_id=1, source_target_pairs={{0,2},{1,3},{2,4},{3,5},{4,6},{5,7},{8,10},{9,11},{10,12},{11,13},... | collective-permute-start | bytes 2654216 | tf_op jit(solution)/shard_map/ppermute | solution.py:59
  724.3 23.8 %collective-permute-start.57 = (bf16[192,2304]{1,0:T(8,128)(2,1)S(1)}, bf16[192,2304]{1,0:T(8,128)(2,1)S(1)}, u32[]{:S(2)}, u32[]{:S(2)}) collective-permute-start(bf16[192,2304]{1,0:T(8,128)(2,1)S(1)} %multiply_convert_fusion.5), channel_id=1, source_target_pairs={{2,0},{3,1},{4,2},{5,3},{6,4},{7,5},{10,8},{11,9},{12,10},{13,11},... | collective-permute-start | bytes 2654216 | tf_op jit(solution)/shard_map/ppermute | solution.py:63
  748.3 25.1 %collective-permute-start.58 = (bf16[192,2304]{1,0:T(8,128)(2,1)S(1)}, bf16[192,2304]{1,0:T(8,128)(2,1)S(1)}, u32[]{:S(2)}, u32[]{:S(2)}) collective-permute-start(bf16[192,2304]{1,0:T(8,128)(2,1)S(1)} %get-tuple-element.410), channel_id=1, source_target_pairs={{0,2},{1,3},{2,4},{3,5},{4,6},{5,7},{8,10},{9,11},{10,12},{11,13},... | collective-permute-start | bytes 2654216 | tf_op jit(solution)/shard_map/ppermute | solution.py:59
  750.6 23.9 %collective-permute-start.59 = (bf16[192,2304]{1,0:T(8,128)(2,1)S(1)}, bf16[192,2304]{1,0:T(8,128)(2,1)S(1)}, u32[]{:S(2)}, u32[]{:S(2)}) collective-permute-start(bf16[192,2304]{1,0:T(8,128)(2,1)S(1)} %get-tuple-element.411), channel_id=1, source_target_pairs={{2,0},{3,1},{4,2},{5,3},{6,4},{7,5},{10,8},{11,9},{12,10},{13,11},... | collective-permute-start | bytes 2654216 | tf_op jit(solution)/shard_map/ppermute | solution.py:63
  775.1 26.2 %collective-permute-start.60 = (bf16[192,2304]{1,0:T(8,128)(2,1)S(1)}, bf16[192,2304]{1,0:T(8,128)(2,1)S(1)}, u32[]{:S(2)}, u32[]{:S(2)}) collective-permute-start(bf16[192,2304]{1,0:T(8,128)(2,1)S(1)} %get-tuple-element.418), channel_id=1, source_target_pairs={{0,2},{1,3},{2,4},{3,5},{4,6},{5,7},{8,10},{9,11},{10,12},{11,13},... | collective-permute-start | bytes 2654216 | tf_op jit(solution)/shard_map/ppermute | solution.py:59
  825.4 24.4 %collective-permute-start.62 = (bf16[192,2304]{1,0:T(8,128)(2,1)}, bf16[192,2304]{1,0:T(8,128)(2,1)}, u32[]{:S(2)}, u32[]{:S(2)}) collective-permute-start(bf16[192,2304]{1,0:T(8,128)(2,1)} %get-tuple-element.424), channel_id=1, source_target_pairs={{0,2},{1,3},{2,4},{3,5},{4,6},{5,7},{8,10},{9,11},{10,12},{11,13},... | collective-permute-start | bytes 2654216 | tf_op jit(solution)/shard_map/ppermute | solution.py:59
  830.9 24.0 %collective-permute-start.63 = (bf16[192,2304]{1,0:T(8,128)(2,1)}, bf16[192,2304]{1,0:T(8,128)(2,1)}, u32[]{:S(2)}, u32[]{:S(2)}) collective-permute-start(bf16[192,2304]{1,0:T(8,128)(2,1)} %get-tuple-element.425), channel_id=1, source_target_pairs={{2,0},{3,1},{4,2},{5,3},{6,4},{7,5},{10,8},{11,9},{12,10},{13,11},... | collective-permute-start | bytes 2654216 | tf_op jit(solution)/shard_map/ppermute | solution.py:63
  865.4 23.0 %collective-permute-start.66 = (bf16[192,2304]{1,0:T(8,128)(2,1)}, bf16[192,2304]{1,0:T(8,128)(2,1)}, u32[]{:S(2)}, u32[]{:S(2)}) collective-permute-start(bf16[192,2304]{1,0:T(8,128)(2,1)} %multiply_convert_fusion.4), channel_id=1, source_target_pairs={{2,0},{3,1},{4,2},{5,3},{6,4},{7,5},{10,8},{11,9},{12,10},{13,11},... | collective-permute-start | bytes 2654216 | tf_op jit(solution)/shard_map/ppermute | solution.py:63
  914.8 25.5 %collective-permute-start.69 = (bf16[192,2304]{1,0:T(8,128)(2,1)}, bf16[192,2304]{1,0:T(8,128)(2,1)S(1)}, u32[]{:S(2)}, u32[]{:S(2)}) collective-permute-start(bf16[192,2304]{1,0:T(8,128)(2,1)} %get-tuple-element.453), channel_id=1, source_target_pairs={{0,2},{1,3},{2,4},{3,5},{4,6},{5,7},{8,10},{9,11},{10,12},{11,13},... | collective-permute-start | bytes 2654216 | tf_op jit(solution)/shard_map/ppermute | solution.py:59
  917.0 23.4 %collective-permute-start.70 = (bf16[192,2304]{1,0:T(8,128)(2,1)S(1)}, bf16[192,2304]{1,0:T(8,128)(2,1)S(1)}, u32[]{:S(2)}, u32[]{:S(2)}) collective-permute-start(bf16[192,2304]{1,0:T(8,128)(2,1)S(1)} %get-tuple-element.454), channel_id=1, source_target_pairs={{2,0},{3,1},{4,2},{5,3},{6,4},{7,5},{10,8},{11,9},{12,10},{13,11},... | collective-permute-start | bytes 2654216 | tf_op jit(solution)/shard_map/ppermute | solution.py:63
  928.1 40.8 %collective-permute-start.86 = (bf16[1152,2304]{1,0:T(8,128)(2,1)}, bf16[1152,2304]{1,0:T(8,128)(2,1)}, u32[]{:S(2)}, u32[]{:S(2)}) collective-permute-start(bf16[1152,2304]{1,0:T(8,128)(2,1)} %slice.441), channel_id=1, source_target_pairs={{0,1},{1,0},{2,3},{3,2},{4,5},{5,4},{6,7},{7,6},{8,9},{9,8},{10,11... | collective-permute-start | bytes 15925256 | tf_op jit(solution)/shard_map/ppermute | solution.py:66
  933.6 116.4 %collective-permute-start.84 = (bf16[1152,2304]{1,0:T(8,128)(2,1)}, bf16[1152,2304]{1,0:T(8,128)(2,1)}, u32[]{:S(2)}, u32[]{:S(2)}) collective-permute-start(bf16[1152,2304]{1,0:T(8,128)(2,1)} %slice.437), channel_id=1, source_target_pairs={{0,1},{1,0},{2,3},{3,2},{4,5},{5,4},{6,7},{7,6},{8,9},{9,8},{10,11... | collective-permute-start | bytes 15925256 | tf_op jit(solution)/shard_map/ppermute | solution.py:66
  936.7 121.1 %collective-permute-start.85 = (bf16[1152,2304]{1,0:T(8,128)(2,1)}, bf16[1152,2304]{1,0:T(8,128)(2,1)}, u32[]{:S(2)}, u32[]{:S(2)}) collective-permute-start(bf16[1152,2304]{1,0:T(8,128)(2,1)} %slice.439), channel_id=1, source_target_pairs={{0,1},{1,0},{2,3},{3,2},{4,5},{5,4},{6,7},{7,6},{8,9},{9,8},{10,11... | collective-permute-start | bytes 15925256 | tf_op jit(solution)/shard_map/ppermute | solution.py:66
  975.1 221.1 %all-reduce.12.cloned.1.call-start = ((), (), s32[]{:S(2)}) async-start(), calls=%async_computation.2 | async-start | bytes 7077888 | tf_op jit(solution)/shard_map/psum | solution.py:608
  975.2 24.8 %collective-permute-start.71 = (bf16[192,2304]{1,0:T(8,128)(2,1)}, bf16[192,2304]{1,0:T(8,128)(2,1)}, u32[]{:S(2)}, u32[]{:S(2)}) collective-permute-start(bf16[192,2304]{1,0:T(8,128)(2,1)} %get-tuple-element.457), channel_id=1, source_target_pairs={{0,2},{1,3},{2,4},{3,5},{4,6},{5,7},{8,10},{9,11},{10,12},{11,13},... | collective-permute-start | bytes 2654216 | tf_op jit(solution)/shard_map/ppermute | solution.py:59
  981.2 23.7 %collective-permute-start.72 = (bf16[192,2304]{1,0:T(8,128)(2,1)}, bf16[192,2304]{1,0:T(8,128)(2,1)}, u32[]{:S(2)}, u32[]{:S(2)}) collective-permute-start(bf16[192,2304]{1,0:T(8,128)(2,1)} %get-tuple-element.458), channel_id=1, source_target_pairs={{2,0},{3,1},{4,2},{5,3},{6,4},{7,5},{10,8},{11,9},{12,10},{13,11},... | collective-permute-start | bytes 2654216 | tf_op jit(solution)/shard_map/ppermute | solution.py:63
  1049.8 359.1 %all-reduce.10.cloned.1.call-start = ((), (), s32[]{:S(2)}) async-start(), calls=%async_computation.1 | async-start | bytes 21233664 | tf_op jit(solution)/shard_map/psum | solution.py:608
  1067.8 25.6 %collective-permute-start.76 = (bf16[208,2304]{1,0:T(8,128)(2,1)S(1)}, bf16[208,2304]{1,0:T(8,128)(2,1)S(1)}, u32[]{:S(2)}, u32[]{:S(2)}) collective-permute-start(bf16[208,2304]{1,0:T(8,128)(2,1)S(1)} %get-tuple-element.484), channel_id=1, source_target_pairs={{0,2},{1,3},{2,4},{3,5},{8,10},{9,11},{10,12},{11,13},{16,18},{17,... | collective-permute-start | bytes 2875400 | tf_op jit(solution)/shard_map/ppermute | solution.py:59
  1093.9 27.1 %collective-permute-start.78 = (bf16[208,2304]{1,0:T(8,128)(2,1)S(1)}, bf16[208,2304]{1,0:T(8,128)(2,1)S(1)}, u32[]{:S(2)}, u32[]{:S(2)}) collective-permute-start(bf16[208,2304]{1,0:T(8,128)(2,1)S(1)} %add_convert_fusion.8), channel_id=1, source_target_pairs={{0,2},{1,3},{2,4},{3,5},{4,6},{5,7},{8,10},{9,11},{10,12},{11,13},... | collective-permute-start | bytes 2875400 | tf_op jit(solution)/shard_map/ppermute | solution.py:59
  1100.9 24.2 %collective-permute-start.79 = (bf16[208,2304]{1,0:T(8,128)(2,1)S(1)}, bf16[208,2304]{1,0:T(8,128)(2,1)S(1)}, u32[]{:S(2)}, u32[]{:S(2)}) collective-permute-start(bf16[208,2304]{1,0:T(8,128)(2,1)S(1)} %add_convert_fusion.7), channel_id=1, source_target_pairs={{2,0},{3,1},{4,2},{5,3},{6,4},{7,5},{10,8},{11,9},{12,10},{13,11},... | collective-permute-start | bytes 2875400 | tf_op jit(solution)/shard_map/ppermute | solution.py:63
  (218 other events, 3900.6 us)
Sparse Core Ops, SparseCore 0:
  975.2 122.4 all-reduce.7
  1101.7 94.4 all-reduce.11
  1200.5 208.3 all-reduce.9

commit v3 on v2

--- a/solution.py
+++ b/solution.py
@@ -65,8 +65,17 @@
     def swap(self, block):
         return lax.ppermute(block, "ctx", self.core_pairs)
 
-    def shift(self, block, k):
-        return jnp.roll(block, k, axis=0)
+    def exchanged(self, items):
+        last = self.z == self.chips - 1
+        items = list(items)
+        first, final = items[1], items[-1]
+        items[1] = jnp.where(last, final, first)
+        items[-1] = jnp.where(last, first, final)
+        return items
+
+    def table(self):
+        order = self.exchanged([jnp.int32(k) for k in range(self.chips)])
+        return [lax.rem(self.z + k, self.chips) for k in order]
 
 
 def tied(*values):
@@ -81,7 +90,7 @@
         self.from_left, self.from_right = [own], [own]
         self.sum_left = self.sum_right = None
 
-    def step(self, work=None, inputs=()):
+    def step(self, work=None, inputs=(), held=()):
         line, n, z = self.line, self.line.chips, self.line.z
         gathers = self.own is not None
         self.s += 1
@@ -93,7 +102,9 @@
             low = s - 1
         j = s - 1 if gathers else s
         if self.sums and j >= 1:
-            sum_r, sum_l = self.parts[n - j], self.parts[j]
+            sum_r, sum_l = self.parts[n - j], self.parts[n - 1 if j == 1 else j]
+            if j == n - 1:
+                sum_l = jnp.where(z == n - 1, self.parts[1], self.parts[n - 1])
             if self.sum_left is not None:
                 sum_r = (sum_r.astype(f32) + self.sum_left.astype(f32)).astype(bf16)
                 sum_l = (sum_l.astype(f32) + self.sum_right.astype(f32)).astype(bf16)
@@ -103,7 +114,7 @@
                 to_right = jnp.where(z >= s - 1, to_right, sum_r)
                 to_left = jnp.where(n - 1 - z >= s - 1, to_left, sum_l)
                 low = 0
-        to_right, to_left, inputs = tied(to_right, to_left, inputs)
+        to_right, to_left, inputs, self.held = tied(to_right, to_left, inputs, held)
         got_left = line.right(to_right, low, high)
         got_right = line.left(to_left, low, high)
         outs = work(*inputs) if work is not None else ()
@@ -115,11 +126,18 @@
             self.sum_left, self.sum_right = got_left, got_right
         return outs
 
-    def blocks(self):
+    def near(self):
+        last = self.line.z == self.line.chips - 1
+        return [self.own, jnp.where(last, self.from_left[1], self.from_right[1])]
+
+    def far(self):
         n, z = self.line.chips, self.line.z
-        return [self.own] + [
-            jnp.where(z + k < n, self.from_right[k], self.from_left[n - k]) for k in range(1, n)
+        blocks = [
+            jnp.where(z + k < n, self.from_right[k], self.from_left[n - k])
+            for k in range(2, n - 1)
         ]
+        final = jnp.where(z == 0, self.from_right[n - 1], self.from_left[1])
+        return blocks + [jnp.where(z == n - 1, self.from_left[n - 1], final)]
 
     def terms(self):
         return (self.parts[0], self.sum_left, self.sum_right)
@@ -132,7 +150,7 @@
 def spans_of(place, info, spans, none):
     label = jnp.full(place.shape, none, jnp.int32)
     for s in range(spans):
-        start, stop = info[2 + s], info[2 + spans + s]
+        start, stop = info[1 + s], info[1 + spans + s]
         label = jnp.where((place >= start) & (place < stop), s, label)
     return label
 
@@ -140,13 +158,13 @@
 def seen_block(query_block, key_block, width, info, spans):
     seen = key_block <= query_block
     for s in range(spans):
-        start, stop = info[2 + s], info[2 + spans + s]
+        start, stop = info[1 + s], info[1 + spans + s]
         seen = seen | ((start < (query_block + 1) * width) & (stop > key_block * width))
     return seen
 
 
 def block_mask(query_block, key_block, rows, info, spans):
-    c = info[1]
+    c = info[0]
     width = 2 * rows
     query_place = (
         query_block * width + c * rows + lax.broadcasted_iota(jnp.int32, (rows, 1), 0)
@@ -161,11 +179,11 @@
 def forward_kernel(spans, heads, info, q_ref, k_ref, v_ref, o_ref, acc_ref, sum_ref):
     chips, width, _ = k_ref.shape
     rows = width // 2
-    query_block = lax.rem(info[0] + pl.program_id(0), chips)
+    query_block = info[1 + 2 * spans + pl.program_id(0)]
     acc_ref[...] = jnp.zeros_like(acc_ref)
     sum_ref[...] = jnp.zeros_like(sum_ref)
     for kk in range(chips):
-        key_block = lax.rem(info[0] + kk, chips)
+        key_block = info[1 + 2 * spans + kk]
 
         @pl.when(seen_block(query_block, key_block, width, info, spans))
         def _():
@@ -203,7 +221,7 @@
 ):
     chips, width, _ = k_ref.shape
     rows = width // 2
-    query_block = lax.rem(info[0] + pl.program_id(0), chips)
+    query_block = info[1 + 2 * spans + pl.program_id(0)]
 
     @pl.when(pl.program_id(0) == 0)
     def _():
@@ -214,7 +232,7 @@
     sum_ref[...] = jnp.zeros_like(sum_ref)
     inner_ref[...] = jnp.zeros_like(inner_ref)
     for kk in range(chips):
-        key_block = lax.rem(info[0] + kk, chips)
+        key_block = info[1 + 2 * spans + kk]
 
         @pl.when(seen_block(query_block, key_block, width, info, spans))
         def _():
@@ -232,7 +250,7 @@
                 t_ref[kk, h] = 1.0 - squashed * squashed
 
     for kk in range(chips):
-        key_block = lax.rem(info[0] + kk, chips)
+        key_block = info[1 + 2 * spans + kk]
 
         @pl.when(seen_block(query_block, key_block, width, info, spans))
         def _():
@@ -359,6 +377,37 @@
     )(hidden, gate_w, up_w)
 
 
+def feed_back_kernel(low_ref, down_ref, gelu_ref, slope_ref, gate_back_ref, up_back_ref):
+    grad = nt(low_ref[...], down_ref[...])
+    gate_back_ref[...] = (grad * slope_ref[...].astype(f32)).astype(bf16)
+    up_back_ref[...] = (grad * gelu_ref[...].astype(f32)).astype(bf16)
+
+
+def feed_back(low, down_w, gelu, slope):
+    m, width = low.shape
+    n = down_w.shape[0]
+    tile = next(t for t in (768, 384, 256, 128) if n % t == 0)
+    spec = pl.BlockSpec((m, tile), lambda i: (0, i))
+    return pl.pallas_call(
+        feed_back_kernel,
+        out_shape=(jax.ShapeDtypeStruct((m, n), bf16),) * 2,
+        grid=(n // tile,),
+        in_specs=[
+            pl.BlockSpec((m, width), lambda i: (0, 0)),
+            pl.BlockSpec((tile, width), lambda i: (i, 0)),
+            spec,
+            spec,
+        ],
+        out_specs=(spec,) * 2,
+        compiler_params=pltpu.CompilerParams(vmem_limit_bytes=56 * 1024 * 1024),
+        cost_estimate=pl.CostEstimate(
+            flops=2 * m * n * width,
+            bytes_accessed=2 * n * width + 2 * m * width + 8 * m * n,
+            transcendentals=0,
+        ),
+    )(low, down_w, gelu, slope)
+
+
 def rotate(vectors, cosine, sine):
     first, second = vectors[..., :HALF], vectors[..., HALF:]
     return jnp.concatenate(
@@ -439,29 +488,17 @@
     def both_rows(block):
         return jnp.concatenate([block, line.swap(block)])
 
-    qkv_weight = jnp.concatenate(
-        [pair_rows(query_weight), group_rows(key_weight), group_rows(value_weight)]
-    )
-    out_weight = pair_rows(output_weight)
-    gate_rows, up_rows, down_rows = map(both_rows, (gate_weight, up_weight, down_weight))
-
     count = inbound_gain.shape[0]
     pad = 16
-    gains_own = jnp.stack([inbound_gain, attended_gain, prefeed_gain, postfeed_gain])
-    gains_other = line.swap(gains_own)
-    gains_row = jnp.where(
-        c == 0,
-        jnp.concatenate([gains_own, gains_other]),
-        jnp.concatenate([gains_other, gains_own]),
-    ).reshape(1, 8 * count)
-    gains_rows = jnp.pad(gains_row, ((0, pad - 1), (0, width - 8 * count)))
-
-    query_width = out_weight.shape[0]
+    gains_own = jnp.concatenate([inbound_gain, attended_gain, prefeed_gain, postfeed_gain])
+    gains_rows = jnp.pad(gains_own[None, :], ((0, pad - 1), (0, width - 4 * count)))
+
+    query_width = 2 * output_weight.shape[0]
     heads = query_width // HEAD_DIM
 
-    block_of = lax.rem(z + jnp.arange(chips, dtype=jnp.int32), chips)
+    table = jnp.stack(line.table()).astype(jnp.int32)
     places = (
-        block_of[:, None] * (2 * rows) + c * rows + jnp.arange(rows, dtype=jnp.int32)[None, :]
+        table[:, None] * (2 * rows) + c * rows + jnp.arange(rows, dtype=jnp.int32)[None, :]
     ).reshape(every)
     inverse = rope_base ** (-(jnp.arange(HALF, dtype=f32) * 2.0 / HEAD_DIM))
     angles = places.astype(f32)[:, None] * inverse[None, :]
@@ -469,14 +506,16 @@
     query_scale = HEAD_DIM ** (-0.5)
 
     def split(block_rows):
-        return [block_rows[k * rows : (k + 1) * rows] for k in range(chips)]
+        return [
+            block_rows[k * rows : (k + 1) * rows] for k in range(block_rows.shape[0] // rows)
+        ]
 
     def join(blocks):
         return jnp.concatenate(blocks)
 
     infos = [
         jnp.concatenate(
-            [jnp.stack([z, c]), span_start[s], span_start[s] + span_len[s]]
+            [c[None], span_start[s], span_start[s] + span_len[s], table]
         ).astype(jnp.int32)
         for s in range(seq_count)
     ]
@@ -486,20 +525,22 @@
             self.s = s
             self.own = tokens[s]
 
-        def project(self, *blocks):
+        def project(self, places, *blocks):
+            count = len(blocks)
             merged = join(blocks)
+            cos, sin = (t[places.start * rows : places.stop * rows] for t in (cosine, sine))
             values = merged.astype(f32)
             root_in = inverse_root(values)
             hidden = (values * root_in * gain[0]).astype(bf16)
             raw = nt(hidden, qkv_weight)
-            queries = raw[:, :query_width].reshape(every, heads, HEAD_DIM)
-            queries = (rotate(queries, cosine, sine) * query_scale).astype(bf16)
-            keys = raw[:, query_width : query_width + HEAD_DIM].reshape(every, 1, HEAD_DIM)
-            keys = rotate(keys, cosine, sine).astype(bf16).reshape(every, HEAD_DIM)
+            queries = raw[:, :query_width].reshape(count * rows, heads, HEAD_DIM)
+            queries = (rotate(queries, cos, sin) * query_scale).astype(bf16)
+            keys = raw[:, query_width : query_width + HEAD_DIM].reshape(count * rows, 1, HEAD_DIM)
+            keys = rotate(keys, cos, sin).astype(bf16).reshape(count * rows, HEAD_DIM)
             values = raw[:, query_width + HEAD_DIM :].astype(bf16)
-            mine = jnp.concatenate([keys, values], axis=1).reshape(chips, rows, 2 * HEAD_DIM)
+            mine = jnp.concatenate([keys, values], axis=1).reshape(count, rows, 2 * HEAD_DIM)
             both = jnp.concatenate([mine, line.swap(mine)], axis=1)
-            queries = queries.reshape(chips, rows, query_width)
+            queries = queries.reshape(count, rows, query_width)
             return merged, root_in, hidden, queries, both[:, :, :HEAD_DIM], both[:, :, HEAD_DIM:]
 
         def attend(self, queries, keys, values):
@@ -520,7 +561,7 @@
             return (hidden_ff,) + tuple(gate_up(hidden_ff, gate_rows, up_rows))
 
         def feed_down(self, product):
-            return nn(product, down_rows).astype(bf16)
+            return (nn(product, down_rows).astype(bf16),)
 
         def after_feed(self, terms):
             feed = total(terms)
@@ -531,12 +572,12 @@
             self.postfeed_term = jnp.sum(self.upstream * normed, axis=0)
             return norm_backward(normed, root, gain[3], self.upstream).astype(bf16)
 
-        def feed_back(self, feed_low, gelu, slope):
-            grad = nt(feed_low, down_rows)
-            return (grad * slope.astype(f32)).astype(bf16), (grad * gelu.astype(f32)).astype(bf16)
+        def feed_back(self, gelu, slope, *blocks):
+            feed_low = join(blocks)
+            return (feed_low,) + tuple(feed_back(feed_low, down_rows, gelu, slope))
 
         def feed_in(self, gate_back, up_back):
-            return (nn(gate_back, gate_rows) + nn(up_back, up_rows)).astype(bf16)
+            return ((nn(gate_back, gate_rows) + nn(up_back, up_rows)).astype(bf16),)
 
         def after_feed_back(self, terms):
             grad = total(terms)
@@ -552,7 +593,7 @@
 
         def attend_back(self, branch_low, queries, keys, values):
             mixed = nt(branch_low, out_weight).astype(bf16)
-            query_rot, key_rot, value_sum = attend_backward(
+            return attend_backward(
                 infos[self.s],
                 queries,
                 keys,
@@ -560,6 +601,8 @@
                 mixed.reshape(chips, rows, query_width),
                 spans,
             )
+
+        def turn_back(self, query_rot, key_rot, value_sum):
             sums = jnp.concatenate([key_rot, value_sum], axis=2)
             sums = sums[:, :rows] + line.swap(sums[:, rows:].astype(bf16)).astype(f32)
             sums = sums.reshape(every, 2 * HEAD_DIM)
@@ -575,10 +618,12 @@
                 axis=1,
             )
 
-        def project_back(self, back, merged, root_in):
+        def project_back(self, near_tokens, far_tokens, near_root, far_root, *sums):
+            back = self.turn_back(*sums)
             grad = nn(back, qkv_weight)
-            inbound_term = jnp.sum(grad * (merged.astype(f32) * root_in), axis=0)
-            return grad.astype(bf16), inbound_term
+            normed = join([near_tokens, far_tokens]).astype(f32) * join([near_root, far_root])
+            inbound_term = jnp.sum(grad * normed, axis=0)
+            return grad.astype(bf16), inbound_term, back
 
         def after_project_back(self, terms):
             grad = total(terms)
@@ -588,18 +633,8 @@
                 bf16
             )
 
-    def weight_grad(left_a, left_b, right_a, right_b):
-        return tn(join([left_a, left_b]), join([right_a, right_b])).astype(bf16)
-
-    def group_of(own, first, first_inputs, middle, last):
-        ex = Exchange(line, own)
-        firsts = ex.step(first, first_inputs)
-        ex.parts = split(firsts[0])
-        middles = []
-        for i in range(chips - 2):
-            middles.append(ex.step(*(middle[i] if i < len(middle) else ())))
-        lasts = ex.step(*last(ex.blocks()))
-        return firsts, middles, lasts, ex.terms()
+    def weight_grad(left_count, *pieces):
+        return (tn(join(pieces[:left_count]), join(pieces[left_count:])).astype(bf16),)
 
     data = lax.axis_size("dp")
 
@@ -611,122 +646,164 @@
         count = grad.shape[0] // 2
         return (grad[:count].astype(f32) + line.swap(grad[count:]).astype(f32)).astype(bf16)
 
+    near, far = slice(0, 2), slice(2, chips)
+
+    def parts_of(*halves):
+        return [block for half in halves for block in split(half)]
+
     a, b = (Sequence(s) for s in range(seq_count))
 
     ex = Exchange(line, jnp.concatenate([a.own, gains_rows]), sums=False)
-    for _ in range(chips - 1):
+    def attention_weights(query_w, key_w, value_w, out_w):
+        merged = jnp.concatenate([pair_rows(query_w), group_rows(key_w), group_rows(value_w)])
+        return merged, pair_rows(out_w)
+
+    ex.step()
+    qkv_weight, out_weight = ex.step(
+        attention_weights, (query_weight, key_weight, value_weight, output_weight)
+    )
+    gate_rows = ex.step(both_rows, (gate_weight,))
+    for _ in range(chips - 4):
         ex.step()
-    blocks = ex.blocks()
-    gain = jnp.stack([block[rows, : 8 * count] for block in blocks])
-    gain = line.shift(gain, z).reshape(chips, 2, 4, count)
+    blocks = ex.near() + ex.far()
+    gain = jnp.stack([block[rows, : 4 * count] for block in blocks])
+    gain_other = line.swap(gain)
+    gain = jnp.stack(
+        [jnp.where(c == 0, gain, gain_other), jnp.where(c == 0, gain_other, gain)], axis=1
+    ).reshape(chips, 8 * count)
+    gain = line.exchanged([gain[k] for k in range(chips)])
+    gain = jnp.roll(jnp.stack(gain), z, axis=0).reshape(chips, 2, 4, count)
     gain = gain.transpose(2, 0, 1, 3).reshape(4, 1, width).astype(f32)
 
     def a_attention(*blocks):
-        projected = a.project(*blocks)
-        attended, out = a.attend(*projected[3:])
-        return (out, attended) + projected
-
-    firsts, _, lasts, terms = group_of(
-        b.own,
-        a_attention,
-        [block[:rows] for block in blocks],
-        [],
-        lambda blocks: (b.project, blocks),
+        halves = [a.project(near, *blocks[near]), a.project(far, *blocks[far])]
+        queries, keys, values = (join([half[i] for half in halves]) for i in range(3, 6))
+        attended, out = a.attend(queries, keys, values)
+        stored = [[half[i] for half in halves] for i in range(3)]
+        return out, (attended, queries, keys, values), stored
+
+    ex = Exchange(line, b.own)
+    out, a_kept, (a.tokens, a.root_in, a.hidden) = ex.step(
+        a_attention, [block[:rows] for block in blocks]
     )
-    _, a.attended, a.tokens, a.root_in, a.hidden, a.queries, a.keys, a.values = firsts
-    b.tokens, b.root_in, b.hidden, b.queries, b.keys, b.values = lasts
-    hidden_a = a.after_branch(terms)
-
-    def b_attention(*projected):
-        attended, out = b.attend(*projected)
-        return out, attended
-
-    firsts, _, lasts, terms = group_of(
-        hidden_a,
-        b_attention,
-        (b.queries, b.keys, b.values),
-        [],
-        lambda blocks: (a.feed, blocks),
-    )
-    b.attended = firsts[1]
-    a.hidden_ff, a.product, a.gelu, a.slope = lasts
-    hidden_b = b.after_branch(terms)
-
-    firsts, _, lasts, terms = group_of(
-        hidden_b,
-        lambda product: (a.feed_down(product),),
-        (a.product,),
-        [],
-        lambda blocks: (b.feed, blocks),
-    )
-    b.hidden_ff, b.product, b.gelu, b.slope = lasts
-    low_a = a.after_feed(terms)
-
-    def a_feed_back(*blocks):
-        feed_low = join(blocks)
-        return (feed_low,) + a.feed_back(feed_low, a.gelu, a.slope)
-
-    firsts, _, lasts, terms = group_of(
-        low_a,
-        lambda product: (b.feed_down(product),),
-        (b.product,),
-        [],
-        lambda blocks: (a_feed_back, blocks),
-    )
-    a.feed_low, a.gate_back, a.up_back = lasts
-    low_b = b.after_feed(terms)
-
-    def b_feed_back(*blocks):
-        feed_low = join(blocks)
-        down_grad = weight_grad(a.product, b.product, a.feed_low, feed_low)
-        return (feed_low, down_grad) + b.feed_back(feed_low, b.gelu, b.slope)
-
-    firsts, _, lasts, terms = group_of(
-        low_b,
-        lambda gate_back, up_back: (a.feed_in(gate_back, up_back),),
-        (a.gate_back, a.up_back),
-        [],
-        lambda blocks: (b_feed_back, blocks),
-    )
-    b.feed_low, down_grad, b.gate_back, b.up_back = lasts
-    down_sum = data_sum(core_sum(down_grad), 0)
-    branch_a = a.after_feed_back(terms)
+    a.attended, a.queries, a.keys, a.values = a_kept
+    ex.parts = split(out)
+
+    def b_project_near(up_w, *blocks):
+        return b.project(near, *blocks), both_rows(up_w)
+
+    b_near, up_rows = ex.step(b_project_near, [up_weight] + ex.near())
+    down_rows = ex.step(both_rows, (down_weight,))
+    for _ in range(chips - 4):
+        ex.step()
+    b_far = ex.step(functools.partial(b.project, far), ex.far())
+    b.tokens, b.root_in, b.hidden = ([b_near[i], b_far[i]] for i in range(3))
+    hidden_a = a.after_branch(ex.terms())
+
+    def b_attention(*halves):
+        queries, keys, values = (join(halves[i::3]) for i in range(3))
+        attended, out = b.attend(queries, keys, values)
+        return out, attended, queries, keys, values
+
+    def feed_phase(x, own, first, inputs):
+        ex = Exchange(line, own)
+        firsts = ex.step(first, inputs)
+        yield firsts, ex
+        hidden, product, gelu, slope = ex.step(x.feed, ex.near())
+        (out,) = ex.step(x.feed_down, (product,))
+        for _ in range(chips - 4):
+            ex.step()
+        x.out_near = out
+        lasts = ex.step(x.feed, ex.far())
+        x.hidden_ff, x.product, x.gelu, x.slope = (
+            [u, v] for u, v in zip((hidden, product, gelu, slope), lasts)
+        )
+        yield lasts, ex
+
+    steps = feed_phase(a, hidden_a, b_attention, b_near[3:] + b_far[3:])
+    (out, b.attended, b.queries, b.keys, b.values), ex = next(steps)
+    ex.parts = split(out)
+    next(steps)
+    hidden_b = b.after_branch(ex.terms())
+
+    steps = feed_phase(b, hidden_b, a.feed_down, (a.product[1],))
+    (out,), ex = next(steps)
+    ex.parts = parts_of(a.out_near, out)
+    next(steps)
+    low_a = a.after_feed(ex.terms())
+
+    def back_phase(x, own, first, inputs, also):
+        ex = Exchange(line, own)
+        firsts = ex.step(first, inputs)
+        yield firsts, ex
+        low, gate_back, up_back = ex.step(
+            functools.partial(x.feed_back, x.gelu[0], x.slope[0]), ex.near()
+        )
+        (x.out_near,) = ex.step(x.feed_in, (gate_back, up_back))
+        for _ in range(chips - 4):
+            ex.step()
+
+        def last(*blocks):
+            outs = x.feed_back(x.gelu[1], x.slope[1], *blocks)
+            return outs, also(low, outs[0])
+
+        lasts, more = ex.step(last, ex.far())
+        x.feed_low, x.gate_back, x.up_back = (
+            [u, v] for u, v in zip((low, gate_back, up_back), lasts)
+        )
+        yield more, ex
+
+    steps = back_phase(a, low_a, b.feed_down, (b.product[1],), lambda low, high: ())
+    (out,), ex = next(steps)
+    ex.parts = parts_of(b.out_near, out)
+    next(steps)
+    low_b = b.after_feed(ex.terms())
+
+    def down_work(low, high):
+        return weight_grad(4, *a.product, *b.product, *a.feed_low, low, high)
+
+    steps = back_phase(b, low_b, a.feed_in, (a.gate_back[1], a.up_back[1]), down_work)
+    (out,), ex = next(steps)
+    ex.parts = parts_of(a.out_near, out)
+    (down_grad,), _ = next(steps)
+    branch_a = a.after_feed_back(ex.terms())
+
+    def b_feed_in(gate_back, up_back, down_grad):
+        return b.feed_in(gate_back, up_back) + (core_sum(down_grad),)
 
     def a_attention_back(*blocks):
         branch_low = join(blocks)
-        return branch_low, a.attend_back(branch_low, a.queries, a.keys, a.values)
-
-    def left_grad(left_a, left_b):
-        return (weight_grad(left_a, left_b, a.hidden_ff, b.hidden_ff),)
-
-    firsts, middles, lasts, terms = group_of(
-        branch_a,
-        lambda gate_back, up_back: (b.feed_in(gate_back, up_back),),
-        (b.gate_back, b.up_back),
-        [(left_grad, (a.gate_back, b.gate_back)), (left_grad, (a.up_back, b.up_back))],
-        lambda blocks: (a_attention_back, blocks),
-    )
-    gate_grad, up_grad = middles[0][0], middles[1][0]
-    gate_sum, up_sum = data_sum((core_sum(gate_grad), core_sum(up_grad)), 1)
-    a.branch_low, a.back = lasts
-    branch_b = b.after_feed_back(terms)
+        return (branch_low,) + tuple(a.attend_back(branch_low, a.queries, a.keys, a.values))
+
+    ex = Exchange(line, branch_a)
+    out, down_grad = ex.step(b_feed_in, (b.gate_back[1], b.up_back[1], down_grad))
+    ex.parts = parts_of(b.out_near, out)
+    left_grad = functools.partial(weight_grad, 4)
+    hidden_ff = a.hidden_ff + b.hidden_ff
+    (gate_grad,) = ex.step(left_grad, a.gate_back + b.gate_back + hidden_ff)
+    gate_grad = ex.step(core_sum, (gate_grad,))
+    early_sums = data_sum((down_grad, gate_grad), 0)
+    for _ in range(chips - 4):
+        ex.step()
+    a.branch_low, *a_sums = ex.step(a_attention_back, ex.near() + ex.far())
+    branch_b = b.after_feed_back(ex.terms())
 
     def b_attention_back(*blocks):
         branch_low = join(blocks)
-        return branch_low, b.attend_back(branch_low, b.queries, b.keys, b.values)
-
-    firsts, _, lasts, terms = group_of(
-        branch_b,
-        a.project_back,
-        (a.back, a.tokens, a.root_in),
-        [],
-        lambda blocks: (b_attention_back, blocks),
-    )
-    a.inbound_term = firsts[1]
-    b.branch_low, b.back = lasts
-    tokens_grad_a = a.after_project_back(terms)
-
-    grad, b.inbound_term = b.project_back(b.back, b.tokens, b.root_in)
+        return (branch_low,) + tuple(b.attend_back(branch_low, b.queries, b.keys, b.values))
+
+    ex = Exchange(line, branch_b)
+    out, a.inbound_term, a.back = ex.step(a.project_back, a.tokens + a.root_in + a_sums)
+    ex.parts = split(out)
+    (up_grad,) = ex.step(left_grad, a.up_back + b.up_back + hidden_ff)
+    up_grad = ex.step(core_sum, (up_grad,))
+    up_sum = data_sum(up_grad, 1)
+    for _ in range(chips - 4):
+        ex.step()
+    b.branch_low, *b_sums = ex.step(b_attention_back, ex.near() + ex.far())
+    tokens_grad_a = a.after_project_back(ex.terms())
+
+    grad, b.inbound_term, b.back = b.project_back(*b.tokens, *b.root_in, *b_sums)
     gain_terms = jnp.stack(
         [
             a.inbound_term + b.inbound_term,
@@ -736,24 +813,19 @@
         ]
     ).astype(bf16)
     gain_terms = gain_terms.reshape(4, chips, 2, count).transpose(1, 2, 0, 3)
-    gain_terms = line.shift(gain_terms.reshape(chips, 1, 8 * count), -z)
+    gain_terms = jnp.roll(gain_terms.reshape(chips, 1, 8 * count), -z, axis=0)
+    gain_terms = jnp.stack(line.exchanged([gain_terms[k] for k in range(chips)]))
     gain_terms = jnp.pad(gain_terms, ((0, 0), (0, pad - 1), (0, width - 8 * count)))
     ex = Exchange(line)
     ex.parts = [jnp.concatenate([part, gain_terms[k]]) for k, part in enumerate(split(grad))]
 
     def attention_grads(back_a, back_b):
-        qkv_grad = weight_grad(back_a, back_b, a.hidden, b.hidden)
-        output_grad = weight_grad(a.attended, b.attended, a.branch_low, b.branch_low)
-        return qkv_grad, output_grad
-
-    qkv_grad, output_grad = ex.step(attention_grads, (a.back, b.back))
-    for _ in range(chips - 2):
-        ex.step()
-    grad = total(ex.terms())
-    tokens_grad_b = b.after_project_back([grad[:rows]])
-
-    late_sums = data_sum(
-        tuple(
+        return weight_grad(2, back_a, back_b, *a.hidden, *b.hidden) + weight_grad(
+            2, a.attended, b.attended, a.branch_low, b.branch_low
+        )
+
+    def attention_sums(qkv_grad, output_grad):
+        return tuple(
             value.astype(bf16)
             for value in (
                 pair_sum(qkv_grad[:query_width]),
@@ -761,9 +833,19 @@
                 group_sum(qkv_grad[query_width + HEAD_DIM :]),
                 pair_sum(output_grad),
             )
-        ),
-        2,
-    )
+        )
+
+    late = ex.step(attention_grads, (a.back, b.back), held=early_sums)
+    down_sum, gate_sum = ex.held
+    late = ex.step(attention_sums, late)
+    ex.step(held=(up_sum,))
+    (up_sum,) = ex.held
+    for _ in range(chips - 4):
+        ex.step()
+    late_sums = data_sum(late, 2)
+    grad = total(ex.terms())
+    tokens_grad_b = b.after_project_back([grad[:rows]])
+
     row = grad[rows, : 8 * count].reshape(2, 4, count)
     mine = jnp.where(c == 0, row[0], row[1])
     other = jnp.where(c == 0, row[1], row[0])

time: 1440 us -> 1280 us (0.89)
  waiting for transfers between devices: 613 us -> 358 us
  other arithmetic: 186 us -> 241 us
  Pallas kernels: 90.9 us -> 144 us
    ppermute x34, waiting for transfers between devices: 220 us -> 85.2 us  [right(): return lax.ppermute(block, 'ctx', self.pairs(1, low, high))]
    psum x3, waiting for transfers between devices: 250 us -> 165 us  [data_sum(): return lax.psum(values, 'dp', axis_index_groups=groups)]
    ppermute x34, waiting for transfers between devices: 140 us -> 97.3 us  [left(): return lax.ppermute(block, 'ctx', self.pairs(-1, n - high, n - low))]
    pallas_call x0 -> x4, Pallas kernels: none -> 42.4 us  [feed_back(): pl.pallas_call(feed_back_kernel, out_shape=(jax.ShapeDtypeStruct((m, n),...]
    concatenate x7 -> x16, other arithmetic: 5.84 us -> 39.9 us  [the longest x3 31.5 us: both_rows(): return jnp.concatenate([block, line.swap(block)])]
    dot_general x6, matrix products: 46 us -> 18 us  [nt(): lax.dot_general(left_side, right_side, (((1,), (1,)), ((), ())), preferre...]
    select_n x14, other arithmetic: 10.2 us -> 36.6 us  [step(): to_left = jnp.where(n - 1 - z >= s - 1, to_left, sum_l)]
    dot_general x10 -> x16, matrix products: 93.7 us -> 114 us  [nn(): lax.dot_general(left_side, right_side, (((1,), (0,)), ((), ())), preferre...]
  transfers between devices with their start and end apart: 91 -> 93, of which waited for: 49 -> 41; matrix products, arithmetic and copies ran while one was open for 29% -> 34% of each run, Pallas kernels for 5% -> 11%
where the time goes in v3:
time: 1280 us; the launch traced here: 1270 us
  waiting for transfers between devices  358 us (28%)
  other arithmetic  241 us (19%)
  matrix products  216 us (17%)
  starting transfers between devices  170 us (13%)
  Pallas kernels  144 us (11%)
  local copies, waits for them, and re-layouts  113 us (9%)
  between operations  17.6 us (1%)
    psum x3, waiting for transfers between devices, data_sum(): return lax.psum(values, 'dp', axis_index_groups=groups)  165 us
    ppermute x34, starting transfers between devices, right(): return lax.ppermute(block, 'ctx', self.pairs(1, low, high))  122 us
    dot_general x16, matrix products, nn(): lax.dot_general(left_side, right_side, (((1,), (0,)), ((), ())), preferre...  114 us
    ppermute x34, waiting for transfers between devices, left(): return lax.ppermute(block, 'ctx', self.pairs(-1, n - high, n - low))  97.3 us
    ppermute x34, waiting for transfers between devices, right(): return lax.ppermute(block, 'ctx', self.pairs(1, low, high))  85.2 us
    dot_general x5, matrix products, tn(): lax.dot_general(left_side, right_side, (((0,), (0,)), ((), ())), preferre...  84.8 us
    pallas_call x4, Pallas kernels, gate_up(): pl.pallas_call(gate_up_kernel, out_shape=(jax.ShapeDtypeStruct((m, n), bf...  57.7 us
    unnamed x457, local copies, waits for them, and re-layouts  52.6 us
  transfers between devices with their start and end apart: 93, of which 41 were waited for; matrix products, arithmetic and copies ran while one was open for 34% of the time, Pallas kernels for 11%

profile of v3, /device:TPU:0, one launch (start us, length us, event | category | flops | bytes accessed | tf_op | source)
XLA Modules:
  0.0 1270.2 jit_solution(17566625740561497473)
XLA Ops:
  19.0 19.1 %collective-permute-done = bf16[208,2304]{1,0:T(8,128)(2,1)S(1)} collective-permute-done((bf16[208,2304]{1,0:T(8,128)(2,1)S(1)}, bf16[208,2304]{1,0:T(8,128)(2,1)S(1)}, u32[]{:S(2)}, u32[]{:S(2)}) %collective-permute-start) | collective-permute-done | bytes 958496 | tf_op jit(solution)/shard_map/ppermute | solution.py:59
  55.7 17.9 %collective-permute-done.3 = bf16[208,2304]{1,0:T(8,128)(2,1)} collective-permute-done((bf16[208,2304]{1,0:T(8,128)(2,1)}, bf16[208,2304]{1,0:T(8,128)(2,1)}, u32[]{:S(2)}, u32[]{:S(2)}) %collective-permute-start.3) | collective-permute-done | bytes 958496 | tf_op jit(solution)/shard_map/ppermute | solution.py:63
  82.7 9.4 pad_maximum_fusion.gate_ref
  92.1 14.4 %collective-permute-done.9 = bf16[208,2304]{1,0:T(8,128)(2,1)S(1)} collective-permute-done((bf16[208,2304]{1,0:T(8,128)(2,1)}, bf16[208,2304]{1,0:T(8,128)(2,1)S(1)}, u32[]{:S(2)}, u32[]{:S(2)}) %collective-permute-start.9) | collective-permute-done | bytes 958496 | tf_op jit(solution)/shard_map/ppermute | solution.py:63
  137.4 7.5 shard_map.246
  177.9 9.5 pad_maximum_fusion.1.up_ref
  202.2 12.6 pad_maximum_fusion.2.down_ref
  237.3 10.5 collective-permute-done.23
  260.9 7.5 shard_map.247
  270.5 6.5 collective-permute-done.26
  287.7 14.4 %shard_map.248 = (bf16[384,2304]{1,0:T(8,128)(2,1)}, bf16[384,2304]{1,0:T(8,128)(2,1)}, bf16[384,2304]{1,0:T(8,128)(2,1)}) custom-call(bf16[384,2304]{1,0:T(8,128)(2,1)} %constant_dynamic-update-slice_fusion.16.h_ref, bf16[2304,2304]{1,0:T(8,128)(2,1)} %pad_maximum_fusion.gate_ref, bf16[2304,2304]{1,0:T(8,128)(2,1)} %pad_maximum_fusion.1.up_ref), custom_call_target="tpu_custom_call" | custom-call | flops 8153726976 | bytes 28311552 | tf_op jit(solution)/shard_map/pallas_call | solution.py:365
  310.6 9.5 convolution_convert_fusion.8
  336.2 14.5 %shard_map.249 = (bf16[384,2304]{1,0:T(8,128)(2,1)}, bf16[384,2304]{1,0:T(8,128)(2,1)}, bf16[384,2304]{1,0:T(8,128)(2,1)}) custom-call(bf16[384,2304]{1,0:T(8,128)(2,1)} %constant_dynamic-update-slice_fusion.18.h_ref, bf16[2304,2304]{1,0:T(8,128)(2,1)} %pad_maximum_fusion.gate_ref, bf16[2304,2304]{1,0:T(8,128)(2,1)} %pad_maximum_fusion.1.up_ref), custom_call_target="tpu_custom_call" | custom-call | flops 8153726976 | bytes 28311552 | tf_op jit(solution)/shard_map/pallas_call | solution.py:365
  362.2 8.3 convolution_convert_fusion.7
  385.9 14.4 %shard_map.250 = (bf16[384,2304]{1,0:T(8,128)(2,1)}, bf16[384,2304]{1,0:T(8,128)(2,1)}, bf16[384,2304]{1,0:T(8,128)(2,1)}) custom-call(bf16[384,2304]{1,0:T(8,128)(2,1)} %constant_dynamic-update-slice_fusion.20.h_ref, bf16[2304,2304]{1,0:T(8,128)(2,1)} %pad_maximum_fusion.gate_ref, bf16[2304,2304]{1,0:T(8,128)(2,1)} %pad_maximum_fusion.1.up_ref), custom_call_target="tpu_custom_call" | custom-call | flops 8153726976 | bytes 28311552 | tf_op jit(solution)/shard_map/pallas_call | solution.py:365
  408.4 9.9 convolution_convert_fusion.6
  431.3 14.4 %shard_map.251 = (bf16[384,2304]{1,0:T(8,128)(2,1)}, bf16[384,2304]{1,0:T(8,128)(2,1)}, bf16[384,2304]{1,0:T(8,128)(2,1)}) custom-call(bf16[384,2304]{1,0:T(8,128)(2,1)} %constant_dynamic-update-slice_fusion.22.h_ref, bf16[2304,2304]{1,0:T(8,128)(2,1)} %pad_maximum_fusion.gate_ref, bf16[2304,2304]{1,0:T(8,128)(2,1)} %pad_maximum_fusion.1.up_ref), custom_call_target="tpu_custom_call" | custom-call | flops 8153726976 | bytes 28311552 | tf_op jit(solution)/shard_map/pallas_call | solution.py:365
  457.9 8.3 convolution_convert_fusion.5
  480.5 10.7 shard_map.252
  500.3 7.4 fusion.217
  509.9 9.7 fusion.53
  530.5 10.6 shard_map.253
  555.2 7.7 fusion.218
  578.9 10.5 shard_map.254
  599.5 7.5 fusion.219
  608.5 9.7 fusion.55
  630.5 21.2 %convolution_convert_fusion.2 = bf16[2304,2304]{1,0:T(8,128)(2,1)} fusion(bf16[1536,2304]{1,0:T(8,128)(2,1)S(1)} %get-tuple-element.841, bf16[384,2304]{1,0:T(8,128)(2,1)} %get-tuple-element.482, bf16[384,2304]{1,0:T(8,128)(2,1)} %get-tuple-element.466, bf16[384,2304]{1,0:T(8,128)(2,1)S(1)} %copy-done.185, bf16[384,2304]{1,0:T(8,128)(2,1)S(1)} %copy-done.183), kind=kOutput, calls=%fused_computation.2 | convolution fusion | flops 16341073920 | bytes 24772608 | tf_op jit(solution)/shard_map/dot_general | solution.py:38
  651.7 10.7 shard_map.255
  689.2 6.7 fusion.56
  695.9 6.2 add_convert_fusion.2
  712.0 23.0 %convolution_convert_fusion.1 = bf16[2304,2304]{1,0:T(8,128)(2,1)} fusion(bf16[384,2304]{1,0:T(8,128)(2,1)} %get-tuple-element.576, bf16[384,2304]{1,0:T(8,128)(2,1)} %get-tuple-element.575, bf16[384,2304]{1,0:T(8,128)(2,1)} %get-tuple-element.574, bf16[384,2304]{1,0:T(8,128)(2,1)} %get-tuple-element.573, ...), kind=kOutput, calls=%fused_computation.1 | convolution fusion | flops 16369385472 | bytes 24772608 | tf_op jit(solution)/shard_map/dot_general | solution.py:38
  757.5 9.5 collective-permute-done.63
  784.3 14.2 %shard_map.256 = (f32[4,192,512]{2,1,0:T(8,128)S(1)}, f32[4,384,256]{2,1,0:T(8,128)S(1)}, f32[4,384,256]{2,1,0:T(8,128)S(1)}) custom-call(s32[9]{0:T(128)S(1)} %copy-done.14, bf16[4,192,512]{2,1,0:T(8,128)(2,1)S(1)} %copy-done.12, bf16[4,384,256]{2,1,0:T(8,128)(2,1)S(1)} %copy-done.4, bf16[4,384,256]{2,1,0:T(8,128)(2,1)S(1)} %copy-done.2, ...), custom_call_target="tpu_custom_call" | custom-call | flops 6039797760 | bytes 12582912 | tf_op jit(solution)/shard_map/pallas_call | solution.py:309
  827.4 8.0 multiply_reduce_fusion.1
  847.1 23.4 %convolution_convert_fusion = bf16[2304,2304]{1,0:T(8,128)(2,1)} fusion(bf16[384,2304]{1,0:T(8,128)(2,1)} %get-tuple-element.627, bf16[384,2304]{1,0:T(8,128)(2,1)} %get-tuple-element.626, bf16[384,2304]{1,0:T(8,128)(2,1)} %get-tuple-element.625, bf16[384,2304]{1,0:T(8,128)(2,1)} %get-tuple-element.624, ...), kind=kOutput, calls=%fused_computation | convolution fusion | flops 16369385472 | bytes 24772608 | tf_op jit(solution)/shard_map/dot_general | solution.py:38
  895.8 8.0 add_convert_fusion
  903.9 9.6 collective-permute-done.73
  938.5 14.4 %shard_map.257 = (f32[4,192,512]{2,1,0:T(8,128)S(1)}, f32[4,384,256]{2,1,0:T(8,128)S(1)}, f32[4,384,256]{2,1,0:T(8,128)S(1)}) custom-call(s32[9]{0:T(128)S(1)} %copy-done.16, bf16[4,192,512]{2,1,0:T(8,128)(2,1)S(1)} %copy-done.10, bf16[4,384,256]{2,1,0:T(8,128)(2,1)S(1)} %copy-done.8, bf16[4,384,256]{2,1,0:T(8,128)(2,1)S(1)} %copy-done.6, ...), custom_call_target="tpu_custom_call" | custom-call | flops 6039797760 | bytes 12582912 | tf_op jit(solution)/shard_map/pallas_call | solution.py:309
  974.0 6.6 fusion.203
  986.6 28.4 %all-reduce.10.cloned.1.call-done = (bf16[1152,2304]{1,0:T(8,128)(2,1)}, bf16[1152,2304]{1,0:T(8,128)(2,1)}) async-done(((bf16[1152,2304]{1,0:T(8,128)(2,1)}, bf16[1152,2304]{1,0:T(8,128)(2,1)}), (bf16[1152,2304]{1,0:T(8,128)(2,1)}, bf16[1152,2304]{1,0:T(8,128)(2,1)})) %all-reduce.10.cloned.1.call-update) | async-done | bytes 10616848 | tf_op jit(solution)/shard_map/psum | solution.py:643
  1019.2 11.7 fusion.47
  1030.9 8.3 collective-permute-done.79
  1056.3 8.9 collective-permute-done.81
  1068.9 71.7 %all-reduce.8.cloned.1.call-done = bf16[1152,2304]{1,0:T(8,128)(2,1)} async-done(((bf16[1152,2304]{1,0:T(8,128)(2,1)}), bf16[1152,2304]{1,0:T(8,128)(2,1)}) %all-reduce.8.cloned.1.call-update) | async-done | bytes 5308432 | tf_op jit(solution)/shard_map/psum | solution.py:643
  1147.9 8.0 convert_element_type.895
  1160.8 7.9 convert_element_type.896
  1182.1 9.4 psum.63
  1192.1 64.6 %all-reduce.12.cloned.1.call-done = (bf16[256,2304]{1,0:T(8,128)(2,1)}, bf16[128,2304]{1,0:T(8,128)(2,1)}, bf16[128,2304]{1,0:T(8,128)(2,1)}, bf16[256,2304]{1,0:T(8,128)(2,1)}) async-done(((bf16[256,2304]{1,0:T(8,128)(2,1)}, bf16[128,2304]{1,0:T(8,128)(2,1)}, bf16[128,2304]{1,0:T(8,128)(2,1)}, bf16[256,2304]{1,0:T(8,128)(2,1)}), (bf16[256,2304]{1,0:T(8,128)(2,1)}, bf16[128,2304]{1,0:T(8,128)(2,1)}, ...) | async-done | bytes 3538960 | tf_op jit(solution)/shard_map/psum | solution.py:643
  (913 shorter events, 589.6 us)
Async XLA Ops:
  7.2 1007.9 %all-reduce.10.cloned.1.call-start = ((), (), s32[]{:S(2)}) async-start(), calls=%async_computation.1 | async-start | bytes 21233664 | tf_op jit(solution)/shard_map/psum | solution.py:643
  12.6 25.5 %collective-permute-start = (bf16[208,2304]{1,0:T(8,128)(2,1)S(1)}, bf16[208,2304]{1,0:T(8,128)(2,1)S(1)}, u32[]{:S(2)}, u32[]{:S(2)}) collective-permute-start(bf16[208,2304]{1,0:T(8,128)(2,1)S(1)} %fusion.136), channel_id=1, source_target_pairs={{0,2},{1,3},{2,4},{3,5},{4,6},{5,7},{8,10},{9,11},{10,12},{11,13},... | collective-permute-start | bytes 2875400 | tf_op jit(solution)/shard_map/ppermute | solution.py:59
  17.7 24.6 %collective-permute-start.1 = (bf16[208,2304]{1,0:T(8,128)(2,1)S(1)}, bf16[208,2304]{1,0:T(8,128)(2,1)S(1)}, u32[]{:S(2)}, u32[]{:S(2)}) collective-permute-start(bf16[208,2304]{1,0:T(8,128)(2,1)S(1)} %fusion.136), channel_id=1, source_target_pairs={{2,0},{3,1},{4,2},{5,3},{6,4},{7,5},{10,8},{11,9},{12,10},{13,11},... | collective-permute-start | bytes 2875400 | tf_op jit(solution)/shard_map/ppermute | solution.py:63
  45.5 28.1 %collective-permute-start.3 = (bf16[208,2304]{1,0:T(8,128)(2,1)}, bf16[208,2304]{1,0:T(8,128)(2,1)}, u32[]{:S(2)}, u32[]{:S(2)}) collective-permute-start(bf16[208,2304]{1,0:T(8,128)(2,1)} %copy-done.123), channel_id=1, source_target_pairs={{2,0},{3,1},{4,2},{5,3},{10,8},{11,9},{12,10},{13,11},{18,16},{19,... | collective-permute-start | bytes 2875400 | tf_op jit(solution)/shard_map/ppermute | solution.py:63
  80.6 25.9 %collective-permute-start.9 = (bf16[208,2304]{1,0:T(8,128)(2,1)}, bf16[208,2304]{1,0:T(8,128)(2,1)S(1)}, u32[]{:S(2)}, u32[]{:S(2)}) collective-permute-start(bf16[208,2304]{1,0:T(8,128)(2,1)} %collective-permute-done.3), channel_id=1, source_target_pairs={{2,0},{3,1},{10,8},{11,9},{18,16},{19,17},{26,24},{27,25}} | collective-permute-start | bytes 2875400 | tf_op jit(solution)/shard_map/ppermute | solution.py:63
  107.0 40.1 %collective-permute-start.11 = (bf16[192,2304]{1,0:T(8,128)(2,1)}, bf16[192,2304]{1,0:T(8,128)(2,1)}, u32[]{:S(2)}, u32[]{:S(2)}) collective-permute-start(bf16[192,2304]{1,0:T(8,128)(2,1)} %get-tuple-element.386), channel_id=1, source_target_pairs={{0,2},{1,3},{2,4},{3,5},{4,6},{5,7},{8,10},{9,11},{10,12},{11,13},... | collective-permute-start | bytes 2654216 | tf_op jit(solution)/shard_map/ppermute | solution.py:59
  109.6 37.4 %collective-permute-start.12 = (bf16[192,2304]{1,0:T(8,128)(2,1)}, bf16[192,2304]{1,0:T(8,128)(2,1)}, u32[]{:S(2)}, u32[]{:S(2)}) collective-permute-start(bf16[192,2304]{1,0:T(8,128)(2,1)} %get-tuple-element.386), channel_id=1, source_target_pairs={{2,0},{3,1},{4,2},{5,3},{6,4},{7,5},{10,8},{11,9},{12,10},{13,11},... | collective-permute-start | bytes 2654216 | tf_op jit(solution)/shard_map/ppermute | solution.py:63
  151.2 26.7 %collective-permute-start.19 = (bf16[1152,2304]{1,0:T(8,128)(2,1)}, bf16[1152,2304]{1,0:T(8,128)(2,1)}, u32[]{:S(2)}, u32[]{:S(2)}) collective-permute-start(bf16[1152,2304]{1,0:T(8,128)(2,1)} %param.23), channel_id=1, source_target_pairs={{0,1},{1,0},{2,3},{3,2},{4,5},{5,4},{6,7},{7,6},{8,9},{9,8},{10,11... | collective-permute-start | bytes 15925256 | tf_op jit(solution)/shard_map/ppermute | solution.py:66
  161.5 25.9 %collective-permute-start.16 = (bf16[192,2304]{1,0:T(8,128)(2,1)}, bf16[192,2304]{1,0:T(8,128)(2,1)}, u32[]{:S(2)}, u32[]{:S(2)}) collective-permute-start(bf16[192,2304]{1,0:T(8,128)(2,1)} %get-tuple-element.384), channel_id=1, source_target_pairs={{0,2},{1,3},{2,4},{3,5},{4,6},{5,7},{8,10},{9,11},{10,12},{11,13},... | collective-permute-start | bytes 2654216 | tf_op jit(solution)/shard_map/ppermute | solution.py:59
  167.0 23.7 %collective-permute-start.17 = (bf16[192,2304]{1,0:T(8,128)(2,1)}, bf16[192,2304]{1,0:T(8,128)(2,1)}, u32[]{:S(2)}, u32[]{:S(2)}) collective-permute-start(bf16[192,2304]{1,0:T(8,128)(2,1)} %get-tuple-element.385), channel_id=1, source_target_pairs={{2,0},{3,1},{4,2},{5,3},{6,4},{7,5},{10,8},{11,9},{12,10},{13,11},... | collective-permute-start | bytes 2654216 | tf_op jit(solution)/shard_map/ppermute | solution.py:63
  193.4 21.4 %collective-permute-start.20 = (bf16[192,2304]{1,0:T(8,128)(2,1)S(1)}, bf16[192,2304]{1,0:T(8,128)(2,1)S(1)}, u32[]{:S(2)}, u32[]{:S(2)}) collective-permute-start(bf16[192,2304]{1,0:T(8,128)(2,1)S(1)} %get-tuple-element.391), channel_id=1, source_target_pairs={{0,2},{1,3},{2,4},{3,5},{4,6},{5,7},{8,10},{9,11},{10,12},{11,13},... | collective-permute-start | bytes 2654216 | tf_op jit(solution)/shard_map/ppermute | solution.py:59
  194.9 23.8 %collective-permute-start.21 = (bf16[192,2304]{1,0:T(8,128)(2,1)S(1)}, bf16[192,2304]{1,0:T(8,128)(2,1)S(1)}, u32[]{:S(2)}, u32[]{:S(2)}) collective-permute-start(bf16[192,2304]{1,0:T(8,128)(2,1)S(1)} %get-tuple-element.392), channel_id=1, source_target_pairs={{2,0},{3,1},{4,2},{5,3},{6,4},{7,5},{10,8},{11,9},{12,10},{13,11},... | collective-permute-start | bytes 2654216 | tf_op jit(solution)/shard_map/ppermute | solution.py:63
  225.6 22.3 %collective-permute-start.23 = (bf16[192,2304]{1,0:T(8,128)(2,1)}, bf16[192,2304]{1,0:T(8,128)(2,1)S(1)}, u32[]{:S(2)}, u32[]{:S(2)}) collective-permute-start(bf16[192,2304]{1,0:T(8,128)(2,1)} %get-tuple-element.396), channel_id=1, source_target_pairs={{0,2},{1,3},{2,4},{3,5},{4,6},{5,7},{8,10},{9,11},{10,12},{11,13},... | collective-permute-start | bytes 2654216 | tf_op jit(solution)/shard_map/ppermute | solution.py:59
  229.0 22.9 %collective-permute-start.24 = (bf16[192,2304]{1,0:T(8,128)(2,1)}, bf16[192,2304]{1,0:T(8,128)(2,1)S(1)}, u32[]{:S(2)}, u32[]{:S(2)}) collective-permute-start(bf16[192,2304]{1,0:T(8,128)(2,1)} %get-tuple-element.397), channel_id=1, source_target_pairs={{2,0},{3,1},{4,2},{5,3},{6,4},{7,5},{10,8},{11,9},{12,10},{13,11},... | collective-permute-start | bytes 2654216 | tf_op jit(solution)/shard_map/ppermute | solution.py:63
  259.4 21.7 %collective-permute-start.27 = (bf16[192,2304]{1,0:T(8,128)(2,1)S(1)}, bf16[192,2304]{1,0:T(8,128)(2,1)S(1)}, u32[]{:S(2)}, u32[]{:S(2)}) collective-permute-start(bf16[192,2304]{1,0:T(8,128)(2,1)S(1)} %multiply_convert_fusion.3), channel_id=1, source_target_pairs={{2,0},{3,1},{4,2},{5,3},{6,4},{7,5},{10,8},{11,9},{12,10},{13,11},... | collective-permute-start | bytes 2654216 | tf_op jit(solution)/shard_map/ppermute | solution.py:63
  284.4 20.8 %collective-permute-start.29 = (bf16[192,2304]{1,0:T(8,128)(2,1)S(1)}, bf16[192,2304]{1,0:T(8,128)(2,1)S(1)}, u32[]{:S(2)}, u32[]{:S(2)}) collective-permute-start(bf16[192,2304]{1,0:T(8,128)(2,1)S(1)} %get-tuple-element.420), channel_id=1, source_target_pairs={{2,0},{3,1},{4,2},{5,3},{6,4},{7,5},{10,8},{11,9},{12,10},{13,11},... | collective-permute-start | bytes 2654216 | tf_op jit(solution)/shard_map/ppermute | solution.py:63
  330.7 20.0 %collective-permute-start.32 = (bf16[192,2304]{1,0:T(8,128)(2,1)}, bf16[192,2304]{1,0:T(8,128)(2,1)S(1)}, u32[]{:S(2)}, u32[]{:S(2)}) collective-permute-start(bf16[192,2304]{1,0:T(8,128)(2,1)} %get-tuple-element.438), channel_id=1, source_target_pairs={{0,2},{1,3},{2,4},{3,5},{4,6},{5,7},{8,10},{9,11},{10,12},{11,13},... | collective-permute-start | bytes 2654216 | tf_op jit(solution)/shard_map/ppermute | solution.py:59
  425.6 20.1 %collective-permute-start.40 = (bf16[192,2304]{1,0:T(8,128)(2,1)}, bf16[192,2304]{1,0:T(8,128)(2,1)S(1)}, u32[]{:S(2)}, u32[]{:S(2)}) collective-permute-start(bf16[192,2304]{1,0:T(8,128)(2,1)} %get-tuple-element.469), channel_id=1, source_target_pairs={{0,2},{1,3},{2,4},{3,5},{4,6},{5,7},{8,10},{9,11},{10,12},{11,13},... | collective-permute-start | bytes 2654216 | tf_op jit(solution)/shard_map/ppermute | solution.py:59
  496.1 23.4 %collective-permute-start.46 = (bf16[192,2304]{1,0:T(8,128)(2,1)S(1)}, bf16[192,2304]{1,0:T(8,128)(2,1)S(1)}, u32[]{:S(2)}, u32[]{:S(2)}) collective-permute-start(bf16[192,2304]{1,0:T(8,128)(2,1)S(1)} %get-tuple-element.498), channel_id=1, source_target_pairs={{0,2},{1,3},{2,4},{3,5},{4,6},{5,7},{8,10},{9,11},{10,12},{11,13},... | collective-permute-start | bytes 2654216 | tf_op jit(solution)/shard_map/ppermute | solution.py:59
  499.0 20.6 %collective-permute-start.47 = (bf16[192,2304]{1,0:T(8,128)(2,1)S(1)}, bf16[192,2304]{1,0:T(8,128)(2,1)S(1)}, u32[]{:S(2)}, u32[]{:S(2)}) collective-permute-start(bf16[192,2304]{1,0:T(8,128)(2,1)S(1)} %get-tuple-element.499), channel_id=1, source_target_pairs={{2,0},{3,1},{4,2},{5,3},{6,4},{7,5},{10,8},{11,9},{12,10},{13,11},... | collective-permute-start | bytes 2654216 | tf_op jit(solution)/shard_map/ppermute | solution.py:63
  596.1 22.1 %collective-permute-start.54 = (bf16[192,2304]{1,0:T(8,128)(2,1)S(1)}, bf16[192,2304]{1,0:T(8,128)(2,1)S(1)}, u32[]{:S(2)}, u32[]{:S(2)}) collective-permute-start(bf16[192,2304]{1,0:T(8,128)(2,1)S(1)} %get-tuple-element.536), channel_id=1, source_target_pairs={{0,2},{1,3},{2,4},{3,5},{4,6},{5,7},{8,10},{9,11},{10,12},{11,13},... | collective-permute-start | bytes 2654216 | tf_op jit(solution)/shard_map/ppermute | solution.py:59
  598.1 20.2 %collective-permute-start.55 = (bf16[192,2304]{1,0:T(8,128)(2,1)S(1)}, bf16[192,2304]{1,0:T(8,128)(2,1)S(1)}, u32[]{:S(2)}, u32[]{:S(2)}) collective-permute-start(bf16[192,2304]{1,0:T(8,128)(2,1)S(1)} %get-tuple-element.537), channel_id=1, source_target_pairs={{2,0},{3,1},{4,2},{5,3},{6,4},{7,5},{10,8},{11,9},{12,10},{13,11},... | collective-permute-start | bytes 2654216 | tf_op jit(solution)/shard_map/ppermute | solution.py:63
  621.4 41.0 %collective-permute-start.56 = (bf16[192,2304]{1,0:T(8,128)(2,1)}, bf16[192,2304]{1,0:T(8,128)(2,1)S(1)}, u32[]{:S(2)}, u32[]{:S(2)}) collective-permute-start(bf16[192,2304]{1,0:T(8,128)(2,1)} %get-tuple-element.542), channel_id=1, source_target_pairs={{0,2},{1,3},{2,4},{3,5},{4,6},{5,7},{8,10},{9,11},{10,12},{11,13},... | collective-permute-start | bytes 2654216 | tf_op jit(solution)/shard_map/ppermute | solution.py:59
  626.0 36.4 %collective-permute-start.57 = (bf16[192,2304]{1,0:T(8,128)(2,1)}, bf16[192,2304]{1,0:T(8,128)(2,1)}, u32[]{:S(2)}, u32[]{:S(2)}) collective-permute-start(bf16[192,2304]{1,0:T(8,128)(2,1)} %get-tuple-element.543), channel_id=1, source_target_pairs={{2,0},{3,1},{4,2},{5,3},{6,4},{7,5},{10,8},{11,9},{12,10},{13,11},... | collective-permute-start | bytes 2654216 | tf_op jit(solution)/shard_map/ppermute | solution.py:63
  675.8 20.1 %collective-permute-start.60 = (bf16[1152,2304]{1,0:T(8,128)(2,1)}, bf16[1152,2304]{1,0:T(8,128)(2,1)}, u32[]{:S(2)}, u32[]{:S(2)}) collective-permute-start(bf16[1152,2304]{1,0:T(8,128)(2,1)} %slice.553), channel_id=1, source_target_pairs={{0,1},{1,0},{2,3},{3,2},{4,5},{5,4},{6,7},{7,6},{8,9},{9,8},{10,11... | collective-permute-start | bytes 15925256 | tf_op jit(solution)/shard_map/ppermute | solution.py:66
  675.8 26.3 %collective-permute-start.58 = (bf16[192,2304]{1,0:T(8,128)(2,1)}, bf16[192,2304]{1,0:T(8,128)(2,1)}, u32[]{:S(2)}, u32[]{:S(2)}) collective-permute-start(bf16[192,2304]{1,0:T(8,128)(2,1)} %multiply_convert_fusion.1), channel_id=1, source_target_pairs={{0,2},{1,3},{2,4},{3,5},{4,6},{5,7},{8,10},{9,11},{10,12},{11,13},... | collective-permute-start | bytes 2654216 | tf_op jit(solution)/shard_map/ppermute | solution.py:59
  681.5 23.7 %collective-permute-start.59 = (bf16[192,2304]{1,0:T(8,128)(2,1)}, bf16[192,2304]{1,0:T(8,128)(2,1)}, u32[]{:S(2)}, u32[]{:S(2)}) collective-permute-start(bf16[192,2304]{1,0:T(8,128)(2,1)} %multiply_convert_fusion.1), channel_id=1, source_target_pairs={{2,0},{3,1},{4,2},{5,3},{6,4},{7,5},{10,8},{11,9},{12,10},{13,11},... | collective-permute-start | bytes 2654216 | tf_op jit(solution)/shard_map/ppermute | solution.py:63
  708.3 26.7 %collective-permute-start.61 = (bf16[192,2304]{1,0:T(8,128)(2,1)}, bf16[192,2304]{1,0:T(8,128)(2,1)}, u32[]{:S(2)}, u32[]{:S(2)}) collective-permute-start(bf16[192,2304]{1,0:T(8,128)(2,1)} %get-tuple-element.571), channel_id=1, source_target_pairs={{0,2},{1,3},{2,4},{3,5},{4,6},{5,7},{8,10},{9,11},{10,12},{11,13},... | collective-permute-start | bytes 2654216 | tf_op jit(solution)/shard_map/ppermute | solution.py:59
  710.7 24.3 %collective-permute-start.62 = (bf16[192,2304]{1,0:T(8,128)(2,1)}, bf16[192,2304]{1,0:T(8,128)(2,1)}, u32[]{:S(2)}, u32[]{:S(2)}) collective-permute-start(bf16[192,2304]{1,0:T(8,128)(2,1)} %get-tuple-element.572), channel_id=1, source_target_pairs={{2,0},{3,1},{4,2},{5,3},{6,4},{7,5},{10,8},{11,9},{12,10},{13,11},... | collective-permute-start | bytes 2654216 | tf_op jit(solution)/shard_map/ppermute | solution.py:63
  742.4 24.5 %collective-permute-start.63 = (bf16[192,2304]{1,0:T(8,128)(2,1)}, bf16[192,2304]{1,0:T(8,128)(2,1)}, u32[]{:S(2)}, u32[]{:S(2)}) collective-permute-start(bf16[192,2304]{1,0:T(8,128)(2,1)} %get-tuple-element.584), channel_id=1, source_target_pairs={{0,2},{1,3},{2,4},{3,5},{4,6},{5,7},{8,10},{9,11},{10,12},{11,13},... | collective-permute-start | bytes 2654216 | tf_op jit(solution)/shard_map/ppermute | solution.py:59
  748.2 23.8 %collective-permute-start.64 = (bf16[192,2304]{1,0:T(8,128)(2,1)}, bf16[192,2304]{1,0:T(8,128)(2,1)}, u32[]{:S(2)}, u32[]{:S(2)}) collective-permute-start(bf16[192,2304]{1,0:T(8,128)(2,1)} %get-tuple-element.585), channel_id=1, source_target_pairs={{2,0},{3,1},{4,2},{5,3},{6,4},{7,5},{10,8},{11,9},{12,10},{13,11},... | collective-permute-start | bytes 2654216 | tf_op jit(solution)/shard_map/ppermute | solution.py:63
  775.3 23.3 %collective-permute-start.66 = (bf16[192,2304]{1,0:T(8,128)(2,1)S(1)}, bf16[192,2304]{1,0:T(8,128)(2,1)S(1)}, u32[]{:S(2)}, u32[]{:S(2)}) collective-permute-start(bf16[192,2304]{1,0:T(8,128)(2,1)S(1)} %get-tuple-element.589), channel_id=1, source_target_pairs={{0,2},{1,3},{2,4},{3,5},{4,6},{5,7},{8,10},{9,11},{10,12},{11,13},... | collective-permute-start | bytes 2654216 | tf_op jit(solution)/shard_map/ppermute | solution.py:59
  776.9 22.5 %collective-permute-start.67 = (bf16[192,2304]{1,0:T(8,128)(2,1)S(1)}, bf16[192,2304]{1,0:T(8,128)(2,1)S(1)}, u32[]{:S(2)}, u32[]{:S(2)}) collective-permute-start(bf16[192,2304]{1,0:T(8,128)(2,1)S(1)} %get-tuple-element.590), channel_id=1, source_target_pairs={{2,0},{3,1},{4,2},{5,3},{6,4},{7,5},{10,8},{11,9},{12,10},{13,11},... | collective-permute-start | bytes 2654216 | tf_op jit(solution)/shard_map/ppermute | solution.py:63
  807.9 332.7 %all-reduce.8.cloned.1.call-start = ((), (), s32[]{:S(2)}) async-start(), calls=%async_computation | async-start | bytes 10616832 | tf_op jit(solution)/shard_map/psum | solution.py:643
  807.9 27.4 %collective-permute-start.68 = (bf16[192,2304]{1,0:T(8,128)(2,1)}, bf16[192,2304]{1,0:T(8,128)(2,1)}, u32[]{:S(2)}, u32[]{:S(2)}) collective-permute-start(bf16[192,2304]{1,0:T(8,128)(2,1)} %multiply_convert_fusion), channel_id=1, source_target_pairs={{0,2},{1,3},{2,4},{3,5},{4,6},{5,7},{8,10},{9,11},{10,12},{11,13},... | collective-permute-start | bytes 2654216 | tf_op jit(solution)/shard_map/ppermute | solution.py:59
  812.7 24.0 %collective-permute-start.69 = (bf16[192,2304]{1,0:T(8,128)(2,1)}, bf16[192,2304]{1,0:T(8,128)(2,1)}, u32[]{:S(2)}, u32[]{:S(2)}) collective-permute-start(bf16[192,2304]{1,0:T(8,128)(2,1)} %multiply_convert_fusion), channel_id=1, source_target_pairs={{2,0},{3,1},{4,2},{5,3},{6,4},{7,5},{10,8},{11,9},{12,10},{13,11},... | collective-permute-start | bytes 2654216 | tf_op jit(solution)/shard_map/ppermute | solution.py:63
  839.7 30.8 %collective-permute-start.71 = (bf16[192,2304]{1,0:T(8,128)(2,1)}, bf16[192,2304]{1,0:T(8,128)(2,1)}, u32[]{:S(2)}, u32[]{:S(2)}) collective-permute-start(bf16[192,2304]{1,0:T(8,128)(2,1)} %get-tuple-element.622), channel_id=1, source_target_pairs={{0,2},{1,3},{2,4},{3,5},{4,6},{5,7},{8,10},{9,11},{10,12},{11,13},... | collective-permute-start | bytes 2654216 | tf_op jit(solution)/shard_map/ppermute | solution.py:59
  845.7 24.9 %collective-permute-start.72 = (bf16[192,2304]{1,0:T(8,128)(2,1)}, bf16[192,2304]{1,0:T(8,128)(2,1)}, u32[]{:S(2)}, u32[]{:S(2)}) collective-permute-start(bf16[192,2304]{1,0:T(8,128)(2,1)} %get-tuple-element.623), channel_id=1, source_target_pairs={{2,0},{3,1},{4,2},{5,3},{6,4},{7,5},{10,8},{11,9},{12,10},{13,11},... | collective-permute-start | bytes 2654216 | tf_op jit(solution)/shard_map/ppermute | solution.py:63
  889.0 24.5 %collective-permute-start.73 = (bf16[192,2304]{1,0:T(8,128)(2,1)}, bf16[192,2304]{1,0:T(8,128)(2,1)}, u32[]{:S(2)}, u32[]{:S(2)}) collective-permute-start(bf16[192,2304]{1,0:T(8,128)(2,1)} %get-tuple-element.635), channel_id=1, source_target_pairs={{0,2},{1,3},{2,4},{3,5},{4,6},{5,7},{8,10},{9,11},{10,12},{11,13},... | collective-permute-start | bytes 2654216 | tf_op jit(solution)/shard_map/ppermute | solution.py:59
  894.5 24.0 %collective-permute-start.74 = (bf16[192,2304]{1,0:T(8,128)(2,1)}, bf16[192,2304]{1,0:T(8,128)(2,1)}, u32[]{:S(2)}, u32[]{:S(2)}) collective-permute-start(bf16[192,2304]{1,0:T(8,128)(2,1)} %get-tuple-element.636), channel_id=1, source_target_pairs={{2,0},{3,1},{4,2},{5,3},{6,4},{7,5},{10,8},{11,9},{12,10},{13,11},... | collective-permute-start | bytes 2654216 | tf_op jit(solution)/shard_map/ppermute | solution.py:63
  923.9 30.2 %collective-permute-start.76 = (bf16[192,2304]{1,0:T(8,128)(2,1)}, bf16[192,2304]{1,0:T(8,128)(2,1)}, u32[]{:S(2)}, u32[]{:S(2)}) collective-permute-start(bf16[192,2304]{1,0:T(8,128)(2,1)} %get-tuple-element.640), channel_id=1, source_target_pairs={{0,2},{1,3},{2,4},{3,5},{4,6},{5,7},{8,10},{9,11},{10,12},{11,13},... | collective-permute-start | bytes 2654216 | tf_op jit(solution)/shard_map/ppermute | solution.py:59
  926.5 27.6 %collective-permute-start.77 = (bf16[192,2304]{1,0:T(8,128)(2,1)}, bf16[192,2304]{1,0:T(8,128)(2,1)}, u32[]{:S(2)}, u32[]{:S(2)}) collective-permute-start(bf16[192,2304]{1,0:T(8,128)(2,1)} %get-tuple-element.641), channel_id=1, source_target_pairs={{2,0},{3,1},{4,2},{5,3},{6,4},{7,5},{10,8},{11,9},{12,10},{13,11},... | collective-permute-start | bytes 2654216 | tf_op jit(solution)/shard_map/ppermute | solution.py:63
  930.0 326.6 %all-reduce.12.cloned.1.call-start = ((), (), s32[]{:S(2)}) async-start(), calls=%async_computation.2 | async-start | bytes 7077888 | tf_op jit(solution)/shard_map/psum | solution.py:643
  1015.1 24.2 %collective-permute-start.79 = (bf16[208,2304]{1,0:T(8,128)(2,1)}, bf16[208,2304]{1,0:T(8,128)(2,1)S(1)}, u32[]{:S(2)}, u32[]{:S(2)}) collective-permute-start(bf16[208,2304]{1,0:T(8,128)(2,1)} %pad_maximum_fusion.10), channel_id=1, source_target_pairs={{0,2},{1,3},{8,10},{9,11},{16,18},{17,19},{24,26},{25,27}} | collective-permute-start | bytes 2875400 | tf_op jit(solution)/shard_map/ppermute | solution.py:59
  1018.5 20.7 %collective-permute-start.80 = (bf16[208,2304]{1,0:T(8,128)(2,1)}, bf16[208,2304]{1,0:T(8,128)(2,1)S(1)}, u32[]{:S(2)}, u32[]{:S(2)}) collective-permute-start(bf16[208,2304]{1,0:T(8,128)(2,1)} %pad_maximum_fusion.10), channel_id=1, source_target_pairs={{6,4},{7,5},{14,12},{15,13},{22,20},{23,21},{30,28},{31,29}} | collective-permute-start | bytes 2875400 | tf_op jit(solution)/shard_map/ppermute | solution.py:63
  1040.9 24.3 %collective-permute-start.81 = (bf16[208,2304]{1,0:T(8,128)(2,1)}, bf16[208,2304]{1,0:T(8,128)(2,1)}, u32[]{:S(2)}, u32[]{:S(2)}) collective-permute-start(bf16[208,2304]{1,0:T(8,128)(2,1)} %get-tuple-element.681), channel_id=1, source_target_pairs={{0,2},{1,3},{2,4},{3,5},{8,10},{9,11},{10,12},{11,13},{16,18},{17,... | collective-permute-start | bytes 2875400 | tf_op jit(solution)/shard_map/ppermute | solution.py:59
  1140.6 28.1 %collective-permute-start.87 = (bf16[208,2304]{1,0:T(8,128)(2,1)}, bf16[208,2304]{1,0:T(8,128)(2,1)}, u32[]{:S(2)}, u32[]{:S(2)}) collective-permute-start(bf16[208,2304]{1,0:T(8,128)(2,1)} %get-tuple-element.688), channel_id=1, source_target_pairs={{0,2},{1,3},{2,4},{3,5},{4,6},{5,7},{8,10},{9,11},{10,12},{11,13},... | collective-permute-start | bytes 2875400 | tf_op jit(solution)/shard_map/ppermute | solution.py:59
  1145.0 24.9 %collective-permute-start.88 = (bf16[208,2304]{1,0:T(8,128)(2,1)}, bf16[208,2304]{1,0:T(8,128)(2,1)}, u32[]{:S(2)}, u32[]{:S(2)}) collective-permute-start(bf16[208,2304]{1,0:T(8,128)(2,1)} %get-tuple-element.689), channel_id=1, source_target_pairs={{2,0},{3,1},{4,2},{5,3},{6,4},{7,5},{10,8},{11,9},{12,10},{13,11},... | collective-permute-start | bytes 2875400 | tf_op jit(solution)/shard_map/ppermute | solution.py:63
  (262 other events, 3045.2 us)
Sparse Core Ops, SparseCore 0:
  808.0 207.0 all-reduce.9
  1018.4 122.1 all-reduce.7
  1160.9 95.7 all-reduce.11

commit v4 on v3

v4 whole, which is shorter than its diff:
```python
import functools

import jax
import jax.numpy as jnp
from jax import lax
from jax.experimental import pallas as pl
from jax.experimental.pallas import tpu as pltpu
from jax.sharding import PartitionSpec as P

HEADS = 8
KV_HEADS = 4
HEAD_DIM = 256
HALF = HEAD_DIM // 2

epsilon = 1e-06
soft_cap = 50.0
rope_base = 10000.0
gelu_a = 0.7978845608028654
gelu_b = 0.044715
query_scale = HEAD_DIM ** (-0.5)

bf16 = jnp.bfloat16
f32 = jnp.float32


def nt(left_side, right_side):
    return lax.dot_general(
        left_side, right_side, (((1,), (1,)), ((), ())), preferred_element_type=f32
    )


def nn(left_side, right_side):
    return lax.dot_general(
        left_side, right_side, (((1,), (0,)), ((), ())), preferred_element_type=f32
    )


def tn(left_side, right_side):
    return lax.dot_general(
        left_side, right_side, (((0,), (0,)), ((), ())), preferred_element_type=f32
    )


def inverse_root(values):
    return lax.rsqrt(jnp.mean(values * values, axis=-1, keepdims=True) + epsilon)


def norm_backward(normed, root, gain, grad):
    scaled = grad * gain
    return root * (scaled - normed * jnp.mean(scaled * normed, axis=-1, keepdims=True))


class Line:
    def __init__(self, size, index):
        self.chips = size // 2
        self.z = index // 2
        self.c = index % 2
        self.core_pairs = [(i, i ^ 1) for i in range(size)]

    def pairs(self, step, low, high):
        return [
            (2 * z + c, 2 * (z + step) + c)
            for z in range(low, high)
            for c in range(2)
            if 0 <= z + step < self.chips
        ]

    def right(self, block, low, high):
        return lax.ppermute(block, "ctx", self.pairs(1, low, high))

    def left(self, block, low, high):
        n = self.chips
        return lax.ppermute(block, "ctx", self.pairs(-1, n - high, n - low))

    def swap(self, block):
        return lax.ppermute(block, "ctx", self.core_pairs)

    def exchanged(self, items):
        last = self.z == self.chips - 1
        items = list(items)
        first, final = items[1], items[-1]
        items[1] = jnp.where(last, final, first)
        items[-1] = jnp.where(last, first, final)
        return items

    def table(self):
        order = self.exchanged([jnp.int32(k) for k in range(self.chips)])
        return [lax.rem(self.z + k, self.chips) for k in order]


def tied(*values):
    return lax.optimization_barrier(values)


class Exchange:
    def __init__(self, line, own=None, sums=True):
        self.line, self.own, self.sums = line, own, sums
        self.parts = None
        self.s = 0
        self.from_left, self.from_right = [own], [own]
        self.sum_left = self.sum_right = None

    def step(self, work=None, inputs=(), held=()):
        line, n, z = self.line, self.line.chips, self.line.z
        gathers = self.own is not None
        self.s += 1
        s = self.s
        to_right = to_left = None
        low, high = 0, n
        if gathers and s <= n - 1:
            to_right, to_left = self.from_left[s - 1], self.from_right[s - 1]
            low = s - 1
        j = s - 1 if gathers else s
        if self.sums and j >= 1:
            sum_r, sum_l = self.parts[n - j], self.parts[n - 1 if j == 1 else j]
            if j == n - 1:
                sum_l = jnp.where(z == n - 1, self.parts[1], self.parts[n - 1])
            if self.sum_left is not None:
                sum_r = (sum_r.astype(f32) + self.sum_left.astype(f32)).astype(bf16)
                sum_l = (sum_l.astype(f32) + self.sum_right.astype(f32)).astype(bf16)
            if to_right is None:
                to_right, to_left, high = sum_r, sum_l, j
            else:
                to_right = jnp.where(z >= s - 1, to_right, sum_r)
                to_left = jnp.where(n - 1 - z >= s - 1, to_left, sum_l)
                low = 0
        to_right, to_left, inputs, self.held = tied(to_right, to_left, inputs, held)
        got_left = line.right(to_right, low, high)
        got_right = line.left(to_left, low, high)
        outs = work(*inputs) if work is not None else ()
        got_left, got_right, outs = tied(got_left, got_right, outs)
        if gathers and s <= n - 1:
            self.from_left.append(got_left)
            self.from_right.append(got_right)
        if self.sums and j >= 1:
            self.sum_left, self.sum_right = got_left, got_right
        return outs

    def give(self, *halves):
        rows = halves[-1].shape[0] // (self.line.chips if len(halves) == 1 else self.line.chips - 2)
        self.first = halves[0]
        self.parts = [
            half[k * rows : (k + 1) * rows]
            for half in halves
            for k in range(half.shape[0] // rows)
        ]

    def near(self):
        last = self.line.z == self.line.chips - 1
        return [self.own, jnp.where(last, self.from_left[1], self.from_right[1])]

    def far(self):
        n, z = self.line.chips, self.line.z
        blocks = [
            jnp.where(z + k < n, self.from_right[k], self.from_left[n - k])
            for k in range(2, n - 1)
        ]
        final = jnp.where(z == 0, self.from_right[n - 1], self.from_left[1])
        return blocks + [jnp.where(z == n - 1, self.from_left[n - 1], final)]

    def terms(self):
        return (self.first, self.sum_left, self.sum_right)


def total(terms):
    rows = terms[-1].shape[0]
    return sum(t[:rows].astype(f32) for t in terms)


def spans_of(place, info, spans, none):
    label = jnp.full(place.shape, none, jnp.int32)
    for s in range(spans):
        start, stop = info[1 + s], info[1 + spans + s]
        label = jnp.where((place >= start) & (place < stop), s, label)
    return label


def seen_block(query_block, key_block, width, info, spans):
    seen = key_block <= query_block
    for s in range(spans):
        start, stop = info[1 + s], info[1 + spans + s]
        seen = seen | ((start < (query_block + 1) * width) & (stop > key_block * width))
    return seen


def block_mask(query_block, key_block, rows, info, spans):
    c = info[0]
    width = 2 * rows
    query_place = (
        query_block * width + c * rows + lax.broadcasted_iota(jnp.int32, (rows, 1), 0)
    )
    j = lax.broadcasted_iota(jnp.int32, (1, width), 1)
    key_place = key_block * width + j + jnp.where(j < rows, c * rows, -c * rows)
    query_span = spans_of(query_place, info, spans, -2)
    key_span = spans_of(key_place, info, spans, -1)
    return (key_place <= query_place) | (key_span == query_span)


def place_of(refs, kk):
    return refs[0][kk] if kk < 2 else refs[1][kk - 2]


def key_block_of(own_refs, other_refs, kk, part):
    cut = slice(part * HEAD_DIM, (part + 1) * HEAD_DIM)
    return jnp.concatenate([place_of(own_refs, kk)[:, cut], place_of(other_refs, kk)[:, cut]])


def forward_kernel(spans, heads, info, *refs):
    queries, own, other = refs[0:2], refs[2:4], refs[4:6]
    o_ref, acc_ref, sum_ref = refs[6:]
    rows = own[0].shape[1]
    chips = own[0].shape[0] + own[1].shape[0]
    width = 2 * rows
    query_block = info[1 + 2 * spans + pl.program_id(0)]
    query = jnp.where(pl.program_id(0) < 2, queries[0][0], queries[1][0])
    acc_ref[...] = jnp.zeros_like(acc_ref)
    sum_ref[...] = jnp.zeros_like(sum_ref)
    for kk in range(chips):
        key_block = info[1 + 2 * spans + kk]

        @pl.when(seen_block(query_block, key_block, width, info, spans))
        def _():
            allowed = block_mask(query_block, key_block, rows, info, spans)
            keys, values = (key_block_of(own, other, kk, part) for part in range(2))
            for h in range(heads):
                scores = nt(query[:, h * HEAD_DIM : (h + 1) * HEAD_DIM], keys)
                weights = jnp.where(
                    allowed, jnp.exp(soft_cap * jnp.tanh(scores * (1.0 / soft_cap))), 0.0
                )
                sum_ref[h] += jnp.sum(weights, axis=1, keepdims=True)
                acc_ref[h] += nn(weights.astype(bf16), values)

    for h in range(heads):
        o_ref[0, :, h * HEAD_DIM : (h + 1) * HEAD_DIM] = (acc_ref[h] / sum_ref[h]).astype(bf16)


def turned_back(vectors, cosine, sine):
    first, second = vectors[:, :HALF], vectors[:, HALF:]
    return first * cosine + second * sine, second * cosine - first * sine


def backward_kernel(spans, heads, info, *refs):
    queries, own, other = refs[0:2], refs[2:4], refs[4:6]
    g_ref, cos_ref, sin_ref, tables = refs[6], refs[7], refs[8], refs[9:13]
    dq_ref, own_ref, other_ref = refs[13:16]
    dk_ref, dv_ref, p_ref, r_ref, t_ref, sum_ref, inner_ref, acc_ref = refs[16:]
    chips, width, _ = dk_ref.shape
    rows = width // 2
    query_block = info[1 + 2 * spans + pl.program_id(0)]
    query = jnp.where(pl.program_id(0) < 2, queries[0][0], queries[1][0])

    @pl.when(pl.program_id(0) == 0)
    def _():
        dk_ref[...] = jnp.zeros_like(dk_ref)
        dv_ref[...] = jnp.zeros_like(dv_ref)

    acc_ref[...] = jnp.zeros_like(acc_ref)
    sum_ref[...] = jnp.zeros_like(sum_ref)
    inner_ref[...] = jnp.zeros_like(inner_ref)
    for kk in range(chips):
        key_block = info[1 + 2 * spans + kk]

        @pl.when(seen_block(query_block, key_block, width, info, spans))
        def _():
            allowed = block_mask(query_block, key_block, rows, info, spans)
            keys, values = (key_block_of(own, other, kk, part) for part in range(2))
            for h in range(heads):
                head = slice(h * HEAD_DIM, (h + 1) * HEAD_DIM)
                squashed = jnp.tanh(nt(query[:, head], keys) * (1.0 / soft_cap))
                weights = jnp.where(allowed, jnp.exp(soft_cap * squashed), 0.0)
                row_grad = nt(g_ref[0, :, head], values)
                sum_ref[h] += jnp.sum(weights, axis=1, keepdims=True)
                inner_ref[h] += jnp.sum(weights * row_grad, axis=1, keepdims=True)
                p_ref[kk, h] = weights
                r_ref[kk, h] = row_grad
                t_ref[kk, h] = 1.0 - squashed * squashed

    for kk in range(chips):
        key_block = info[1 + 2 * spans + kk]

        @pl.when(seen_block(query_block, key_block, width, info, spans))
        def _():
            keys = key_block_of(own, other, kk, 0)
            for h in range(heads):
                head = slice(h * HEAD_DIM, (h + 1) * HEAD_DIM)
                inverse = 1.0 / sum_ref[h]
                weights = p_ref[kk, h] * inverse
                inner = inner_ref[h] * inverse
                score_grad = (weights * (r_ref[kk, h] - inner) * t_ref[kk, h]).astype(bf16)
                acc_ref[h] += nn(score_grad, keys)
                dk_ref[kk] += tn(score_grad, query[:, head])
                dv_ref[kk] += tn(weights.astype(bf16), g_ref[0, :, head])

    for h in range(heads):
        first, second = turned_back(acc_ref[h], cos_ref[0], sin_ref[0])
        dq_ref[0, :, h * HEAD_DIM : h * HEAD_DIM + HALF] = (first * query_scale).astype(bf16)
        dq_ref[0, :, h * HEAD_DIM + HALF : (h + 1) * HEAD_DIM] = (second * query_scale).astype(bf16)

    @pl.when(pl.program_id(0) == chips - 1)
    def _():
        for kk in range(chips):
            for part, out in ((0, own_ref), (1, other_ref)):
                some = slice(part * rows, (part + 1) * rows)
                first, second = turned_back(
                    dk_ref[kk, some], tables[2 * part][kk], tables[2 * part + 1][kk]
                )
                out[kk, :, :HALF] = first.astype(out.dtype)
                out[kk, :, HALF:HEAD_DIM] = second.astype(out.dtype)
                out[kk, :, HEAD_DIM:] = dv_ref[kk, some].astype(out.dtype)


def block_spec(shape):
    return pl.BlockSpec((1,) + tuple(shape[1:]), lambda i, info: (i, 0, 0))


def near_spec(shape):
    return pl.BlockSpec((1,) + tuple(shape[1:]), lambda i, info: (jnp.minimum(i, 1), 0, 0))


def far_spec(shape):
    return pl.BlockSpec((1,) + tuple(shape[1:]), lambda i, info: (jnp.maximum(i - 2, 0), 0, 0))


def whole_spec(shape):
    return pl.BlockSpec(tuple(shape), lambda i, info: (0,) * len(shape))


light = pl.CostEstimate(flops=1024, bytes_accessed=1024, transcendentals=0)


def attend_forward(info, queries, own, other, spans):
    (near, rows, features), far = queries[0].shape, queries[1].shape[0]
    chips, heads = near + far, features // HEAD_DIM
    arrays = (*queries, *own, *other)
    out = jax.ShapeDtypeStruct((chips, rows, features), bf16)
    return pl.pallas_call(
        functools.partial(forward_kernel, spans, heads),
        out_shape=out,
        grid_spec=pltpu.PrefetchScalarGridSpec(
            num_scalar_prefetch=1,
            grid=(chips,),
            in_specs=[near_spec(queries[0].shape), far_spec(queries[1].shape)]
            + [whole_spec(x.shape) for x in arrays[2:]],
            out_specs=block_spec(out.shape),
            scratch_shapes=[
                pltpu.VMEM((heads, rows, HEAD_DIM), f32),
                pltpu.VMEM((heads, rows, 1), f32),
            ],
        ),
        compiler_params=pltpu.CompilerParams(vmem_limit_bytes=32 * 1024 * 1024),
        cost_estimate=light,
    )(info, *arrays)


def attend_backward(info, queries, own, other, grads, tables, spans):
    chips, rows, features = grads.shape
    heads = features // HEAD_DIM
    arrays = (*queries, *own, *other, grads, tables[0], tables[1], *tables)
    square = pltpu.VMEM((chips, heads, rows, 2 * rows), f32)
    pairs = (chips, rows, 2 * HEAD_DIM)
    return pl.pallas_call(
        functools.partial(backward_kernel, spans, heads),
        out_shape=(
            jax.ShapeDtypeStruct(grads.shape, bf16),
            jax.ShapeDtypeStruct(pairs, f32),
            jax.ShapeDtypeStruct(pairs, bf16),
        ),
        grid_spec=pltpu.PrefetchScalarGridSpec(
            num_scalar_prefetch=1,
            grid=(chips,),
            in_specs=[near_spec(queries[0].shape), far_spec(queries[1].shape)]
            + [whole_spec(x.shape) for x in arrays[2:6]]
            + [block_spec(x.shape) for x in arrays[6:9]]
            + [whole_spec(x.shape) for x in arrays[9:]],
            out_specs=(block_spec(grads.shape), whole_spec(pairs), whole_spec(pairs)),
            scratch_shapes=[
                pltpu.VMEM((chips, 2 * rows, HEAD_DIM), f32),
                pltpu.VMEM((chips, 2 * rows, HEAD_DIM), f32),
                square,
                square,
                square,
                pltpu.VMEM((heads, rows, 1), f32),
                pltpu.VMEM((heads, rows, 1), f32),
                pltpu.VMEM((heads, rows, HEAD_DIM), f32),
            ],
        ),
        compiler_params=pltpu.CompilerParams(vmem_limit_bytes=48 * 1024 * 1024),
        cost_estimate=light,
    )(info, *arrays)


def row_call(kernel, grid, ins, outs, *arrays):
    return pl.pallas_call(
        kernel,
        out_shape=tuple(out[0] for out in outs),
        grid=(grid,),
        in_specs=[pl.BlockSpec(*spec) for spec in ins],
        out_specs=tuple(pl.BlockSpec(*out[1:]) for out in outs),
        compiler_params=pltpu.CompilerParams(vmem_limit_bytes=40 * 1024 * 1024),
        cost_estimate=light,
    )(*arrays)


def add_rows(ref, rows):
    @pl.when(pl.program_id(0) == 0)
    def _():
        ref[...] = jnp.zeros_like(ref)

    ref[...] += jnp.sum(rows, axis=0, keepdims=True)


def summed(refs):
    return sum(ref[...].astype(f32) for ref in refs)


def project_kernel(heads, x_ref, gain_ref, w_ref, cos_ref, sin_ref, hidden_ref, q_ref, kv_ref):
    values = x_ref[...].astype(f32)
    hidden = (values * inverse_root(values) * gain_ref[0:1]).astype(bf16)
    hidden_ref[...] = hidden
    raw = nt(hidden, w_ref[...])
    cosine, sine = cos_ref[...], sin_ref[...]
    for h in range(heads + 1):
        start = h * HEAD_DIM
        first, second = raw[:, start : start + HALF], raw[:, start + HALF : start + HEAD_DIM]
        turned = first * cosine - second * sine, second * cosine + first * sine
        if h < heads:
            q_ref[:, start : start + HALF] = (turned[0] * query_scale).astype(bf16)
            q_ref[:, start + HALF : start + HEAD_DIM] = (turned[1] * query_scale).astype(bf16)
        else:
            kv_ref[:, :HALF] = turned[0].astype(bf16)
            kv_ref[:, HALF:HEAD_DIM] = turned[1].astype(bf16)
    kv_ref[:, HEAD_DIM:] = raw[:, (heads + 1) * HEAD_DIM :].astype(bf16)


def project(tokens, gains, weight, cosine, sine, rows):
    m, width = tokens.shape
    features = weight.shape[0] - 2 * HEAD_DIM
    whole = lambda i: (0, 0)
    block = lambda i: (i, 0)
    return row_call(
        functools.partial(project_kernel, features // HEAD_DIM),
        m // rows,
        [
            ((rows, width), block),
            (gains.shape, whole),
            (weight.shape, whole),
            ((rows, HALF), block),
            ((rows, HALF), block),
        ],
        [
            (jax.ShapeDtypeStruct((m, n), bf16), (rows, n), block)
            for n in (width, features, 2 * HEAD_DIM)
        ],
        tokens,
        gains,
        weight,
        cosine,
        sine,
    )


def project_back_kernel(dq_ref, own_ref, got_ref, w_ref, near_ref, far_ref, *outs):
    grad_ref, back_ref, inbound_ref = outs
    pairs = (own_ref[...] + got_ref[...].astype(f32)).astype(bf16)
    back = jnp.concatenate([dq_ref[...], pairs], axis=1)
    back_ref[...] = back
    grad = nn(back, w_ref[...])
    grad_ref[...] = grad.astype(bf16)
    values = jnp.where(pl.program_id(0) < 2, near_ref[...], far_ref[...]).astype(f32)
    add_rows(inbound_ref, grad * (values * inverse_root(values)))


def project_back(query_back, own, got, weight, near, far, rows):
    m, features = query_back.shape
    count, width = weight.shape
    block = lambda i: (i, 0)
    whole = lambda i: (0, 0)
    pairs = ((rows, 2 * HEAD_DIM), block)
    return row_call(
        project_back_kernel,
        m // rows,
        [
            ((rows, features), block),
            pairs,
            pairs,
            (weight.shape, whole),
            ((rows, width), lambda i: (jnp.minimum(i, 1), 0)),
            ((rows, width), lambda i: (jnp.maximum(i - 2, 0), 0)),
        ],
        [
            (jax.ShapeDtypeStruct((m, width), bf16), (rows, width), block),
            (jax.ShapeDtypeStruct((m, count), bf16), (rows, count), block),
            (jax.ShapeDtypeStruct((1, width), f32), (1, width), whole),
        ],
        query_back,
        own,
        got,
        weight,
        near,
        far,
    )


def branch_kernel(p_ref, l_ref, r_ref, own_ref, gain_ref, branch_ref, middle_ref, hidden_ref):
    branch = summed((p_ref, l_ref, r_ref))
    branch_ref[...] = branch
    middle = own_ref[...].astype(f32) + branch * inverse_root(branch) * gain_ref[1:2]
    middle_ref[...] = middle
    hidden_ref[...] = (middle * inverse_root(middle) * gain_ref[2:3]).astype(bf16)


def feed_kernel(p_ref, l_ref, r_ref, middle_ref, cot_ref, gain_ref, out_ref, low_ref, term_ref):
    feed = summed((p_ref, l_ref, r_ref))
    root = inverse_root(feed)
    normed = feed * root
    gain = gain_ref[3:4]
    upstream = cot_ref[...].astype(f32)
    out_ref[...] = (middle_ref[...] + normed * gain).astype(bf16)
    low_ref[...] = norm_backward(normed, root, gain, upstream).astype(bf16)
    add_rows(term_ref, upstream * normed)


def feed_back_norm_kernel(p_ref, l_ref, r_ref, middle_ref, branch_ref, cot_ref, gain_ref, *outs):
    grad_ref, low_ref, prefeed_ref, attended_ref = outs
    grad = summed((p_ref, l_ref, r_ref))
    middle = middle_ref[...]
    root = inverse_root(middle)
    normed = middle * root
    add_rows(prefeed_ref, grad * normed)
    middle_grad = cot_ref[...].astype(f32) + norm_backward(normed, root, gain_ref[2:3], grad)
    grad_ref[...] = middle_grad
    branch = branch_ref[...]
    root = inverse_root(branch)
    normed = branch * root
    add_rows(attended_ref, middle_grad * normed)
    low_ref[...] = norm_backward(normed, root, gain_ref[1:2], middle_grad).astype(bf16)


def norm_call(kernel, terms, arrays, gains, sequence, outs):
    rows, width = terms[1].shape
    tile = rows // 2
    block = ((tile, width), lambda i: (i, 0))
    one = ((None, tile, width), lambda i: (sequence, i, 0))
    whole = lambda i: (0, 0)
    return row_call(
        kernel,
        2,
        [block] * 3 + [one if x.ndim == 3 else block for x in arrays] + [(gains.shape, whole)],
        [
            (jax.ShapeDtypeStruct((1, width), f32), (1, width), whole)
            if kind is None
            else (jax.ShapeDtypeStruct((rows, width), kind), *block)
            for kind in outs
        ],
        *terms,
        *arrays,
        gains,
    )


def gate_up_kernel(h_ref, gate_ref, up_ref, product_ref, gelu_ref, slope_ref):
    gate = nt(h_ref[...], gate_ref[...])
    up = nt(h_ref[...], up_ref[...])
    square = gate * gate
    tanh = jnp.tanh(gate * (gelu_a + (gelu_a * gelu_b) * square))
    half = 0.5 + 0.5 * tanh
    gelu = gate * half
    slope = half + gate * (0.5 - 0.5 * tanh * tanh) * (gelu_a + (3.0 * gelu_a * gelu_b) * square)
    product_ref[...] = (gelu * up).astype(bf16)
    gelu_ref[...] = gelu.astype(bf16)
    slope_ref[...] = (up * slope).astype(bf16)


def gate_up(hidden, gate_w, up_w):
    m, width = hidden.shape
    n = gate_w.shape[0]
    tile = next(t for t in (768, 384, 256, 128) if n % t == 0)
    weight_spec = pl.BlockSpec((tile, width), lambda i: (i, 0))
    out_spec = pl.BlockSpec((m, tile), lambda i: (0, i))
    return pl.pallas_call(
        gate_up_kernel,
        out_shape=(jax.ShapeDtypeStruct((m, n), bf16),) * 3,
        grid=(n // tile,),
        in_specs=[pl.BlockSpec((m, width), lambda i: (0, 0)), weight_spec, weight_spec],
        out_specs=(out_spec,) * 3,
        compiler_params=pltpu.CompilerParams(vmem_limit_bytes=56 * 1024 * 1024),
        cost_estimate=light,
    )(hidden, gate_w, up_w)


def mix_kernel(*refs):
    count = len(refs) // 2
    out = sum(nn(refs[i][...], refs[count + i][...]) for i in range(count))
    refs[-1][...] = out.astype(bf16)


def mix(lefts, weights):
    m, depth = lefts[0].shape
    n = weights[0].shape[1]
    tile = next(t for t in (768, 384, 256, 128) if n % t == 0)
    return pl.pallas_call(
        mix_kernel,
        out_shape=jax.ShapeDtypeStruct((m, n), bf16),
        grid=(n // tile,),
        in_specs=[pl.BlockSpec((m, depth), lambda i: (0, 0))] * len(lefts)
        + [pl.BlockSpec((depth, tile), lambda i: (0, i))] * len(weights),
        out_specs=pl.BlockSpec((m, tile), lambda i: (0, i)),
        compiler_params=pltpu.CompilerParams(vmem_limit_bytes=56 * 1024 * 1024),
        cost_estimate=light,
    )(*lefts, *weights)


def feed_back_kernel(low_ref, down_ref, gelu_ref, slope_ref, gate_back_ref, up_back_ref):
    grad = nt(low_ref[...], down_ref[...])
    gate_back_ref[...] = (grad * slope_ref[...].astype(f32)).astype(bf16)
    up_back_ref[...] = (grad * gelu_ref[...].astype(f32)).astype(bf16)


def feed_back(low, down_w, gelu, slope):
    m, width = low.shape
    n = down_w.shape[0]
    tile = next(t for t in (768, 384, 256, 128) if n % t == 0)
    spec = pl.BlockSpec((m, tile), lambda i: (0, i))
    return pl.pallas_call(
        feed_back_kernel,
        out_shape=(jax.ShapeDtypeStruct((m, n), bf16),) * 2,
        grid=(n // tile,),
        in_specs=[
            pl.BlockSpec((m, width), lambda i: (0, 0)),
            pl.BlockSpec((tile, width), lambda i: (i, 0)),
            spec,
            spec,
        ],
        out_specs=(spec,) * 2,
        compiler_params=pltpu.CompilerParams(vmem_limit_bytes=56 * 1024 * 1024),
        cost_estimate=light,
    )(low, down_w, gelu, slope)


def on_device(
    tokens,
    span_start,
    span_len,
    query_weight,
    key_weight,
    value_weight,
    output_weight,
    gate_weight,
    up_weight,
    down_weight,
    inbound_gain,
    attended_gain,
    prefeed_gain,
    postfeed_gain,
    cotangent,
):
    seq_count, rows, width = tokens.shape
    size = lax.axis_size("ctx")
    index = lax.axis_index("ctx")
    line = Line(size, index)
    chips, z, c = line.chips, line.z, line.c
    spans = span_start.shape[1]
    group = size // KV_HEADS
    member = index % group
    every = chips * rows

    def pair_rows(block):
        other = line.swap(block)
        return jnp.concatenate([jnp.where(c == 0, block, other), jnp.where(c == 0, other, block)])

    def shifted(block, k):
        pairs = [(i, i - i % group + (i % group + k) % group) for i in range(size)]
        return lax.ppermute(block, "ctx", pairs)

    def group_rows(block):
        if group == 2:
            return pair_rows(block)
        count = block.shape[0]
        out = jnp.zeros((group * count, width), block.dtype)
        out = lax.dynamic_update_slice(out, block, (member * count, 0))
        for k in range(1, group):
            place = lax.rem(member + group - k, group) * count
            out = lax.dynamic_update_slice(out, shifted(block, k), (place, 0))
        return out

    def group_sum(grad):
        count = grad.shape[0] // group
        own = lax.dynamic_slice(grad, (member * count, 0), (count, width)).astype(f32)
        for k in range(1, group):
            place = lax.rem(member + k, group) * count
            sent = lax.dynamic_slice(grad, (place, 0), (count, width))
            own = own + shifted(sent.astype(bf16), k).astype(f32)
        return own

    def pair_sum(grad):
        count = grad.shape[0] // 2
        own = lax.dynamic_slice(grad, (c * count, 0), (count, width)).astype(f32)
        sent = lax.dynamic_slice(grad, ((1 - c) * count, 0), (count, width))
        return own + line.swap(sent.astype(bf16)).astype(f32)

    def both_rows(block):
        return jnp.concatenate([block, line.swap(block)])

    count = inbound_gain.shape[0]
    pad = 16
    gains_own = jnp.concatenate([inbound_gain, attended_gain, prefeed_gain, postfeed_gain])
    gains_rows = jnp.pad(gains_own[None, :], ((0, pad - 1), (0, width - 4 * count)))

    query_width = 2 * output_weight.shape[0]
    heads = query_width // HEAD_DIM

    table = jnp.stack(line.table()).astype(jnp.int32)
    places = (
        table[:, None] * (2 * rows) + c * rows + jnp.arange(rows, dtype=jnp.int32)[None, :]
    ).reshape(every)
    inverse = rope_base ** (-(jnp.arange(HALF, dtype=f32) * 2.0 / HEAD_DIM))

    def turns(places):
        angles = places.astype(f32)[:, None] * inverse[None, :]
        return jnp.cos(angles), jnp.sin(angles)

    cosine, sine = turns(places)
    tables = [
        t.reshape(chips, rows, HALF)
        for t in (cosine, sine) + turns(places + jnp.where(c == 0, rows, -rows))
    ]

    def split(block_rows):
        return [
            block_rows[k * rows : (k + 1) * rows] for k in range(block_rows.shape[0] // rows)
        ]

    def join(blocks):
        return jnp.concatenate(blocks)

    infos = [
        jnp.concatenate(
            [c[None], span_start[s], span_start[s] + span_len[s], table]
        ).astype(jnp.int32)
        for s in range(seq_count)
    ]

    class Sequence:
        def __init__(self, s):
            self.s = s
            self.own = tokens[s]

        def project(self, places, *blocks):
            count = len(blocks)
            merged = join(blocks)
            some = slice(places.start * rows, places.stop * rows)
            hidden, queries, pairs = project(
                merged, gain, qkv_weight, cosine[some], sine[some], rows
            )
            pairs = pairs.reshape(count, rows, 2 * HEAD_DIM)
            queries = queries.reshape(count, rows, query_width)
            return merged, hidden, queries, pairs, line.swap(pairs)

        def attend(self, *halves):
            queries, own, other = halves[0::3], halves[1::3], halves[2::3]
            attended = attend_forward(infos[self.s], queries, own, other, spans)
            attended = attended.reshape(every, query_width)
            return nn(attended, out_weight).astype(bf16), attended, queries, own, other

        def after_branch(self, terms):
            self.branch, self.middle, hidden = norm_call(
                branch_kernel, terms, (tokens,), gain, self.s, (f32, f32, bf16)
            )
            return hidden

        def feed(self, *blocks):
            hidden_ff = join(blocks)
            return (hidden_ff,) + tuple(gate_up(hidden_ff, gate_rows, up_rows))

        def feed_down(self, product):
            return (mix([product], [down_rows]),)

        def after_feed(self, terms):
            self.output, low, self.postfeed_term = norm_call(
                feed_kernel, terms, (self.middle, cotangent), gain, self.s, (bf16, bf16, None)
            )
            return low

        def feed_back(self, gelu, slope, *blocks):
            feed_low = join(blocks)
            return (feed_low,) + tuple(feed_back(feed_low, down_rows, gelu, slope))

        def feed_in(self, gate_back, up_back):
            return (mix([gate_back, up_back], [gate_rows, up_rows]),)

        def after_feed_back(self, terms):
            self.middle_grad, low, self.prefeed_term, self.attended_term = norm_call(
                feed_back_norm_kernel,
                terms,
                (self.middle, self.branch, cotangent),
                gain,
                self.s,
                (f32, bf16, None, None),
            )
            return low

        def attend_back(self, *blocks):
            branch_low = join(blocks)
            mixed = nt(branch_low, out_weight).astype(bf16).reshape(chips, rows, query_width)
            return (branch_low,) + tuple(
                attend_backward(
                    infos[self.s], self.queries, self.pairs, self.others, mixed, tables, spans
                )
            )

        def project_back(self, near_tokens, far_tokens, query_back, own, other):
            got = line.swap(other)
            return project_back(
                query_back.reshape(every, query_width),
                own.reshape(every, 2 * HEAD_DIM),
                got.reshape(every, 2 * HEAD_DIM),
                qkv_weight,
                near_tokens,
                far_tokens,
                rows,
            )

        def after_project_back(self, terms):
            grad = total(terms)
            values = self.own.astype(f32)
            root = inverse_root(values)
            return (self.middle_grad + norm_backward(values * root, root, gain[0:1], grad)).astype(
                bf16
            )

    def weight_grad(left_count, *pieces):
        return (tn(join(pieces[:left_count]), join(pieces[left_count:])).astype(bf16),)

    data = lax.axis_size("dp")

    def data_sum(values, order):
        groups = [[(i + order) % data for i in range(data)]]
        return lax.psum(values, "dp", axis_index_groups=groups)

    near, far = slice(0, 2), slice(2, chips)

    a, b = (Sequence(s) for s in range(seq_count))

    ex = Exchange(line, jnp.concatenate([a.own, gains_rows]), sums=False)
    def attention_weights(query_w, key_w, value_w):
        return jnp.concatenate([pair_rows(query_w), group_rows(key_w), group_rows(value_w)])

    ex.step()
    qkv_weight = ex.step(attention_weights, (query_weight, key_weight, value_weight))
    out_weight, gate_rows = ex.step(
        lambda out_w, gate_w: (pair_rows(out_w), both_rows(gate_w)), (output_weight, gate_weight)
    )
    for _ in range(chips - 4):
        ex.step()
    blocks = ex.near() + ex.far()
    gain = jnp.stack([block[rows, : 4 * count] for block in blocks])
    gain_other = line.swap(gain)
    gain = jnp.stack(
        [jnp.where(c == 0, gain, gain_other), jnp.where(c == 0, gain_other, gain)], axis=1
    ).reshape(chips, 8 * count)
    gain = line.exchanged([gain[k] for k in range(chips)])
    gain = jnp.roll(jnp.stack(gain), z, axis=0).reshape(chips, 2, 4, count)
    gain = gain.transpose(2, 0, 1, 3).reshape(4, width).astype(f32)

    def a_attention(*blocks):
        halves = [a.project(near, *blocks[near]), a.project(far, *blocks[far])]
        out, *kept = a.attend(*halves[0][2:], *halves[1][2:])
        return out, kept, [[half[i] for half in halves] for i in range(2)]

    ex = Exchange(line, b.own)
    out, (a.attended, a.queries, a.pairs, a.others), (a.tokens, a.hidden) = ex.step(
        a_attention, [block[:rows] for block in blocks]
    )
    ex.give(out)

    def b_project_near(up_w, *blocks):
        return b.project(near, *blocks), both_rows(up_w)

    b_near, up_rows = ex.step(b_project_near, [up_weight] + ex.near())
    down_rows = ex.step(both_rows, (down_weight,))
    for _ in range(chips - 4):
        ex.step()
    b_far = ex.step(functools.partial(b.project, far), ex.far())
    b.tokens, b.hidden = ([b_near[i], b_far[i]] for i in range(2))
    hidden_a = a.after_branch(ex.terms())

    def feed_phase(x, own, first, inputs):
        ex = Exchange(line, own)
        firsts = ex.step(first, inputs)
        yield firsts, ex
        hidden, product, gelu, slope = ex.step(x.feed, ex.near())
        (out,) = ex.step(x.feed_down, (product,))
        for _ in range(chips - 4):
            ex.step()
        x.out_near = out
        lasts = ex.step(x.feed, ex.far())
        x.hidden_ff, x.product, x.gelu, x.slope = (
            [u, v] for u, v in zip((hidden, product, gelu, slope), lasts)
        )
        yield lasts, ex

    steps = feed_phase(a, hidden_a, b.attend, b_near[2:] + b_far[2:])
    (out, b.attended, b.queries, b.pairs, b.others), ex = next(steps)
    ex.give(out)
    next(steps)
    hidden_b = b.after_branch(ex.terms())

    steps = feed_phase(b, hidden_b, a.feed_down, (a.product[1],))
    (out,), ex = next(steps)
    ex.give(a.out_near, out)
    next(steps)
    low_a = a.after_feed(ex.terms())

    def back_phase(x, own, first, inputs):
        ex = Exchange(line, own)
        firsts = ex.step(first, inputs)
        yield firsts, ex
        low, gate_back, up_back = ex.step(
            functools.partial(x.feed_back, x.gelu[0], x.slope[0]), ex.near()
        )
        (x.out_near,) = ex.step(x.feed_in, (gate_back, up_back))
        for _ in range(chips - 4):
            ex.step()

        lasts = ex.step(functools.partial(x.feed_back, x.gelu[1], x.slope[1]), ex.far())
        x.feed_low, x.gate_back, x.up_back = (
            [u, v] for u, v in zip((low, gate_back, up_back), lasts)
        )
        yield lasts, ex

    steps = back_phase(a, low_a, b.feed_down, (b.product[1],))
    (out,), ex = next(steps)
    ex.give(b.out_near, out)
    next(steps)
    low_b = b.after_feed(ex.terms())

    def grad_part(left, right):
        return tn(join(left), join(right)).astype(bf16)

    def grad_other(left, right, part):
        count = left.shape[1] // 2
        return (tn(left[:, count:], right) + part[count:].astype(f32)).astype(bf16)

    def grad_own(left, right, part, other):
        count = left.shape[1] // 2
        got = line.swap(other).astype(f32)
        return (tn(left[:, :count], right) + part[:count].astype(f32) + got).astype(bf16)

    ex = Exchange(line, low_b)
    (out,) = ex.step(a.feed_in, (a.gate_back[1], a.up_back[1]))
    ex.give(a.out_near, out)

    def part_work(*pieces):
        return grad_part(pieces[:2], pieces[2:4]), grad_part(pieces[4:6], pieces[6:])

    part_down, part_gate = ex.step(
        part_work, a.product + a.feed_low + a.gate_back + a.hidden_ff
    )

    def part_more(*pieces):
        return (grad_part(pieces[:2], pieces[2:4]),) + tuple(
            join(pieces[i : i + 2]) for i in range(4, 12, 2)
        )

    part_up, b_gelu, b_slope, b_product, b_hidden_ff = ex.step(
        part_more, a.up_back + a.hidden_ff + b.gelu + b.slope + b.product + b.hidden_ff
    )
    for _ in range(chips - 4):
        ex.step()

    def b_feed_back(part, *blocks):
        low, gate_back, up_back = b.feed_back(b_gelu, b_slope, *blocks)
        return low, gate_back, up_back, grad_other(b_product, low, part)

    b_low, b_gate_back, b_up_back, down_other = ex.step(
        b_feed_back, [part_down] + ex.near() + ex.far()
    )
    branch_a = a.after_feed_back(ex.terms())

    def b_feed_in(gate_back, up_back, down_other):
        return b.feed_in(gate_back, up_back) + (
            grad_other(gate_back, b_hidden_ff, part_gate),
            grad_own(b_product, b_low, part_down, down_other),
        )

    ex = Exchange(line, branch_a)
    out, gate_other, down_grad = ex.step(b_feed_in, (b_gate_back, b_up_back, down_other))
    ex.give(out)

    def gate_work(gate_back, up_back, gate_other):
        return (
            grad_other(up_back, b_hidden_ff, part_up),
            grad_own(gate_back, b_hidden_ff, part_gate, gate_other),
        )

    up_other, gate_grad = ex.step(gate_work, (b_gate_back, b_up_back, gate_other))

    def up_work(up_back, up_other):
        return (grad_own(up_back, b_hidden_ff, part_up, up_other),)

    (up_grad,) = ex.step(up_work, (b_up_back, up_other))
    early_sums = data_sum((down_grad, gate_grad), 0)
    up_sum = data_sum(up_grad, 1)
    for _ in range(chips - 4):
        ex.step()
    a.branch_low, *a_sums = ex.step(a.attend_back, ex.near() + ex.far())
    branch_b = b.after_feed_back(ex.terms())

    ex = Exchange(line, branch_b)
    out, a.back, a.inbound_term = ex.step(a.project_back, a.tokens + a_sums)
    ex.give(out)
    ex.step()
    ex.step()
    for _ in range(chips - 4):
        ex.step()
    b.branch_low, *b_sums = ex.step(b.attend_back, ex.near() + ex.far())
    tokens_grad_a = a.after_project_back(ex.terms())

    grad, b.back, b.inbound_term = b.project_back(*b.tokens, *b_sums)
    gain_terms = jnp.concatenate(
        [
            a.inbound_term + b.inbound_term,
            a.attended_term + b.attended_term,
            a.prefeed_term + b.prefeed_term,
            a.postfeed_term + b.postfeed_term,
        ]
    ).astype(bf16)
    gain_terms = gain_terms.reshape(4, chips, 2, count).transpose(1, 2, 0, 3)
    gain_terms = jnp.roll(gain_terms.reshape(chips, 1, 8 * count), -z, axis=0)
    gain_terms = jnp.stack(line.exchanged([gain_terms[k] for k in range(chips)]))
    gain_terms = jnp.pad(gain_terms, ((0, 0), (0, pad - 1), (0, width - 8 * count)))
    ex = Exchange(line)
    ex.parts = [jnp.concatenate([part, gain_terms[k]]) for k, part in enumerate(split(grad))]
    ex.first = ex.parts[0]

    def attention_grads(back_a, back_b):
        return weight_grad(2, back_a, back_b, *a.hidden, *b.hidden) + weight_grad(
            2, a.attended, b.attended, a.branch_low, b.branch_low
        )

    def attention_sums(qkv_grad, output_grad):
        return tuple(
            value.astype(bf16)
            for value in (
                pair_sum(qkv_grad[:query_width]),
                group_sum(qkv_grad[query_width : query_width + HEAD_DIM]),
                group_sum(qkv_grad[query_width + HEAD_DIM :]),
                pair_sum(output_grad),
            )
        )

    late = ex.step(attention_grads, (a.back, b.back), held=early_sums)
    down_sum, gate_sum = ex.held

    def sums_work(down_sum, gate_sum, *late):
        return attention_sums(*late), down_sum.astype(f32), gate_sum.astype(f32)

    late, down_sum, gate_sum = ex.step(sums_work, (down_sum, gate_sum, *late))
    for _ in range(chips - 4):
        ex.step()
    ex.step(held=(up_sum,))
    (up_sum,) = ex.held
    late_sums = data_sum(late, 2)
    grad = total(ex.terms())
    tokens_grad_b = b.after_project_back([grad[:rows]])

    row = grad[rows, : 8 * count].reshape(2, 4, count)
    mine = jnp.where(c == 0, row[0], row[1])
    other = jnp.where(c == 0, row[1], row[0])
    gain_sums = lax.psum(mine + line.swap(other.astype(bf16)).astype(f32), "dp")

    done = tied(
        jnp.stack([a.output, b.output]),
        jnp.stack([tokens_grad_a, tokens_grad_b]),
        gate_sum,
        up_sum.astype(f32),
        down_sum,
        gain_sums,
        late_sums,
    )
    late_sums = [value.astype(f32) for value in done[6]]
    return (*done[:2], *late_sums, *done[2:5], *done[5])


def solution(mesh):
    rows = P("ctx", None)
    gain = P("ctx")
    tokens = P("dp", "ctx", None)
    spans = P("dp", None)
    return jax.shard_map(
        on_device,
        mesh=mesh,
        in_specs=(tokens, spans, spans) + (rows,) * 7 + (gain,) * 4 + (tokens,),
        out_specs=(tokens, tokens) + (rows,) * 7 + (gain,) * 4,
        check_vma=False,
    )
```

time: 1280 us -> 1230 us (0.961)
  Pallas kernels: 144 us -> 282 us
  matrix products: 216 us -> 128 us
  other arithmetic: 241 us -> 163 us
  local copies, waits for them, and re-layouts: 113 us -> 92.9 us
    pallas_call x0 -> x19, Pallas kernels: none -> 137 us  [the longest x7 86.3 us: mix(): pl.pallas_call(mix_kernel, out_shape=jax.ShapeDtypeStruct((m, n), bf16),...]
    dot_general x16 -> x2, matrix products: 114 us -> 3.99 us  [nn(): lax.dot_general(left_side, right_side, (((1,), (0,)), ((), ())), preferre...]
    convert_element_type x28 -> x8, other arithmetic: 55 us -> 18.8 us  [the longest x2 10.1 us: sums_work(): return (attention_sums(*late), down_sum.astype(f32), gate_sum.astype(f32))]
    dot_general x5 -> x11, matrix products: 84.8 us -> 118 us  [tn(): lax.dot_general(left_side, right_side, (((0,), (0,)), ((), ())), preferre...]
    psum x3, waiting for transfers between devices: 165 us -> 134 us  [data_sum(): return lax.psum(values, 'dp', axis_index_groups=groups)]
    slice x24 -> x2, local copies, waits for them, and re-layouts: 22 us -> 2.19 us  [the longest x1 1.31 us: after_project_back(): gain[0:1]]
    ppermute x34, waiting for transfers between devices: 85.2 us -> 104 us  [right(): return lax.ppermute(block, 'ctx', self.pairs(1, low, high))]
    unnamed x457 -> x423, local copies, waits for them, and re-layouts: 52.6 us -> 68.6 us
  transfers between devices with their start and end apart: 93 -> 93, of which waited for: 41 -> 48; matrix products, arithmetic and copies ran while one was open for 34% -> 22% of each run, Pallas kernels for 11% -> 22%
where the time goes in v4:
time: 1230 us; the launch traced here: 1220 us
  waiting for transfers between devices  357 us (29%)
  Pallas kernels  282 us (23%)
  starting transfers between devices  174 us (14%)
  other arithmetic  163 us (13%)
  matrix products  128 us (10%)
  local copies, waits for them, and re-layouts  92.9 us (8%)
  between operations  16.7 us (1%)
    psum x3, waiting for transfers between devices, data_sum(): return lax.psum(values, 'dp', axis_index_groups=groups)  134 us
    ppermute x34, starting transfers between devices, right(): return lax.ppermute(block, 'ctx', self.pairs(1, low, high))  124 us
    dot_general x11, matrix products, tn(): lax.dot_general(left_side, right_side, (((0,), (0,)), ((), ())), preferre...  118 us
    ppermute x34, waiting for transfers between devices, right(): return lax.ppermute(block, 'ctx', self.pairs(1, low, high))  104 us
    ppermute x34, waiting for transfers between devices, left(): return lax.ppermute(block, 'ctx', self.pairs(-1, n - high, n - low))  104 us
    pallas_call x7, Pallas kernels, mix(): pl.pallas_call(mix_kernel, out_shape=jax.ShapeDtypeStruct((m, n), bf16),...  86.3 us
    unnamed x423, local copies, waits for them, and re-layouts  68.6 us
    pallas_call x4, Pallas kernels, gate_up(): pl.pallas_call(gate_up_kernel, out_shape=(jax.ShapeDtypeStruct((m, n), bf...  57.7 us
  transfers between devices with their start and end apart: 93, of which 48 were waited for; matrix products, arithmetic and copies ran while one was open for 22% of the time, Pallas kernels for 22%

profile of v4, /device:TPU:0, one launch (start us, length us, event | category | flops | bytes accessed | tf_op | source)
XLA Modules:
  0.0 1223.4 jit_solution(12024622206441095560)
XLA Ops:
  16.4 19.1 %collective-permute-done = bf16[208,2304]{1,0:T(8,128)(2,1)S(1)} collective-permute-done((bf16[208,2304]{1,0:T(8,128)(2,1)S(1)}, bf16[208,2304]{1,0:T(8,128)(2,1)S(1)}, u32[]{:S(2)}, u32[]{:S(2)}) %collective-permute-start) | collective-permute-done | bytes 958496 | tf_op jit(solution)/shard_map/ppermute | solution.py:69
  49.1 21.3 %collective-permute-done.3 = bf16[208,2304]{1,0:T(8,128)(2,1)} collective-permute-done((bf16[208,2304]{1,0:T(8,128)(2,1)}, bf16[208,2304]{1,0:T(8,128)(2,1)}, u32[]{:S(2)}, u32[]{:S(2)}) %collective-permute-start.3) | collective-permute-done | bytes 958496 | tf_op jit(solution)/shard_map/ppermute | solution.py:73
  82.6 9.5 pad_maximum_fusion.gate_ref.refs_2_
  92.1 9.3 collective-permute-done.8
  136.7 8.4 shard_map.248
  166.2 10.0 pad_maximum_fusion.1.up_ref.refs_3_
  190.6 12.1 pad_maximum_fusion.2.refs_1_.down_ref
  220.7 9.5 collective-permute-done.23.l_ref
  245.7 7.5 shard_map.252
  273.3 14.4 %shard_map.253 = (bf16[384,2304]{1,0:T(8,128)(2,1)}, bf16[384,2304]{1,0:T(8,128)(2,1)}, bf16[384,2304]{1,0:T(8,128)(2,1)}) custom-call(bf16[384,2304]{1,0:T(8,128)(2,1)} %constant_dynamic-update-slice_fusion.8.h_ref, bf16[2304,2304]{1,0:T(8,128)(2,1)} %pad_maximum_fusion.gate_ref.refs_2_, bf16[2304,2304]{1,0:T(8,128)(2,1)} %pad_maximum_fusion.1.up_ref.refs_3_), custom_call_target="tpu_custom_call" | custom-call | flops 1024 | bytes 1024 | tf_op jit(solution)/shard_map/pallas_call | solution.py:580
  297.3 8.7 shard_map.254.p_ref
  306.0 6.3 collective-permute-done.30
  325.1 14.3 %shard_map.255 = (bf16[384,2304]{1,0:T(8,128)(2,1)}, bf16[384,2304]{1,0:T(8,128)(2,1)}, bf16[384,2304]{1,0:T(8,128)(2,1)}) custom-call(bf16[384,2304]{1,0:T(8,128)(2,1)} %constant_dynamic-update-slice_fusion.10.h_ref, bf16[2304,2304]{1,0:T(8,128)(2,1)} %pad_maximum_fusion.gate_ref.refs_2_, bf16[2304,2304]{1,0:T(8,128)(2,1)} %pad_maximum_fusion.1.up_ref.refs_3_), custom_call_target="tpu_custom_call" | custom-call | flops 1024 | bytes 1024 | tf_op jit(solution)/shard_map/pallas_call | solution.py:580
  351.8 8.7 shard_map.257
  377.4 14.5 %shard_map.258 = (bf16[384,2304]{1,0:T(8,128)(2,1)}, bf16[384,2304]{1,0:T(8,128)(2,1)}, bf16[384,2304]{1,0:T(8,128)(2,1)}) custom-call(bf16[384,2304]{1,0:T(8,128)(2,1)} %copy-done.120, bf16[2304,2304]{1,0:T(8,128)(2,1)} %pad_maximum_fusion.gate_ref.refs_2_, bf16[2304,2304]{1,0:T(8,128)(2,1)} %pad_maximum_fusion.1.up_ref.refs_3_), custom_call_target="tpu_custom_call" | custom-call | flops 1024 | bytes 1024 | tf_op jit(solution)/shard_map/pallas_call | solution.py:580
  401.1 8.8 shard_map.259.p_ref
  426.3 14.5 %shard_map.260 = (bf16[384,2304]{1,0:T(8,128)(2,1)}, bf16[384,2304]{1,0:T(8,128)(2,1)}, bf16[384,2304]{1,0:T(8,128)(2,1)}) custom-call(bf16[384,2304]{1,0:T(8,128)(2,1)} %constant_dynamic-update-slice_fusion.14.h_ref, bf16[2304,2304]{1,0:T(8,128)(2,1)} %pad_maximum_fusion.gate_ref.refs_2_, bf16[2304,2304]{1,0:T(8,128)(2,1)} %pad_maximum_fusion.1.up_ref.refs_3_), custom_call_target="tpu_custom_call" | custom-call | flops 1024 | bytes 1024 | tf_op jit(solution)/shard_map/pallas_call | solution.py:580
  451.3 8.7 shard_map.262
  476.1 10.7 shard_map.263
  496.3 14.1 %shard_map.264.p_ref = bf16[384,2304]{1,0:T(8,128)(2,1)} custom-call(bf16[384,2304]{1,0:T(8,128)(2,1)} %get-tuple-element.614.refs_0_, bf16[384,2304]{1,0:T(8,128)(2,1)} %get-tuple-element.628.refs_1_, bf16[2304,2304]{1,0:T(8,128)(2,1)} %pad_maximum_fusion.gate_ref.refs_2_, bf16[2304,2304]{1,0:T(8,128)(2,1)} %pad_maximum_fusion.1.up_ref.refs_3_), custom_call_target="tpu_custom_call" | custom-call | flops 1024 | bytes 1024 | tf_op jit(solution)/shard_map/pallas_call | solution.py:601
  523.7 10.7 shard_map.265
  544.9 14.0 %shard_map.267 = bf16[384,2304]{1,0:T(8,128)(2,1)} custom-call(bf16[384,2304]{1,0:T(8,128)(2,1)} %get-tuple-element.615.refs_0_, bf16[384,2304]{1,0:T(8,128)(2,1)} %get-tuple-element.629.refs_1_, bf16[2304,2304]{1,0:T(8,128)(2,1)} %pad_maximum_fusion.gate_ref.refs_2_, bf16[2304,2304]{1,0:T(8,128)(2,1)} %pad_maximum_fusion.1.up_ref.refs_3_), custom_call_target="tpu_custom_call" | custom-call | flops 1024 | bytes 1024 | tf_op jit(solution)/shard_map/pallas_call | solution.py:601
  567.5 12.3 %convolution_convert_fusion.2 = bf16[2304,2304]{1,0:T(8,128)(2,1)} fusion(bf16[384,2304]{1,0:T(8,128)(2,1)S(1)} %copy-done.172, bf16[384,2304]{1,0:T(8,128)(2,1)S(1)} %copy-done.171, bf16[384,2304]{1,0:T(8,128)(2,1)} %constant_dynamic-update-slice_fusion.18.low_ref, bf16[384,2304]{1,0:T(8,128)(2,1)S(1)} %copy-done.131), kind=kOutput, calls=%fused_computation.2 | convolution fusion | flops 8173191168 | bytes 17694720 | tf_op jit(solution)/shard_map/dot_general | solution.py:39
  579.8 13.0 %convolution_convert_fusion.1 = bf16[2304,2304]{1,0:T(8,128)(2,1)} fusion(bf16[384,2304]{1,0:T(8,128)(2,1)S(1)} %copy-done.166, bf16[384,2304]{1,0:T(8,128)(2,1)S(1)} %copy-done.164, bf16[384,2304]{1,0:T(8,128)(2,1)} %constant_dynamic-update-slice_fusion.10.h_ref, bf16[384,2304]{1,0:T(8,128)(2,1)} %constant_dynamic-update-slice_fusion.8.h_ref), kind=kOutput, calls=%fused_computation.1 | convolution fusion | flops 8173191168 | bytes 17694720 | tf_op jit(solution)/shard_map/dot_general | solution.py:39
  606.5 12.9 %convolution_convert_fusion = bf16[2304,2304]{1,0:T(8,128)(2,1)} fusion(bf16[384,2304]{1,0:T(8,128)(2,1)S(1)} %copy-done.165, bf16[384,2304]{1,0:T(8,128)(2,1)S(1)} %copy-done.163, bf16[384,2304]{1,0:T(8,128)(2,1)} %constant_dynamic-update-slice_fusion.10.h_ref, bf16[384,2304]{1,0:T(8,128)(2,1)} %constant_dynamic-update-slice_fusion.8.h_ref), kind=kOutput, calls=%fused_computation | convolution fusion | flops 8173191168 | bytes 17694720 | tf_op jit(solution)/shard_map/dot_general | solution.py:39
  640.2 15.2 %shard_map.268 = (bf16[768,2304]{1,0:T(8,128)(2,1)}, bf16[768,2304]{1,0:T(8,128)(2,1)}) custom-call(bf16[768,2304]{1,0:T(8,128)(2,1)} %constant_dynamic-update-slice_fusion.20.low_ref, bf16[2304,2304]{1,0:T(8,128)(2,1)} %pad_maximum_fusion.2.refs_1_.down_ref, bf16[768,2304]{1,0:T(8,128)(2,1)} %pad_maximum_fusion.3.gelu_ref, ...), custom_call_target="tpu_custom_call" | custom-call | flops 1024 | bytes 1024 | tf_op jit(solution)/shard_map/pallas_call | solution.py:624
  655.4 11.0 fusion.3
  679.9 23.2 %shard_map.270.p_ref = bf16[768,2304]{1,0:T(8,128)(2,1)} custom-call(bf16[768,2304]{1,0:T(8,128)(2,1)} %get-tuple-element.679.refs_0_, bf16[768,2304]{1,0:T(8,128)(2,1)} %get-tuple-element.686.refs_1_, bf16[2304,2304]{1,0:T(8,128)(2,1)} %pad_maximum_fusion.gate_ref.refs_2_, bf16[2304,2304]{1,0:T(8,128)(2,1)} %pad_maximum_fusion.1.up_ref.refs_3_), custom_call_target="tpu_custom_call" | custom-call | flops 1024 | bytes 1024 | tf_op jit(solution)/shard_map/pallas_call | solution.py:601
  703.1 7.5 fusion.4
  710.6 10.5 fusion.5
  724.5 5.8 collective-permute-start.61
  731.8 8.3 fusion.6
  740.1 8.9 fusion.7
  771.8 13.4 %fusion.8 = bf16[1152,2304]{1,0:T(8,128)(2,1)} fusion(bf16[768,2304]{1,0:T(8,128)(2,1)} %pad_maximum_fusion.6, bf16[1152,2304]{1,0:T(8,128)(2,1)} %collective-permute-done.66, bf16[2304,2304]{1,0:T(8,128)(2,1)} %convolution_convert_fusion, bf16[768,2304]{1,0:T(8,128)(2,1)} %get-tuple-element.686.refs_1_), kind=kOutput, calls=%fused_computation.17 | convolution fusion | flops 4090134528 | bytes 21233664 | tf_op jit(solution)/shard_map/dot_general | solution.py:39
  810.8 17.6 %shard_map.271 = (bf16[4,192,512]{2,1,0:T(8,128)(2,1)S(1)}, f32[4,192,512]{2,1,0:T(8,128)}, bf16[4,192,512]{2,1,0:T(8,128)(2,1)S(1)}) custom-call(s32[9]{0:T(128)S(1)} %copy-done.108, bf16[2,192,512]{2,1,0:T(8,128)(2,1)S(1)} %bitcast.103, bf16[2,192,512]{2,1,0:T(8,128)(2,1)S(1)} %bitcast.105, bf16[2,192,512]{2,1,0:T(8,128)(2,1)} %bitcast.18.refs_2_, ...), custom_call_target="tpu_custom_call" | custom-call | flops 1024 | bytes 1024 | tf_op jit(solution)/shard_map/pallas_call | solution.py:361
  845.2 7.7 shard_map.273
  865.6 15.4 %collective-permute-done.72 = bf16[192,2304]{1,0:T(8,128)(2,1)S(1)} collective-permute-done((bf16[192,2304]{1,0:T(8,128)(2,1)S(1)}, bf16[192,2304]{1,0:T(8,128)(2,1)S(1)}, u32[]{:S(2)}, u32[]{:S(2)}) %collective-permute-start.72) | collective-permute-done | bytes 884768 | tf_op jit(solution)/shard_map/ppermute | solution.py:69
  892.1 13.3 %collective-permute-done.74 = bf16[192,2304]{1,0:T(8,128)(2,1)} collective-permute-done((bf16[192,2304]{1,0:T(8,128)(2,1)}, bf16[192,2304]{1,0:T(8,128)(2,1)}, u32[]{:S(2)}, u32[]{:S(2)}) %collective-permute-start.74) | collective-permute-done | bytes 884768 | tf_op jit(solution)/shard_map/ppermute | solution.py:69
  923.4 17.3 %shard_map.274 = (bf16[4,192,512]{2,1,0:T(8,128)(2,1)S(1)}, f32[4,192,512]{2,1,0:T(8,128)}, bf16[4,192,512]{2,1,0:T(8,128)(2,1)}) custom-call(s32[9]{0:T(128)S(1)} %copy-done.106, bf16[2,192,512]{2,1,0:T(8,128)(2,1)S(1)} %bitcast.93, bf16[2,192,512]{2,1,0:T(8,128)(2,1)S(1)} %bitcast.98, bf16[2,192,512]{2,1,0:T(8,128)(2,1)S(1)} %bitcast.96, ...), custom_call_target="tpu_custom_call" | custom-call | flops 1024 | bytes 1024 | tf_op jit(solution)/shard_map/pallas_call | solution.py:361
  942.3 9.2 fusion.24
  951.4 7.9 shard_map.275
  974.5 11.6 fusion.21
  986.2 9.2 collective-permute-done.79
  1025.8 69.8 %all-reduce.8.cloned.1.call-done = bf16[1152,2304]{1,0:T(8,128)(2,1)} async-done(((bf16[1152,2304]{1,0:T(8,128)(2,1)}), bf16[1152,2304]{1,0:T(8,128)(2,1)}) %all-reduce.8.cloned.1.call-update) | async-done | bytes 5308432 | tf_op jit(solution)/shard_map/psum | solution.py:838
  1106.0 7.4 convert_element_type.616
  1113.4 6.4 collective-permute-done.87
  1136.8 9.1 psum.59
  1145.9 63.5 %all-reduce.12.cloned.1.call-done = (bf16[256,2304]{1,0:T(8,128)(2,1)}, bf16[128,2304]{1,0:T(8,128)(2,1)}, bf16[128,2304]{1,0:T(8,128)(2,1)}, bf16[256,2304]{1,0:T(8,128)(2,1)}) async-done(((bf16[256,2304]{1,0:T(8,128)(2,1)}, bf16[128,2304]{1,0:T(8,128)(2,1)}, bf16[128,2304]{1,0:T(8,128)(2,1)}, bf16[256,2304]{1,0:T(8,128)(2,1)}), (bf16[256,2304]{1,0:T(8,128)(2,1)}, bf16[128,2304]{1,0:T(8,128)(2,1)}, ...) | async-done | bytes 3538960 | tf_op jit(solution)/shard_map/psum | solution.py:838
  (754 shorter events, 544.1 us)
Async XLA Ops:
  7.3 962.8 %all-reduce.10.cloned.1.call-start = ((), (), s32[]{:S(2)}) async-start(), calls=%async_computation.1 | async-start | bytes 21233664 | tf_op jit(solution)/shard_map/psum | solution.py:838
  10.1 25.4 %collective-permute-start = (bf16[208,2304]{1,0:T(8,128)(2,1)S(1)}, bf16[208,2304]{1,0:T(8,128)(2,1)S(1)}, u32[]{:S(2)}, u32[]{:S(2)}) collective-permute-start(bf16[208,2304]{1,0:T(8,128)(2,1)S(1)} %fusion.104), channel_id=1, source_target_pairs={{0,2},{1,3},{2,4},{3,5},{4,6},{5,7},{8,10},{9,11},{10,12},{11,13},... | collective-permute-start | bytes 2875400 | tf_op jit(solution)/shard_map/ppermute | solution.py:69
  15.1 24.6 %collective-permute-start.1 = (bf16[208,2304]{1,0:T(8,128)(2,1)S(1)}, bf16[208,2304]{1,0:T(8,128)(2,1)S(1)}, u32[]{:S(2)}, u32[]{:S(2)}) collective-permute-start(bf16[208,2304]{1,0:T(8,128)(2,1)S(1)} %fusion.104), channel_id=1, source_target_pairs={{2,0},{3,1},{4,2},{5,3},{6,4},{7,5},{10,8},{11,9},{12,10},{13,11},... | collective-permute-start | bytes 2875400 | tf_op jit(solution)/shard_map/ppermute | solution.py:73
  42.2 28.2 %collective-permute-start.3 = (bf16[208,2304]{1,0:T(8,128)(2,1)}, bf16[208,2304]{1,0:T(8,128)(2,1)}, u32[]{:S(2)}, u32[]{:S(2)}) collective-permute-start(bf16[208,2304]{1,0:T(8,128)(2,1)} %copy-done.177), channel_id=1, source_target_pairs={{2,0},{3,1},{4,2},{5,3},{10,8},{11,9},{12,10},{13,11},{18,16},{19,... | collective-permute-start | bytes 2875400 | tf_op jit(solution)/shard_map/ppermute | solution.py:73
  76.2 25.3 %collective-permute-start.8 = (bf16[208,2304]{1,0:T(8,128)(2,1)}, bf16[208,2304]{1,0:T(8,128)(2,1)S(1)}, u32[]{:S(2)}, u32[]{:S(2)}) collective-permute-start(bf16[208,2304]{1,0:T(8,128)(2,1)} %collective-permute-done.3), channel_id=1, source_target_pairs={{2,0},{3,1},{10,8},{11,9},{18,16},{19,17},{26,24},{27,25}} | collective-permute-start | bytes 2875400 | tf_op jit(solution)/shard_map/ppermute | solution.py:73
  102.0 45.2 %collective-permute-start.11 = (bf16[192,2304]{1,0:T(8,128)(2,1)}, bf16[192,2304]{1,0:T(8,128)(2,1)}, u32[]{:S(2)}, u32[]{:S(2)}) collective-permute-start(bf16[192,2304]{1,0:T(8,128)(2,1)} %get-tuple-element.452), channel_id=1, source_target_pairs={{0,2},{1,3},{2,4},{3,5},{4,6},{5,7},{8,10},{9,11},{10,12},{11,13},... | collective-permute-start | bytes 2654216 | tf_op jit(solution)/shard_map/ppermute | solution.py:69
  104.6 42.6 %collective-permute-start.12 = (bf16[192,2304]{1,0:T(8,128)(2,1)}, bf16[192,2304]{1,0:T(8,128)(2,1)}, u32[]{:S(2)}, u32[]{:S(2)}) collective-permute-start(bf16[192,2304]{1,0:T(8,128)(2,1)} %get-tuple-element.452), channel_id=1, source_target_pairs={{2,0},{3,1},{4,2},{5,3},{6,4},{7,5},{10,8},{11,9},{12,10},{13,11},... | collective-permute-start | bytes 2654216 | tf_op jit(solution)/shard_map/ppermute | solution.py:73
  151.5 24.7 %collective-permute-start.16 = (bf16[192,2304]{1,0:T(8,128)(2,1)}, bf16[192,2304]{1,0:T(8,128)(2,1)S(1)}, u32[]{:S(2)}, u32[]{:S(2)}) collective-permute-start(bf16[192,2304]{1,0:T(8,128)(2,1)} %get-tuple-element.450), channel_id=1, source_target_pairs={{0,2},{1,3},{2,4},{3,5},{4,6},{5,7},{8,10},{9,11},{10,12},{11,13},... | collective-permute-start | bytes 2654216 | tf_op jit(solution)/shard_map/ppermute | solution.py:69
  157.5 23.7 %collective-permute-start.17 = (bf16[192,2304]{1,0:T(8,128)(2,1)}, bf16[192,2304]{1,0:T(8,128)(2,1)S(1)}, u32[]{:S(2)}, u32[]{:S(2)}) collective-permute-start(bf16[192,2304]{1,0:T(8,128)(2,1)} %get-tuple-element.451), channel_id=1, source_target_pairs={{2,0},{3,1},{4,2},{5,3},{6,4},{7,5},{10,8},{11,9},{12,10},{13,11},... | collective-permute-start | bytes 2654216 | tf_op jit(solution)/shard_map/ppermute | solution.py:73
  181.9 21.7 %collective-permute-start.20 = (bf16[192,2304]{1,0:T(8,128)(2,1)S(1)}, bf16[192,2304]{1,0:T(8,128)(2,1)S(1)}, u32[]{:S(2)}, u32[]{:S(2)}) collective-permute-start(bf16[192,2304]{1,0:T(8,128)(2,1)S(1)} %get-tuple-element.460), channel_id=1, source_target_pairs={{0,2},{1,3},{2,4},{3,5},{4,6},{5,7},{8,10},{9,11},{10,12},{11,13},... | collective-permute-start | bytes 2654216 | tf_op jit(solution)/shard_map/ppermute | solution.py:69
  184.1 23.7 %collective-permute-start.21 = (bf16[192,2304]{1,0:T(8,128)(2,1)S(1)}, bf16[192,2304]{1,0:T(8,128)(2,1)S(1)}, u32[]{:S(2)}, u32[]{:S(2)}) collective-permute-start(bf16[192,2304]{1,0:T(8,128)(2,1)S(1)} %get-tuple-element.461), channel_id=1, source_target_pairs={{2,0},{3,1},{4,2},{5,3},{6,4},{7,5},{10,8},{11,9},{12,10},{13,11},... | collective-permute-start | bytes 2654216 | tf_op jit(solution)/shard_map/ppermute | solution.py:73
  208.4 21.9 %collective-permute-start.23 = (bf16[192,2304]{1,0:T(8,128)(2,1)S(1)}, bf16[192,2304]{1,0:T(8,128)(2,1)S(1)}, u32[]{:S(2)}, u32[]{:S(2)}) collective-permute-start(bf16[192,2304]{1,0:T(8,128)(2,1)S(1)} %get-tuple-element.465), channel_id=1, source_target_pairs={{0,2},{1,3},{2,4},{3,5},{4,6},{5,7},{8,10},{9,11},{10,12},{11,13},... | collective-permute-start | bytes 2654216 | tf_op jit(solution)/shard_map/ppermute | solution.py:69
  211.9 22.6 %collective-permute-start.24 = (bf16[192,2304]{1,0:T(8,128)(2,1)S(1)}, bf16[192,2304]{1,0:T(8,128)(2,1)S(1)}, u32[]{:S(2)}, u32[]{:S(2)}) collective-permute-start(bf16[192,2304]{1,0:T(8,128)(2,1)S(1)} %get-tuple-element.466), channel_id=1, source_target_pairs={{2,0},{3,1},{4,2},{5,3},{6,4},{7,5},{10,8},{11,9},{12,10},{13,11},... | collective-permute-start | bytes 2654216 | tf_op jit(solution)/shard_map/ppermute | solution.py:73
  238.9 20.3 %collective-permute-start.26 = (bf16[192,2304]{1,0:T(8,128)(2,1)}, bf16[192,2304]{1,0:T(8,128)(2,1)}, u32[]{:S(2)}, u32[]{:S(2)}) collective-permute-start(bf16[192,2304]{1,0:T(8,128)(2,1)} %get-tuple-element.494), channel_id=1, source_target_pairs={{0,2},{1,3},{2,4},{3,5},{4,6},{5,7},{8,10},{9,11},{10,12},{11,13},... | collective-permute-start | bytes 2654216 | tf_op jit(solution)/shard_map/ppermute | solution.py:69
  242.3 22.0 %collective-permute-start.27 = (bf16[192,2304]{1,0:T(8,128)(2,1)}, bf16[192,2304]{1,0:T(8,128)(2,1)}, u32[]{:S(2)}, u32[]{:S(2)}) collective-permute-start(bf16[192,2304]{1,0:T(8,128)(2,1)} %get-tuple-element.494), channel_id=1, source_target_pairs={{2,0},{3,1},{4,2},{5,3},{6,4},{7,5},{10,8},{11,9},{12,10},{13,11},... | collective-permute-start | bytes 2654216 | tf_op jit(solution)/shard_map/ppermute | solution.py:73
  267.1 20.7 %collective-permute-start.28 = (bf16[192,2304]{1,0:T(8,128)(2,1)}, bf16[192,2304]{1,0:T(8,128)(2,1)S(1)}, u32[]{:S(2)}, u32[]{:S(2)}) collective-permute-start(bf16[192,2304]{1,0:T(8,128)(2,1)} %get-tuple-element.492), channel_id=1, source_target_pairs={{0,2},{1,3},{2,4},{3,5},{4,6},{5,7},{8,10},{9,11},{10,12},{11,13},... | collective-permute-start | bytes 2654216 | tf_op jit(solution)/shard_map/ppermute | solution.py:69
  268.7 21.1 %collective-permute-start.29 = (bf16[192,2304]{1,0:T(8,128)(2,1)}, bf16[192,2304]{1,0:T(8,128)(2,1)}, u32[]{:S(2)}, u32[]{:S(2)}) collective-permute-start(bf16[192,2304]{1,0:T(8,128)(2,1)} %get-tuple-element.493), channel_id=1, source_target_pairs={{2,0},{3,1},{4,2},{5,3},{6,4},{7,5},{10,8},{11,9},{12,10},{13,11},... | collective-permute-start | bytes 2654216 | tf_op jit(solution)/shard_map/ppermute | solution.py:73
  296.0 20.4 %collective-permute-start.31 = (bf16[192,2304]{1,0:T(8,128)(2,1)}, bf16[192,2304]{1,0:T(8,128)(2,1)S(1)}, u32[]{:S(2)}, u32[]{:S(2)}) collective-permute-start(bf16[192,2304]{1,0:T(8,128)(2,1)} %get-tuple-element.505), channel_id=1, source_target_pairs={{2,0},{3,1},{4,2},{5,3},{6,4},{7,5},{10,8},{11,9},{12,10},{13,11},... | collective-permute-start | bytes 2654216 | tf_op jit(solution)/shard_map/ppermute | solution.py:73
  318.2 21.3 %collective-permute-start.32 = (bf16[192,2304]{1,0:T(8,128)(2,1)}, bf16[192,2304]{1,0:T(8,128)(2,1)S(1)}, u32[]{:S(2)}, u32[]{:S(2)}) collective-permute-start(bf16[192,2304]{1,0:T(8,128)(2,1)} %get-tuple-element.511), channel_id=1, source_target_pairs={{0,2},{1,3},{2,4},{3,5},{4,6},{5,7},{8,10},{9,11},{10,12},{11,13},... | collective-permute-start | bytes 2654216 | tf_op jit(solution)/shard_map/ppermute | solution.py:69
  371.6 20.3 %collective-permute-start.36 = (bf16[192,2304]{1,0:T(8,128)(2,1)}, bf16[192,2304]{1,0:T(8,128)(2,1)S(1)}, u32[]{:S(2)}, u32[]{:S(2)}) collective-permute-start(bf16[192,2304]{1,0:T(8,128)(2,1)} %get-tuple-element.528), channel_id=1, source_target_pairs={{0,2},{1,3},{2,4},{3,5},{4,6},{5,7},{8,10},{9,11},{10,12},{11,13},... | collective-permute-start | bytes 2654216 | tf_op jit(solution)/shard_map/ppermute | solution.py:69
  561.2 31.6 %collective-permute-start.52 = (bf16[192,2304]{1,0:T(8,128)(2,1)S(1)}, bf16[192,2304]{1,0:T(8,128)(2,1)S(1)}, u32[]{:S(2)}, u32[]{:S(2)}) collective-permute-start(bf16[192,2304]{1,0:T(8,128)(2,1)S(1)} %get-tuple-element.608), channel_id=1, source_target_pairs={{0,2},{1,3},{2,4},{3,5},{4,6},{5,7},{8,10},{9,11},{10,12},{11,13},... | collective-permute-start | bytes 2654216 | tf_op jit(solution)/shard_map/ppermute | solution.py:69
  566.0 26.7 %collective-permute-start.53 = (bf16[192,2304]{1,0:T(8,128)(2,1)S(1)}, bf16[192,2304]{1,0:T(8,128)(2,1)}, u32[]{:S(2)}, u32[]{:S(2)}) collective-permute-start(bf16[192,2304]{1,0:T(8,128)(2,1)S(1)} %get-tuple-element.609), channel_id=1, source_target_pairs={{2,0},{3,1},{4,2},{5,3},{6,4},{7,5},{10,8},{11,9},{12,10},{13,11},... | collective-permute-start | bytes 2654216 | tf_op jit(solution)/shard_map/ppermute | solution.py:73
  595.0 30.1 %collective-permute-start.54 = (bf16[192,2304]{1,0:T(8,128)(2,1)S(1)}, bf16[192,2304]{1,0:T(8,128)(2,1)S(1)}, u32[]{:S(2)}, u32[]{:S(2)}) collective-permute-start(bf16[192,2304]{1,0:T(8,128)(2,1)S(1)} %get-tuple-element.626), channel_id=1, source_target_pairs={{0,2},{1,3},{2,4},{3,5},{4,6},{5,7},{8,10},{9,11},{10,12},{11,13},... | collective-permute-start | bytes 2654216 | tf_op jit(solution)/shard_map/ppermute | solution.py:69
  599.9 25.3 %collective-permute-start.55 = (bf16[192,2304]{1,0:T(8,128)(2,1)S(1)}, bf16[192,2304]{1,0:T(8,128)(2,1)S(1)}, u32[]{:S(2)}, u32[]{:S(2)}) collective-permute-start(bf16[192,2304]{1,0:T(8,128)(2,1)S(1)} %get-tuple-element.627), channel_id=1, source_target_pairs={{2,0},{3,1},{4,2},{5,3},{6,4},{7,5},{10,8},{11,9},{12,10},{13,11},... | collective-permute-start | bytes 2654216 | tf_op jit(solution)/shard_map/ppermute | solution.py:73
  628.4 38.0 %collective-permute-start.56 = (bf16[192,2304]{1,0:T(8,128)(2,1)}, bf16[192,2304]{1,0:T(8,128)(2,1)S(1)}, u32[]{:S(2)}, u32[]{:S(2)}) collective-permute-start(bf16[192,2304]{1,0:T(8,128)(2,1)} %get-tuple-element.643), channel_id=1, source_target_pairs={{0,2},{1,3},{2,4},{3,5},{4,6},{5,7},{8,10},{9,11},{10,12},{11,13},... | collective-permute-start | bytes 2654216 | tf_op jit(solution)/shard_map/ppermute | solution.py:69
  633.7 32.7 %collective-permute-start.57 = (bf16[192,2304]{1,0:T(8,128)(2,1)}, bf16[192,2304]{1,0:T(8,128)(2,1)}, u32[]{:S(2)}, u32[]{:S(2)}) collective-permute-start(bf16[192,2304]{1,0:T(8,128)(2,1)} %get-tuple-element.644), channel_id=1, source_target_pairs={{2,0},{3,1},{4,2},{5,3},{6,4},{7,5},{10,8},{11,9},{12,10},{13,11},... | collective-permute-start | bytes 2654216 | tf_op jit(solution)/shard_map/ppermute | solution.py:73
  672.4 38.2 %collective-permute-start.60 = (bf16[1152,2304]{1,0:T(8,128)(2,1)}, bf16[1152,2304]{1,0:T(8,128)(2,1)}, u32[]{:S(2)}, u32[]{:S(2)}) collective-permute-start(bf16[1152,2304]{1,0:T(8,128)(2,1)} %fusion.3), channel_id=1, source_target_pairs={{0,1},{1,0},{2,3},{3,2},{4,5},{5,4},{6,7},{7,6},{8,9},{9,8},{10,11... | collective-permute-start | bytes 15925256 | tf_op jit(solution)/shard_map/ppermute | solution.py:76
  672.5 48.7 %collective-permute-start.58 = (bf16[192,2304]{1,0:T(8,128)(2,1)}, bf16[192,2304]{1,0:T(8,128)(2,1)S(1)}, u32[]{:S(2)}, u32[]{:S(2)}) collective-permute-start(bf16[192,2304]{1,0:T(8,128)(2,1)} %get-tuple-element.692), channel_id=1, source_target_pairs={{0,2},{1,3},{2,4},{3,5},{4,6},{5,7},{8,10},{9,11},{10,12},{11,13},... | collective-permute-start | bytes 2654216 | tf_op jit(solution)/shard_map/ppermute | solution.py:69
  678.2 43.0 %collective-permute-start.59 = (bf16[192,2304]{1,0:T(8,128)(2,1)}, bf16[192,2304]{1,0:T(8,128)(2,1)}, u32[]{:S(2)}, u32[]{:S(2)}) collective-permute-start(bf16[192,2304]{1,0:T(8,128)(2,1)} %get-tuple-element.692), channel_id=1, source_target_pairs={{2,0},{3,1},{4,2},{5,3},{6,4},{7,5},{10,8},{11,9},{12,10},{13,11},... | collective-permute-start | bytes 2654216 | tf_op jit(solution)/shard_map/ppermute | solution.py:73
  724.5 24.5 %collective-permute-start.61 = (bf16[192,2304]{1,0:T(8,128)(2,1)}, bf16[192,2304]{1,0:T(8,128)(2,1)}, u32[]{:S(2)}, u32[]{:S(2)}) collective-permute-start(bf16[192,2304]{1,0:T(8,128)(2,1)} %get-tuple-element.675), channel_id=1, source_target_pairs={{0,2},{1,3},{2,4},{3,5},{4,6},{5,7},{8,10},{9,11},{10,12},{11,13},... | collective-permute-start | bytes 2654216 | tf_op jit(solution)/shard_map/ppermute | solution.py:69
  730.3 24.1 %collective-permute-start.62 = (bf16[192,2304]{1,0:T(8,128)(2,1)}, bf16[192,2304]{1,0:T(8,128)(2,1)}, u32[]{:S(2)}, u32[]{:S(2)}) collective-permute-start(bf16[192,2304]{1,0:T(8,128)(2,1)} %get-tuple-element.676), channel_id=1, source_target_pairs={{2,0},{3,1},{4,2},{5,3},{6,4},{7,5},{10,8},{11,9},{12,10},{13,11},... | collective-permute-start | bytes 2654216 | tf_op jit(solution)/shard_map/ppermute | solution.py:73
  759.1 336.6 %all-reduce.8.cloned.1.call-start = ((), (), s32[]{:S(2)}) async-start(), calls=%async_computation | async-start | bytes 10616832 | tf_op jit(solution)/shard_map/psum | solution.py:838
  764.7 24.1 %collective-permute-start.64 = (bf16[192,2304]{1,0:T(8,128)(2,1)}, bf16[192,2304]{1,0:T(8,128)(2,1)}, u32[]{:S(2)}, u32[]{:S(2)}) collective-permute-start(bf16[192,2304]{1,0:T(8,128)(2,1)} %get-tuple-element.684), channel_id=1, source_target_pairs={{0,2},{1,3},{2,4},{3,5},{4,6},{5,7},{8,10},{9,11},{10,12},{11,13},... | collective-permute-start | bytes 2654216 | tf_op jit(solution)/shard_map/ppermute | solution.py:69
  770.5 23.4 %collective-permute-start.65 = (bf16[192,2304]{1,0:T(8,128)(2,1)}, bf16[192,2304]{1,0:T(8,128)(2,1)}, u32[]{:S(2)}, u32[]{:S(2)}) collective-permute-start(bf16[192,2304]{1,0:T(8,128)(2,1)} %get-tuple-element.685), channel_id=1, source_target_pairs={{2,0},{3,1},{4,2},{5,3},{6,4},{7,5},{10,8},{11,9},{12,10},{13,11},... | collective-permute-start | bytes 2654216 | tf_op jit(solution)/shard_map/ppermute | solution.py:73
  798.4 31.8 %collective-permute-start.67 = (bf16[192,2304]{1,0:T(8,128)(2,1)}, bf16[192,2304]{1,0:T(8,128)(2,1)}, u32[]{:S(2)}, u32[]{:S(2)}) collective-permute-start(bf16[192,2304]{1,0:T(8,128)(2,1)} %get-tuple-element.690), channel_id=1, source_target_pairs={{0,2},{1,3},{2,4},{3,5},{4,6},{5,7},{8,10},{9,11},{10,12},{11,13},... | collective-permute-start | bytes 2654216 | tf_op jit(solution)/shard_map/ppermute | solution.py:69
  802.3 28.0 %collective-permute-start.68 = (bf16[192,2304]{1,0:T(8,128)(2,1)}, bf16[192,2304]{1,0:T(8,128)(2,1)}, u32[]{:S(2)}, u32[]{:S(2)}) collective-permute-start(bf16[192,2304]{1,0:T(8,128)(2,1)} %get-tuple-element.691), channel_id=1, source_target_pairs={{2,0},{3,1},{4,2},{5,3},{6,4},{7,5},{10,8},{11,9},{12,10},{13,11},... | collective-permute-start | bytes 2654216 | tf_op jit(solution)/shard_map/ppermute | solution.py:73
  835.9 21.9 %collective-permute-start.69 = (bf16[192,2304]{1,0:T(8,128)(2,1)S(1)}, bf16[192,2304]{1,0:T(8,128)(2,1)S(1)}, u32[]{:S(2)}, u32[]{:S(2)}) collective-permute-start(bf16[192,2304]{1,0:T(8,128)(2,1)S(1)} %get-tuple-element.737), channel_id=1, source_target_pairs={{0,2},{1,3},{2,4},{3,5},{4,6},{5,7},{8,10},{9,11},{10,12},{11,13},... | collective-permute-start | bytes 2654216 | tf_op jit(solution)/shard_map/ppermute | solution.py:69
  840.3 21.7 %collective-permute-start.70 = (bf16[192,2304]{1,0:T(8,128)(2,1)S(1)}, bf16[192,2304]{1,0:T(8,128)(2,1)S(1)}, u32[]{:S(2)}, u32[]{:S(2)}) collective-permute-start(bf16[192,2304]{1,0:T(8,128)(2,1)S(1)} %get-tuple-element.737), channel_id=1, source_target_pairs={{2,0},{3,1},{4,2},{5,3},{6,4},{7,5},{10,8},{11,9},{12,10},{13,11},... | collective-permute-start | bytes 2654216 | tf_op jit(solution)/shard_map/ppermute | solution.py:73
  864.3 20.9 %collective-permute-start.73 = (bf16[192,2304]{1,0:T(8,128)(2,1)S(1)}, bf16[192,2304]{1,0:T(8,128)(2,1)S(1)}, u32[]{:S(2)}, u32[]{:S(2)}) collective-permute-start(bf16[192,2304]{1,0:T(8,128)(2,1)S(1)} %get-tuple-element.728), channel_id=1, source_target_pairs={{2,0},{3,1},{4,2},{5,3},{6,4},{7,5},{10,8},{11,9},{12,10},{13,11},... | collective-permute-start | bytes 2654216 | tf_op jit(solution)/shard_map/ppermute | solution.py:73
  890.3 20.1 %collective-permute-start.75 = (bf16[192,2304]{1,0:T(8,128)(2,1)}, bf16[192,2304]{1,0:T(8,128)(2,1)}, u32[]{:S(2)}, u32[]{:S(2)}) collective-permute-start(bf16[192,2304]{1,0:T(8,128)(2,1)} %get-tuple-element.732), channel_id=1, source_target_pairs={{2,0},{3,1},{4,2},{5,3},{6,4},{7,5},{10,8},{11,9},{12,10},{13,11},... | collective-permute-start | bytes 2654216 | tf_op jit(solution)/shard_map/ppermute | solution.py:73
  891.8 317.5 %all-reduce.12.cloned.1.call-start = ((), (), s32[]{:S(2)}) async-start(), calls=%async_computation.2 | async-start | bytes 7077888 | tf_op jit(solution)/shard_map/psum | solution.py:838
  915.0 25.8 %collective-permute-start.76 = (bf16[192,2304]{1,0:T(8,128)(2,1)S(1)}, bf16[192,2304]{1,0:T(8,128)(2,1)S(1)}, u32[]{:S(2)}, u32[]{:S(2)}) collective-permute-start(bf16[192,2304]{1,0:T(8,128)(2,1)S(1)} %get-tuple-element.735), channel_id=1, source_target_pairs={{0,2},{1,3},{2,4},{3,5},{4,6},{5,7},{8,10},{9,11},{10,12},{11,13},... | collective-permute-start | bytes 2654216 | tf_op jit(solution)/shard_map/ppermute | solution.py:69
  916.5 24.3 %collective-permute-start.77 = (bf16[192,2304]{1,0:T(8,128)(2,1)S(1)}, bf16[192,2304]{1,0:T(8,128)(2,1)S(1)}, u32[]{:S(2)}, u32[]{:S(2)}) collective-permute-start(bf16[192,2304]{1,0:T(8,128)(2,1)S(1)} %get-tuple-element.736), channel_id=1, source_target_pairs={{2,0},{3,1},{4,2},{5,3},{6,4},{7,5},{10,8},{11,9},{12,10},{13,11},... | collective-permute-start | bytes 2654216 | tf_op jit(solution)/shard_map/ppermute | solution.py:73
  970.1 25.3 %collective-permute-start.79 = (bf16[208,2304]{1,0:T(8,128)(2,1)}, bf16[208,2304]{1,0:T(8,128)(2,1)S(1)}, u32[]{:S(2)}, u32[]{:S(2)}) collective-permute-start(bf16[208,2304]{1,0:T(8,128)(2,1)} %pad_maximum_fusion.12), channel_id=1, source_target_pairs={{0,2},{1,3},{8,10},{9,11},{16,18},{17,19},{24,26},{25,27}} | collective-permute-start | bytes 2875400 | tf_op jit(solution)/shard_map/ppermute | solution.py:69
  973.8 21.6 %collective-permute-start.80 = (bf16[208,2304]{1,0:T(8,128)(2,1)}, bf16[208,2304]{1,0:T(8,128)(2,1)S(1)}, u32[]{:S(2)}, u32[]{:S(2)}) collective-permute-start(bf16[208,2304]{1,0:T(8,128)(2,1)} %pad_maximum_fusion.12), channel_id=1, source_target_pairs={{6,4},{7,5},{14,12},{15,13},{22,20},{23,21},{30,28},{31,29}} | collective-permute-start | bytes 2875400 | tf_op jit(solution)/shard_map/ppermute | solution.py:73
  997.1 25.3 %collective-permute-start.81 = (bf16[208,2304]{1,0:T(8,128)(2,1)}, bf16[208,2304]{1,0:T(8,128)(2,1)}, u32[]{:S(2)}, u32[]{:S(2)}) collective-permute-start(bf16[208,2304]{1,0:T(8,128)(2,1)} %get-tuple-element.789), channel_id=1, source_target_pairs={{0,2},{1,3},{2,4},{3,5},{8,10},{9,11},{10,12},{11,13},{16,18},{17,... | collective-permute-start | bytes 2875400 | tf_op jit(solution)/shard_map/ppermute | solution.py:69
  1095.6 24.2 %collective-permute-start.87 = (bf16[208,2304]{1,0:T(8,128)(2,1)}, bf16[208,2304]{1,0:T(8,128)(2,1)}, u32[]{:S(2)}, u32[]{:S(2)}) collective-permute-start(bf16[208,2304]{1,0:T(8,128)(2,1)} %get-tuple-element.798), channel_id=1, source_target_pairs={{0,2},{1,3},{2,4},{3,5},{4,6},{5,7},{8,10},{9,11},{10,12},{11,13},... | collective-permute-start | bytes 2875400 | tf_op jit(solution)/shard_map/ppermute | solution.py:69
  1099.9 24.9 %collective-permute-start.88 = (bf16[208,2304]{1,0:T(8,128)(2,1)}, bf16[208,2304]{1,0:T(8,128)(2,1)}, u32[]{:S(2)}, u32[]{:S(2)}) collective-permute-start(bf16[208,2304]{1,0:T(8,128)(2,1)} %get-tuple-element.799), channel_id=1, source_target_pairs={{2,0},{3,1},{4,2},{5,3},{6,4},{7,5},{10,8},{11,9},{12,10},{13,11},... | collective-permute-start | bytes 2875400 | tf_op jit(solution)/shard_map/ppermute | solution.py:73
  (248 other events, 2578.0 us)
Sparse Core Ops, SparseCore 0:
  759.2 210.8 all-reduce.9
  973.4 122.1 all-reduce.7
  1113.5 95.7 all-reduce.11

commit v5 on v4

--- a/solution.py
+++ b/solution.py
@@ -347,7 +347,7 @@
                 pltpu.VMEM((heads, rows, 1), f32),
             ],
         ),
-        compiler_params=pltpu.CompilerParams(vmem_limit_bytes=32 * 1024 * 1024),
+        compiler_params=pltpu.CompilerParams(vmem_limit_bytes=20 * 1024 * 1024),
         cost_estimate=light,
     )(info, *arrays)
 
@@ -384,7 +384,7 @@
                 pltpu.VMEM((heads, rows, HEAD_DIM), f32),
             ],
         ),
-        compiler_params=pltpu.CompilerParams(vmem_limit_bytes=48 * 1024 * 1024),
+        compiler_params=pltpu.CompilerParams(vmem_limit_bytes=30 * 1024 * 1024),
         cost_estimate=light,
     )(info, *arrays)
 
@@ -396,7 +396,7 @@
         grid=(grid,),
         in_specs=[pl.BlockSpec(*spec) for spec in ins],
         out_specs=tuple(pl.BlockSpec(*out[1:]) for out in outs),
-        compiler_params=pltpu.CompilerParams(vmem_limit_bytes=40 * 1024 * 1024),
+        compiler_params=pltpu.CompilerParams(vmem_limit_bytes=24 * 1024 * 1024),
         cost_estimate=light,
     )(*arrays)
 
@@ -583,7 +583,7 @@
         grid=(n // tile,),
         in_specs=[pl.BlockSpec((m, width), lambda i: (0, 0)), weight_spec, weight_spec],
         out_specs=(out_spec,) * 3,
-        compiler_params=pltpu.CompilerParams(vmem_limit_bytes=56 * 1024 * 1024),
+        compiler_params=pltpu.CompilerParams(vmem_limit_bytes=30 * 1024 * 1024),
         cost_estimate=light,
     )(hidden, gate_w, up_w)
 
@@ -605,7 +605,7 @@
         in_specs=[pl.BlockSpec((m, depth), lambda i: (0, 0))] * len(lefts)
         + [pl.BlockSpec((depth, tile), lambda i: (0, i))] * len(weights),
         out_specs=pl.BlockSpec((m, tile), lambda i: (0, i)),
-        compiler_params=pltpu.CompilerParams(vmem_limit_bytes=56 * 1024 * 1024),
+        compiler_params=pltpu.CompilerParams(vmem_limit_bytes=(26 if m <= 384 else 36) * 1024 * 1024),
         cost_estimate=light,
     )(*lefts, *weights)
 
@@ -632,7 +632,7 @@
             spec,
         ],
         out_specs=(spec,) * 2,
-        compiler_params=pltpu.CompilerParams(vmem_limit_bytes=56 * 1024 * 1024),
+        compiler_params=pltpu.CompilerParams(vmem_limit_bytes=30 * 1024 * 1024),
         cost_estimate=light,
     )(low, down_w, gelu, slope)
 
@@ -837,6 +837,35 @@
         groups = [[(i + order) % data for i in range(data)]]
         return lax.psum(values, "dp", axis_index_groups=groups)
 
+    def swapped(block, bit):
+        return lax.ppermute(block, "dp", [(i, i ^ bit) for i in range(data)])
+
+    def data_exchange_sum(value, order):
+        if data != 4:
+            return data_sum(value, order).astype(f32)
+        place = lax.axis_index("dp")
+        ways = ((place % 2, 1), (place // 2, 2))
+
+        def reduced(block, way):
+            bit_value, bit = way
+            half = block.shape[0] // 2
+            kept = lax.dynamic_slice(block, (bit_value * half, 0), (half, block.shape[1]))
+            sent = lax.dynamic_slice(block, ((1 - bit_value) * half, 0), (half, block.shape[1]))
+            return (kept.astype(f32) + swapped(sent, bit).astype(f32)).astype(bf16)
+
+        def gathered(block, way):
+            bit_value, bit = way
+            got = swapped(block, bit)
+            low = bit_value == 0
+            return jnp.concatenate([jnp.where(low, block, got), jnp.where(low, got, block)])
+
+        middle = value.shape[1] // 2
+        halves = [value[:, :middle], value[:, middle:]]
+        orders = [ways, ways[::-1]]
+        for step, pick in ((reduced, 0), (reduced, 1), (gathered, 1), (gathered, 0)):
+            halves = [step(half, one[pick]) for half, one in zip(halves, orders)]
+        return jnp.concatenate(halves, axis=1).astype(f32)
+
     near, far = slice(0, 2), slice(2, chips)
 
     a, b = (Sequence(s) for s in range(seq_count))
@@ -845,10 +874,16 @@
     def attention_weights(query_w, key_w, value_w):
         return jnp.concatenate([pair_rows(query_w), group_rows(key_w), group_rows(value_w)])
 
-    ex.step()
-    qkv_weight = ex.step(attention_weights, (query_weight, key_weight, value_weight))
-    out_weight, gate_rows = ex.step(
-        lambda out_w, gate_w: (pair_rows(out_w), both_rows(gate_w)), (output_weight, gate_weight)
+    gate_other = ex.step(line.swap, (gate_weight,))
+
+    def first_weights(gate_w, gate_other, *attention):
+        return attention_weights(*attention), jnp.concatenate([gate_w, gate_other])
+
+    qkv_weight, gate_rows = ex.step(
+        first_weights, (gate_weight, gate_other, query_weight, key_weight, value_weight)
+    )
+    out_weight, up_rows = ex.step(
+        lambda out_w, up_w: (pair_rows(out_w), both_rows(up_w)), (output_weight, up_weight)
     )
     for _ in range(chips - 4):
         ex.step()
@@ -873,10 +908,7 @@
     )
     ex.give(out)
 
-    def b_project_near(up_w, *blocks):
-        return b.project(near, *blocks), both_rows(up_w)
-
-    b_near, up_rows = ex.step(b_project_near, [up_weight] + ex.near())
+    b_near = ex.step(functools.partial(b.project, near), ex.near())
     down_rows = ex.step(both_rows, (down_weight,))
     for _ in range(chips - 4):
         ex.step()
@@ -1058,28 +1090,36 @@
     late, down_sum, gate_sum = ex.step(sums_work, (down_sum, gate_sum, *late))
     for _ in range(chips - 4):
         ex.step()
-    ex.step(held=(up_sum,))
-    (up_sum,) = ex.held
-    late_sums = data_sum(late, 2)
+    ex.step()
+    late_sum = data_exchange_sum(jnp.concatenate(late), 2)
     grad = total(ex.terms())
     tokens_grad_b = b.after_project_back([grad[:rows]])
 
     row = grad[rows, : 8 * count].reshape(2, 4, count)
     mine = jnp.where(c == 0, row[0], row[1])
     other = jnp.where(c == 0, row[1], row[0])
-    gain_sums = lax.psum(mine + line.swap(other.astype(bf16)).astype(f32), "dp")
-
-    done = tied(
+    gain_sums = mine + line.swap(other.astype(bf16)).astype(f32)
+    if data == 4:
+        for bit in (1, 2):
+            gain_sums = gain_sums + swapped(gain_sums, bit)
+    else:
+        gain_sums = lax.psum(gain_sums, "dp")
+
+    late_sums, row = [], 0
+    for value in late:
+        late_sums.append(late_sum[row : row + value.shape[0]])
+        row += value.shape[0]
+    *done, up_sum = tied(
         jnp.stack([a.output, b.output]),
         jnp.stack([tokens_grad_a, tokens_grad_b]),
+        *late_sums,
         gate_sum,
-        up_sum.astype(f32),
         down_sum,
         gain_sums,
-        late_sums,
-    )
-    late_sums = [value.astype(f32) for value in done[6]]
-    return (*done[:2], *late_sums, *done[2:5], *done[5])
+        up_sum,
+    )
+    up_sum = up_sum.astype(f32)
+    return (*done[:7], up_sum, done[7], *done[8])
 
 
 def solution(mesh):

time: 1230 us -> 1150 us (0.935)
  Pallas kernels: 282 us -> 222 us
  waiting for transfers between devices: 357 us -> 329 us
  local copies, waits for them, and re-layouts: 92.9 us -> 108 us
    psum x3 -> x2, waiting for transfers between devices: 134 us -> 11.1 us  [data_sum(): return lax.psum(values, 'dp', axis_index_groups=groups)]
    ppermute x0 -> x10, waiting for transfers between devices: none -> 74.2 us  [swapped(): return lax.ppermute(block, 'dp', [(i, i ^ bit) for i in range(data)])]
    ppermute x34, waiting for transfers between devices: 104 us -> 130 us  [right(): return lax.ppermute(block, 'ctx', self.pairs(1, low, high))]
    pallas_call x7, Pallas kernels: 86.3 us -> 62.6 us  [mix(): pl.pallas_call(mix_kernel, out_shape=jax.ShapeDtypeStruct((m, n), bf16),...]
    concatenate x3 -> x2, other arithmetic: 31.7 us -> 16.9 us  [both_rows(): return jnp.concatenate([block, line.swap(block)])]
    pallas_call x3, Pallas kernels: 36.5 us -> 22.3 us  [feed_back(): pl.pallas_call(feed_back_kernel, out_shape=(jax.ShapeDtypeStruct((m, n),...]
    unnamed x423 -> x510, local copies, waits for them, and re-layouts: 68.6 us -> 80.3 us
  transfers between devices with their start and end apart: 93 -> 102, of which waited for: 48 -> 50; matrix products, arithmetic and copies ran while one was open for 22% -> 22% of each run, Pallas kernels for 22% -> 18%
where the time goes in v5:
time: 1150 us; the launch traced here: 1140 us
  waiting for transfers between devices  329 us (29%)
  Pallas kernels  222 us (19%)
  starting transfers between devices  185 us (16%)
  other arithmetic  152 us (13%)
  matrix products  130 us (11%)
  local copies, waits for them, and re-layouts  108 us (9%)
  between operations  18.6 us (2%)
    ppermute x34, waiting for transfers between devices, right(): return lax.ppermute(block, 'ctx', self.pairs(1, low, high))  130 us
    ppermute x34, starting transfers between devices, right(): return lax.ppermute(block, 'ctx', self.pairs(1, low, high))  127 us
    dot_general x11, matrix products, tn(): lax.dot_general(left_side, right_side, (((0,), (0,)), ((), ())), preferre...  120 us
    ppermute x34, waiting for transfers between devices, left(): return lax.ppermute(block, 'ctx', self.pairs(-1, n - high, n - low))  96.3 us
    unnamed x510, local copies, waits for them, and re-layouts  80.3 us
    ppermute x10, waiting for transfers between devices, swapped(): return lax.ppermute(block, 'dp', [(i, i ^ bit) for i in range(data)])  74.2 us
    pallas_call x7, Pallas kernels, mix(): pl.pallas_call(mix_kernel, out_shape=jax.ShapeDtypeStruct((m, n), bf16),...  62.6 us
    pallas_call x4, Pallas kernels, gate_up(): pl.pallas_call(gate_up_kernel, out_shape=(jax.ShapeDtypeStruct((m, n), bf...  48.8 us
  transfers between devices with their start and end apart: 102, of which 50 were waited for; matrix products, arithmetic and copies ran while one was open for 22% of the time, Pallas kernels for 18%

profile of v5, /device:TPU:0, one launch (start us, length us, event | category | flops | bytes accessed | tf_op | source)
XLA Modules:
  0.0 1144.0 jit_solution(5043927658922074044)
XLA Ops:
  18.2 19.2 %collective-permute-done = bf16[208,2304]{1,0:T(8,128)(2,1)} collective-permute-done((bf16[208,2304]{1,0:T(8,128)(2,1)}, bf16[208,2304]{1,0:T(8,128)(2,1)}, u32[]{:S(2)}, u32[]{:S(2)}) %collective-permute-start) | collective-permute-done | bytes 958496 | tf_op jit(solution)/shard_map/ppermute | solution.py:69
  46.1 9.4 pad_maximum_fusion.gate_ref.refs_2_
  59.0 11.2 collective-permute-done.4
  82.4 9.4 pad_maximum_fusion.1.up_ref.refs_3_
  91.8 9.5 collective-permute-done.9
  137.6 7.9 shard_map.248
  166.7 9.2 collective-permute-done.17
  193.1 7.5 pad_maximum_fusion.2.refs_1_.down_ref
  222.8 9.1 collective-permute-done.23.l_ref
  246.9 6.9 shard_map.252
  272.2 12.4 %shard_map.253 = (bf16[384,2304]{1,0:T(8,128)(2,1)S(1)}, bf16[384,2304]{1,0:T(8,128)(2,1)S(1)}, bf16[384,2304]{1,0:T(8,128)(2,1)S(1)}) custom-call(bf16[384,2304]{1,0:T(8,128)(2,1)S(1)} %constant_dynamic-update-slice_fusion.8.h_ref, bf16[2304,2304]{1,0:T(8,128)(2,1)S(1)} %bitcast.95, bf16[2304,2304]{1,0:T(8,128)(2,1)} %pad_maximum_fusion.1.up_ref.refs_3_), custom_call_target="tpu_custom_call" | custom-call | flops 1024 | bytes 1024 | tf_op jit(solution)/shard_map/pallas_call | solution.py:580
  301.3 8.6 collective-permute-done.30
  328.5 11.7 %shard_map.255 = (bf16[384,2304]{1,0:T(8,128)(2,1)S(1)}, bf16[384,2304]{1,0:T(8,128)(2,1)S(1)}, bf16[384,2304]{1,0:T(8,128)(2,1)S(1)}) custom-call(bf16[384,2304]{1,0:T(8,128)(2,1)S(1)} %copy-done.58, bf16[2304,2304]{1,0:T(8,128)(2,1)S(1)} %copy-done, bf16[2304,2304]{1,0:T(8,128)(2,1)} %pad_maximum_fusion.1.up_ref.refs_3_), custom_call_target="tpu_custom_call" | custom-call | flops 1024 | bytes 1024 | tf_op jit(solution)/shard_map/pallas_call | solution.py:580
  357.4 7.2 collective-permute-done.34
  377.8 12.3 %shard_map.258 = (bf16[384,2304]{1,0:T(8,128)(2,1)S(1)}, bf16[384,2304]{1,0:T(8,128)(2,1)S(1)}, bf16[384,2304]{1,0:T(8,128)(2,1)S(1)}) custom-call(bf16[384,2304]{1,0:T(8,128)(2,1)S(1)} %constant_dynamic-update-slice_fusion.12.h_ref, bf16[2304,2304]{1,0:T(8,128)(2,1)S(1)} %copy-done.1, bf16[2304,2304]{1,0:T(8,128)(2,1)} %pad_maximum_fusion.1.up_ref.refs_3_), custom_call_target="tpu_custom_call" | custom-call | flops 1024 | bytes 1024 | tf_op jit(solution)/shard_map/pallas_call | solution.py:580
  425.6 12.4 %shard_map.260 = (bf16[384,2304]{1,0:T(8,128)(2,1)S(1)}, bf16[384,2304]{1,0:T(8,128)(2,1)S(1)}, bf16[384,2304]{1,0:T(8,128)(2,1)S(1)}) custom-call(bf16[384,2304]{1,0:T(8,128)(2,1)S(1)} %constant_dynamic-update-slice_fusion.14.h_ref, bf16[2304,2304]{1,0:T(8,128)(2,1)S(1)} %copy-done.2, bf16[2304,2304]{1,0:T(8,128)(2,1)} %pad_maximum_fusion.1.up_ref.refs_3_), custom_call_target="tpu_custom_call" | custom-call | flops 1024 | bytes 1024 | tf_op jit(solution)/shard_map/pallas_call | solution.py:580
  453.1 5.9 collective-permute-done.42
  482.4 5.8 collective-permute-start.46
  499.0 10.2 shard_map.264.p_ref
  525.9 7.9 collective-permute-done.48.l_ref
  553.6 10.2 shard_map.267
  573.0 12.4 %convolution_convert_fusion.2 = bf16[2304,2304]{1,0:T(8,128)(2,1)} fusion(bf16[384,2304]{1,0:T(8,128)(2,1)} %copy-done.100, bf16[384,2304]{1,0:T(8,128)(2,1)S(1)} %copy-done.99, bf16[384,2304]{1,0:T(8,128)(2,1)S(1)} %copy-done.63, bf16[384,2304]{1,0:T(8,128)(2,1)S(1)} %copy-done.61), kind=kOutput, calls=%fused_computation.2 | convolution fusion | flops 8173191168 | bytes 17694720 | tf_op jit(solution)/shard_map/dot_general | solution.py:39
  585.4 11.1 convolution_convert_fusion.1
  608.7 12.9 %convolution_convert_fusion = bf16[2304,2304]{1,0:T(8,128)(2,1)} fusion(bf16[384,2304]{1,0:T(8,128)(2,1)} %copy-done.84, bf16[384,2304]{1,0:T(8,128)(2,1)} %copy-done.80, bf16[384,2304]{1,0:T(8,128)(2,1)S(1)} %copy-done.59, bf16[384,2304]{1,0:T(8,128)(2,1)S(1)} %copy-done.56), kind=kOutput, calls=%fused_computation | convolution fusion | flops 8173191168 | bytes 17694720 | tf_op jit(solution)/shard_map/dot_general | solution.py:39
  637.1 11.7 %shard_map.268 = (bf16[768,2304]{1,0:T(8,128)(2,1)S(1)}, bf16[768,2304]{1,0:T(8,128)(2,1)S(1)}) custom-call(bf16[768,2304]{1,0:T(8,128)(2,1)S(1)} %constant_dynamic-update-slice_fusion.20.low_ref, bf16[2304,2304]{1,0:T(8,128)(2,1)} %pad_maximum_fusion.2.refs_1_.down_ref, bf16[768,2304]{1,0:T(8,128)(2,1)S(1)} %pad_maximum_fusion.3.gelu_ref, ...), custom_call_target="tpu_custom_call" | custom-call | flops 1024 | bytes 1024 | tf_op jit(solution)/shard_map/pallas_call | solution.py:624
  652.4 12.1 %fusion.3 = bf16[1152,2304]{1,0:T(8,128)(2,1)} fusion(bf16[768,2304]{1,0:T(8,128)(2,1)} %copy-done.49, bf16[2304,2304]{1,0:T(8,128)(2,1)} %convolution_convert_fusion.2, bf16[768,2304]{1,0:T(8,128)(2,1)} %pad_maximum_fusion.5), kind=kOutput, calls=%fused_computation.12 | convolution fusion | flops 4084826112 | bytes 15925248 | tf_op jit(solution)/shard_map/dot_general | solution.py:39
  674.4 20.3 %shard_map.270.p_ref = bf16[768,2304]{1,0:T(8,128)(2,1)S(1)} custom-call(bf16[768,2304]{1,0:T(8,128)(2,1)S(1)} %copy-done.71, bf16[768,2304]{1,0:T(8,128)(2,1)S(1)} %get-tuple-element.691.refs_1_, bf16[2304,2304]{1,0:T(8,128)(2,1)} %pad_maximum_fusion.gate_ref.refs_2_, bf16[2304,2304]{1,0:T(8,128)(2,1)} %pad_maximum_fusion.1.up_ref.refs_3_), custom_call_target="tpu_custom_call" | custom-call | flops 1024 | bytes 1024 | tf_op jit(solution)/shard_map/pallas_call | solution.py:601
  694.8 9.7 fusion.4
  704.5 10.0 fusion.5
  724.6 8.4 fusion.6
  733.0 9.5 fusion.7
  761.1 13.3 %fusion.8 = bf16[1152,2304]{1,0:T(8,128)(2,1)} fusion(bf16[768,2304]{1,0:T(8,128)(2,1)} %pad_maximum_fusion.6, bf16[1152,2304]{1,0:T(8,128)(2,1)} %collective-permute-done.66, bf16[2304,2304]{1,0:T(8,128)(2,1)} %convolution_convert_fusion, bf16[768,2304]{1,0:T(8,128)(2,1)} %copy-done.69), kind=kOutput, calls=%fused_computation.17 | convolution fusion | flops 4090134528 | bytes 21233664 | tf_op jit(solution)/shard_map/dot_general | solution.py:39
  795.8 15.1 %shard_map.271 = (bf16[4,192,512]{2,1,0:T(8,128)(2,1)S(1)}, f32[4,192,512]{2,1,0:T(8,128)S(1)}, bf16[4,192,512]{2,1,0:T(8,128)(2,1)S(1)}) custom-call(s32[9]{0:T(128)S(1)} %copy-done.165, bf16[2,192,512]{2,1,0:T(8,128)(2,1)S(1)} %bitcast.115, bf16[2,192,512]{2,1,0:T(8,128)(2,1)S(1)} %bitcast.117, bf16[2,192,512]{2,1,0:T(8,128)(2,1)} %bitcast.18.refs_2_, ...), custom_call_target="tpu_custom_call" | custom-call | flops 1024 | bytes 1024 | tf_op jit(solution)/shard_map/pallas_call | solution.py:361
  829.3 7.5 collective-permute-done.69
  846.7 15.3 %collective-permute-done.72 = bf16[192,2304]{1,0:T(8,128)(2,1)S(1)} collective-permute-done((bf16[192,2304]{1,0:T(8,128)(2,1)}, bf16[192,2304]{1,0:T(8,128)(2,1)S(1)}, u32[]{:S(2)}, u32[]{:S(2)}) %collective-permute-start.72) | collective-permute-done | bytes 884768 | tf_op jit(solution)/shard_map/ppermute | solution.py:69
  882.2 6.6 collective-permute-done.74
  906.8 14.7 %shard_map.274 = (bf16[4,192,512]{2,1,0:T(8,128)(2,1)S(1)}, f32[4,192,512]{2,1,0:T(8,128)S(1)}, bf16[4,192,512]{2,1,0:T(8,128)(2,1)}) custom-call(s32[9]{0:T(128)S(1)} %copy-done.163, bf16[2,192,512]{2,1,0:T(8,128)(2,1)S(1)} %bitcast.105, bf16[2,192,512]{2,1,0:T(8,128)(2,1)S(1)} %bitcast.110, bf16[2,192,512]{2,1,0:T(8,128)(2,1)S(1)} %bitcast.108, ...), custom_call_target="tpu_custom_call" | custom-call | flops 1024 | bytes 1024 | tf_op jit(solution)/shard_map/pallas_call | solution.py:361
  923.0 9.0 fusion.24
  932.1 6.3 shard_map.275
  948.1 11.1 all-reduce.8.cloned.1.call-done
  963.5 11.6 %fusion.21 = bf16[1024,2304]{1,0:T(8,128)(2,1)S(1)} fusion(bf16[384,2304]{1,0:T(8,128)(2,1)} %copy-done.170, bf16[384,2304]{1,0:T(8,128)(2,1)} %copy-done.169, bf16[384,2304]{1,0:T(8,128)(2,1)} %copy-done.168, bf16[384,2304]{1,0:T(8,128)(2,1)S(1)} %copy-done.167, bf16[768,1024]{1,0:T(8,128)(2,1)} %copy-done.172, bf16[768,1024]{1,0:T(8,128)(2,1)} %copy-done.171), kind=kOutput, calls=%fused_computation.33 | convolution fusion | flops 7284719616 | bytes 14942208 | tf_op jit(solution)/shard_map/dot_general | solution.py:39
  975.2 8.3 collective-permute-done.79
  1012.0 8.3 collective-permute-start.87
  1021.9 18.7 %collective-permute-done.93 = bf16[384,1152]{1,0:T(8,128)(2,1)S(1)} collective-permute-done((bf16[384,1152]{1,0:T(8,128)(2,1)S(1)}, bf16[384,1152]{1,0:T(8,128)(2,1)S(1)}, u32[]{:S(2)}, u32[]{:S(2)}) %collective-permute-start.93) | collective-permute-done | bytes 884768 | tf_op jit(solution)/shard_map/ppermute | solution.py:841
  1069.9 10.1 collective-permute-done.95
  1081.2 6.9 collective-permute-done.91
  1089.7 33.2 %collective-permute-done.96 = bf16[384,1152]{1,0:T(8,128)(2,1)S(1)} collective-permute-done((bf16[384,1152]{1,0:T(8,128)(2,1)S(1)}, bf16[384,1152]{1,0:T(8,128)(2,1)S(1)}, u32[]{:S(2)}, u32[]{:S(2)}) %collective-permute-start.96) | collective-permute-done | bytes 884768 | tf_op jit(solution)/shard_map/ppermute | solution.py:841
  1128.7 7.4 convert_element_type.659
  (880 shorter events, 599.9 us)
Async XLA Ops:
  7.3 952.0 %all-reduce.8.cloned.1.call-start = ((), (), s32[]{:S(2)}) async-start(), calls=%async_computation.1 | async-start | bytes 21233664 | tf_op jit(solution)/shard_map/psum | solution.py:838
  11.0 31.5 %collective-permute-start.2 = (bf16[1152,2304]{1,0:T(8,128)(2,1)}, bf16[1152,2304]{1,0:T(8,128)(2,1)}, u32[]{:S(2)}, u32[]{:S(2)}) collective-permute-start(bf16[1152,2304]{1,0:T(8,128)(2,1)} %param.22), channel_id=1, source_target_pairs={{0,1},{1,0},{2,3},{3,2},{4,5},{5,4},{6,7},{7,6},{8,9},{9,8},{10,11... | collective-permute-start | bytes 15925256 | tf_op jit(solution)/shard_map/ppermute | solution.py:76
  11.5 25.9 %collective-permute-start = (bf16[208,2304]{1,0:T(8,128)(2,1)}, bf16[208,2304]{1,0:T(8,128)(2,1)}, u32[]{:S(2)}, u32[]{:S(2)}) collective-permute-start(bf16[208,2304]{1,0:T(8,128)(2,1)} %fusion.104), channel_id=1, source_target_pairs={{0,2},{1,3},{2,4},{3,5},{4,6},{5,7},{8,10},{9,11},{10,12},{11,13},... | collective-permute-start | bytes 2875400 | tf_op jit(solution)/shard_map/ppermute | solution.py:69
  16.9 25.6 %collective-permute-start.1 = (bf16[208,2304]{1,0:T(8,128)(2,1)}, bf16[208,2304]{1,0:T(8,128)(2,1)}, u32[]{:S(2)}, u32[]{:S(2)}) collective-permute-start(bf16[208,2304]{1,0:T(8,128)(2,1)} %fusion.104), channel_id=1, source_target_pairs={{2,0},{3,1},{4,2},{5,3},{6,4},{7,5},{10,8},{11,9},{12,10},{13,11},... | collective-permute-start | bytes 2875400 | tf_op jit(solution)/shard_map/ppermute | solution.py:73
  44.1 26.2 %collective-permute-start.4 = (bf16[208,2304]{1,0:T(8,128)(2,1)}, bf16[208,2304]{1,0:T(8,128)(2,1)}, u32[]{:S(2)}, u32[]{:S(2)}) collective-permute-start(bf16[208,2304]{1,0:T(8,128)(2,1)} %collective-permute-done.1), channel_id=1, source_target_pairs={{2,0},{3,1},{4,2},{5,3},{10,8},{11,9},{12,10},{13,11},{18,16},{19,... | collective-permute-start | bytes 2875400 | tf_op jit(solution)/shard_map/ppermute | solution.py:73
  76.1 25.3 %collective-permute-start.9 = (bf16[208,2304]{1,0:T(8,128)(2,1)}, bf16[208,2304]{1,0:T(8,128)(2,1)S(1)}, u32[]{:S(2)}, u32[]{:S(2)}) collective-permute-start(bf16[208,2304]{1,0:T(8,128)(2,1)} %collective-permute-done.4), channel_id=1, source_target_pairs={{2,0},{3,1},{10,8},{11,9},{18,16},{19,17},{26,24},{27,25}} | collective-permute-start | bytes 2875400 | tf_op jit(solution)/shard_map/ppermute | solution.py:73
  103.2 44.4 %collective-permute-start.12 = (bf16[192,2304]{1,0:T(8,128)(2,1)}, bf16[192,2304]{1,0:T(8,128)(2,1)}, u32[]{:S(2)}, u32[]{:S(2)}) collective-permute-start(bf16[192,2304]{1,0:T(8,128)(2,1)} %get-tuple-element.458), channel_id=1, source_target_pairs={{0,2},{1,3},{2,4},{3,5},{4,6},{5,7},{8,10},{9,11},{10,12},{11,13},... | collective-permute-start | bytes 2654216 | tf_op jit(solution)/shard_map/ppermute | solution.py:69
  105.8 41.8 %collective-permute-start.13 = (bf16[192,2304]{1,0:T(8,128)(2,1)}, bf16[192,2304]{1,0:T(8,128)(2,1)}, u32[]{:S(2)}, u32[]{:S(2)}) collective-permute-start(bf16[192,2304]{1,0:T(8,128)(2,1)} %get-tuple-element.458), channel_id=1, source_target_pairs={{2,0},{3,1},{4,2},{5,3},{6,4},{7,5},{10,8},{11,9},{12,10},{13,11},... | collective-permute-start | bytes 2654216 | tf_op jit(solution)/shard_map/ppermute | solution.py:73
  151.7 24.2 %collective-permute-start.17 = (bf16[192,2304]{1,0:T(8,128)(2,1)}, bf16[192,2304]{1,0:T(8,128)(2,1)}, u32[]{:S(2)}, u32[]{:S(2)}) collective-permute-start(bf16[192,2304]{1,0:T(8,128)(2,1)} %get-tuple-element.456), channel_id=1, source_target_pairs={{0,2},{1,3},{2,4},{3,5},{4,6},{5,7},{8,10},{9,11},{10,12},{11,13},... | collective-permute-start | bytes 2654216 | tf_op jit(solution)/shard_map/ppermute | solution.py:69
  157.4 23.6 %collective-permute-start.18 = (bf16[192,2304]{1,0:T(8,128)(2,1)}, bf16[192,2304]{1,0:T(8,128)(2,1)}, u32[]{:S(2)}, u32[]{:S(2)}) collective-permute-start(bf16[192,2304]{1,0:T(8,128)(2,1)} %get-tuple-element.457), channel_id=1, source_target_pairs={{2,0},{3,1},{4,2},{5,3},{6,4},{7,5},{10,8},{11,9},{12,10},{13,11},... | collective-permute-start | bytes 2654216 | tf_op jit(solution)/shard_map/ppermute | solution.py:73
  184.2 21.1 %collective-permute-start.20 = (bf16[192,2304]{1,0:T(8,128)(2,1)S(1)}, bf16[192,2304]{1,0:T(8,128)(2,1)S(1)}, u32[]{:S(2)}, u32[]{:S(2)}) collective-permute-start(bf16[192,2304]{1,0:T(8,128)(2,1)S(1)} %get-tuple-element.465), channel_id=1, source_target_pairs={{0,2},{1,3},{2,4},{3,5},{4,6},{5,7},{8,10},{9,11},{10,12},{11,13},... | collective-permute-start | bytes 2654216 | tf_op jit(solution)/shard_map/ppermute | solution.py:69
  186.1 23.4 %collective-permute-start.21 = (bf16[192,2304]{1,0:T(8,128)(2,1)S(1)}, bf16[192,2304]{1,0:T(8,128)(2,1)S(1)}, u32[]{:S(2)}, u32[]{:S(2)}) collective-permute-start(bf16[192,2304]{1,0:T(8,128)(2,1)S(1)} %get-tuple-element.466), channel_id=1, source_target_pairs={{2,0},{3,1},{4,2},{5,3},{6,4},{7,5},{10,8},{11,9},{12,10},{13,11},... | collective-permute-start | bytes 2654216 | tf_op jit(solution)/shard_map/ppermute | solution.py:73
  210.1 21.8 %collective-permute-start.23 = (bf16[192,2304]{1,0:T(8,128)(2,1)S(1)}, bf16[192,2304]{1,0:T(8,128)(2,1)S(1)}, u32[]{:S(2)}, u32[]{:S(2)}) collective-permute-start(bf16[192,2304]{1,0:T(8,128)(2,1)S(1)} %get-tuple-element.470), channel_id=1, source_target_pairs={{0,2},{1,3},{2,4},{3,5},{4,6},{5,7},{8,10},{9,11},{10,12},{11,13},... | collective-permute-start | bytes 2654216 | tf_op jit(solution)/shard_map/ppermute | solution.py:69
  213.5 22.6 %collective-permute-start.24 = (bf16[192,2304]{1,0:T(8,128)(2,1)S(1)}, bf16[192,2304]{1,0:T(8,128)(2,1)S(1)}, u32[]{:S(2)}, u32[]{:S(2)}) collective-permute-start(bf16[192,2304]{1,0:T(8,128)(2,1)S(1)} %get-tuple-element.471), channel_id=1, source_target_pairs={{2,0},{3,1},{4,2},{5,3},{6,4},{7,5},{10,8},{11,9},{12,10},{13,11},... | collective-permute-start | bytes 2654216 | tf_op jit(solution)/shard_map/ppermute | solution.py:73
  243.5 22.0 %collective-permute-start.27 = (bf16[192,2304]{1,0:T(8,128)(2,1)}, bf16[192,2304]{1,0:T(8,128)(2,1)}, u32[]{:S(2)}, u32[]{:S(2)}) collective-permute-start(bf16[192,2304]{1,0:T(8,128)(2,1)} %get-tuple-element.499), channel_id=1, source_target_pairs={{2,0},{3,1},{4,2},{5,3},{6,4},{7,5},{10,8},{11,9},{12,10},{13,11},... | collective-permute-start | bytes 2654216 | tf_op jit(solution)/shard_map/ppermute | solution.py:73
  315.9 24.3 %collective-permute-start.32 = (bf16[192,2304]{1,0:T(8,128)(2,1)}, bf16[192,2304]{1,0:T(8,128)(2,1)}, u32[]{:S(2)}, u32[]{:S(2)}) collective-permute-start(bf16[192,2304]{1,0:T(8,128)(2,1)} %get-tuple-element.516), channel_id=1, source_target_pairs={{0,2},{1,3},{2,4},{3,5},{4,6},{5,7},{8,10},{9,11},{10,12},{11,13},... | collective-permute-start | bytes 2654216 | tf_op jit(solution)/shard_map/ppermute | solution.py:69
  416.6 21.4 %collective-permute-start.40 = (bf16[192,2304]{1,0:T(8,128)(2,1)}, bf16[192,2304]{1,0:T(8,128)(2,1)}, u32[]{:S(2)}, u32[]{:S(2)}) collective-permute-start(bf16[192,2304]{1,0:T(8,128)(2,1)} %get-tuple-element.548), channel_id=1, source_target_pairs={{0,2},{1,3},{2,4},{3,5},{4,6},{5,7},{8,10},{9,11},{10,12},{11,13},... | collective-permute-start | bytes 2654216 | tf_op jit(solution)/shard_map/ppermute | solution.py:69
  482.4 26.9 %collective-permute-start.46 = (bf16[192,2304]{1,0:T(8,128)(2,1)}, bf16[192,2304]{1,0:T(8,128)(2,1)}, u32[]{:S(2)}, u32[]{:S(2)}) collective-permute-start(bf16[192,2304]{1,0:T(8,128)(2,1)} %get-tuple-element.580), channel_id=1, source_target_pairs={{0,2},{1,3},{2,4},{3,5},{4,6},{5,7},{8,10},{9,11},{10,12},{11,13},... | collective-permute-start | bytes 2654216 | tf_op jit(solution)/shard_map/ppermute | solution.py:69
  541.3 22.6 %collective-permute-start.50 = (bf16[192,2304]{1,0:T(8,128)(2,1)S(1)}, bf16[192,2304]{1,0:T(8,128)(2,1)S(1)}, u32[]{:S(2)}, u32[]{:S(2)}) collective-permute-start(bf16[192,2304]{1,0:T(8,128)(2,1)S(1)} %get-tuple-element.650), channel_id=1, source_target_pairs={{0,2},{1,3},{2,4},{3,5},{4,6},{5,7},{8,10},{9,11},{10,12},{11,13},... | collective-permute-start | bytes 2654216 | tf_op jit(solution)/shard_map/ppermute | solution.py:69
  542.8 21.1 %collective-permute-start.51 = (bf16[192,2304]{1,0:T(8,128)(2,1)S(1)}, bf16[192,2304]{1,0:T(8,128)(2,1)S(1)}, u32[]{:S(2)}, u32[]{:S(2)}) collective-permute-start(bf16[192,2304]{1,0:T(8,128)(2,1)S(1)} %get-tuple-element.650), channel_id=1, source_target_pairs={{2,0},{3,1},{4,2},{5,3},{6,4},{7,5},{10,8},{11,9},{12,10},{13,11},... | collective-permute-start | bytes 2654216 | tf_op jit(solution)/shard_map/ppermute | solution.py:73
  565.7 30.8 %collective-permute-start.52 = (bf16[192,2304]{1,0:T(8,128)(2,1)}, bf16[192,2304]{1,0:T(8,128)(2,1)}, u32[]{:S(2)}, u32[]{:S(2)}) collective-permute-start(bf16[192,2304]{1,0:T(8,128)(2,1)} %get-tuple-element.613), channel_id=1, source_target_pairs={{0,2},{1,3},{2,4},{3,5},{4,6},{5,7},{8,10},{9,11},{10,12},{11,13},... | collective-permute-start | bytes 2654216 | tf_op jit(solution)/shard_map/ppermute | solution.py:69
  571.5 25.0 %collective-permute-start.53 = (bf16[192,2304]{1,0:T(8,128)(2,1)}, bf16[192,2304]{1,0:T(8,128)(2,1)}, u32[]{:S(2)}, u32[]{:S(2)}) collective-permute-start(bf16[192,2304]{1,0:T(8,128)(2,1)} %get-tuple-element.614), channel_id=1, source_target_pairs={{2,0},{3,1},{4,2},{5,3},{6,4},{7,5},{10,8},{11,9},{12,10},{13,11},... | collective-permute-start | bytes 2654216 | tf_op jit(solution)/shard_map/ppermute | solution.py:73
  601.1 26.1 %collective-permute-start.54 = (bf16[192,2304]{1,0:T(8,128)(2,1)}, bf16[192,2304]{1,0:T(8,128)(2,1)}, u32[]{:S(2)}, u32[]{:S(2)}) collective-permute-start(bf16[192,2304]{1,0:T(8,128)(2,1)} %get-tuple-element.631), channel_id=1, source_target_pairs={{0,2},{1,3},{2,4},{3,5},{4,6},{5,7},{8,10},{9,11},{10,12},{11,13},... | collective-permute-start | bytes 2654216 | tf_op jit(solution)/shard_map/ppermute | solution.py:69
  630.9 33.7 %collective-permute-start.56 = (bf16[192,2304]{1,0:T(8,128)(2,1)S(1)}, bf16[192,2304]{1,0:T(8,128)(2,1)S(1)}, u32[]{:S(2)}, u32[]{:S(2)}) collective-permute-start(bf16[192,2304]{1,0:T(8,128)(2,1)S(1)} %get-tuple-element.648), channel_id=1, source_target_pairs={{0,2},{1,3},{2,4},{3,5},{4,6},{5,7},{8,10},{9,11},{10,12},{11,13},... | collective-permute-start | bytes 2654216 | tf_op jit(solution)/shard_map/ppermute | solution.py:69
  635.5 29.0 %collective-permute-start.57 = (bf16[192,2304]{1,0:T(8,128)(2,1)S(1)}, bf16[192,2304]{1,0:T(8,128)(2,1)S(1)}, u32[]{:S(2)}, u32[]{:S(2)}) collective-permute-start(bf16[192,2304]{1,0:T(8,128)(2,1)S(1)} %get-tuple-element.649), channel_id=1, source_target_pairs={{2,0},{3,1},{4,2},{5,3},{6,4},{7,5},{10,8},{11,9},{12,10},{13,11},... | collective-permute-start | bytes 2654216 | tf_op jit(solution)/shard_map/ppermute | solution.py:73
  667.7 36.7 %collective-permute-start.60 = (bf16[1152,2304]{1,0:T(8,128)(2,1)}, bf16[1152,2304]{1,0:T(8,128)(2,1)}, u32[]{:S(2)}, u32[]{:S(2)}) collective-permute-start(bf16[1152,2304]{1,0:T(8,128)(2,1)} %fusion.3), channel_id=1, source_target_pairs={{0,1},{1,0},{2,3},{3,2},{4,5},{5,4},{6,7},{7,6},{8,9},{9,8},{10,11... | collective-permute-start | bytes 15925256 | tf_op jit(solution)/shard_map/ppermute | solution.py:76
  667.8 46.7 %collective-permute-start.58 = (bf16[192,2304]{1,0:T(8,128)(2,1)S(1)}, bf16[192,2304]{1,0:T(8,128)(2,1)S(1)}, u32[]{:S(2)}, u32[]{:S(2)}) collective-permute-start(bf16[192,2304]{1,0:T(8,128)(2,1)S(1)} %get-tuple-element.697), channel_id=1, source_target_pairs={{0,2},{1,3},{2,4},{3,5},{4,6},{5,7},{8,10},{9,11},{10,12},{11,13},... | collective-permute-start | bytes 2654216 | tf_op jit(solution)/shard_map/ppermute | solution.py:69
  672.7 41.8 %collective-permute-start.59 = (bf16[192,2304]{1,0:T(8,128)(2,1)S(1)}, bf16[192,2304]{1,0:T(8,128)(2,1)}, u32[]{:S(2)}, u32[]{:S(2)}) collective-permute-start(bf16[192,2304]{1,0:T(8,128)(2,1)S(1)} %get-tuple-element.697), channel_id=1, source_target_pairs={{2,0},{3,1},{4,2},{5,3},{6,4},{7,5},{10,8},{11,9},{12,10},{13,11},... | collective-permute-start | bytes 2654216 | tf_op jit(solution)/shard_map/ppermute | solution.py:73
  717.6 24.8 %collective-permute-start.61 = (bf16[192,2304]{1,0:T(8,128)(2,1)}, bf16[192,2304]{1,0:T(8,128)(2,1)}, u32[]{:S(2)}, u32[]{:S(2)}) collective-permute-start(bf16[192,2304]{1,0:T(8,128)(2,1)} %get-tuple-element.680), channel_id=1, source_target_pairs={{0,2},{1,3},{2,4},{3,5},{4,6},{5,7},{8,10},{9,11},{10,12},{11,13},... | collective-permute-start | bytes 2654216 | tf_op jit(solution)/shard_map/ppermute | solution.py:69
  723.1 24.0 %collective-permute-start.62 = (bf16[192,2304]{1,0:T(8,128)(2,1)}, bf16[192,2304]{1,0:T(8,128)(2,1)}, u32[]{:S(2)}, u32[]{:S(2)}) collective-permute-start(bf16[192,2304]{1,0:T(8,128)(2,1)} %get-tuple-element.681), channel_id=1, source_target_pairs={{2,0},{3,1},{4,2},{5,3},{6,4},{7,5},{10,8},{11,9},{12,10},{13,11},... | collective-permute-start | bytes 2654216 | tf_op jit(solution)/shard_map/ppermute | solution.py:73
  751.7 377.0 %all-reduce.6.cloned.1.call-start = ((), (), s32[]{:S(2)}) async-start(), calls=%async_computation | async-start | bytes 10616832 | tf_op jit(solution)/shard_map/psum | solution.py:838
  759.8 23.5 %collective-permute-start.65 = (bf16[192,2304]{1,0:T(8,128)(2,1)}, bf16[192,2304]{1,0:T(8,128)(2,1)}, u32[]{:S(2)}, u32[]{:S(2)}) collective-permute-start(bf16[192,2304]{1,0:T(8,128)(2,1)} %get-tuple-element.690), channel_id=1, source_target_pairs={{2,0},{3,1},{4,2},{5,3},{6,4},{7,5},{10,8},{11,9},{12,10},{13,11},... | collective-permute-start | bytes 2654216 | tf_op jit(solution)/shard_map/ppermute | solution.py:73
  786.8 24.1 %collective-permute-start.67 = (bf16[192,2304]{1,0:T(8,128)(2,1)S(1)}, bf16[192,2304]{1,0:T(8,128)(2,1)S(1)}, u32[]{:S(2)}, u32[]{:S(2)}) collective-permute-start(bf16[192,2304]{1,0:T(8,128)(2,1)S(1)} %get-tuple-element.695), channel_id=1, source_target_pairs={{0,2},{1,3},{2,4},{3,5},{4,6},{5,7},{8,10},{9,11},{10,12},{11,13},... | collective-permute-start | bytes 2654216 | tf_op jit(solution)/shard_map/ppermute | solution.py:69
  788.9 22.0 %collective-permute-start.68 = (bf16[192,2304]{1,0:T(8,128)(2,1)S(1)}, bf16[192,2304]{1,0:T(8,128)(2,1)S(1)}, u32[]{:S(2)}, u32[]{:S(2)}) collective-permute-start(bf16[192,2304]{1,0:T(8,128)(2,1)S(1)} %get-tuple-element.696), channel_id=1, source_target_pairs={{2,0},{3,1},{4,2},{5,3},{6,4},{7,5},{10,8},{11,9},{12,10},{13,11},... | collective-permute-start | bytes 2654216 | tf_op jit(solution)/shard_map/ppermute | solution.py:73
  815.3 21.5 %collective-permute-start.69 = (bf16[192,2304]{1,0:T(8,128)(2,1)S(1)}, bf16[192,2304]{1,0:T(8,128)(2,1)S(1)}, u32[]{:S(2)}, u32[]{:S(2)}) collective-permute-start(bf16[192,2304]{1,0:T(8,128)(2,1)S(1)} %get-tuple-element.742), channel_id=1, source_target_pairs={{0,2},{1,3},{2,4},{3,5},{4,6},{5,7},{8,10},{9,11},{10,12},{11,13},... | collective-permute-start | bytes 2654216 | tf_op jit(solution)/shard_map/ppermute | solution.py:69
  897.8 24.9 %collective-permute-start.76 = (bf16[192,2304]{1,0:T(8,128)(2,1)S(1)}, bf16[192,2304]{1,0:T(8,128)(2,1)}, u32[]{:S(2)}, u32[]{:S(2)}) collective-permute-start(bf16[192,2304]{1,0:T(8,128)(2,1)S(1)} %get-tuple-element.740), channel_id=1, source_target_pairs={{0,2},{1,3},{2,4},{3,5},{4,6},{5,7},{8,10},{9,11},{10,12},{11,13},... | collective-permute-start | bytes 2654216 | tf_op jit(solution)/shard_map/ppermute | solution.py:69
  900.1 22.5 %collective-permute-start.77 = (bf16[192,2304]{1,0:T(8,128)(2,1)S(1)}, bf16[192,2304]{1,0:T(8,128)(2,1)}, u32[]{:S(2)}, u32[]{:S(2)}) collective-permute-start(bf16[192,2304]{1,0:T(8,128)(2,1)S(1)} %get-tuple-element.741), channel_id=1, source_target_pairs={{2,0},{3,1},{4,2},{5,3},{6,4},{7,5},{10,8},{11,9},{12,10},{13,11},... | collective-permute-start | bytes 2654216 | tf_op jit(solution)/shard_map/ppermute | solution.py:73
  959.2 24.3 %collective-permute-start.79 = (bf16[208,2304]{1,0:T(8,128)(2,1)}, bf16[208,2304]{1,0:T(8,128)(2,1)S(1)}, u32[]{:S(2)}, u32[]{:S(2)}) collective-permute-start(bf16[208,2304]{1,0:T(8,128)(2,1)} %pad_maximum_fusion.12), channel_id=1, source_target_pairs={{0,2},{1,3},{8,10},{9,11},{16,18},{17,19},{24,26},{25,27}} | collective-permute-start | bytes 2875400 | tf_op jit(solution)/shard_map/ppermute | solution.py:69
  984.3 24.3 %collective-permute-start.81 = (bf16[208,2304]{1,0:T(8,128)(2,1)S(1)}, bf16[208,2304]{1,0:T(8,128)(2,1)S(1)}, u32[]{:S(2)}, u32[]{:S(2)}) collective-permute-start(bf16[208,2304]{1,0:T(8,128)(2,1)S(1)} %get-tuple-element.794), channel_id=1, source_target_pairs={{0,2},{1,3},{2,4},{3,5},{8,10},{9,11},{10,12},{11,13},{16,18},{17,... | collective-permute-start | bytes 2875400 | tf_op jit(solution)/shard_map/ppermute | solution.py:69
  1009.2 31.3 %collective-permute-start.93 = (bf16[384,1152]{1,0:T(8,128)(2,1)S(1)}, bf16[384,1152]{1,0:T(8,128)(2,1)S(1)}, u32[]{:S(2)}, u32[]{:S(2)}) collective-permute-start(bf16[384,1152]{1,0:T(8,128)(2,1)S(1)} %constant_dynamic-slice_fusion.1), channel_id=1, source_target_pairs={{0,16},{8,24},{16,0},{24,8},{1,17},{9,25},{17,1},{25,9},{2,18},{10... | collective-permute-start | bytes 2654216 | tf_op jit(solution)/shard_map/ppermute | solution.py:841
  1010.6 32.6 %collective-permute-start.89 = (bf16[384,1152]{1,0:T(8,128)(2,1)S(1)}, bf16[384,1152]{1,0:T(8,128)(2,1)S(1)}, u32[]{:S(2)}, u32[]{:S(2)}) collective-permute-start(bf16[384,1152]{1,0:T(8,128)(2,1)S(1)} %constant_dynamic-slice_fusion.3), channel_id=1, source_target_pairs={{0,8},{8,0},{16,24},{24,16},{1,9},{9,1},{17,25},{25,17},{2,10},{10... | collective-permute-start | bytes 2654216 | tf_op jit(solution)/shard_map/ppermute | solution.py:841
  1012.0 32.8 %collective-permute-start.87 = (bf16[208,2304]{1,0:T(8,128)(2,1)S(1)}, bf16[208,2304]{1,0:T(8,128)(2,1)S(1)}, u32[]{:S(2)}, u32[]{:S(2)}) collective-permute-start(bf16[208,2304]{1,0:T(8,128)(2,1)S(1)} %get-tuple-element.802), channel_id=1, source_target_pairs={{0,2},{1,3},{2,4},{3,5},{4,6},{5,7},{8,10},{9,11},{10,12},{11,13},... | collective-permute-start | bytes 2875400 | tf_op jit(solution)/shard_map/ppermute | solution.py:69
  1020.3 24.5 %collective-permute-start.88 = (bf16[208,2304]{1,0:T(8,128)(2,1)S(1)}, bf16[208,2304]{1,0:T(8,128)(2,1)S(1)}, u32[]{:S(2)}, u32[]{:S(2)}) collective-permute-start(bf16[208,2304]{1,0:T(8,128)(2,1)S(1)} %get-tuple-element.803), channel_id=1, source_target_pairs={{2,0},{3,1},{4,2},{5,3},{6,4},{7,5},{10,8},{11,9},{12,10},{13,11},... | collective-permute-start | bytes 2875400 | tf_op jit(solution)/shard_map/ppermute | solution.py:73
  1041.7 22.5 %collective-permute-start.94 = (bf16[192,1152]{1,0:T(8,128)(2,1)}, bf16[192,1152]{1,0:T(8,128)(2,1)}, u32[]{:S(2)}, u32[]{:S(2)}) collective-permute-start(bf16[192,1152]{1,0:T(8,128)(2,1)} %constant_dynamic-slice_fusion), channel_id=1, source_target_pairs={{0,8},{8,0},{16,24},{24,16},{1,9},{9,1},{17,25},{25,17},{2,10},{10... | collective-permute-start | bytes 1327112 | tf_op jit(solution)/shard_map/ppermute | solution.py:841
  1044.3 22.9 %collective-permute-start.90 = (bf16[192,1152]{1,0:T(8,128)(2,1)}, bf16[192,1152]{1,0:T(8,128)(2,1)}, u32[]{:S(2)}, u32[]{:S(2)}) collective-permute-start(bf16[192,1152]{1,0:T(8,128)(2,1)} %constant_dynamic-slice_fusion.2), channel_id=1, source_target_pairs={{0,16},{8,24},{16,0},{24,8},{1,17},{9,25},{17,1},{25,9},{2,18},{10... | collective-permute-start | bytes 1327112 | tf_op jit(solution)/shard_map/ppermute | solution.py:841
  1064.0 25.7 %collective-permute-start.99 = (f32[4,288]{1,0:T(4,128)S(1)}, f32[4,288]{1,0:T(4,128)S(1)}, u32[]{:S(2)}, u32[]{:S(2)}) collective-permute-start(f32[4,288]{1,0:T(4,128)S(1)} %add.445), channel_id=1, source_target_pairs={{0,16},{8,24},{16,0},{24,8},{1,17},{9,25},{17,1},{25,9},{2,18},{10... | collective-permute-start | bytes 13832 | tf_op jit(solution)/shard_map/ppermute | solution.py:841
  1080.2 42.7 %collective-permute-start.96 = (bf16[384,1152]{1,0:T(8,128)(2,1)S(1)}, bf16[384,1152]{1,0:T(8,128)(2,1)S(1)}, u32[]{:S(2)}, u32[]{:S(2)}) collective-permute-start(bf16[384,1152]{1,0:T(8,128)(2,1)S(1)} %pad_maximum_fusion.14), channel_id=1, source_target_pairs={{0,16},{8,24},{16,0},{24,8},{1,17},{9,25},{17,1},{25,9},{2,18},{10... | collective-permute-start | bytes 2654216 | tf_op jit(solution)/shard_map/ppermute | solution.py:841
  1088.3 34.9 %collective-permute-start.92 = (bf16[384,1152]{1,0:T(8,128)(2,1)S(1)}, bf16[384,1152]{1,0:T(8,128)(2,1)S(1)}, u32[]{:S(2)}, u32[]{:S(2)}) collective-permute-start(bf16[384,1152]{1,0:T(8,128)(2,1)S(1)} %pad_maximum_fusion.13), channel_id=1, source_target_pairs={{0,8},{8,0},{16,24},{24,16},{1,9},{9,1},{17,25},{25,17},{2,10},{10... | collective-permute-start | bytes 2654216 | tf_op jit(solution)/shard_map/ppermute | solution.py:841
  (299 other events, 3198.3 us)
Sparse Core Ops, SparseCore 0:
  751.8 207.3 all-reduce.7
  962.5 163.4 all-reduce.5

commit v6 on v5

--- a/solution.py
+++ b/solution.py
@@ -605,7 +605,7 @@
         in_specs=[pl.BlockSpec((m, depth), lambda i: (0, 0))] * len(lefts)
         + [pl.BlockSpec((depth, tile), lambda i: (0, i))] * len(weights),
         out_specs=pl.BlockSpec((m, tile), lambda i: (0, i)),
-        compiler_params=pltpu.CompilerParams(vmem_limit_bytes=(26 if m <= 384 else 36) * 1024 * 1024),
+        compiler_params=pltpu.CompilerParams(vmem_limit_bytes=(44 if m <= 384 else 36) * 1024 * 1024),
         cost_estimate=light,
     )(*lefts, *weights)
 
@@ -960,8 +960,14 @@
         )
         yield lasts, ex
 
-    steps = back_phase(a, low_a, b.feed_down, (b.product[1],))
-    (out,), ex = next(steps)
+    def b_down(product, *pieces):
+        merged = [join(pieces[i : i + 2]) for i in range(0, len(pieces), 2)]
+        return (*b.feed_down(product), *merged)
+
+    steps = back_phase(
+        a, low_a, b_down, [b.product[1]] + b.gelu + b.slope + b.product + b.hidden_ff
+    )
+    (out, b_gelu, b_slope, b_product, b_hidden_ff), ex = next(steps)
     ex.give(b.out_near, out)
     next(steps)
     low_b = b.after_feed(ex.terms())
@@ -983,19 +989,13 @@
     ex.give(a.out_near, out)
 
     def part_work(*pieces):
-        return grad_part(pieces[:2], pieces[2:4]), grad_part(pieces[4:6], pieces[6:])
-
-    part_down, part_gate = ex.step(
-        part_work, a.product + a.feed_low + a.gate_back + a.hidden_ff
-    )
-
-    def part_more(*pieces):
-        return (grad_part(pieces[:2], pieces[2:4]),) + tuple(
-            join(pieces[i : i + 2]) for i in range(4, 12, 2)
+        return tuple(
+            grad_part(pieces[i : i + 2], pieces[i + 2 : i + 4]) for i in range(0, len(pieces), 4)
         )
 
-    part_up, b_gelu, b_slope, b_product, b_hidden_ff = ex.step(
-        part_more, a.up_back + a.hidden_ff + b.gelu + b.slope + b.product + b.hidden_ff
+    (part_down,) = ex.step(part_work, a.product + a.feed_low)
+    part_gate, part_up = ex.step(
+        part_work, a.gate_back + a.hidden_ff + a.up_back + a.hidden_ff
     )
     for _ in range(chips - 4):
         ex.step()
@@ -1019,18 +1019,16 @@
     out, gate_other, down_grad = ex.step(b_feed_in, (b_gate_back, b_up_back, down_other))
     ex.give(out)
 
-    def gate_work(gate_back, up_back, gate_other):
-        return (
-            grad_other(up_back, b_hidden_ff, part_up),
-            grad_own(gate_back, b_hidden_ff, part_gate, gate_other),
-        )
-
-    up_other, gate_grad = ex.step(gate_work, (b_gate_back, b_up_back, gate_other))
-
-    def up_work(up_back, up_other):
-        return (grad_own(up_back, b_hidden_ff, part_up, up_other),)
-
-    (up_grad,) = ex.step(up_work, (b_up_back, up_other))
+    def gate_work(gate_back, gate_other):
+        return (grad_own(gate_back, b_hidden_ff, part_gate, gate_other),)
+
+    (gate_grad,) = ex.step(gate_work, (b_gate_back, gate_other))
+
+    def up_work(up_back, part):
+        other = grad_other(up_back, b_hidden_ff, part)
+        return (grad_own(up_back, b_hidden_ff, part, other),)
+
+    (up_grad,) = ex.step(up_work, (b_up_back, part_up))
     early_sums = data_sum((down_grad, gate_grad), 0)
     up_sum = data_sum(up_grad, 1)
     for _ in range(chips - 4):

time: 1150 us -> 1130 us (0.983)
  local copies, waits for them, and re-layouts: 108 us -> 81.7 us
  Pallas kernels: 222 us -> 237 us
  starting transfers between devices: 185 us -> 172 us
    unnamed x510 -> x530, local copies, waits for them, and re-layouts: 80.3 us -> 57.6 us
    ppermute x34, starting transfers between devices: 127 us -> 113 us  [right(): return lax.ppermute(block, 'ctx', self.pairs(1, low, high))]
  transfers between devices with their start and end apart: 102 -> 102, of which waited for: 50 -> 59; matrix products, arithmetic and copies ran while one was open for 22% -> 21% of each run, Pallas kernels for 18% -> 20%
where the time goes in v6:
time: 1130 us; the launch traced here: 1120 us
  waiting for transfers between devices  339 us (30%)
  Pallas kernels  237 us (21%)
  starting transfers between devices  172 us (15%)
  other arithmetic  149 us (13%)
  matrix products  125 us (11%)
  local copies, waits for them, and re-layouts  81.7 us (7%)
  between operations  18.4 us (2%)
    ppermute x34, waiting for transfers between devices, right(): return lax.ppermute(block, 'ctx', self.pairs(1, low, high))  131 us
    dot_general x11, matrix products, tn(): lax.dot_general(left_side, right_side, (((0,), (0,)), ((), ())), preferre...  115 us
    ppermute x34, starting transfers between devices, right(): return lax.ppermute(block, 'ctx', self.pairs(1, low, high))  113 us
    ppermute x34, waiting for transfers between devices, left(): return lax.ppermute(block, 'ctx', self.pairs(-1, n - high, n - low))  105 us
    ppermute x10, waiting for transfers between devices, swapped(): return lax.ppermute(block, 'dp', [(i, i ^ bit) for i in range(data)])  73.6 us
    pallas_call x7, Pallas kernels, mix(): pl.pallas_call(mix_kernel, out_shape=jax.ShapeDtypeStruct((m, n), bf16),...  73.1 us
    unnamed x530, local copies, waits for them, and re-layouts  57.6 us
    pallas_call x4, Pallas kernels, gate_up(): pl.pallas_call(gate_up_kernel, out_shape=(jax.ShapeDtypeStruct((m, n), bf...  49.4 us
  transfers between devices with their start and end apart: 102, of which 59 were waited for; matrix products, arithmetic and copies ran while one was open for 21% of the time, Pallas kernels for 20%

profile of v6, /device:TPU:0, one launch (start us, length us, event | category | flops | bytes accessed | tf_op | source)
XLA Modules:
  0.0 1121.4 jit_solution(12695740589001282077)
XLA Ops:
  18.2 19.2 %collective-permute-done = bf16[208,2304]{1,0:T(8,128)(2,1)} collective-permute-done((bf16[208,2304]{1,0:T(8,128)(2,1)}, bf16[208,2304]{1,0:T(8,128)(2,1)}, u32[]{:S(2)}, u32[]{:S(2)}) %collective-permute-start) | collective-permute-done | bytes 958496 | tf_op jit(solution)/shard_map/ppermute | solution.py:69
  46.1 9.4 pad_maximum_fusion.gate_ref.refs_2_
  59.0 11.2 %collective-permute-done.4 = bf16[208,2304]{1,0:T(8,128)(2,1)} collective-permute-done((bf16[208,2304]{1,0:T(8,128)(2,1)}, bf16[208,2304]{1,0:T(8,128)(2,1)}, u32[]{:S(2)}, u32[]{:S(2)}) %collective-permute-start.4) | collective-permute-done | bytes 958496 | tf_op jit(solution)/shard_map/ppermute | solution.py:73
  82.5 11.4 %pad_maximum_fusion.1.up_ref.refs_3_ = bf16[2304,2304]{1,0:T(8,128)(2,1)} fusion(bf16[1152,2304]{1,0:T(8,128)(2,1)} %collective-permute-done.11, bf16[1152,2304]{1,0:T(8,128)(2,1)S(1)} %bitcast.132), kind=kLoop, calls=%fused_computation.19 | loop fusion | flops 21233664 | bytes 21233664 | tf_op jit(solution)/shard_map/concatenate | solution.py:702
  93.9 7.9 collective-permute-done.9
  138.0 7.9 shard_map.248
  168.8 7.5 collective-permute-done.17
  193.2 7.5 pad_maximum_fusion.2.refs_1_.down_ref
  221.0 11.1 collective-permute-done.23.l_ref
  245.2 9.4 shard_map.252
  271.7 12.3 %shard_map.253 = (bf16[384,2304]{1,0:T(8,128)(2,1)S(1)}, bf16[384,2304]{1,0:T(8,128)(2,1)S(1)}, bf16[384,2304]{1,0:T(8,128)(2,1)S(1)}) custom-call(bf16[384,2304]{1,0:T(8,128)(2,1)S(1)} %constant_dynamic-update-slice_fusion.8.h_ref, bf16[2304,2304]{1,0:T(8,128)(2,1)S(1)} %bitcast.95, bf16[2304,2304]{1,0:T(8,128)(2,1)} %pad_maximum_fusion.1.up_ref.refs_3_), custom_call_target="tpu_custom_call" | custom-call | flops 1024 | bytes 1024 | tf_op jit(solution)/shard_map/pallas_call | solution.py:580
  295.1 7.2 shard_map.254.p_ref
  302.2 7.5 collective-permute-done.30
  320.8 12.4 %shard_map.255 = (bf16[384,2304]{1,0:T(8,128)(2,1)S(1)}, bf16[384,2304]{1,0:T(8,128)(2,1)S(1)}, bf16[384,2304]{1,0:T(8,128)(2,1)S(1)}) custom-call(bf16[384,2304]{1,0:T(8,128)(2,1)S(1)} %constant_dynamic-update-slice_fusion.10.h_ref, bf16[2304,2304]{1,0:T(8,128)(2,1)S(1)} %bitcast.95, bf16[2304,2304]{1,0:T(8,128)(2,1)} %pad_maximum_fusion.1.up_ref.refs_3_), custom_call_target="tpu_custom_call" | custom-call | flops 1024 | bytes 1024 | tf_op jit(solution)/shard_map/pallas_call | solution.py:580
  346.8 7.2 shard_map.257
  367.4 12.4 %shard_map.258 = (bf16[384,2304]{1,0:T(8,128)(2,1)S(1)}, bf16[384,2304]{1,0:T(8,128)(2,1)S(1)}, bf16[384,2304]{1,0:T(8,128)(2,1)S(1)}) custom-call(bf16[384,2304]{1,0:T(8,128)(2,1)S(1)} %constant_dynamic-update-slice_fusion.12.h_ref, bf16[2304,2304]{1,0:T(8,128)(2,1)S(1)} %bitcast.95, bf16[2304,2304]{1,0:T(8,128)(2,1)} %pad_maximum_fusion.1.up_ref.refs_3_), custom_call_target="tpu_custom_call" | custom-call | flops 1024 | bytes 1024 | tf_op jit(solution)/shard_map/pallas_call | solution.py:580
  388.9 7.2 shard_map.259.p_ref
  411.4 12.4 %shard_map.260 = (bf16[384,2304]{1,0:T(8,128)(2,1)S(1)}, bf16[384,2304]{1,0:T(8,128)(2,1)S(1)}, bf16[384,2304]{1,0:T(8,128)(2,1)S(1)}) custom-call(bf16[384,2304]{1,0:T(8,128)(2,1)S(1)} %constant_dynamic-update-slice_fusion.14.h_ref, bf16[2304,2304]{1,0:T(8,128)(2,1)S(1)} %bitcast.95, bf16[2304,2304]{1,0:T(8,128)(2,1)} %pad_maximum_fusion.1.up_ref.refs_3_), custom_call_target="tpu_custom_call" | custom-call | flops 1024 | bytes 1024 | tf_op jit(solution)/shard_map/pallas_call | solution.py:580
  434.7 7.2 shard_map.262
  484.2 12.1 %shard_map.264.p_ref = bf16[384,2304]{1,0:T(8,128)(2,1)S(1)} custom-call(bf16[384,2304]{1,0:T(8,128)(2,1)S(1)} %copy-done.86, bf16[384,2304]{1,0:T(8,128)(2,1)S(1)} %copy-done.83, bf16[2304,2304]{1,0:T(8,128)(2,1)} %pad_maximum_fusion.gate_ref.refs_2_, bf16[2304,2304]{1,0:T(8,128)(2,1)} %pad_maximum_fusion.1.up_ref.refs_3_), custom_call_target="tpu_custom_call" | custom-call | flops 1024 | bytes 1024 | tf_op jit(solution)/shard_map/pallas_call | solution.py:601
  513.7 6.9 collective-permute-done.48.l_ref
  533.1 12.2 %shard_map.267 = bf16[384,2304]{1,0:T(8,128)(2,1)S(1)} custom-call(bf16[384,2304]{1,0:T(8,128)(2,1)S(1)} %copy-done.92, bf16[384,2304]{1,0:T(8,128)(2,1)S(1)} %copy-done.89, bf16[2304,2304]{1,0:T(8,128)(2,1)} %pad_maximum_fusion.gate_ref.refs_2_, bf16[2304,2304]{1,0:T(8,128)(2,1)} %pad_maximum_fusion.1.up_ref.refs_3_), custom_call_target="tpu_custom_call" | custom-call | flops 1024 | bytes 1024 | tf_op jit(solution)/shard_map/pallas_call | solution.py:601
  553.1 11.1 convolution_convert_fusion.2
  577.9 11.0 convolution_convert_fusion.1
  588.9 11.2 convolution_convert_fusion
  611.6 11.7 %shard_map.268 = (bf16[768,2304]{1,0:T(8,128)(2,1)S(1)}, bf16[768,2304]{1,0:T(8,128)(2,1)S(1)}) custom-call(bf16[768,2304]{1,0:T(8,128)(2,1)S(1)} %constant_dynamic-update-slice_fusion.20.low_ref, bf16[2304,2304]{1,0:T(8,128)(2,1)} %pad_maximum_fusion.2.refs_1_.down_ref, bf16[768,2304]{1,0:T(8,128)(2,1)S(1)} %copy-done.12, bf16[768,2304]{1,0:T(8,128)(2,1)S(1)} %copy-done.13), custom_call_target="tpu_custom_call" | custom-call | flops 1024 | bytes 1024 | tf_op jit(solution)/shard_map/pallas_call | solution.py:624
  623.3 10.2 fusion.3
  644.3 20.2 %shard_map.270.p_ref = bf16[768,2304]{1,0:T(8,128)(2,1)S(1)} custom-call(bf16[768,2304]{1,0:T(8,128)(2,1)S(1)} %get-tuple-element.680.refs_0_, bf16[768,2304]{1,0:T(8,128)(2,1)S(1)} %get-tuple-element.687.refs_1_, bf16[2304,2304]{1,0:T(8,128)(2,1)} %pad_maximum_fusion.gate_ref.refs_2_, bf16[2304,2304]{1,0:T(8,128)(2,1)} %pad_maximum_fusion.1.up_ref.refs_3_), custom_call_target="tpu_custom_call" | custom-call | flops 1024 | bytes 1024 | tf_op jit(solution)/shard_map/pallas_call | solution.py:601
  664.6 9.6 fusion.4
  674.2 9.5 fusion.5
  694.6 9.5 fusion.6
  719.7 9.1 fusion.8
  738.2 13.3 %fusion.7 = bf16[1152,2304]{1,0:T(8,128)(2,1)} fusion(bf16[768,2304]{1,0:T(8,128)(2,1)} %pad_maximum_fusion.6, bf16[1152,2304]{1,0:T(8,128)(2,1)} %collective-permute-done.66, bf16[2304,2304]{1,0:T(8,128)(2,1)} %convolution_convert_fusion, bf16[768,2304]{1,0:T(8,128)(2,1)} %copy-done.72), kind=kOutput, calls=%fused_computation.16 | convolution fusion | flops 4090134528 | bytes 21233664 | tf_op jit(solution)/shard_map/dot_general | solution.py:39
  772.3 15.1 %shard_map.271 = (bf16[4,192,512]{2,1,0:T(8,128)(2,1)S(1)}, f32[4,192,512]{2,1,0:T(8,128)S(1)}, bf16[4,192,512]{2,1,0:T(8,128)(2,1)S(1)}) custom-call(s32[9]{0:T(128)S(1)} %copy-done.168, bf16[2,192,512]{2,1,0:T(8,128)(2,1)S(1)} %bitcast.112, bf16[2,192,512]{2,1,0:T(8,128)(2,1)S(1)} %bitcast.114, bf16[2,192,512]{2,1,0:T(8,128)(2,1)} %bitcast.18.refs_2_, ...), custom_call_target="tpu_custom_call" | custom-call | flops 1024 | bytes 1024 | tf_op jit(solution)/shard_map/pallas_call | solution.py:361
  805.3 8.8 collective-permute-done.69
  823.3 15.8 %collective-permute-done.72 = bf16[192,2304]{1,0:T(8,128)(2,1)S(1)} collective-permute-done((bf16[192,2304]{1,0:T(8,128)(2,1)}, bf16[192,2304]{1,0:T(8,128)(2,1)S(1)}, u32[]{:S(2)}, u32[]{:S(2)}) %collective-permute-start.72) | collective-permute-done | bytes 884768 | tf_op jit(solution)/shard_map/ppermute | solution.py:69
  856.4 9.4 collective-permute-done.74
  883.3 18.1 %shard_map.274 = (bf16[4,192,512]{2,1,0:T(8,128)(2,1)S(1)}, f32[4,192,512]{2,1,0:T(8,128)S(1)}, bf16[4,192,512]{2,1,0:T(8,128)(2,1)}) custom-call(s32[9]{0:T(128)S(1)} %copy-done.166, bf16[2,192,512]{2,1,0:T(8,128)(2,1)S(1)} %bitcast.105, bf16[2,192,512]{2,1,0:T(8,128)(2,1)S(1)} %bitcast.107, bf16[2,192,512]{2,1,0:T(8,128)(2,1)} %bitcast.22.refs_2_, ...), custom_call_target="tpu_custom_call" | custom-call | flops 1024 | bytes 1024 | tf_op jit(solution)/shard_map/pallas_call | solution.py:361
  901.7 9.1 fusion.24
  927.0 9.8 all-reduce.8.cloned.1.call-done
  941.2 11.6 %fusion.21 = bf16[1024,2304]{1,0:T(8,128)(2,1)S(1)} fusion(bf16[384,2304]{1,0:T(8,128)(2,1)} %copy-done.174, bf16[384,2304]{1,0:T(8,128)(2,1)} %copy-done.173, bf16[384,2304]{1,0:T(8,128)(2,1)S(1)} %copy-done.172, bf16[384,2304]{1,0:T(8,128)(2,1)S(1)} %copy-done.170, bf16[768,1024]{1,0:T(8,128)(2,1)} %copy-done.176, bf16[768,1024]{1,0:T(8,128)(2,1)} %copy-done.175), kind=kOutput, calls=%fused_computation.33 | convolution fusion | flops 7284719616 | bytes 14942208 | tf_op jit(solution)/shard_map/dot_general | solution.py:39
  952.7 8.4 collective-permute-done.79
  989.6 8.3 collective-permute-start.87
  999.4 18.8 %collective-permute-done.93 = bf16[384,1152]{1,0:T(8,128)(2,1)S(1)} collective-permute-done((bf16[384,1152]{1,0:T(8,128)(2,1)S(1)}, bf16[384,1152]{1,0:T(8,128)(2,1)S(1)}, u32[]{:S(2)}, u32[]{:S(2)}) %collective-permute-start.93) | collective-permute-done | bytes 884768 | tf_op jit(solution)/shard_map/ppermute | solution.py:841
  1047.6 10.1 collective-permute-done.95
  1058.8 6.9 collective-permute-done.91
  1067.3 33.2 %collective-permute-done.96 = bf16[384,1152]{1,0:T(8,128)(2,1)S(1)} collective-permute-done((bf16[384,1152]{1,0:T(8,128)(2,1)S(1)}, bf16[384,1152]{1,0:T(8,128)(2,1)S(1)}, u32[]{:S(2)}, u32[]{:S(2)}) %collective-permute-start.96) | collective-permute-done | bytes 884768 | tf_op jit(solution)/shard_map/ppermute | solution.py:841
  1106.4 7.4 convert_element_type.659
  (901 shorter events, 566.7 us)
Async XLA Ops:
  7.3 929.6 %all-reduce.8.cloned.1.call-start = ((), (), s32[]{:S(2)}) async-start(), calls=%async_computation.1 | async-start | bytes 21233664 | tf_op jit(solution)/shard_map/psum | solution.py:838
  11.0 31.5 %collective-permute-start.2 = (bf16[1152,2304]{1,0:T(8,128)(2,1)}, bf16[1152,2304]{1,0:T(8,128)(2,1)}, u32[]{:S(2)}, u32[]{:S(2)}) collective-permute-start(bf16[1152,2304]{1,0:T(8,128)(2,1)} %param.22), channel_id=1, source_target_pairs={{0,1},{1,0},{2,3},{3,2},{4,5},{5,4},{6,7},{7,6},{8,9},{9,8},{10,11... | collective-permute-start | bytes 15925256 | tf_op jit(solution)/shard_map/ppermute | solution.py:76
  11.5 25.9 %collective-permute-start = (bf16[208,2304]{1,0:T(8,128)(2,1)}, bf16[208,2304]{1,0:T(8,128)(2,1)}, u32[]{:S(2)}, u32[]{:S(2)}) collective-permute-start(bf16[208,2304]{1,0:T(8,128)(2,1)} %fusion.104), channel_id=1, source_target_pairs={{0,2},{1,3},{2,4},{3,5},{4,6},{5,7},{8,10},{9,11},{10,12},{11,13},... | collective-permute-start | bytes 2875400 | tf_op jit(solution)/shard_map/ppermute | solution.py:69
  16.9 25.6 %collective-permute-start.1 = (bf16[208,2304]{1,0:T(8,128)(2,1)}, bf16[208,2304]{1,0:T(8,128)(2,1)}, u32[]{:S(2)}, u32[]{:S(2)}) collective-permute-start(bf16[208,2304]{1,0:T(8,128)(2,1)} %fusion.104), channel_id=1, source_target_pairs={{2,0},{3,1},{4,2},{5,3},{6,4},{7,5},{10,8},{11,9},{12,10},{13,11},... | collective-permute-start | bytes 2875400 | tf_op jit(solution)/shard_map/ppermute | solution.py:73
  44.1 26.2 %collective-permute-start.4 = (bf16[208,2304]{1,0:T(8,128)(2,1)}, bf16[208,2304]{1,0:T(8,128)(2,1)}, u32[]{:S(2)}, u32[]{:S(2)}) collective-permute-start(bf16[208,2304]{1,0:T(8,128)(2,1)} %collective-permute-done.1), channel_id=1, source_target_pairs={{2,0},{3,1},{4,2},{5,3},{10,8},{11,9},{12,10},{13,11},{18,16},{19,... | collective-permute-start | bytes 2875400 | tf_op jit(solution)/shard_map/ppermute | solution.py:73
  76.2 25.5 %collective-permute-start.9 = (bf16[208,2304]{1,0:T(8,128)(2,1)}, bf16[208,2304]{1,0:T(8,128)(2,1)S(1)}, u32[]{:S(2)}, u32[]{:S(2)}) collective-permute-start(bf16[208,2304]{1,0:T(8,128)(2,1)} %collective-permute-done.4), channel_id=1, source_target_pairs={{2,0},{3,1},{10,8},{11,9},{18,16},{19,17},{26,24},{27,25}} | collective-permute-start | bytes 2875400 | tf_op jit(solution)/shard_map/ppermute | solution.py:73
  103.6 44.4 %collective-permute-start.12 = (bf16[192,2304]{1,0:T(8,128)(2,1)}, bf16[192,2304]{1,0:T(8,128)(2,1)}, u32[]{:S(2)}, u32[]{:S(2)}) collective-permute-start(bf16[192,2304]{1,0:T(8,128)(2,1)} %get-tuple-element.456), channel_id=1, source_target_pairs={{0,2},{1,3},{2,4},{3,5},{4,6},{5,7},{8,10},{9,11},{10,12},{11,13},... | collective-permute-start | bytes 2654216 | tf_op jit(solution)/shard_map/ppermute | solution.py:69
  106.3 41.7 %collective-permute-start.13 = (bf16[192,2304]{1,0:T(8,128)(2,1)}, bf16[192,2304]{1,0:T(8,128)(2,1)}, u32[]{:S(2)}, u32[]{:S(2)}) collective-permute-start(bf16[192,2304]{1,0:T(8,128)(2,1)} %get-tuple-element.456), channel_id=1, source_target_pairs={{2,0},{3,1},{4,2},{5,3},{6,4},{7,5},{10,8},{11,9},{12,10},{13,11},... | collective-permute-start | bytes 2654216 | tf_op jit(solution)/shard_map/ppermute | solution.py:73
  152.1 24.2 %collective-permute-start.17 = (bf16[192,2304]{1,0:T(8,128)(2,1)}, bf16[192,2304]{1,0:T(8,128)(2,1)}, u32[]{:S(2)}, u32[]{:S(2)}) collective-permute-start(bf16[192,2304]{1,0:T(8,128)(2,1)} %get-tuple-element.454), channel_id=1, source_target_pairs={{0,2},{1,3},{2,4},{3,5},{4,6},{5,7},{8,10},{9,11},{10,12},{11,13},... | collective-permute-start | bytes 2654216 | tf_op jit(solution)/shard_map/ppermute | solution.py:69
  157.7 23.6 %collective-permute-start.18 = (bf16[192,2304]{1,0:T(8,128)(2,1)}, bf16[192,2304]{1,0:T(8,128)(2,1)}, u32[]{:S(2)}, u32[]{:S(2)}) collective-permute-start(bf16[192,2304]{1,0:T(8,128)(2,1)} %get-tuple-element.455), channel_id=1, source_target_pairs={{2,0},{3,1},{4,2},{5,3},{6,4},{7,5},{10,8},{11,9},{12,10},{13,11},... | collective-permute-start | bytes 2654216 | tf_op jit(solution)/shard_map/ppermute | solution.py:73
  184.2 21.1 %collective-permute-start.20 = (bf16[192,2304]{1,0:T(8,128)(2,1)S(1)}, bf16[192,2304]{1,0:T(8,128)(2,1)S(1)}, u32[]{:S(2)}, u32[]{:S(2)}) collective-permute-start(bf16[192,2304]{1,0:T(8,128)(2,1)S(1)} %get-tuple-element.463), channel_id=1, source_target_pairs={{0,2},{1,3},{2,4},{3,5},{4,6},{5,7},{8,10},{9,11},{10,12},{11,13},... | collective-permute-start | bytes 2654216 | tf_op jit(solution)/shard_map/ppermute | solution.py:69
  185.9 23.6 %collective-permute-start.21 = (bf16[192,2304]{1,0:T(8,128)(2,1)S(1)}, bf16[192,2304]{1,0:T(8,128)(2,1)S(1)}, u32[]{:S(2)}, u32[]{:S(2)}) collective-permute-start(bf16[192,2304]{1,0:T(8,128)(2,1)S(1)} %get-tuple-element.464), channel_id=1, source_target_pairs={{2,0},{3,1},{4,2},{5,3},{6,4},{7,5},{10,8},{11,9},{12,10},{13,11},... | collective-permute-start | bytes 2654216 | tf_op jit(solution)/shard_map/ppermute | solution.py:73
  210.2 21.9 %collective-permute-start.23 = (bf16[192,2304]{1,0:T(8,128)(2,1)S(1)}, bf16[192,2304]{1,0:T(8,128)(2,1)S(1)}, u32[]{:S(2)}, u32[]{:S(2)}) collective-permute-start(bf16[192,2304]{1,0:T(8,128)(2,1)S(1)} %get-tuple-element.468), channel_id=1, source_target_pairs={{0,2},{1,3},{2,4},{3,5},{4,6},{5,7},{8,10},{9,11},{10,12},{11,13},... | collective-permute-start | bytes 2654216 | tf_op jit(solution)/shard_map/ppermute | solution.py:69
  213.6 22.7 %collective-permute-start.24 = (bf16[192,2304]{1,0:T(8,128)(2,1)S(1)}, bf16[192,2304]{1,0:T(8,128)(2,1)S(1)}, u32[]{:S(2)}, u32[]{:S(2)}) collective-permute-start(bf16[192,2304]{1,0:T(8,128)(2,1)S(1)} %get-tuple-element.469), channel_id=1, source_target_pairs={{2,0},{3,1},{4,2},{5,3},{6,4},{7,5},{10,8},{11,9},{12,10},{13,11},... | collective-permute-start | bytes 2654216 | tf_op jit(solution)/shard_map/ppermute | solution.py:73
  243.8 22.1 %collective-permute-start.27 = (bf16[192,2304]{1,0:T(8,128)(2,1)}, bf16[192,2304]{1,0:T(8,128)(2,1)}, u32[]{:S(2)}, u32[]{:S(2)}) collective-permute-start(bf16[192,2304]{1,0:T(8,128)(2,1)} %get-tuple-element.497), channel_id=1, source_target_pairs={{2,0},{3,1},{4,2},{5,3},{6,4},{7,5},{10,8},{11,9},{12,10},{13,11},... | collective-permute-start | bytes 2654216 | tf_op jit(solution)/shard_map/ppermute | solution.py:73
  269.1 20.7 %collective-permute-start.29 = (bf16[192,2304]{1,0:T(8,128)(2,1)S(1)}, bf16[192,2304]{1,0:T(8,128)(2,1)S(1)}, u32[]{:S(2)}, u32[]{:S(2)}) collective-permute-start(bf16[192,2304]{1,0:T(8,128)(2,1)S(1)} %get-tuple-element.496), channel_id=1, source_target_pairs={{2,0},{3,1},{4,2},{5,3},{6,4},{7,5},{10,8},{11,9},{12,10},{13,11},... | collective-permute-start | bytes 2654216 | tf_op jit(solution)/shard_map/ppermute | solution.py:73
  427.8 25.2 %collective-permute-start.42 = (bf16[192,2304]{1,0:T(8,128)(2,1)}, bf16[192,2304]{1,0:T(8,128)(2,1)}, u32[]{:S(2)}, u32[]{:S(2)}) collective-permute-start(bf16[192,2304]{1,0:T(8,128)(2,1)} %get-tuple-element.582), channel_id=1, source_target_pairs={{0,2},{1,3},{2,4},{3,5},{4,6},{5,7},{8,10},{9,11},{10,12},{11,13},... | collective-permute-start | bytes 2654216 | tf_op jit(solution)/shard_map/ppermute | solution.py:69
  572.7 27.4 %collective-permute-start.54 = (bf16[192,2304]{1,0:T(8,128)(2,1)}, bf16[192,2304]{1,0:T(8,128)(2,1)S(1)}, u32[]{:S(2)}, u32[]{:S(2)}) collective-permute-start(bf16[192,2304]{1,0:T(8,128)(2,1)} %get-tuple-element.633), channel_id=1, source_target_pairs={{0,2},{1,3},{2,4},{3,5},{4,6},{5,7},{8,10},{9,11},{10,12},{11,13},... | collective-permute-start | bytes 2654216 | tf_op jit(solution)/shard_map/ppermute | solution.py:69
  576.4 23.7 %collective-permute-start.55 = (bf16[192,2304]{1,0:T(8,128)(2,1)}, bf16[192,2304]{1,0:T(8,128)(2,1)S(1)}, u32[]{:S(2)}, u32[]{:S(2)}) collective-permute-start(bf16[192,2304]{1,0:T(8,128)(2,1)} %get-tuple-element.634), channel_id=1, source_target_pairs={{2,0},{3,1},{4,2},{5,3},{6,4},{7,5},{10,8},{11,9},{12,10},{13,11},... | collective-permute-start | bytes 2654216 | tf_op jit(solution)/shard_map/ppermute | solution.py:73
  603.3 30.2 %collective-permute-start.56 = (bf16[192,2304]{1,0:T(8,128)(2,1)}, bf16[192,2304]{1,0:T(8,128)(2,1)S(1)}, u32[]{:S(2)}, u32[]{:S(2)}) collective-permute-start(bf16[192,2304]{1,0:T(8,128)(2,1)} %get-tuple-element.646), channel_id=1, source_target_pairs={{0,2},{1,3},{2,4},{3,5},{4,6},{5,7},{8,10},{9,11},{10,12},{11,13},... | collective-permute-start | bytes 2654216 | tf_op jit(solution)/shard_map/ppermute | solution.py:69
  608.0 25.5 %collective-permute-start.57 = (bf16[192,2304]{1,0:T(8,128)(2,1)}, bf16[192,2304]{1,0:T(8,128)(2,1)S(1)}, u32[]{:S(2)}, u32[]{:S(2)}) collective-permute-start(bf16[192,2304]{1,0:T(8,128)(2,1)} %get-tuple-element.647), channel_id=1, source_target_pairs={{2,0},{3,1},{4,2},{5,3},{6,4},{7,5},{10,8},{11,9},{12,10},{13,11},... | collective-permute-start | bytes 2654216 | tf_op jit(solution)/shard_map/ppermute | solution.py:73
  637.8 36.5 %collective-permute-start.60 = (bf16[1152,2304]{1,0:T(8,128)(2,1)}, bf16[1152,2304]{1,0:T(8,128)(2,1)}, u32[]{:S(2)}, u32[]{:S(2)}) collective-permute-start(bf16[1152,2304]{1,0:T(8,128)(2,1)} %fusion.3), channel_id=1, source_target_pairs={{0,1},{1,0},{2,3},{3,2},{4,5},{5,4},{6,7},{7,6},{8,9},{9,8},{10,11... | collective-permute-start | bytes 15925256 | tf_op jit(solution)/shard_map/ppermute | solution.py:76
  637.8 45.9 %collective-permute-start.58 = (bf16[192,2304]{1,0:T(8,128)(2,1)S(1)}, bf16[192,2304]{1,0:T(8,128)(2,1)S(1)}, u32[]{:S(2)}, u32[]{:S(2)}) collective-permute-start(bf16[192,2304]{1,0:T(8,128)(2,1)S(1)} %get-tuple-element.693), channel_id=1, source_target_pairs={{0,2},{1,3},{2,4},{3,5},{4,6},{5,7},{8,10},{9,11},{10,12},{11,13},... | collective-permute-start | bytes 2654216 | tf_op jit(solution)/shard_map/ppermute | solution.py:69
  642.7 41.0 %collective-permute-start.59 = (bf16[192,2304]{1,0:T(8,128)(2,1)S(1)}, bf16[192,2304]{1,0:T(8,128)(2,1)S(1)}, u32[]{:S(2)}, u32[]{:S(2)}) collective-permute-start(bf16[192,2304]{1,0:T(8,128)(2,1)S(1)} %get-tuple-element.693), channel_id=1, source_target_pairs={{2,0},{3,1},{4,2},{5,3},{6,4},{7,5},{10,8},{11,9},{12,10},{13,11},... | collective-permute-start | bytes 2654216 | tf_op jit(solution)/shard_map/ppermute | solution.py:73
  685.5 24.4 %collective-permute-start.61 = (bf16[192,2304]{1,0:T(8,128)(2,1)}, bf16[192,2304]{1,0:T(8,128)(2,1)}, u32[]{:S(2)}, u32[]{:S(2)}) collective-permute-start(bf16[192,2304]{1,0:T(8,128)(2,1)} %get-tuple-element.678), channel_id=1, source_target_pairs={{0,2},{1,3},{2,4},{3,5},{4,6},{5,7},{8,10},{9,11},{10,12},{11,13},... | collective-permute-start | bytes 2654216 | tf_op jit(solution)/shard_map/ppermute | solution.py:69
  691.2 23.8 %collective-permute-start.62 = (bf16[192,2304]{1,0:T(8,128)(2,1)}, bf16[192,2304]{1,0:T(8,128)(2,1)}, u32[]{:S(2)}, u32[]{:S(2)}) collective-permute-start(bf16[192,2304]{1,0:T(8,128)(2,1)} %get-tuple-element.679), channel_id=1, source_target_pairs={{2,0},{3,1},{4,2},{5,3},{6,4},{7,5},{10,8},{11,9},{12,10},{13,11},... | collective-permute-start | bytes 2654216 | tf_op jit(solution)/shard_map/ppermute | solution.py:73
  728.8 377.5 %all-reduce.6.cloned.1.call-start = ((), (), s32[]{:S(2)}) async-start(), calls=%async_computation | async-start | bytes 10616832 | tf_op jit(solution)/shard_map/psum | solution.py:838
  734.5 20.9 %collective-permute-start.64 = (bf16[192,2304]{1,0:T(8,128)(2,1)}, bf16[192,2304]{1,0:T(8,128)(2,1)}, u32[]{:S(2)}, u32[]{:S(2)}) collective-permute-start(bf16[192,2304]{1,0:T(8,128)(2,1)} %get-tuple-element.685), channel_id=1, source_target_pairs={{0,2},{1,3},{2,4},{3,5},{4,6},{5,7},{8,10},{9,11},{10,12},{11,13},... | collective-permute-start | bytes 2654216 | tf_op jit(solution)/shard_map/ppermute | solution.py:69
  736.9 23.5 %collective-permute-start.65 = (bf16[192,2304]{1,0:T(8,128)(2,1)}, bf16[192,2304]{1,0:T(8,128)(2,1)}, u32[]{:S(2)}, u32[]{:S(2)}) collective-permute-start(bf16[192,2304]{1,0:T(8,128)(2,1)} %get-tuple-element.686), channel_id=1, source_target_pairs={{2,0},{3,1},{4,2},{5,3},{6,4},{7,5},{10,8},{11,9},{12,10},{13,11},... | collective-permute-start | bytes 2654216 | tf_op jit(solution)/shard_map/ppermute | solution.py:73
  763.8 23.6 %collective-permute-start.67 = (bf16[192,2304]{1,0:T(8,128)(2,1)S(1)}, bf16[192,2304]{1,0:T(8,128)(2,1)S(1)}, u32[]{:S(2)}, u32[]{:S(2)}) collective-permute-start(bf16[192,2304]{1,0:T(8,128)(2,1)S(1)} %get-tuple-element.691), channel_id=1, source_target_pairs={{0,2},{1,3},{2,4},{3,5},{4,6},{5,7},{8,10},{9,11},{10,12},{11,13},... | collective-permute-start | bytes 2654216 | tf_op jit(solution)/shard_map/ppermute | solution.py:69
  765.4 22.5 %collective-permute-start.68 = (bf16[192,2304]{1,0:T(8,128)(2,1)S(1)}, bf16[192,2304]{1,0:T(8,128)(2,1)S(1)}, u32[]{:S(2)}, u32[]{:S(2)}) collective-permute-start(bf16[192,2304]{1,0:T(8,128)(2,1)S(1)} %get-tuple-element.692), channel_id=1, source_target_pairs={{2,0},{3,1},{4,2},{5,3},{6,4},{7,5},{10,8},{11,9},{12,10},{13,11},... | collective-permute-start | bytes 2654216 | tf_op jit(solution)/shard_map/ppermute | solution.py:73
  792.2 21.9 %collective-permute-start.69 = (bf16[192,2304]{1,0:T(8,128)(2,1)S(1)}, bf16[192,2304]{1,0:T(8,128)(2,1)S(1)}, u32[]{:S(2)}, u32[]{:S(2)}) collective-permute-start(bf16[192,2304]{1,0:T(8,128)(2,1)S(1)} %get-tuple-element.738), channel_id=1, source_target_pairs={{0,2},{1,3},{2,4},{3,5},{4,6},{5,7},{8,10},{9,11},{10,12},{11,13},... | collective-permute-start | bytes 2654216 | tf_op jit(solution)/shard_map/ppermute | solution.py:69
  796.2 22.1 %collective-permute-start.70 = (bf16[192,2304]{1,0:T(8,128)(2,1)S(1)}, bf16[192,2304]{1,0:T(8,128)(2,1)S(1)}, u32[]{:S(2)}, u32[]{:S(2)}) collective-permute-start(bf16[192,2304]{1,0:T(8,128)(2,1)S(1)} %get-tuple-element.738), channel_id=1, source_target_pairs={{2,0},{3,1},{4,2},{5,3},{6,4},{7,5},{10,8},{11,9},{12,10},{13,11},... | collective-permute-start | bytes 2654216 | tf_op jit(solution)/shard_map/ppermute | solution.py:73
  821.9 21.2 %collective-permute-start.73 = (bf16[192,2304]{1,0:T(8,128)(2,1)S(1)}, bf16[192,2304]{1,0:T(8,128)(2,1)}, u32[]{:S(2)}, u32[]{:S(2)}) collective-permute-start(bf16[192,2304]{1,0:T(8,128)(2,1)S(1)} %get-tuple-element.729), channel_id=1, source_target_pairs={{2,0},{3,1},{4,2},{5,3},{6,4},{7,5},{10,8},{11,9},{12,10},{13,11},... | collective-permute-start | bytes 2654216 | tf_op jit(solution)/shard_map/ppermute | solution.py:73
  874.3 27.1 %collective-permute-start.76 = (bf16[192,2304]{1,0:T(8,128)(2,1)S(1)}, bf16[192,2304]{1,0:T(8,128)(2,1)}, u32[]{:S(2)}, u32[]{:S(2)}) collective-permute-start(bf16[192,2304]{1,0:T(8,128)(2,1)S(1)} %get-tuple-element.736), channel_id=1, source_target_pairs={{0,2},{1,3},{2,4},{3,5},{4,6},{5,7},{8,10},{9,11},{10,12},{11,13},... | collective-permute-start | bytes 2654216 | tf_op jit(solution)/shard_map/ppermute | solution.py:69
  876.6 24.8 %collective-permute-start.77 = (bf16[192,2304]{1,0:T(8,128)(2,1)S(1)}, bf16[192,2304]{1,0:T(8,128)(2,1)}, u32[]{:S(2)}, u32[]{:S(2)}) collective-permute-start(bf16[192,2304]{1,0:T(8,128)(2,1)S(1)} %get-tuple-element.737), channel_id=1, source_target_pairs={{2,0},{3,1},{4,2},{5,3},{6,4},{7,5},{10,8},{11,9},{12,10},{13,11},... | collective-permute-start | bytes 2654216 | tf_op jit(solution)/shard_map/ppermute | solution.py:73
  936.8 24.3 %collective-permute-start.79 = (bf16[208,2304]{1,0:T(8,128)(2,1)}, bf16[208,2304]{1,0:T(8,128)(2,1)S(1)}, u32[]{:S(2)}, u32[]{:S(2)}) collective-permute-start(bf16[208,2304]{1,0:T(8,128)(2,1)} %pad_maximum_fusion.12), channel_id=1, source_target_pairs={{0,2},{1,3},{8,10},{9,11},{16,18},{17,19},{24,26},{25,27}} | collective-permute-start | bytes 2875400 | tf_op jit(solution)/shard_map/ppermute | solution.py:69
  940.4 20.7 %collective-permute-start.80 = (bf16[208,2304]{1,0:T(8,128)(2,1)}, bf16[208,2304]{1,0:T(8,128)(2,1)S(1)}, u32[]{:S(2)}, u32[]{:S(2)}) collective-permute-start(bf16[208,2304]{1,0:T(8,128)(2,1)} %pad_maximum_fusion.12), channel_id=1, source_target_pairs={{6,4},{7,5},{14,12},{15,13},{22,20},{23,21},{30,28},{31,29}} | collective-permute-start | bytes 2875400 | tf_op jit(solution)/shard_map/ppermute | solution.py:73
  961.9 24.3 %collective-permute-start.81 = (bf16[208,2304]{1,0:T(8,128)(2,1)S(1)}, bf16[208,2304]{1,0:T(8,128)(2,1)S(1)}, u32[]{:S(2)}, u32[]{:S(2)}) collective-permute-start(bf16[208,2304]{1,0:T(8,128)(2,1)S(1)} %get-tuple-element.790), channel_id=1, source_target_pairs={{0,2},{1,3},{2,4},{3,5},{8,10},{9,11},{10,12},{11,13},{16,18},{17,... | collective-permute-start | bytes 2875400 | tf_op jit(solution)/shard_map/ppermute | solution.py:69
  986.8 31.3 %collective-permute-start.93 = (bf16[384,1152]{1,0:T(8,128)(2,1)S(1)}, bf16[384,1152]{1,0:T(8,128)(2,1)S(1)}, u32[]{:S(2)}, u32[]{:S(2)}) collective-permute-start(bf16[384,1152]{1,0:T(8,128)(2,1)S(1)} %constant_dynamic-slice_fusion.1), channel_id=1, source_target_pairs={{0,16},{8,24},{16,0},{24,8},{1,17},{9,25},{17,1},{25,9},{2,18},{10... | collective-permute-start | bytes 2654216 | tf_op jit(solution)/shard_map/ppermute | solution.py:841
  988.2 32.6 %collective-permute-start.89 = (bf16[384,1152]{1,0:T(8,128)(2,1)S(1)}, bf16[384,1152]{1,0:T(8,128)(2,1)S(1)}, u32[]{:S(2)}, u32[]{:S(2)}) collective-permute-start(bf16[384,1152]{1,0:T(8,128)(2,1)S(1)} %constant_dynamic-slice_fusion.3), channel_id=1, source_target_pairs={{0,8},{8,0},{16,24},{24,16},{1,9},{9,1},{17,25},{25,17},{2,10},{10... | collective-permute-start | bytes 2654216 | tf_op jit(solution)/shard_map/ppermute | solution.py:841
  989.6 32.8 %collective-permute-start.87 = (bf16[208,2304]{1,0:T(8,128)(2,1)S(1)}, bf16[208,2304]{1,0:T(8,128)(2,1)S(1)}, u32[]{:S(2)}, u32[]{:S(2)}) collective-permute-start(bf16[208,2304]{1,0:T(8,128)(2,1)S(1)} %get-tuple-element.798), channel_id=1, source_target_pairs={{0,2},{1,3},{2,4},{3,5},{4,6},{5,7},{8,10},{9,11},{10,12},{11,13},... | collective-permute-start | bytes 2875400 | tf_op jit(solution)/shard_map/ppermute | solution.py:69
  997.9 24.5 %collective-permute-start.88 = (bf16[208,2304]{1,0:T(8,128)(2,1)S(1)}, bf16[208,2304]{1,0:T(8,128)(2,1)S(1)}, u32[]{:S(2)}, u32[]{:S(2)}) collective-permute-start(bf16[208,2304]{1,0:T(8,128)(2,1)S(1)} %get-tuple-element.799), channel_id=1, source_target_pairs={{2,0},{3,1},{4,2},{5,3},{6,4},{7,5},{10,8},{11,9},{12,10},{13,11},... | collective-permute-start | bytes 2875400 | tf_op jit(solution)/shard_map/ppermute | solution.py:73
  1019.3 22.6 %collective-permute-start.94 = (bf16[192,1152]{1,0:T(8,128)(2,1)}, bf16[192,1152]{1,0:T(8,128)(2,1)}, u32[]{:S(2)}, u32[]{:S(2)}) collective-permute-start(bf16[192,1152]{1,0:T(8,128)(2,1)} %constant_dynamic-slice_fusion), channel_id=1, source_target_pairs={{0,8},{8,0},{16,24},{24,16},{1,9},{9,1},{17,25},{25,17},{2,10},{10... | collective-permute-start | bytes 1327112 | tf_op jit(solution)/shard_map/ppermute | solution.py:841
  1021.9 23.0 %collective-permute-start.90 = (bf16[192,1152]{1,0:T(8,128)(2,1)}, bf16[192,1152]{1,0:T(8,128)(2,1)}, u32[]{:S(2)}, u32[]{:S(2)}) collective-permute-start(bf16[192,1152]{1,0:T(8,128)(2,1)} %constant_dynamic-slice_fusion.2), channel_id=1, source_target_pairs={{0,16},{8,24},{16,0},{24,8},{1,17},{9,25},{17,1},{25,9},{2,18},{10... | collective-permute-start | bytes 1327112 | tf_op jit(solution)/shard_map/ppermute | solution.py:841
  1041.6 25.7 %collective-permute-start.99 = (f32[4,288]{1,0:T(4,128)S(1)}, f32[4,288]{1,0:T(4,128)S(1)}, u32[]{:S(2)}, u32[]{:S(2)}) collective-permute-start(f32[4,288]{1,0:T(4,128)S(1)} %add.445), channel_id=1, source_target_pairs={{0,16},{8,24},{16,0},{24,8},{1,17},{9,25},{17,1},{25,9},{2,18},{10... | collective-permute-start | bytes 13832 | tf_op jit(solution)/shard_map/ppermute | solution.py:841
  1057.8 42.7 %collective-permute-start.96 = (bf16[384,1152]{1,0:T(8,128)(2,1)S(1)}, bf16[384,1152]{1,0:T(8,128)(2,1)S(1)}, u32[]{:S(2)}, u32[]{:S(2)}) collective-permute-start(bf16[384,1152]{1,0:T(8,128)(2,1)S(1)} %pad_maximum_fusion.14), channel_id=1, source_target_pairs={{0,16},{8,24},{16,0},{24,8},{1,17},{9,25},{17,1},{25,9},{2,18},{10... | collective-permute-start | bytes 2654216 | tf_op jit(solution)/shard_map/ppermute | solution.py:841
  1065.9 34.9 %collective-permute-start.92 = (bf16[384,1152]{1,0:T(8,128)(2,1)S(1)}, bf16[384,1152]{1,0:T(8,128)(2,1)S(1)}, u32[]{:S(2)}, u32[]{:S(2)}) collective-permute-start(bf16[384,1152]{1,0:T(8,128)(2,1)S(1)} %pad_maximum_fusion.13), channel_id=1, source_target_pairs={{0,8},{8,0},{16,24},{24,16},{1,9},{9,1},{17,25},{25,17},{2,10},{10... | collective-permute-start | bytes 2654216 | tf_op jit(solution)/shard_map/ppermute | solution.py:841
  (309 other events, 3199.4 us)
Sparse Core Ops, SparseCore 0:
  728.9 207.8 all-reduce.7
  940.1 163.5 all-reduce.5
